TPU v7x, 32 devices: a whole 2x2x4 slice. The times are simulated.
32 devices in a mesh: seq: 16 (over z, y, core), tp: 2 (over x).
Axes of the slice: x: 2, y: 2, z: 4, core: 2. Of those that a mesh axis runs over, the one named last changes fastest.
Arguments:
- stream: bfloat16 [2048, 8192], P('seq', 'tp'), may hold values from -6 to 6
- hidden: bfloat16 [14336, 2048], P('seq'), may hold values from -6 to 6
- final_gain: bfloat16 [8192], P('tp'), may hold values from 0.099609375 to 1.8984375
- value_head: bfloat16 [8192], P('tp'), may hold values from -0.0625 to 0.0625
- rewards: float32 [2048], P('seq'), may hold values from -3 to 3
- kl_terms: float32 [2048], P('seq'), may hold values from -6 to 6
- resets: int32 [2048], P('seq'), may hold values 0 or 1
Outputs:
- values: float32 [2048], P('seq')
- returns: float32 [2048], P('seq')
- grad_head: float32 [8192], P('tp')
- grad_down: bfloat16 [14336, 8192], P('seq', 'tp')
All inputs are finite; a program needn't handle non-finite values. No bound on the sum of `resets` on one device may be relied on, other than what follows from the above.
Results may differ from a plain program's by a relative error of at most 0.0049.
Values may be sent and summed in bfloat16 or wider, within the bound.
No kernel may reach another device: no remote copies, remote signals or barrier semaphores. Data moves between devices by JAX's collectives and lax.ppermute only.
A program may use at most 64 MiB of HBM per device.

v0:
```python
import jax
import jax.numpy as jnp
from jax import lax
from jax.sharding import PartitionSpec as P

D = 8192


epsilon = 1e-05


def body(stream, hidden, final_gain, value_head, rewards, kl_terms, resets):
    tok_local = stream.shape[0]
    seq_count = lax.axis_size("seq")
    stream_f = stream.astype(jnp.float32)
    head_vector = final_gain.astype(jnp.float32) * value_head.astype(jnp.float32)
    sum_squares, head_dot = lax.psum(
        (jnp.sum(stream_f * stream_f, axis=-1), jnp.sum(stream_f * head_vector, axis=-1)), "tp"
    )
    inv_rms = lax.rsqrt(sum_squares / D + epsilon)
    values = inv_rms * head_dot
    step_reward = rewards - 0.2 * kl_terms
    before = jnp.cumsum(resets) - resets
    total_resets = jnp.sum(resets)
    positions = jnp.arange(tok_local)
    reach_mask = (positions[None, :] >= positions[:, None]) & (before[None, :] == before[:, None])
    local_return = jnp.sum(jnp.where(reach_mask, step_reward[None, :], 0.0), axis=1)
    passing = jnp.where(before == total_resets, 1.0, 0.0).astype(jnp.float32)
    shard_value = local_return[0]
    shard_pass = passing[0]
    all_value, all_pass = (
        lax.all_gather(shard_value[None], "seq", axis=0, tiled=True),
        lax.all_gather(shard_pass[None], "seq", axis=0, tiled=True),
    )
    shard_ids = jnp.arange(seq_count)
    own_index = lax.axis_index("seq")
    blocked = jnp.where(all_pass > 0.5, 0, 1).astype(jnp.int32)
    blocked_upto = jnp.cumsum(blocked)
    own_blocked = jnp.sum(jnp.where(shard_ids == own_index, blocked_upto, 0))
    open_path = (shard_ids > own_index) & (blocked_upto - blocked - own_blocked == 0)
    incoming = jnp.sum(jnp.where(open_path, all_value, 0.0))
    returns = local_return + passing * incoming
    value_error = values - returns
    head_total = lax.psum(jnp.sum((value_error * inv_rms)[:, None] * stream_f, axis=0), "seq")
    grad_head = final_gain.astype(jnp.float32) * head_total
    dstream = (
        value_error[:, None]
        * (inv_rms[:, None] * head_vector - (inv_rms**3 * head_dot / D)[:, None] * stream_f)
    ).astype(jnp.bfloat16)
    grad_sum = jnp.dot(
        hidden,
        lax.all_gather(dstream, "seq", axis=0, tiled=True),
        preferred_element_type=jnp.float32,
    )
    grad_down = grad_sum.astype(jnp.bfloat16)
    return (values, returns, grad_head, grad_down)


def solution(mesh):
    placed = (P("seq", "tp"), P("seq", None), P("tp"), P("tp"), P("seq"), P("seq"), P("seq"))
    return jax.shard_map(
        body,
        mesh=mesh,
        in_specs=placed,
        out_specs=(P("seq"), P("seq"), P("tp"), P("seq", "tp")),
        check_vma=False,
    )
```

profile of v0, /device:TPU:0, one launch (start us, length us, event | category | flops | bytes accessed | tf_op | source)
XLA Modules:
  0.0 226.4 jit_solution(15800078067784917497)
XLA Ops:
  7.2 0.0 copy-start
  7.2 0.0 all-gather.2.cloned.1.call-start
  7.2 1.4 reduce_sum.66
  8.6 0.8 copy.17
  9.4 0.2 reduce-window.18
  9.5 0.1 reduce
  9.6 1.2 dynamic-slice
  10.9 1.3 compare_select_fusion.2
  12.2 0.2 select_reduce_fusion
  12.4 0.7 slice_dynamic-update-slice_fusion.1
  13.2 0.7 slice_dynamic-update-slice_fusion
  13.9 34.9 %all-reduce.2 = (f32[16]{0:T(128)S(1)}, f32[16]{0:T(128)S(1)}) all-reduce(f32[16]{0:T(128)S(1)} %slice_dynamic-update-slice_fusion, f32[16]{0:T(128)S(1)} %slice_dynamic-update-slice_fusion.1), channel_id=1, replica_groups=mesh['seq'=16,'tp'=2] {'seq'}, use_global_device_ids=true, to_apply=%add.1 | all-reduce | flops 32 | bytes 256
  48.8 0.1 copy.18
  48.9 0.1 reduce.1
  49.1 0.7 convert_multiply_fusion.5
  49.8 0.0 copy-start.1
  49.8 1.7 fusion
  51.4 4.9 %all-reduce.3 = (f32[128]{0:T(128)S(1)}, f32[128]{0:T(128)S(1)}) all-reduce(f32[128]{0:T(128)S(1)} %get-tuple-element.17, f32[128]{0:T(128)S(1)} %get-tuple-element.16), channel_id=1, replica_groups=mesh['seq'=16,'tp'=2] {'tp'}, use_global_device_ids=true, to_apply=%region_3.0 | all-reduce | flops 256 | bytes 2048 | tf_op jit(solution)/shard_map/psum | solution.py:17
  56.4 0.6 fusion.8
  57.0 1.2 fusion.10
  58.3 1.2 fusion.12
  59.4 0.0 copy-done
  59.4 1.7 fusion.5
  61.1 0.0 all-gather.2.cloned.1.call-update
  61.2 59.4 %psum.23 = f32[4096]{0:T(1024)S(1)} all-reduce(f32[4096]{0:T(1024)S(1)} %get-tuple-element.29), channel_id=1, replica_groups=mesh['seq'=16,'tp'=2] {'seq'}, use_global_device_ids=true, to_apply=%region_11.12 | all-reduce | flops 4096 | bytes 32768 | tf_op jit(solution)/shard_map/psum | solution.py:44
  120.5 0.0 copy-done.1
  120.5 0.6 convert_multiply_fusion.4
  121.1 64.8 %all-gather.2.cloned.1.call-done = bf16[2048,4096]{1,0:T(8,128)(2,1)} async-done(((bf16[128,4096]{1,0:T(8,128)(2,1)}), bf16[2048,4096]{1,0:T(8,128)(2,1)}) %all-gather.2.cloned.1.call-update) | async-done | bytes 16777232 | tf_op jit(solution)/shard_map/all_gather | solution.py:52
  186.0 22.8 %convert_bitcast_fusion = bf16[896,4096]{0,1:T(8,128)(2,1)} fusion(bf16[2048,4096]{1,0:T(8,128)(2,1)} %all-gather.2.cloned.1.call-done, bf16[896,2048]{1,0:T(8,128)(2,1)} %param.8), kind=kOutput, calls=%fused_computation | convolution fusion | flops 15036055552 | bytes 27787264 | tf_op jit(solution)/shard_map/dot_general | solution.py:50
  208.8 10.8 %copy.19 = bf16[896,4096]{1,0:T(8,128)(2,1)} copy(bf16[896,4096]{0,1:T(8,128)(2,1)} %convert_bitcast_fusion) | data formatting | bytes 14680064
  (4 shorter events, 0.0 us)
Async XLA Ops:
  7.2 52.3 %copy-start = (bf16[128,4096]{1,0:T(8,128)(2,1)S(1)}, bf16[128,4096]{1,0:T(8,128)(2,1)}, u32[]{:S(2)}) copy-start(bf16[128,4096]{1,0:T(8,128)(2,1)} %param.7) | copy-start | bytes 3145732
  7.2 178.8 %all-gather.2.cloned.1.call-start = ((), (), s32[]{:S(2)}) async-start(), calls=%async_computation | async-start | bytes 17825792 | tf_op jit(solution)/shard_map/all_gather | solution.py:52
  49.8 70.8 %copy-start.1 = (bf16[4096]{0:T(1024)(128)(2,1)S(1)}, bf16[4096]{0:T(1024)(128)(2,1)}, u32[]{:S(2)}) copy-start(bf16[4096]{0:T(1024)(128)(2,1)} %param.9) | copy-start | bytes 24580
Sparse Core Ops, SparseCore 0:
  61.3 124.6 all-gather.1
where the time goes:
time: 227 us; the launch traced here: 226 us
  blocking collectives  99.2 us (44%)
  waiting for transfers between devices  64.9 us (29%)
  matrix products  22.8 us (10%)
  local copies, waits for them, and re-layouts  14.4 us (6%)
  between operations  14.1 us (6%)
  other arithmetic  11.1 us (5%)
    all_gather x1, waiting for transfers between devices, body(): lax.all_gather(dstream, 'seq', axis=0, tiled=True)  64.8 us
    psum x1, blocking collectives, body(): lax.psum(jnp.sum((value_error * inv_rms)[:, None] * stream_f, axis=0), 's...  59.4 us
    unnamed x1, blocking collectives  34.9 us
    dot_general x1, matrix products, body(): jnp.dot(hidden, lax.all_gather(dstream, 'seq', axis=0, tiled=True), prefe...  22.8 us
    unnamed x10, local copies, waits for them, and re-layouts  13.5 us
    psum x1, blocking collectives, body(): lax.psum((jnp.sum(stream_f * stream_f, axis=-1), jnp.sum(stream_f * head_...  4.94 us
  transfers between devices with their start and end apart: 1, of which 1 were waited for; matrix products, arithmetic and copies ran while one was open for 0% of the time, Pallas kernels for 0%

commit v1 on v0

v1 whole, which is shorter than its diff:
```python
import jax
import jax.numpy as jnp
from jax import lax
from jax.experimental import pallas as pl
from jax.experimental.pallas import tpu as pltpu
from jax.sharding import PartitionSpec as P

EPSILON = 1e-05


def product_kernel(gathered, hidden, coefs, head, gain, grad_down, grad_head):
    stream_f = gathered[...].astype(jnp.float32)
    error = coefs[:, 0:1]
    scale = coefs[:, 1:2]
    pull = coefs[:, 2:3]
    weight = coefs[:, 3:4]
    dstream = (error * (scale * head[...] - pull * stream_f)).astype(jnp.bfloat16)
    grad_head[...] = gain[...] * jnp.sum(weight * stream_f, axis=0, keepdims=True)
    grad_down[...] = jnp.dot(hidden[...], dstream, preferred_element_type=jnp.float32).astype(jnp.bfloat16)


def product(gathered, hidden, coefs, head, gain):
    tokens, width = gathered.shape
    units = hidden.shape[0]
    tile = min(width, max(128, (1 << 20) // tokens))
    steps = width // tile
    return pl.pallas_call(
        product_kernel,
        grid=(steps,),
        in_specs=[
            pl.BlockSpec((tokens, tile), lambda i: (0, i)),
            pl.BlockSpec((units, tokens), lambda i: (0, 0)),
            pl.BlockSpec((tokens, 4), lambda i: (0, 0)),
            pl.BlockSpec((1, tile), lambda i: (0, i)),
            pl.BlockSpec((1, tile), lambda i: (0, i)),
        ],
        out_specs=[
            pl.BlockSpec((units, tile), lambda i: (0, i)),
            pl.BlockSpec((1, tile), lambda i: (0, i)),
        ],
        out_shape=[
            jax.ShapeDtypeStruct((units, width), jnp.bfloat16),
            jax.ShapeDtypeStruct((1, width), jnp.float32),
        ],
        compiler_params=pltpu.CompilerParams(vmem_limit_bytes=48 * 1024 * 1024),
        cost_estimate=pl.CostEstimate(
            flops=2 * units * tokens * width,
            bytes_accessed=2 * (units * tokens + tokens * width + units * width),
            transcendentals=0,
        ),
    )(gathered, hidden, coefs, head, gain)


def all_returns(step_reward, resets):
    shards, tok = step_reward.shape
    position = jnp.arange(tok)
    before = jnp.cumsum(resets, axis=1) - resets
    total = jnp.sum(resets, axis=1, keepdims=True)
    reach = (position[None, :] >= position[:, None])[None] & (before[:, None, :] == before[:, :, None])
    local = jnp.sum(jnp.where(reach, step_reward[:, None, :], 0.0), axis=2)
    passing = before == total
    blocked = jnp.where(passing[:, 0], 0.0, 1.0)
    upto = jnp.cumsum(blocked)
    ids = jnp.arange(shards)
    open_path = (ids[None, :] > ids[:, None]) & ((upto - blocked)[None, :] == upto[:, None])
    incoming = jnp.sum(jnp.where(open_path, local[None, :, 0], 0.0), axis=1)
    return local + jnp.where(passing, incoming[:, None], 0.0)


def make_body(width, shards, halves):
    def body(stream, hidden, final_gain, value_head, rewards, kl_terms, resets):
        tok = stream.shape[0]
        gathered = lax.all_gather(stream, "seq", axis=0, tiled=True)
        stream_f = stream.astype(jnp.float32)
        gain = final_gain.astype(jnp.float32)
        head = gain * value_head.astype(jnp.float32)
        share = jnp.where(lax.axis_index("tp") == 0, 1.0, 0.0)
        own = jnp.stack(
            [
                jnp.sum(stream_f * stream_f, axis=-1),
                jnp.sum(stream_f * head, axis=-1),
                (rewards - 0.2 * kl_terms) * share,
                resets.astype(jnp.float32) * share,
            ]
        )
        me = lax.axis_index("seq")
        mine = jnp.arange(shards)[:, None, None] == me
        facts = lax.psum(jnp.where(mine, own[None], 0.0), ("seq", "tp"))
        sum_squares, along, step_reward, cut = (facts[:, k] for k in range(4))
        scale = lax.rsqrt(sum_squares / width + EPSILON)
        values = scale * along
        returns = all_returns(step_reward, cut)
        error = values - returns
        pull = scale**3 * along / width
        coefs = jnp.stack([error, scale, pull, error * scale], axis=-1).reshape(shards * tok, 4)
        grad_down, grad_head = product(gathered, hidden, coefs, head[None], gain[None])
        pick = lambda a: lax.dynamic_index_in_dim(a, me, 0, keepdims=False)
        return (pick(values), pick(returns), grad_head[0], grad_down)

    return body


def solution(mesh):
    placed = (P("seq", "tp"), P("seq", None), P("tp"), P("tp"), P("seq"), P("seq"), P("seq"))

    def run(stream, *rest):
        body = make_body(stream.shape[1], mesh.shape["seq"], mesh.shape["tp"])
        return jax.shard_map(
            body,
            mesh=mesh,
            in_specs=placed,
            out_specs=(P("seq"), P("seq"), P("tp"), P("seq", "tp")),
            check_vma=False,
        )(stream, *rest)

    return run
```

time: 227 us -> 174 us (0.77)
  blocking collectives: 99.2 us -> 45.2 us
  Pallas kernels: 0 us -> 23.5 us
  matrix products: 22.8 us -> 0 us
  waiting for transfers between devices: 64.9 us -> 80.5 us
  local copies, waits for them, and re-layouts: 14.4 us -> 3.26 us
  other arithmetic: 11.1 us -> 6.53 us
    unnamed x1 -> x0, blocking collectives: 34.9 us -> none
    pallas_call x0 -> x1, Pallas kernels: none -> 23.5 us  [product(): pl.pallas_call(product_kernel, grid=(steps,), in_specs=[pl.BlockSpec((tok...]
    dot_general x1 -> x0, matrix products: 22.8 us -> none  [body(): jnp.dot(hidden, lax.all_gather(dstream, 'seq', axis=0, tiled=True), prefe...]
    psum x2 -> x1, blocking collectives: 64.3 us -> 45.2 us  [body(): facts = lax.psum(jnp.where(mine, own[None], 0.0), ('seq', 'tp'))]
    all_gather x1, waiting for transfers between devices: 64.8 us -> 79.9 us  [body(): gathered = lax.all_gather(stream, 'seq', axis=0, tiled=True)]
    unnamed x10 -> x8, local copies, waits for them, and re-layouts: 13.5 us -> 2.05 us
    reduce_sum x4 -> x2, other arithmetic: 3.42 us -> 0.83 us  [the longest x1 0.65 us: all_returns(): local = jnp.sum(jnp.where(reach, step_reward[:, None, :], 0.0), axis=2)]
  transfers between devices with their start and end apart: 1 -> 1, of which waited for: 1 -> 1; matrix products, arithmetic and copies ran while one was open for 0% -> 4% of each run, Pallas kernels for 0% -> 0%
where the time goes in v1:
time: 174 us; the launch traced here: 173 us
  waiting for transfers between devices  80.5 us (46%)
  blocking collectives  45.2 us (26%)
  Pallas kernels  23.5 us (14%)
  between operations  14.2 us (8%)
  other arithmetic  6.53 us (4%)
  local copies, waits for them, and re-layouts  3.26 us (2%)
    all_gather x1, waiting for transfers between devices, body(): gathered = lax.all_gather(stream, 'seq', axis=0, tiled=True)  79.9 us
    psum x1, blocking collectives, body(): facts = lax.psum(jnp.where(mine, own[None], 0.0), ('seq', 'tp'))  45.2 us
    pallas_call x1, Pallas kernels, product(): pl.pallas_call(product_kernel, grid=(steps,), in_specs=[pl.BlockSpec((tok...  23.5 us
  transfers between devices with their start and end apart: 1, of which 1 were waited for; matrix products, arithmetic and copies ran while one was open for 4% of the time, Pallas kernels for 0%

profile of v1, /device:TPU:0, one launch (start us, length us, event | category | flops | bytes accessed | tf_op | source)
XLA Modules:
  0.0 173.2 jit_solution(17818719614751797766)
XLA Ops:
  7.2 0.0 copy-start.1
  7.2 0.0 copy-start.3
  7.2 0.0 copy-start.2
  7.2 0.0 all-gather.2.cloned.1.call-start
  7.2 0.7 all-gather.2.cloned.1.call-update
  7.9 0.7 convert_element_type.13
  8.6 0.7 convert_multiply_fusion.2
  9.4 1.7 fusion
  11.0 0.0 copy-done.1
  11.0 0.0 copy-done.3
  11.0 0.0 copy-done.2
  11.1 0.1 broadcast_select_fusion
  11.2 45.2 %psum.7 = f32[16,4,128]{2,0,1:T(8,128)S(1)} all-reduce(f32[16,4,128]{2,0,1:T(8,128)S(1)} %broadcast_select_fusion), channel_id=1, replica_groups=mesh['seq'=16,'tp'=2] {'seq','tp'}, use_global_device_ids=true, to_apply=%region_2.3 | all-reduce | flops 8192 | bytes 65536 | tf_op jit(solution)/shard_map/psum | solution.py:88
  56.4 0.1 fusion.17
  56.5 0.3 reduce_window_sum.22
  56.8 0.1 broadcast_compare_fusion
  56.9 0.1 fusion.10
  57.0 0.1 reduce.1
  57.2 0.6 select_reduce_fusion
  57.8 0.1 slice_reduce_fusion
  57.9 0.2 select_reduce_fusion.1
  58.1 0.6 dynamic-slice.1
  58.7 0.1 eq.74
  58.8 0.1 broadcast_in_dim.103
  58.9 0.4 copy.25.coefs
  59.3 0.5 fusion.12
  59.8 1.2 fusion.14
  61.0 79.9 %all-gather.2.cloned.1.call-done.gathered = bf16[2048,4096]{1,0:T(8,128)(2,1)} async-done(((bf16[128,4096]{1,0:T(8,128)(2,1)}), bf16[2048,4096]{1,0:T(8,128)(2,1)}) %all-gather.2.cloned.1.call-update) | async-done | bytes 16777232 | tf_op jit(solution)/shard_map/all_gather | solution.py:73
  140.9 0.0 copy-start
  140.9 2.0 %copy-done = bf16[896,2048]{1,0:T(8,128)(2,1)S(1)} copy-done((bf16[896,2048]{1,0:T(8,128)(2,1)S(1)}, bf16[896,2048]{1,0:T(8,128)(2,1)}, u32[]{:S(2)}) %copy-start) | copy-done | bytes 3670040
  142.9 23.5 %shard_map.102 = (bf16[896,4096]{1,0:T(8,128)(2,1)}, f32[1,4096]{1,0:T(1,128)}) custom-call(bf16[2048,4096]{1,0:T(8,128)(2,1)} %all-gather.2.cloned.1.call-done.gathered, bf16[896,2048]{1,0:T(8,128)(2,1)S(1)} %copy-done, f32[2048,4]{1,0:T(8,128)S(1)} %copy.25.coefs, f32[1,4096]{1,0:T(1,128)S(1)} %bitcast.32, f32[1,4096]{1,0:T(1,128)S(1)} %bitcast.33), custom_call_target="tpu_custom_call" | custom-call | flops 15032385536 | bytes 27787264 | tf_op jit(solution)/shard_map/pallas_call | solution.py:27
  (9 shorter events, 0.2 us)
Async XLA Ops:
  7.2 3.9 %copy-start.1 = (s32[128]{0:T(128)S(1)}, s32[128]{0:T(128)}, u32[]{:S(2)}) copy-start(s32[128]{0:T(128)} %param.13) | copy-start | bytes 1540
  7.2 3.8 %copy-start.3 = (f32[128]{0:T(128)S(1)}, f32[128]{0:T(128)}, u32[]{:S(2)}) copy-start(f32[128]{0:T(128)} %param.12) | copy-start | bytes 1540
  7.2 3.8 %copy-start.2 = (f32[128]{0:T(128)S(1)}, f32[128]{0:T(128)}, u32[]{:S(2)}) copy-start(f32[128]{0:T(128)} %param.11) | copy-start | bytes 1540
  7.2 133.7 %all-gather.2.cloned.1.call-start = ((), (), s32[]{:S(2)}) async-start(), calls=%async_computation | async-start | bytes 17825792 | tf_op jit(solution)/shard_map/all_gather | solution.py:73
  140.9 2.0 %copy-start = (bf16[896,2048]{1,0:T(8,128)(2,1)S(1)}, bf16[896,2048]{1,0:T(8,128)(2,1)}, u32[]{:S(2)}) copy-start(bf16[896,2048]{1,0:T(8,128)(2,1)} %hidden.1) | copy-start | bytes 11010052
Sparse Core Ops, SparseCore 0:
  10.2 130.6 all-gather.1

commit v2 on v1

v2 whole, which is shorter than its diff:
```python
import functools

import jax
import jax.numpy as jnp
from jax import lax
from jax.experimental import pallas as pl
from jax.experimental.pallas import tpu as pltpu
from jax.sharding import PartitionSpec as P

EPSILON = 1e-05


def butterfly_sum(x, axis):
    count = lax.axis_size(axis)
    step = 1
    while step < count:
        x = x + lax.ppermute(x, axis, [(i, i ^ step) for i in range(count)])
        step *= 2
    return x


def butterfly_step(x, axis):
    count = lax.axis_size(axis)
    step = x.shape[0]
    if step >= count:
        return x
    other = lax.ppermute(x, axis, [(i, i ^ step) for i in range(count)])
    low = (lax.axis_index(axis) & step) == 0
    return jnp.concatenate([jnp.where(low, x, other), jnp.where(low, other, x)])


class Paths:
    def __init__(self, count):
        self.count = count
        self.m = count // 4
        self.order = list(range(0, self.m, 2)) + list(range(self.m - 1 - self.m % 2, 0, -2))
        self.place = [self.order.index(z) for z in range(self.m)]
        self.across = [(i, i ^ 2) for i in range(count)]
        self.core = [(i, i ^ 1) for i in range(count)]
        self.ring = [self._ring(1), self._ring(-1)]

    def _ring(self, way):
        pairs = []
        for i in range(self.count):
            z, rest = divmod(i, 4)
            by = way if i % 2 == 0 else -way
            pairs.append((i, self.order[(self.place[z] + by) % self.m] * 4 + rest))
        return pairs

    def owner(self, me, block):
        steps, across, kind = block
        place = jnp.array(self.place, jnp.int32)[me // 4]
        way = jnp.where((me % 2 == 0) == (kind == 0), -1, 1)
        z = jnp.array(self.order, jnp.int32)[(place + way * steps) % self.m]
        return z * 4 + (me % 4 ^ (2 * across + kind))


class Flights:
    def __init__(self, **arrays):
        self.have = arrays

    def event(self, waits, sends=()):
        names = list(dict.fromkeys([*waits, *(source for _, source, _ in sends)]))
        self.have.update(zip(names, lax.optimization_barrier(tuple(self.have[n] for n in names))))
        for name, source, pairs in sends:
            self.have[name] = lax.ppermute(self.have[source], "seq", pairs)


def early_blocks(m):
    return [(k, a, kind) for k in range(m - 1) for a in range(2) for kind in range(2) if k < m - 2 or a == 0]


def late_blocks(m):
    return [(m - 2, 1, 0), (m - 2, 1, 1)] + [(m - 1, a, kind) for a in range(2) for kind in range(2)]


def run_plan(stream, hidden, core_index, own_facts, paths, early_own, early_other):
    half = stream.shape[1] // 2
    m, ring, across, core = paths.m, paths.ring, paths.across, paths.core
    cut = lambda c: lax.dynamic_slice_in_dim(stream, c * half, half, 1)
    f = Flights(hidden=hidden, stream=stream, away=cut(1 - core_index))
    f.have[0, 0, 0] = cut(core_index)
    have = f.have

    def facts_step():
        have["facts"] = butterfly_step(have["facts"], "seq")

    f.event([], [((1, 0, 0), (0, 0, 0), ring[0]), ((0, 1, 0), (0, 0, 0), across), ((0, 0, 1), "away", core), ("other hidden", "hidden", core)])
    f.event(
        [(0, 0, 1), "stream"],
        [((1, 0, 1), (0, 0, 1), ring[1]), ((0, 1, 1), (0, 0, 1), across)],
    )
    have["sums"] = own_facts(have["stream"])
    f.event([(1, 0, 0), (0, 1, 0), "sums", "other hidden"], [((2, 0, 0), (1, 0, 0), ring[0]), ((1, 1, 0), (1, 0, 0), across)])
    have["facts"] = butterfly_sum(have["sums"], "tp")[None]
    facts_step()
    f.event([(1, 0, 1), (0, 1, 1), "facts"], [((2, 0, 1), (1, 0, 1), ring[1]), ((1, 1, 1), (1, 0, 1), across)])
    for k in range(2, m):
        for kind in range(2):
            facts_step()
            if k < m - 1:
                sends = [((k + 1, 0, kind), (k, 0, kind), ring[kind]), ((k, 1, kind), (k, 0, kind), across)]
            elif kind == 0:
                sends = [((k, 1, kind), (k - 1, 1, kind), ring[kind])]
            else:
                sends = [((k, 1, kind), (k, 0, kind), across)]
            waits = [(k, 0, kind), (k - 1, 1, kind), "facts"]
            if k == m - 1 and kind == 1:
                waits.append("early own")
            f.event(waits, sends)
            if k == m - 1 and kind == 0:
                while have["facts"].shape[0] < paths.count:
                    facts_step()
                blocks = early_blocks(m)
                have["early own"], have["early dstream"], have["early parts"] = early_own(
                    have["facts"], blocks, [have[b] for b in blocks]
                )
    have["early other"] = early_other(have["early dstream"], have["other hidden"])
    f.event([(m - 1, 1, 0), (m - 1, 1, 1), "early other"])
    return have


PARAMS = pltpu.CompilerParams(vmem_limit_bytes=56 * 1024 * 1024)


def cost(units, k, width, extra):
    return pl.CostEstimate(
        flops=2 * units * k * width, bytes_accessed=2 * (units * k + k * width) + extra, transcendentals=0
    )


def pick_kernel(owners, hidden, picked):
    picked[...] = hidden[...]


def pick(hidden, owners, tok):
    units = hidden.shape[0]
    count = owners.shape[0]
    return pl.pallas_call(
        pick_kernel,
        grid_spec=pltpu.PrefetchScalarGridSpec(
            num_scalar_prefetch=1,
            grid=(count,),
            in_specs=[pl.BlockSpec((units, tok), lambda b, owners: (0, owners[b]))],
            out_specs=pl.BlockSpec((units, tok), lambda b, owners: (0, b)),
        ),
        out_shape=jax.ShapeDtypeStruct((units, count * tok), hidden.dtype),
        compiler_params=PARAMS,
        cost_estimate=cost(units, 0, 0, 4 * units * count * tok),
    )(owners, hidden)


def form(owners, coefs, head, blocks, dstream, parts):
    tok = blocks[0].shape[0]
    parts[...] = jnp.zeros_like(parts)
    for b, ref in enumerate(blocks):
        owner = owners[b]
        rows = pl.ds(pl.multiple_of(owner * tok, tok), tok)
        stream_f = ref[...].astype(jnp.float32)
        weight = coefs[rows, 0:1]
        pulled = coefs[rows, 1:2] * stream_f
        dstream[b * tok : (b + 1) * tok, :] = (weight * head[...] - pulled).astype(jnp.bfloat16)
        parts[pl.ds(owner, 1), :] = jnp.sum(weight * stream_f, axis=0, keepdims=True)


def form_kernel(count, added, owners, picked, coefs, head, *refs):
    blocks, refs = refs[:count], refs[count:]
    out, dstream, parts = refs[added:]
    form(owners, coefs, head, blocks, dstream, parts)
    total = jnp.dot(picked[...], dstream[...], preferred_element_type=jnp.float32)
    if added:
        total += refs[0][...]
    out[...] = total.astype(out.dtype)


def tile_of(tokens, half):
    return min(half, max(128, (1 << 20) // tokens))


def form_product(blocks, owners, picked, coefs, head, total, out_type):
    count = len(blocks)
    tok, half = blocks[0].shape
    units = picked.shape[0]
    tokens = coefs.shape[0]
    tile = tile_of(tokens, half)
    whole = lambda i, *_: (0, 0)
    at = lambda i, *_: (0, i)
    sums = [] if total is None else [total]
    return pl.pallas_call(
        functools.partial(form_kernel, count, len(sums)),
        grid_spec=pltpu.PrefetchScalarGridSpec(
            num_scalar_prefetch=1,
            grid=(half // tile,),
            in_specs=[
                pl.BlockSpec((units, count * tok), whole, pipeline_mode=pl.Buffered(1)),
                pl.BlockSpec((tokens, 2), whole, pipeline_mode=pl.Buffered(1)),
                pl.BlockSpec((1, tile), at),
            ]
            + [pl.BlockSpec((tok, tile), at)] * count
            + [pl.BlockSpec((units, tile), at)] * len(sums),
            out_specs=[
                pl.BlockSpec((units, tile), at),
                pl.BlockSpec((count * tok, tile), at),
                pl.BlockSpec((tokens // tok, tile), at),
            ],
        ),
        out_shape=[
            jax.ShapeDtypeStruct((units, half), out_type),
            jax.ShapeDtypeStruct((count * tok, half), jnp.bfloat16),
            jax.ShapeDtypeStruct((tokens // tok, half), jnp.float32),
        ],
        compiler_params=PARAMS,
        cost_estimate=cost(units, count * tok, half, 6 * units * half),
    )(owners, picked, coefs, head, *blocks, *sums)


def plain_kernel(added, where, picked, dstream, *refs):
    total = jnp.dot(picked[...], dstream[...], preferred_element_type=jnp.float32)
    if added:
        total += refs[0][...]
    refs[-1][...] = total.astype(refs[-1].dtype)


def plain_product(picked, dstream, total, out_type, where=None):
    units, k = picked.shape
    half = dstream.shape[1]
    tile = min(512, half)
    steps = half // tile
    at = lambda i, *_: (0, i)
    sums = [] if total is None else [total]
    wide = where is not None
    return pl.pallas_call(
        functools.partial(plain_kernel, len(sums)),
        grid_spec=pltpu.PrefetchScalarGridSpec(
            num_scalar_prefetch=1,
            grid=(steps,),
            in_specs=[
                pl.BlockSpec((units, k), lambda i, *_: (0, 0), pipeline_mode=pl.Buffered(1)),
                pl.BlockSpec((k, tile), at),
            ]
            + [pl.BlockSpec((units, tile), at)] * len(sums),
            out_specs=pl.BlockSpec((units, tile), lambda i, w: (0, w[0] * steps + i)),
        ),
        out_shape=jax.ShapeDtypeStruct((units, half * (2 if wide else 1)), out_type),
        compiler_params=PARAMS,
        cost_estimate=cost(units, k, half, 6 * units * half),
    )(where if wide else jnp.zeros((1,), jnp.int32), picked, dstream, *sums)


def put_kernel(where, part, whole, out):
    out[...] = part[...]


def put(whole, part, where):
    units, half = part.shape
    tile = min(512, half)
    steps = half // tile
    return pl.pallas_call(
        put_kernel,
        grid_spec=pltpu.PrefetchScalarGridSpec(
            num_scalar_prefetch=1,
            grid=(steps,),
            in_specs=[pl.BlockSpec((units, tile), lambda i, w: (0, i)), pl.BlockSpec(memory_space=pl.ANY)],
            out_specs=pl.BlockSpec((units, tile), lambda i, w: (0, w[0] * steps + i)),
        ),
        out_shape=jax.ShapeDtypeStruct(whole.shape, whole.dtype),
        input_output_aliases={2: 0},
        compiler_params=PARAMS,
        cost_estimate=cost(0, 0, 0, 4 * units * half),
    )(where, part, whole)


def all_returns(step_reward, resets):
    shards, tok = step_reward.shape
    position = jnp.arange(tok)
    before = jnp.cumsum(resets, axis=1) - resets
    total = jnp.sum(resets, axis=1, keepdims=True)
    reach = (position[None, :] >= position[:, None])[None] & (before[:, None, :] == before[:, :, None])
    local = jnp.sum(jnp.where(reach, step_reward[:, None, :], 0.0), axis=2)
    passing = before == total
    blocked = jnp.where(passing[:, 0], 0.0, 1.0)
    upto = jnp.cumsum(blocked)
    ids = jnp.arange(shards)
    open_path = (ids[None, :] > ids[:, None]) & ((upto - blocked)[None, :] == upto[:, None])
    incoming = jnp.sum(jnp.where(open_path, local[None, :, 0], 0.0), axis=1)
    return local + jnp.where(passing, incoming[:, None], 0.0)


def make_body(width, shards):
    paths = Paths(shards)

    def body(stream, hidden, final_gain, value_head, rewards, kl_terms, resets):
        tok, local = stream.shape
        half = local // 2
        me = lax.axis_index("seq")
        mine = me % 2
        gain = final_gain.astype(jnp.float32)
        head = gain * value_head.astype(jnp.float32)
        head_half = lax.dynamic_slice_in_dim(head, mine * half, half)[None]
        owners = lambda blocks: jnp.stack([paths.owner(me, b) for b in blocks])
        to_core = lambda x: lax.ppermute(x, "seq", paths.core)
        early, late = owners(early_blocks(paths.m)), owners(late_blocks(paths.m))
        made = {}

        def own_facts(stream):
            stream_f = stream.astype(jnp.float32)
            share = jnp.where(lax.axis_index("tp") == 0, 1.0, 0.0)
            return jnp.stack(
                [
                    jnp.sum(stream_f * stream_f, axis=-1),
                    jnp.sum(stream_f * head, axis=-1),
                    (rewards - 0.2 * kl_terms) * share,
                    resets.astype(jnp.float32) * share,
                ]
            )

        def early_own(facts, _, blocks):
            sum_squares, along, step_reward, cut = (facts[:, k] for k in range(4))
            scale = lax.rsqrt(sum_squares / width + EPSILON)
            values = scale * along
            returns = all_returns(step_reward, cut)
            error = values - returns
            pull = scale**3 * along / width
            coefs = jnp.stack([error * scale, error * pull], axis=-1).reshape(shards * tok, 2)
            made.update(values=values, returns=returns, coefs=coefs)
            return form_product(blocks, early, pick(hidden, early, tok), coefs, head_half, None, jnp.float32)

        def early_other(dstream, other_hidden):
            return plain_product(pick(other_hidden, early, tok), dstream, None, jnp.float32)

        have = run_plan(stream, hidden, mine, own_facts, paths, early_own, early_other)
        blocks = [have[b] for b in late_blocks(paths.m)]
        out, dstream, parts = form_product(
            blocks, late, pick(have["other hidden"], late, tok), made["coefs"], head_half, have["early other"], jnp.bfloat16
        )
        out = to_core(out)
        grad_head = jnp.sum(parts + have["early parts"], axis=0)
        other_head = to_core(grad_head)
        grad_head = gain * jnp.where(
            mine == 0, jnp.concatenate([grad_head, other_head]), jnp.concatenate([other_head, grad_head])
        )
        where = mine[None].astype(jnp.int32)
        grad_down = plain_product(pick(hidden, late, tok), dstream, have["early own"], jnp.bfloat16, where)
        grad_down = put(grad_down, out, 1 - where)
        own = lambda a: lax.dynamic_index_in_dim(a, me, 0, keepdims=False)
        return (own(made["values"]), own(made["returns"]), grad_head, grad_down)

    return body


def solution(mesh):
    placed = (P("seq", "tp"), P("seq", None), P("tp"), P("tp"), P("seq"), P("seq"), P("seq"))

    def run(stream, *rest):
        return jax.shard_map(
            make_body(stream.shape[1], mesh.shape["seq"]),
            mesh=mesh,
            in_specs=placed,
            out_specs=(P("seq"), P("seq"), P("tp"), P("seq", "tp")),
            check_vma=False,
        )(stream, *rest)

    return run
```

time: 174 us -> 158 us (0.908)
  waiting for transfers between devices: 80.5 us -> 26.6 us
  Pallas kernels: 23.5 us -> 70 us
  blocking collectives: 45.2 us -> 0 us
  starting transfers between devices: 0.04 us -> 33.2 us
  local copies, waits for them, and re-layouts: 3.26 us -> 8.96 us
  between operations: 14.2 us -> 11.4 us
    all_gather x1 -> x0, waiting for transfers between devices: 79.9 us -> none  [body(): gathered = lax.all_gather(stream, 'seq', axis=0, tiled=True)]
    pallas_call x1 -> x9, Pallas kernels: 23.5 us -> 70 us  [the longest x4 25.4 us: pick(): pl.pallas_call(pick_kernel, grid_spec=pltpu.PrefetchScalarGridSpec(num_sc...]
    psum x1 -> x0, blocking collectives: 45.2 us -> none  [body(): facts = lax.psum(jnp.where(mine, own[None], 0.0), ('seq', 'tp'))]
    ppermute x0 -> x23, starting transfers between devices: none -> 33.2 us  [the longest x16 28.1 us: event(): self.have[name] = lax.ppermute(self.have[source], 'seq', pairs)]
    ppermute x0 -> x23, waiting for transfers between devices: none -> 26.6 us  [the longest x16 16.2 us: event(): self.have[name] = lax.ppermute(self.have[source], 'seq', pairs)]
    dynamic_slice x1 -> x5, local copies, waits for them, and re-layouts: 0.59 us -> 4.39 us  [the longest x1 1.27 us: run_plan(): cut = lambda c: lax.dynamic_slice_in_dim(stream, c * half, half, 1)]
    another operation x1 -> x3, local copies, waits for them, and re-layouts: 0.36 us -> 2.62 us  [the longest x1 1.38 us: early_own(): jnp.stack([error * scale, error * pull], axis=-1).reshape(shards * tok, 2)]
  transfers between devices with their start and end apart: 1 -> 23, of which waited for: 1 -> 4; matrix products, arithmetic and copies ran while one was open for 4% -> 8% of each run, Pallas kernels for 0% -> 35%
where the time goes in v2:
time: 158 us; the launch traced here: 157 us
  Pallas kernels  70 us (44%)
  starting transfers between devices  33.2 us (21%)
  waiting for transfers between devices  26.6 us (17%)
  between operations  11.4 us (7%)
  local copies, waits for them, and re-layouts  8.96 us (6%)
  other arithmetic  7.13 us (5%)
    ppermute x16, starting transfers between devices, event(): self.have[name] = lax.ppermute(self.have[source], 'seq', pairs)  28.1 us
    pallas_call x4, Pallas kernels, pick(): pl.pallas_call(pick_kernel, grid_spec=pltpu.PrefetchScalarGridSpec(num_sc...  25.4 us
    pallas_call x2, Pallas kernels, form_product(): pl.pallas_call(functools.partial(form_kernel, count, len(sums)), grid_spe...  22.5 us
    pallas_call x2, Pallas kernels, plain_product(): pl.pallas_call(functools.partial(plain_kernel, len(sums)), grid_spec=pltp...  17.6 us
    ppermute x16, waiting for transfers between devices, event(): self.have[name] = lax.ppermute(self.have[source], 'seq', pairs)  16.2 us
    ppermute x4, waiting for transfers between devices, butterfly_step(): other = lax.ppermute(x, axis, [(i, i ^ step) for i in range(count)])  8.79 us
    pallas_call x1, Pallas kernels, put(): pl.pallas_call(put_kernel, grid_spec=pltpu.PrefetchScalarGridSpec(num_sca...  4.43 us
  transfers between devices with their start and end apart: 23, of which 4 were waited for; matrix products, arithmetic and copies ran while one was open for 8% of the time, Pallas kernels for 35%

profile of v2, /device:TPU:0, one launch (start us, length us, event | category | flops | bytes accessed | tf_op | source)
XLA Modules:
  0.0 157.2 jit_solution(12969862900385336179)
XLA Ops:
  0.6 0.0 copy-start.10
  0.7 1.3 constant_dynamic-slice_fusion.3
  2.0 0.5 collective-permute-start.3
  2.5 0.1 collective-permute-start.2
  2.6 4.0 %collective-permute-start = (bf16[128,2048]{1,0:T(8,128)(2,1)S(1)}, bf16[128,2048]{1,0:T(8,128)(2,1)S(1)}, u32[]{:S(2)}, u32[]{:S(2)}) collective-permute-start(bf16[128,2048]{1,0:T(8,128)(2,1)S(1)} %get-tuple-element.37.refs_0_), channel_id=1, source_target_pairs={{0,16},{2,10},{4,20},{6,14},{8,0},{10,26},{12,4},{14,30},{16,24},{... | collective-permute-start | bytes 1572872 | tf_op jit(solution)/shard_map/ppermute | solution.py:66
  6.6 1.5 collective-permute-start.1
  8.1 0.7 convert_multiply_fusion.3
  8.8 0.7 multiply_bitcast_fusion
  9.5 2.3 %collective-permute-start.6 = (bf16[128,2048]{1,0:T(8,128)(2,1)S(1)}, bf16[128,2048]{1,0:T(8,128)(2,1)}, u32[]{:S(2)}, u32[]{:S(2)}) collective-permute-start(bf16[128,2048]{1,0:T(8,128)(2,1)S(1)} %collective-permute-done.2.refs_1_), channel_id=1, source_target_pairs={{0,8},{2,18},{4,12},{6,22},{8,24},{10,2},{12,28},{14,6},{16,0},{18... | collective-permute-start | bytes 1572872 | tf_op jit(solution)/shard_map/ppermute | solution.py:66
  11.8 1.5 collective-permute-start.7
  13.4 1.7 %fusion = (f32[128]{0:T(128)S(1)}, f32[128]{0:T(128)S(1)}) fusion(bf16[128,4096]{1,0:T(8,128)(2,1)} %param.39, f32[4096]{0:T(1024)S(1)} %convert_multiply_fusion.3), kind=kLoop, calls=%fused_computation.2 | loop fusion | flops 2621184 | bytes 1065984 | tf_op jit(solution)/shard_map/reduce_sum | solution.py:310
  15.0 9.8 %collective-permute-done.refs_4_ = bf16[128,2048]{1,0:T(8,128)(2,1)S(1)} collective-permute-done((bf16[128,2048]{1,0:T(8,128)(2,1)S(1)}, bf16[128,2048]{1,0:T(8,128)(2,1)S(1)}, u32[]{:S(2)}, u32[]{:S(2)}) %collective-permute-start) | collective-permute-done | bytes 524320 | tf_op jit(solution)/shard_map/ppermute | solution.py:66
  24.8 0.0 collective-permute-done.1.refs_2_
  24.8 3.0 %collective-permute-start.8 = (f32[4,128]{1,0:T(4,128)S(1)}, f32[4,128]{1,0:T(4,128)S(1)}, u32[]{:S(2)}, u32[]{:S(2)}) collective-permute-start(f32[4,128]{1,0:T(4,128)S(1)} %pad_maximum_fusion.5), channel_id=1, source_target_pairs={{0,1},{1,0},{2,3},{3,2},{4,5},{5,4},{6,7},{7,6},{8,9},{9,8},{10,11... | collective-permute-start | bytes 6152 | tf_op jit(solution)/shard_map/ppermute | solution.py:17
  27.8 1.6 collective-permute-done.8
  29.4 0.0 collective-permute-start.9
  29.4 0.0 collective-permute-start.4
  29.4 2.1 %collective-permute-start.5 = (bf16[128,2048]{1,0:T(8,128)(2,1)S(1)}, bf16[128,2048]{1,0:T(8,128)(2,1)}, u32[]{:S(2)}, u32[]{:S(2)}) collective-permute-start(bf16[128,2048]{1,0:T(8,128)(2,1)S(1)} %collective-permute-done.refs_4_), channel_id=1, source_target_pairs={{0,4},{2,6},{4,0},{6,2},{8,12},{10,14},{12,8},{14,10},{16,20},{18,... | collective-permute-start | bytes 1572872 | tf_op jit(solution)/shard_map/ppermute | solution.py:66
  31.5 0.0 collective-permute-done.6.refs_5_
  31.6 1.1 collective-permute-start.10
  32.7 1.0 collective-permute-start.13
  33.7 2.0 %collective-permute-start.14 = (bf16[128,2048]{1,0:T(8,128)(2,1)}, bf16[128,2048]{1,0:T(8,128)(2,1)}, u32[]{:S(2)}, u32[]{:S(2)}) collective-permute-start(bf16[128,2048]{1,0:T(8,128)(2,1)} %collective-permute-done.6.refs_5_), channel_id=1, source_target_pairs={{0,4},{2,6},{4,0},{6,2},{8,12},{10,14},{12,8},{14,10},{16,20},{18,... | collective-permute-start | bytes 1572872 | tf_op jit(solution)/shard_map/ppermute | solution.py:66
  35.6 8.8 %collective-permute-done.10 = f32[2,4,128]{2,0,1:T(2,128)S(1)} collective-permute-done((f32[2,4,128]{2,0,1:T(2,128)S(1)}, f32[2,4,128]{2,0,1:T(2,128)S(1)}, u32[]{:S(2)}, u32[]{:S(2)}) %collective-permute-start.10) | collective-permute-done | bytes 4128 | tf_op jit(solution)/shard_map/ppermute | solution.py:27
  44.4 6.4 %collective-permute-done.4.refs_8_ = bf16[128,2048]{1,0:T(8,128)(2,1)} collective-permute-done((bf16[128,2048]{1,0:T(8,128)(2,1)S(1)}, bf16[128,2048]{1,0:T(8,128)(2,1)}, u32[]{:S(2)}, u32[]{:S(2)}) %collective-permute-start.4) | collective-permute-done | bytes 524320 | tf_op jit(solution)/shard_map/ppermute | solution.py:66
  50.8 5.2 %collective-permute-start.11 = (bf16[128,2048]{1,0:T(8,128)(2,1)}, bf16[128,2048]{1,0:T(8,128)(2,1)S(1)}, u32[]{:S(2)}, u32[]{:S(2)}) collective-permute-start(bf16[128,2048]{1,0:T(8,128)(2,1)} %collective-permute-done.4.refs_8_), channel_id=1, source_target_pairs={{0,16},{2,10},{4,20},{6,14},{8,0},{10,26},{12,4},{14,30},{16,24},{... | collective-permute-start | bytes 1572872 | tf_op jit(solution)/shard_map/ppermute | solution.py:66
  56.0 1.5 collective-permute-start.12
  57.6 0.5 collective-permute-start.16
  58.2 1.2 dynamic_slice.116
  65.4 0.6 dynamic_slice.128
  66.0 0.7 fusion.15
  69.9 0.6 stack.97.owners
  70.5 7.3 %shard_map.391.picked = bf16[896,1280]{1,0:T(8,128)(2,1)} custom-call(s32[10]{0:T(128)} %stack.97.owners, bf16[896,2048]{1,0:T(8,128)(2,1)} %hidden.3), custom_call_target="tpu_custom_call" | custom-call | bytes 4587520 | tf_op jit(solution)/shard_map/pallas_call | solution.py:139
  77.8 2.5 %collective-permute-start.17 = (bf16[128,2048]{1,0:T(8,128)(2,1)}, bf16[128,2048]{1,0:T(8,128)(2,1)S(1)}, u32[]{:S(2)}, u32[]{:S(2)}) collective-permute-start(bf16[128,2048]{1,0:T(8,128)(2,1)} %collective-permute-done.13.refs_9_), channel_id=1, source_target_pairs={{0,8},{2,18},{4,12},{6,22},{8,24},{10,2},{12,28},{14,6},{16,0},{18... | collective-permute-start | bytes 1572872 | tf_op jit(solution)/shard_map/ppermute | solution.py:66
  80.3 0.7 collective-permute-start.18
  81.0 0.1 fusion.14
  81.2 0.3 reduce_window_sum.22
  81.4 0.1 broadcast_compare_fusion
  81.5 0.7 select_reduce_fusion
  82.2 0.1 slice_reduce_fusion
  82.3 0.1 fusion.7
  82.4 0.1 reduce.1
  82.6 0.2 select_reduce_fusion.1
  82.7 0.1 broadcast_in_dim.82
  82.8 0.1 eq.152
  83.0 1.4 copy.59.coefs
  84.4 1.5 collective-permute-start.19
  85.8 11.8 %shard_map.392 = (f32[896,2048]{1,0:T(8,128)}, bf16[1280,2048]{1,0:T(8,128)(2,1)}, f32[16,2048]{1,0:T(8,128)}) custom-call(s32[10]{0:T(128)} %stack.97.owners, bf16[896,1280]{1,0:T(8,128)(2,1)} %shard_map.391.picked, f32[2048,2]{1,0:T(8,128)} %copy.59.coefs, f32[1,2048]{1,0:T(1,128)} %bitcast.76, bf16[128,2048]{1,0:T(8,128)(2,1)} %copy-done.6, ...), custom_call_target="tpu_custom_call" | custom-call | flops 4697620480 | bytes 18546688 | tf_op jit(solution)/shard_map/pallas_call | solution.py:189
  97.7 1.6 %collective-permute-start.20 = (bf16[128,2048]{1,0:T(8,128)(2,1)S(1)}, bf16[128,2048]{1,0:T(8,128)(2,1)S(1)}, u32[]{:S(2)}, u32[]{:S(2)}) collective-permute-start(bf16[128,2048]{1,0:T(8,128)(2,1)S(1)} %collective-permute-done.17.refs_3_), channel_id=1, source_target_pairs={{0,4},{2,6},{4,0},{6,2},{8,12},{10,14},{12,8},{14,10},{16,20},{18,... | collective-permute-start | bytes 1572872 | tf_op jit(solution)/shard_map/ppermute | solution.py:66
  100.6 0.7 stack.85.owners
  101.3 7.5 %shard_map.393.picked = bf16[896,1280]{1,0:T(8,128)(2,1)} custom-call(s32[10]{0:T(128)} %stack.97.owners, bf16[896,2048]{1,0:T(8,128)(2,1)} %collective-permute-done.3.hidden), custom_call_target="tpu_custom_call" | custom-call | bytes 4587520 | tf_op jit(solution)/shard_map/pallas_call | solution.py:139
  108.8 5.2 %shard_map.390.picked = bf16[896,768]{1,0:T(8,128)(2,1)} custom-call(s32[6]{0:T(128)} %stack.85.owners, bf16[896,2048]{1,0:T(8,128)(2,1)} %collective-permute-done.3.hidden), custom_call_target="tpu_custom_call" | custom-call | bytes 2752512 | tf_op jit(solution)/shard_map/pallas_call | solution.py:139
  114.0 9.5 %shard_map.394.refs_6_ = f32[896,2048]{1,0:T(8,128)} custom-call(s32[1]{0:T(128)} %constant.251.clone.1.where, bf16[896,1280]{1,0:T(8,128)(2,1)} %shard_map.393.picked, bf16[1280,2048]{1,0:T(8,128)(2,1)} %get-tuple-element.61.dstream), custom_call_target="tpu_custom_call" | custom-call | flops 4697620480 | bytes 18546688 | tf_op jit(solution)/shard_map/pallas_call | solution.py:232
  123.5 0.8 copy-done.4
  124.3 0.8 copy-done.5
  125.1 10.6 %shard_map.395 = (bf16[896,2048]{1,0:T(8,128)(2,1)}, bf16[768,2048]{1,0:T(8,128)(2,1)}, f32[16,2048]{1,0:T(8,128)}) custom-call(s32[6]{0:T(128)} %stack.85.owners, bf16[896,768]{1,0:T(8,128)(2,1)} %shard_map.390.picked, f32[2048,2]{1,0:T(8,128)} %copy.59.coefs, f32[1,2048]{1,0:T(1,128)} %bitcast.77, bf16[128,2048]{1,0:T(8,128)(2,1)} %copy-done.1, ...), custom_call_target="tpu_custom_call" | custom-call | flops 2818572288 | bytes 15532032 | tf_op jit(solution)/shard_map/pallas_call | solution.py:189
  135.8 0.1 collective-permute-start.22
  135.9 5.4 %shard_map.396.picked = bf16[896,768]{1,0:T(8,128)(2,1)} custom-call(s32[6]{0:T(128)} %stack.85.owners, bf16[896,2048]{1,0:T(8,128)(2,1)} %hidden.3), custom_call_target="tpu_custom_call" | custom-call | bytes 2752512 | tf_op jit(solution)/shard_map/pallas_call | solution.py:139
  141.2 0.6 dynamic-slice.1
  141.8 0.5 fusion.9
  142.3 1.2 fusion.11
  143.5 0.4 collective-permute-start.21
  144.0 8.2 %shard_map.397.whole = bf16[896,4096]{1,0:T(8,128)(2,1)} custom-call(s32[1]{0:T(128)} %bitcast.43.where, bf16[896,768]{1,0:T(8,128)(2,1)} %shard_map.396.picked, bf16[768,2048]{1,0:T(8,128)(2,1)} %get-tuple-element.68.dstream, f32[896,2048]{1,0:T(8,128)} %get-tuple-element.69.refs_0_), custom_call_target="tpu_custom_call" | custom-call | flops 2818572288 | bytes 15532032 | tf_op jit(solution)/shard_map/pallas_call | solution.py:232
  152.2 0.6 convert_multiply_fusion.2
  152.8 4.4 %shard_map.398 = bf16[896,4096]{1,0:T(8,128)(2,1)} custom-call(s32[1]{0:T(128)S(6)} %sub.84.where, bf16[896,2048]{1,0:T(8,128)(2,1)} %collective-permute-done.22.part, bf16[896,4096]{1,0:T(8,128)(2,1)} %shard_map.397.whole), custom_call_target="tpu_custom_call", output_to_operand_aliasing={{}: (2, {})} | custom-call | bytes 7340032 | tf_op jit(solution)/shard_map/pallas_call | solution.py:258
  (63 shorter events, 0.3 us)
Async XLA Ops:
  0.6 65.4 %copy-start.10 = (s32[4]{0:T(128)S(1)}, s32[4]{0:T(128)}, u32[]{:S(2)}) copy-start(s32[4]{0:T(128)} %constant.254.clone) | copy-start | bytes 52
  1.9 75.8 %copy-start.6 = (bf16[128,2048]{1,0:T(8,128)(2,1)}, bf16[128,2048]{1,0:T(8,128)(2,1)S(1)}, u32[]{:S(2)}) copy-start(bf16[128,2048]{1,0:T(8,128)(2,1)S(1)} %get-tuple-element.37.refs_0_) | copy-start | bytes 1572868
  2.0 22.9 %collective-permute-start.3 = (bf16[896,2048]{1,0:T(8,128)(2,1)}, bf16[896,2048]{1,0:T(8,128)(2,1)}, u32[]{:S(2)}, u32[]{:S(2)}) collective-permute-start(bf16[896,2048]{1,0:T(8,128)(2,1)} %hidden.3), channel_id=1, source_target_pairs={{0,2},{2,0},{4,6},{6,4},{8,10},{10,8},{12,14},{14,12},{16,18},{18,... | collective-permute-start | bytes 11010056 | tf_op jit(solution)/shard_map/ppermute | solution.py:66
  2.5 7.0 %collective-permute-start.2 = (bf16[128,2048]{1,0:T(8,128)(2,1)S(1)}, bf16[128,2048]{1,0:T(8,128)(2,1)S(1)}, u32[]{:S(2)}, u32[]{:S(2)}) collective-permute-start(bf16[128,2048]{1,0:T(8,128)(2,1)S(1)} %get-tuple-element.38), channel_id=1, source_target_pairs={{0,2},{2,0},{4,6},{6,4},{8,10},{10,8},{12,14},{14,12},{16,18},{18,... | collective-permute-start | bytes 1572872 | tf_op jit(solution)/shard_map/ppermute | solution.py:66
  2.6 22.3 %collective-permute-start = (bf16[128,2048]{1,0:T(8,128)(2,1)S(1)}, bf16[128,2048]{1,0:T(8,128)(2,1)S(1)}, u32[]{:S(2)}, u32[]{:S(2)}) collective-permute-start(bf16[128,2048]{1,0:T(8,128)(2,1)S(1)} %get-tuple-element.37.refs_0_), channel_id=1, source_target_pairs={{0,16},{2,10},{4,20},{6,14},{8,0},{10,26},{12,4},{14,30},{16,24},{... | collective-permute-start | bytes 1572872 | tf_op jit(solution)/shard_map/ppermute | solution.py:66
  6.6 18.3 %collective-permute-start.1 = (bf16[128,2048]{1,0:T(8,128)(2,1)S(1)}, bf16[128,2048]{1,0:T(8,128)(2,1)S(1)}, u32[]{:S(2)}, u32[]{:S(2)}) collective-permute-start(bf16[128,2048]{1,0:T(8,128)(2,1)S(1)} %get-tuple-element.37.refs_0_), channel_id=1, source_target_pairs={{0,4},{2,6},{4,0},{6,2},{8,12},{10,14},{12,8},{14,10},{16,20},{18,... | collective-permute-start | bytes 1572872 | tf_op jit(solution)/shard_map/ppermute | solution.py:66
  9.5 41.3 %copy-start.11 = (bf16[128,2048]{1,0:T(8,128)(2,1)}, bf16[128,2048]{1,0:T(8,128)(2,1)S(1)}, u32[]{:S(2)}) copy-start(bf16[128,2048]{1,0:T(8,128)(2,1)S(1)} %collective-permute-done.2.refs_1_) | copy-start | bytes 1572868
  9.5 22.0 %collective-permute-start.6 = (bf16[128,2048]{1,0:T(8,128)(2,1)S(1)}, bf16[128,2048]{1,0:T(8,128)(2,1)}, u32[]{:S(2)}, u32[]{:S(2)}) collective-permute-start(bf16[128,2048]{1,0:T(8,128)(2,1)S(1)} %collective-permute-done.2.refs_1_), channel_id=1, source_target_pairs={{0,8},{2,18},{4,12},{6,22},{8,24},{10,2},{12,28},{14,6},{16,0},{18... | collective-permute-start | bytes 1572872 | tf_op jit(solution)/shard_map/ppermute | solution.py:66
  11.8 19.7 %collective-permute-start.7 = (bf16[128,2048]{1,0:T(8,128)(2,1)S(1)}, bf16[128,2048]{1,0:T(8,128)(2,1)S(1)}, u32[]{:S(2)}, u32[]{:S(2)}) collective-permute-start(bf16[128,2048]{1,0:T(8,128)(2,1)S(1)} %collective-permute-done.2.refs_1_), channel_id=1, source_target_pairs={{0,4},{2,6},{4,0},{6,2},{8,12},{10,14},{12,8},{14,10},{16,20},{18,... | collective-permute-start | bytes 1572872 | tf_op jit(solution)/shard_map/ppermute | solution.py:66
  24.8 45.6 %copy-start.12 = (bf16[128,2048]{1,0:T(8,128)(2,1)}, bf16[128,2048]{1,0:T(8,128)(2,1)S(1)}, u32[]{:S(2)}) copy-start(bf16[128,2048]{1,0:T(8,128)(2,1)S(1)} %collective-permute-done.refs_4_) | copy-start | bytes 1572868
  24.8 32.7 %copy-start.13 = (bf16[128,2048]{1,0:T(8,128)(2,1)}, bf16[128,2048]{1,0:T(8,128)(2,1)S(1)}, u32[]{:S(2)}) copy-start(bf16[128,2048]{1,0:T(8,128)(2,1)S(1)} %collective-permute-done.1.refs_2_) | copy-start | bytes 1572868
  24.8 4.5 %collective-permute-start.8 = (f32[4,128]{1,0:T(4,128)S(1)}, f32[4,128]{1,0:T(4,128)S(1)}, u32[]{:S(2)}, u32[]{:S(2)}) collective-permute-start(f32[4,128]{1,0:T(4,128)S(1)} %pad_maximum_fusion.5), channel_id=1, source_target_pairs={{0,1},{1,0},{2,3},{3,2},{4,5},{5,4},{6,7},{7,6},{8,9},{9,8},{10,11... | collective-permute-start | bytes 6152 | tf_op jit(solution)/shard_map/ppermute | solution.py:17
  29.4 2.1 %collective-permute-start.9 = (f32[1,4,128]{2,0,1:T(1,128)S(1)}, f32[1,4,128]{2,0,1:T(1,128)S(1)}, u32[]{:S(2)}, u32[]{:S(2)}) collective-permute-start(f32[1,4,128]{2,0,1:T(1,128)S(1)} %bitcast.81), channel_id=1, source_target_pairs={{0,2},{2,0},{4,6},{6,4},{8,10},{10,8},{12,14},{14,12},{16,18},{18,... | collective-permute-start | bytes 6152 | tf_op jit(solution)/shard_map/ppermute | solution.py:27
  29.4 21.4 %collective-permute-start.4 = (bf16[128,2048]{1,0:T(8,128)(2,1)S(1)}, bf16[128,2048]{1,0:T(8,128)(2,1)}, u32[]{:S(2)}, u32[]{:S(2)}) collective-permute-start(bf16[128,2048]{1,0:T(8,128)(2,1)S(1)} %collective-permute-done.refs_4_), channel_id=1, source_target_pairs={{0,16},{2,10},{4,20},{6,14},{8,0},{10,26},{12,4},{14,30},{16,24},{... | collective-permute-start | bytes 1572872 | tf_op jit(solution)/shard_map/ppermute | solution.py:66
  29.4 21.4 %collective-permute-start.5 = (bf16[128,2048]{1,0:T(8,128)(2,1)S(1)}, bf16[128,2048]{1,0:T(8,128)(2,1)}, u32[]{:S(2)}, u32[]{:S(2)}) collective-permute-start(bf16[128,2048]{1,0:T(8,128)(2,1)S(1)} %collective-permute-done.refs_4_), channel_id=1, source_target_pairs={{0,4},{2,6},{4,0},{6,2},{8,12},{10,14},{12,8},{14,10},{16,20},{18,... | collective-permute-start | bytes 1572872 | tf_op jit(solution)/shard_map/ppermute | solution.py:66
  31.6 19.3 %copy-start.14 = (bf16[128,2048]{1,0:T(8,128)(2,1)}, bf16[128,2048]{1,0:T(8,128)(2,1)S(1)}, u32[]{:S(2)}) copy-start(bf16[128,2048]{1,0:T(8,128)(2,1)S(1)} %collective-permute-done.7.refs_3_) | copy-start | bytes 1572868
  31.6 12.8 %collective-permute-start.10 = (f32[2,4,128]{2,0,1:T(2,128)S(1)}, f32[2,4,128]{2,0,1:T(2,128)S(1)}, u32[]{:S(2)}, u32[]{:S(2)}) collective-permute-start(f32[2,4,128]{2,0,1:T(2,128)S(1)} %pad_maximum_fusion.4), channel_id=1, source_target_pairs={{0,4},{2,6},{4,0},{6,2},{8,12},{10,14},{12,8},{14,10},{16,20},{18,... | collective-permute-start | bytes 12296 | tf_op jit(solution)/shard_map/ppermute | solution.py:27
  32.7 24.9 %collective-permute-start.13 = (bf16[128,2048]{1,0:T(8,128)(2,1)}, bf16[128,2048]{1,0:T(8,128)(2,1)}, u32[]{:S(2)}, u32[]{:S(2)}) collective-permute-start(bf16[128,2048]{1,0:T(8,128)(2,1)} %collective-permute-done.6.refs_5_), channel_id=1, source_target_pairs={{0,8},{2,18},{4,12},{6,22},{8,24},{10,2},{12,28},{14,6},{16,0},{18... | collective-permute-start | bytes 1572872 | tf_op jit(solution)/shard_map/ppermute | solution.py:66
  33.7 23.9 %collective-permute-start.14 = (bf16[128,2048]{1,0:T(8,128)(2,1)}, bf16[128,2048]{1,0:T(8,128)(2,1)}, u32[]{:S(2)}, u32[]{:S(2)}) collective-permute-start(bf16[128,2048]{1,0:T(8,128)(2,1)} %collective-permute-done.6.refs_5_), channel_id=1, source_target_pairs={{0,4},{2,6},{4,0},{6,2},{8,12},{10,14},{12,8},{14,10},{16,20},{18,... | collective-permute-start | bytes 1572872 | tf_op jit(solution)/shard_map/ppermute | solution.py:66
  50.8 6.7 %collective-permute-start.15 = (f32[4,4,128]{2,0,1:T(4,128)S(1)}, f32[4,4,128]{2,0,1:T(4,128)S(1)}, u32[]{:S(2)}, u32[]{:S(2)}) collective-permute-start(f32[4,4,128]{2,0,1:T(4,128)S(1)} %pad_maximum_fusion.3), channel_id=1, source_target_pairs={{0,8},{2,10},{4,12},{6,14},{8,0},{10,2},{12,4},{14,6},{16,24},{18,... | collective-permute-start | bytes 24584 | tf_op jit(solution)/shard_map/ppermute | solution.py:27
  50.8 30.2 %collective-permute-start.11 = (bf16[128,2048]{1,0:T(8,128)(2,1)}, bf16[128,2048]{1,0:T(8,128)(2,1)S(1)}, u32[]{:S(2)}, u32[]{:S(2)}) collective-permute-start(bf16[128,2048]{1,0:T(8,128)(2,1)} %collective-permute-done.4.refs_8_), channel_id=1, source_target_pairs={{0,16},{2,10},{4,20},{6,14},{8,0},{10,26},{12,4},{14,30},{16,24},{... | collective-permute-start | bytes 1572872 | tf_op jit(solution)/shard_map/ppermute | solution.py:66
  56.0 25.0 %collective-permute-start.12 = (bf16[128,2048]{1,0:T(8,128)(2,1)}, bf16[128,2048]{1,0:T(8,128)(2,1)S(1)}, u32[]{:S(2)}, u32[]{:S(2)}) collective-permute-start(bf16[128,2048]{1,0:T(8,128)(2,1)} %collective-permute-done.4.refs_8_), channel_id=1, source_target_pairs={{0,4},{2,6},{4,0},{6,2},{8,12},{10,14},{12,8},{14,10},{16,20},{18,... | collective-permute-start | bytes 1572872 | tf_op jit(solution)/shard_map/ppermute | solution.py:66
  57.6 23.4 %collective-permute-start.16 = (f32[8,4,128]{2,0,1:T(8,128)S(1)}, f32[8,4,128]{2,0,1:T(8,128)S(1)}, u32[]{:S(2)}, u32[]{:S(2)}) collective-permute-start(f32[8,4,128]{2,0,1:T(8,128)S(1)} %pad_maximum_fusion.1), channel_id=1, source_target_pairs={{0,16},{2,18},{4,20},{6,22},{8,24},{10,26},{12,28},{14,30},{16,0},... | collective-permute-start | bytes 49160 | tf_op jit(solution)/shard_map/ppermute | solution.py:27
  77.8 19.9 %collective-permute-start.17 = (bf16[128,2048]{1,0:T(8,128)(2,1)}, bf16[128,2048]{1,0:T(8,128)(2,1)S(1)}, u32[]{:S(2)}, u32[]{:S(2)}) collective-permute-start(bf16[128,2048]{1,0:T(8,128)(2,1)} %collective-permute-done.13.refs_9_), channel_id=1, source_target_pairs={{0,8},{2,18},{4,12},{6,22},{8,24},{10,2},{12,28},{14,6},{16,0},{18... | collective-permute-start | bytes 1572872 | tf_op jit(solution)/shard_map/ppermute | solution.py:66
  80.3 17.5 %collective-permute-start.18 = (bf16[128,2048]{1,0:T(8,128)(2,1)}, bf16[128,2048]{1,0:T(8,128)(2,1)S(1)}, u32[]{:S(2)}, u32[]{:S(2)}) collective-permute-start(bf16[128,2048]{1,0:T(8,128)(2,1)} %collective-permute-done.13.refs_9_), channel_id=1, source_target_pairs={{0,4},{2,6},{4,0},{6,2},{8,12},{10,14},{12,8},{14,10},{16,20},{18,... | collective-permute-start | bytes 1572872 | tf_op jit(solution)/shard_map/ppermute | solution.py:66
  81.0 16.7 %copy-start = (bf16[128,2048]{1,0:T(8,128)(2,1)}, bf16[128,2048]{1,0:T(8,128)(2,1)S(1)}, u32[]{:S(2)}) copy-start(bf16[128,2048]{1,0:T(8,128)(2,1)S(1)} %collective-permute-done.11.refs_2_) | copy-start | bytes 1572868
  81.0 16.7 %copy-start.1 = (bf16[128,2048]{1,0:T(8,128)(2,1)}, bf16[128,2048]{1,0:T(8,128)(2,1)S(1)}, u32[]{:S(2)}) copy-start(bf16[128,2048]{1,0:T(8,128)(2,1)S(1)} %collective-permute-done.12.refs_0_) | copy-start | bytes 1572868
  84.4 39.1 %collective-permute-start.19 = (bf16[128,2048]{1,0:T(8,128)(2,1)S(1)}, bf16[128,2048]{1,0:T(8,128)(2,1)S(1)}, u32[]{:S(2)}, u32[]{:S(2)}) collective-permute-start(bf16[128,2048]{1,0:T(8,128)(2,1)S(1)} %collective-permute-done.12.refs_0_), channel_id=1, source_target_pairs={{0,16},{2,10},{4,20},{6,14},{8,0},{10,26},{12,4},{14,30},{16,24},{... | collective-permute-start | bytes 1572872 | tf_op jit(solution)/shard_map/ppermute | solution.py:66
  97.7 16.3 %copy-start.2 = (bf16[128,2048]{1,0:T(8,128)(2,1)}, bf16[128,2048]{1,0:T(8,128)(2,1)S(1)}, u32[]{:S(2)}) copy-start(bf16[128,2048]{1,0:T(8,128)(2,1)S(1)} %collective-permute-done.17.refs_3_) | copy-start | bytes 1572868
  97.7 16.3 %copy-start.3 = (bf16[128,2048]{1,0:T(8,128)(2,1)}, bf16[128,2048]{1,0:T(8,128)(2,1)S(1)}, u32[]{:S(2)}) copy-start(bf16[128,2048]{1,0:T(8,128)(2,1)S(1)} %collective-permute-done.18.refs_1_) | copy-start | bytes 1572868
  97.7 25.7 %collective-permute-start.20 = (bf16[128,2048]{1,0:T(8,128)(2,1)S(1)}, bf16[128,2048]{1,0:T(8,128)(2,1)S(1)}, u32[]{:S(2)}, u32[]{:S(2)}) collective-permute-start(bf16[128,2048]{1,0:T(8,128)(2,1)S(1)} %collective-permute-done.17.refs_3_), channel_id=1, source_target_pairs={{0,4},{2,6},{4,0},{6,2},{8,12},{10,14},{12,8},{14,10},{16,20},{18,... | collective-permute-start | bytes 1572872 | tf_op jit(solution)/shard_map/ppermute | solution.py:66
  123.5 0.8 copy-start.4
  124.3 0.8 copy-start.5
  135.8 7.7 %copy-start.7 = (f32[16,2048]{1,0:T(8,128)S(1)}, f32[16,2048]{1,0:T(8,128)}, u32[]{:S(2)}) copy-start(f32[16,2048]{1,0:T(8,128)} %get-tuple-element.66) | copy-start | bytes 393220
  135.8 7.7 %copy-start.8 = (f32[16,2048]{1,0:T(8,128)S(1)}, f32[16,2048]{1,0:T(8,128)}, u32[]{:S(2)}) copy-start(f32[16,2048]{1,0:T(8,128)} %get-tuple-element.65) | copy-start | bytes 393220
  135.8 17.0 %collective-permute-start.22 = (bf16[896,2048]{1,0:T(8,128)(2,1)}, bf16[896,2048]{1,0:T(8,128)(2,1)}, u32[]{:S(2)}, u32[]{:S(2)}) collective-permute-start(bf16[896,2048]{1,0:T(8,128)(2,1)} %get-tuple-element.67), channel_id=1, source_target_pairs={{0,2},{2,0},{4,6},{6,4},{8,10},{10,8},{12,14},{14,12},{16,18},{18,... | collective-permute-start | bytes 11010056 | tf_op jit(solution)/shard_map/ppermute | solution.py:301
  143.5 8.6 %collective-permute-start.21 = (f32[2048]{0:T(1024)S(1)}, f32[2048]{0:T(1024)S(1)}, u32[]{:S(2)}, u32[]{:S(2)}) collective-permute-start(f32[2048]{0:T(1024)S(1)} %add_reduce_fusion), channel_id=1, source_target_pairs={{0,2},{2,0},{4,6},{6,4},{8,10},{10,8},{12,14},{14,12},{16,18},{18,... | collective-permute-start | bytes 24584 | tf_op jit(solution)/shard_map/ppermute | solution.py:301
  144.0 8.2 %copy-start.9 = (bf16[4096]{0:T(1024)(128)(2,1)S(1)}, bf16[4096]{0:T(1024)(128)(2,1)}, u32[]{:S(2)}) copy-start(bf16[4096]{0:T(1024)(128)(2,1)} %param.41) | copy-start | bytes 24580

commit v3 on v2

v3 whole, which is shorter than its diff:
```python
import functools

import jax
import jax.numpy as jnp
import numpy as np
from jax import lax
from jax.experimental import pallas as pl
from jax.experimental.pallas import tpu as pltpu
from jax.sharding import PartitionSpec as P

EPSILON = 1e-05


def butterfly_sum(x, axis):
    count = lax.axis_size(axis)
    step = 1
    while step < count:
        x = x + lax.ppermute(x, axis, [(i, i ^ step) for i in range(count)])
        step *= 2
    return x


def butterfly_step(x, axis):
    count = lax.axis_size(axis)
    step = x.shape[0]
    if step >= count:
        return x
    other = lax.ppermute(x, axis, [(i, i ^ step) for i in range(count)])
    low = (lax.axis_index(axis) & step) == 0
    return jnp.concatenate([jnp.where(low, x, other), jnp.where(low, other, x)])


class Paths:
    def __init__(self, count):
        self.count = count
        self.m = count // 4
        self.order = list(range(0, self.m, 2)) + list(range(self.m - 1 - self.m % 2, 0, -2))
        self.place = [self.order.index(z) for z in range(self.m)]
        self.across = [(i, i ^ 2) for i in range(count)]
        self.core = [(i, i ^ 1) for i in range(count)]
        self.ring = [self._ring(1), self._ring(-1)]

    def _ring(self, way):
        pairs = []
        for i in range(self.count):
            z, rest = divmod(i, 4)
            by = way if i % 2 == 0 else -way
            pairs.append((i, self.order[(self.place[z] + by) % self.m] * 4 + rest))
        return pairs

    def owners(self, blocks):
        table = np.zeros((self.count, len(blocks)), np.int32)
        for me in range(self.count):
            z, rest = divmod(me, 4)
            for b, (steps, across, kind) in enumerate(blocks):
                way = -1 if (me % 2 == 0) == (kind == 0) else 1
                table[me, b] = self.order[(self.place[z] + way * steps) % self.m] * 4 + (rest ^ (2 * across + kind))
        return table


class Flights:
    def __init__(self, **arrays):
        self.have = arrays

    def event(self, waits, sends=()):
        names = list(dict.fromkeys([*waits, *(source for _, source, _ in sends)]))
        self.have.update(zip(names, lax.optimization_barrier(tuple(self.have[n] for n in names))))
        for name, source, pairs in sends:
            self.have[name] = lax.ppermute(self.have[source], "seq", pairs)


def early_blocks(m):
    return [(k, a, kind) for k in range(m - 1) for a in range(2) for kind in range(2) if k < m - 2 or a == 0]


def late_blocks(m):
    return [(m - 2, 1, 0), (m - 2, 1, 1)] + [(m - 1, a, kind) for a in range(2) for kind in range(2)]


def run_plan(stream, core_index, own_facts, paths, pick_both, early_own, early_other):
    half = stream.shape[1] // 2
    m, ring, across, core = paths.m, paths.ring, paths.across, paths.core
    cut = lambda c: lax.dynamic_slice_in_dim(stream, c * half, half, 1)
    f = Flights(stream=stream, away=cut(1 - core_index))
    f.have[0, 0, 0] = cut(core_index)
    have = f.have

    def facts_step():
        have["facts"] = butterfly_step(have["facts"], "seq")

    f.event([], [((1, 0, 0), (0, 0, 0), ring[0]), ((0, 1, 0), (0, 0, 0), across), ((0, 0, 1), "away", core)])
    f.event(
        [(0, 0, 1), "stream"],
        [((1, 0, 1), (0, 0, 1), ring[1]), ((0, 1, 1), (0, 0, 1), across)],
    )
    have["sums"] = own_facts(have["stream"])
    have["own picks"], have["away picks"] = pick_both()
    f.event([(1, 0, 0), (0, 1, 0), "sums", "own picks", "away picks"], [((2, 0, 0), (1, 0, 0), ring[0]), ((1, 1, 0), (1, 0, 0), across)])
    have["facts"] = butterfly_sum(have["sums"], "tp")[None]
    facts_step()
    f.event([(1, 0, 1), (0, 1, 1), "facts"], [((2, 0, 1), (1, 0, 1), ring[1]), ((1, 1, 1), (1, 0, 1), across)])
    for k in range(2, m):
        for kind in range(2):
            facts_step()
            if k < m - 1:
                sends = [((k + 1, 0, kind), (k, 0, kind), ring[kind]), ((k, 1, kind), (k, 0, kind), across)]
            elif kind == 0:
                sends = [((k, 1, kind), (k - 1, 1, kind), ring[kind])]
            else:
                sends = [((k, 1, kind), (k, 0, kind), across)]
            waits = [(k, 0, kind), (k - 1, 1, kind), "facts"]
            if k == m - 2 and kind == 1:
                sends.append(("other picks", "away picks", core))
            if k == m - 1 and kind == 1:
                waits += ["other picks", "early own"]
            f.event(waits, sends)
            if k == m - 1 and kind == 0:
                while have["facts"].shape[0] < paths.count:
                    facts_step()
                blocks = early_blocks(m)
                have["early own"], have["early dstream"], have["early parts"] = early_own(
                    have["facts"], have["own picks"], [have[b] for b in blocks]
                )
    have["early other"] = early_other(have["early dstream"], have["other picks"])
    f.event([(m - 1, 1, 0), (m - 1, 1, 1), "early other"])
    return have


PARAMS = pltpu.CompilerParams(vmem_limit_bytes=60 * 1024 * 1024)


def cost(units, k, width, extra):
    return pl.CostEstimate(
        flops=2 * units * k * width, bytes_accessed=2 * (units * k + k * width) + extra, transcendentals=0
    )


def pick_kernel(tok, owners, hidden, *picked):
    count = hidden.shape[1] // tok
    for n, out in enumerate(picked):
        for b in range(count):
            columns = pl.ds(pl.multiple_of(owners[n * count + b] * tok, tok), tok)
            out[:, b * tok : (b + 1) * tok] = hidden[:, columns]


def pick(hidden, owners, orders, tok):
    units, tokens = hidden.shape
    rows = next(r for r in range(128, 0, -16) if units % r == 0)
    spec = pl.BlockSpec((rows, tokens), lambda i, *_: (i, 0))
    return pl.pallas_call(
        functools.partial(pick_kernel, tok),
        grid_spec=pltpu.PrefetchScalarGridSpec(
            num_scalar_prefetch=1, grid=(units // rows,), in_specs=[spec], out_specs=[spec] * orders
        ),
        out_shape=[jax.ShapeDtypeStruct(hidden.shape, hidden.dtype)] * orders,
        compiler_params=PARAMS,
        cost_estimate=cost(units, 0, 0, 2 * (1 + orders) * units * tokens),
    )(owners, hidden)


def spread(tok, owners, first, coefs, weights, pulls):
    for b in range(weights.shape[0] // tok):
        coef = coefs[:, pl.ds(pl.multiple_of(owners[first + b] * tok, tok), tok)].T
        rows = slice(b * tok, (b + 1) * tok)
        weights[rows, :] = jnp.broadcast_to(coef[:, 0:1], (tok, 128))
        pulls[rows, :] = jnp.broadcast_to(coef[:, 1:2], (tok, 128))


def form(owners, first, weights, pulls, head, blocks, dstream, parts):
    tok, tile = blocks[0].shape
    parts[...] = jnp.zeros_like(parts)
    for b, ref in enumerate(blocks):
        rows = slice(b * tok, (b + 1) * tok)
        sums = []
        for at in range(0, tile, 128):
            lanes = slice(at, at + 128)
            stream_f = ref[:, lanes].astype(jnp.float32)
            weight = weights[rows, :]
            dstream[rows, lanes] = (weight * head[:, lanes] - pulls[rows, :] * stream_f).astype(jnp.bfloat16)
            sums.append(jnp.sum(weight * stream_f, axis=0, keepdims=True))
        parts[pl.ds(owners[first + b], 1), :] = jnp.concatenate(sums, axis=1)


def form_kernel(count, first, start, added, owners, picked, coefs, head, *refs):
    blocks, refs = refs[:count], refs[count:]
    out, dstream, parts, weights, pulls = refs[added:]

    @pl.when(pl.program_id(0) == 0)
    def _():
        spread(blocks[0].shape[0], owners, first, coefs, weights, pulls)

    form(owners, first, weights, pulls, head, blocks, dstream, parts)
    total = jnp.dot(picked[:, start : start + dstream.shape[0]], dstream[...], preferred_element_type=jnp.float32)
    if added:
        total += refs[0][...]
    out[...] = total.astype(out.dtype)


def tile_of(tokens, width):
    return next(t for t in (512 if tokens <= 4096 else 256, 128, width) if width % t == 0)


def picked_spec(units, start, k):
    return pl.BlockSpec((units, start + k), lambda i, *_: (0, 0), pipeline_mode=pl.Buffered(1))


def form_product(blocks, owners, first, picked, coefs, head, total, out_type):
    count = len(blocks)
    tok, half = blocks[0].shape
    units, tokens = picked.shape
    k = count * tok
    tile = tile_of(tokens, half)
    at = lambda i, *_: (0, i)
    sums = [] if total is None else [total]
    return pl.pallas_call(
        functools.partial(form_kernel, count, first, first * tok, len(sums)),
        grid_spec=pltpu.PrefetchScalarGridSpec(
            num_scalar_prefetch=1,
            grid=(half // tile,),
            in_specs=[
                picked_spec(units, first * tok, k),
                pl.BlockSpec(coefs.shape, lambda i, *_: (0, 0), pipeline_mode=pl.Buffered(1)),
                pl.BlockSpec((1, tile), at),
            ]
            + [pl.BlockSpec((tok, tile), at)] * count
            + [pl.BlockSpec((units, tile), at)] * len(sums),
            out_specs=[
                pl.BlockSpec((units, tile), at),
                pl.BlockSpec((k, tile), at),
                pl.BlockSpec((tokens // tok, tile), at),
            ],
            scratch_shapes=[pltpu.VMEM((k, 128), jnp.float32)] * 2,
        ),
        out_shape=[
            jax.ShapeDtypeStruct((units, half), out_type),
            jax.ShapeDtypeStruct((k, half), jnp.bfloat16),
            jax.ShapeDtypeStruct((tokens // tok, half), jnp.float32),
        ],
        compiler_params=PARAMS,
        cost_estimate=cost(units, k * (1 if sums else 10), half, 6 * units * half),
    )(owners, picked, coefs, head, *blocks, *sums)


def plain_kernel(start, added, where, picked, dstream, *refs):
    total = jnp.dot(picked[:, start : start + dstream.shape[0]], dstream[...], preferred_element_type=jnp.float32)
    if added:
        total += refs[0][...]
    refs[-1][...] = total.astype(refs[-1].dtype)


def plain_product(picked, start, dstream, total, out_type, where=None):
    units, tokens = picked.shape
    k, half = dstream.shape
    tile = tile_of(tokens, half)
    steps = half // tile
    at = lambda i, *_: (0, i)
    sums = [] if total is None else [total]
    wide = where is not None
    return pl.pallas_call(
        functools.partial(plain_kernel, start, len(sums)),
        grid_spec=pltpu.PrefetchScalarGridSpec(
            num_scalar_prefetch=1,
            grid=(steps,),
            in_specs=[picked_spec(units, start, k), pl.BlockSpec((k, tile), at)]
            + [pl.BlockSpec((units, tile), at)] * len(sums),
            out_specs=pl.BlockSpec((units, tile), lambda i, w: (0, w[0] * steps + i)),
        ),
        out_shape=jax.ShapeDtypeStruct((units, half * (2 if wide else 1)), out_type),
        compiler_params=PARAMS,
        cost_estimate=cost(units, k, half, 6 * units * half),
    )(where if wide else jnp.zeros((1,), jnp.int32), picked, dstream, *sums)


def put_kernel(pieces, where, part, whole, out, held, sems_in, sems_out):
    units, width = part.shape
    start = pl.multiple_of(where[0] * width, width)
    rows = [pl.ds(n * (units // pieces), units // pieces) for n in range(pieces)]
    fetch = [pltpu.make_async_copy(part.at[r, :], held.at[r, :], sems_in.at[n]) for n, r in enumerate(rows)]
    place = [
        pltpu.make_async_copy(held.at[r, :], out.at[r, pl.ds(start, width)], sems_out.at[n]) for n, r in enumerate(rows)
    ]
    for copy in fetch:
        copy.start()
    for n in range(pieces):
        fetch[n].wait()
        place[n].start()
    for copy in place:
        copy.wait()


def put(whole, part, where):
    units, width = part.shape
    pieces = next(n for n in (7, 4, 2, 1) if units % (16 * n) == 0)
    return pl.pallas_call(
        functools.partial(put_kernel, pieces),
        grid_spec=pltpu.PrefetchScalarGridSpec(
            num_scalar_prefetch=1,
            grid=(),
            in_specs=[pl.BlockSpec(memory_space=pl.ANY)] * 2,
            out_specs=pl.BlockSpec(memory_space=pl.ANY),
            scratch_shapes=[
                pltpu.VMEM(part.shape, part.dtype),
                pltpu.SemaphoreType.DMA((pieces,)),
                pltpu.SemaphoreType.DMA((pieces,)),
            ],
        ),
        out_shape=jax.ShapeDtypeStruct(whole.shape, whole.dtype),
        input_output_aliases={2: 0},
        compiler_params=PARAMS,
        cost_estimate=cost(0, 0, 0, 4 * units * width),
    )(where, part, whole)


def all_returns(step_reward, resets):
    shards, tok = step_reward.shape
    position = jnp.arange(tok)
    before = jnp.cumsum(resets, axis=1) - resets
    total = jnp.sum(resets, axis=1, keepdims=True)
    reach = (position[None, :] >= position[:, None])[None] & (before[:, None, :] == before[:, :, None])
    local = jnp.sum(jnp.where(reach, step_reward[:, None, :], 0.0), axis=2)
    passing = before == total
    blocked = jnp.where(passing[:, 0], 0.0, 1.0)
    upto = jnp.cumsum(blocked)
    ids = jnp.arange(shards)
    open_path = (ids[None, :] > ids[:, None]) & ((upto - blocked)[None, :] == upto[:, None])
    incoming = jnp.sum(jnp.where(open_path, local[None, :, 0], 0.0), axis=1)
    return local + jnp.where(passing, incoming[:, None], 0.0)


def make_body(width, shards):
    paths = Paths(shards)

    def body(stream, hidden, final_gain, value_head, rewards, kl_terms, resets):
        tok, local = stream.shape
        half = local // 2
        me = lax.axis_index("seq")
        mine = me % 2
        gain = final_gain.astype(jnp.float32)
        head = gain * value_head.astype(jnp.float32)
        head_half = lax.dynamic_slice_in_dim(head, mine * half, half)[None]
        to_core = lambda x: lax.ppermute(x, "seq", paths.core)
        early, late = early_blocks(paths.m), late_blocks(paths.m)
        table = paths.owners(late + early)
        both = np.concatenate([table, table[np.arange(shards) ^ 1]], axis=1)
        owners = lax.dynamic_index_in_dim(jnp.asarray(both), me, 0, keepdims=False)
        pick_both = lambda: pick(hidden, owners, 2, tok)
        early_start = len(late) * tok
        made = {}

        def own_facts(stream):
            stream_f = stream.astype(jnp.float32)
            share = jnp.where(lax.axis_index("tp") == 0, 1.0, 0.0)
            return jnp.stack(
                [
                    jnp.sum(stream_f * stream_f, axis=-1),
                    jnp.sum(stream_f * head, axis=-1),
                    (rewards - 0.2 * kl_terms) * share,
                    resets.astype(jnp.float32) * share,
                ]
            )

        def early_own(facts, picked, blocks):
            sum_squares, along, step_reward, cut = (facts[:, k] for k in range(4))
            scale = lax.rsqrt(sum_squares / width + EPSILON)
            values = scale * along
            returns = all_returns(step_reward, cut)
            error = values - returns
            pull = scale**3 * along / width
            coefs = jnp.stack([error * scale, error * pull]).reshape(2, shards * tok)
            coefs = jnp.pad(coefs, ((0, 6), (0, 0)))
            made.update(values=values, returns=returns, coefs=coefs)
            return form_product(blocks, owners, len(late), picked, coefs, head_half, None, jnp.float32)

        def early_other(dstream, picked):
            return plain_product(picked, early_start, dstream, None, jnp.float32)

        have = run_plan(stream, mine, own_facts, paths, pick_both, early_own, early_other)
        blocks = [have[b] for b in late]
        out, dstream, parts = form_product(
            blocks, owners, 0, have["other picks"], made["coefs"], head_half, have["early other"], jnp.bfloat16
        )
        swapped = to_core(out)
        grad_head = jnp.sum(parts + have["early parts"], axis=0)
        other_head = to_core(grad_head)
        grad_head = gain * jnp.where(
            mine == 0, jnp.concatenate([grad_head, other_head]), jnp.concatenate([other_head, grad_head])
        )
        where = mine[None].astype(jnp.int32)
        grad_down = plain_product(have["own picks"], 0, dstream, have["early own"], jnp.bfloat16, where)
        grad_down = put(grad_down, swapped, 1 - where)
        own = lambda a: lax.dynamic_index_in_dim(a, me, 0, keepdims=False)
        return (own(made["values"]), own(made["returns"]), grad_head, grad_down)

    return body


def solution(mesh):
    placed = (P("seq", "tp"), P("seq", None), P("tp"), P("tp"), P("seq"), P("seq"), P("seq"))

    def run(stream, *rest):
        return jax.shard_map(
            make_body(stream.shape[1], mesh.shape["seq"]),
            mesh=mesh,
            in_specs=placed,
            out_specs=(P("seq"), P("seq"), P("tp"), P("seq", "tp")),
            check_vma=False,
        )(stream, *rest)

    return run
```

time: 158 us -> 125 us (0.79)
  Pallas kernels: 70 us -> 52.6 us
  between operations: 11.4 us -> 1 us
  starting transfers between devices: 33.2 us -> 24.5 us
  waiting for transfers between devices: 26.6 us -> 35 us
  local copies, waits for them, and re-layouts: 8.96 us -> 5.7 us
    pallas_call x9 -> x6, Pallas kernels: 70 us -> 52.6 us  [the longest x2 23.4 us: form_product(): pl.pallas_call(functools.partial(form_kernel, count, first, first * tok,...]
    ppermute x16, waiting for transfers between devices: 16.2 us -> 24.3 us  [event(): self.have[name] = lax.ppermute(self.have[source], 'seq', pairs)]
    ppermute x16, starting transfers between devices: 28.1 us -> 22.3 us  [event(): self.have[name] = lax.ppermute(self.have[source], 'seq', pairs)]
    another operation x3 -> x0, local copies, waits for them, and re-layouts: 2.62 us -> none  [the longest x1 1.38 us: early_own(): jnp.stack([error * scale, error * pull], axis=-1).reshape(shards * tok, 2)]
    dynamic_slice x2 -> x0, local copies, waits for them, and re-layouts: 1.92 us -> none  [the longest x1 1.24 us: owner(): place = jnp.array(self.place, jnp.int32)[me // 4]]
    ppermute x4, starting transfers between devices: 1.64 us -> 0.01 us  [butterfly_step(): other = lax.ppermute(x, axis, [(i, i ^ step) for i in range(count)])]
  transfers between devices with their start and end apart: 23 -> 23, of which waited for: 4 -> 9; matrix products, arithmetic and copies ran while one was open for 8% -> 7% of each run, Pallas kernels for 35% -> 31%
where the time goes in v3:
time: 125 us
  Pallas kernels  52.6 us (42%)
  waiting for transfers between devices  35 us (28%)
  starting transfers between devices  24.5 us (20%)
  other arithmetic  6.05 us (5%)
  local copies, waits for them, and re-layouts  5.7 us (5%)
    ppermute x16, waiting for transfers between devices, event(): self.have[name] = lax.ppermute(self.have[source], 'seq', pairs)  24.3 us
    pallas_call x2, Pallas kernels, form_product(): pl.pallas_call(functools.partial(form_kernel, count, first, first * tok,...  23.4 us
    ppermute x16, starting transfers between devices, event(): self.have[name] = lax.ppermute(self.have[source], 'seq', pairs)  22.3 us
    pallas_call x2, Pallas kernels, plain_product(): pl.pallas_call(functools.partial(plain_kernel, start, len(sums)), grid_sp...  18 us
    ppermute x4, waiting for transfers between devices, butterfly_step(): other = lax.ppermute(x, axis, [(i, i ^ step) for i in range(count)])  8.64 us
    pallas_call x1, Pallas kernels, pick(): pl.pallas_call(functools.partial(pick_kernel, tok), grid_spec=pltpu.Prefe...  8.14 us
    pallas_call x1, Pallas kernels, put(): pl.pallas_call(functools.partial(put_kernel, pieces), grid_spec=pltpu.Pre...  3.02 us
  transfers between devices with their start and end apart: 23, of which 9 were waited for; matrix products, arithmetic and copies ran while one was open for 7% of the time, Pallas kernels for 31%

profile of v3, /device:TPU:0, one launch (start us, length us, event | category | flops | bytes accessed | tf_op | source)
XLA Modules:
  0.0 124.9 jit_solution(6782928928352533284)
XLA Ops:
  0.7 1.4 %constant_dynamic-slice_fusion.4 = (bf16[128,2048]{1,0:T(8,128)(2,1)S(1)}, bf16[128,2048]{1,0:T(8,128)(2,1)S(1)}) fusion(bf16[128,4096]{1,0:T(8,128)(2,1)} %param.8, s32[]{:T(128)S(6)} %select_n.122, s32[]{:T(128)S(6)} %select_n.121), kind=kLoop, calls=%fused_computation.47 | loop fusion | bytes 2097160 | tf_op jit(solution)/shard_map/dynamic_slice | solution.py:83
  2.1 4.1 %collective-permute-start = (bf16[128,2048]{1,0:T(8,128)(2,1)S(1)}, bf16[128,2048]{1,0:T(8,128)(2,1)S(1)}, u32[]{:S(2)}, u32[]{:S(2)}) collective-permute-start(bf16[128,2048]{1,0:T(8,128)(2,1)S(1)} %get-tuple-element.41.refs_0_), channel_id=1, source_target_pairs={{0,16},{2,10},{4,20},{6,14},{8,0},{10,26},{12,4},{14,30},{16,24},{... | collective-permute-start | bytes 1572872 | tf_op jit(solution)/shard_map/ppermute | solution.py:69
  6.2 1.5 %collective-permute-start.1 = (bf16[128,2048]{1,0:T(8,128)(2,1)S(1)}, bf16[128,2048]{1,0:T(8,128)(2,1)}, u32[]{:S(2)}, u32[]{:S(2)}) collective-permute-start(bf16[128,2048]{1,0:T(8,128)(2,1)S(1)} %get-tuple-element.41.refs_0_), channel_id=1, source_target_pairs={{0,4},{2,6},{4,0},{6,2},{8,12},{10,14},{12,8},{14,10},{16,20},{18,... | collective-permute-start | bytes 1572872 | tf_op jit(solution)/shard_map/ppermute | solution.py:69
  7.7 0.0 collective-permute-start.2
  7.7 1.2 fusion.8.owners
  8.9 8.1 %shard_map.111 = (bf16[896,2048]{1,0:T(8,128)(2,1)}, bf16[896,2048]{1,0:T(8,128)(2,1)}) custom-call(s32[32]{0:T(128)} %fusion.8.owners, bf16[896,2048]{1,0:T(8,128)(2,1)} %hidden.1), custom_call_target="tpu_custom_call" | custom-call | bytes 11010048 | tf_op jit(solution)/shard_map/pallas_call | solution.py:150
  17.1 0.0 collective-permute-done.2.refs_1_
  17.1 0.9 collective-permute-start.5
  18.0 0.6 collective-permute-start.6
  18.6 0.4 fusion
  19.0 0.0 collective-permute-done.1.refs_2_
  19.1 1.6 %collective-permute-start.7 = (f32[4,128]{1,0:T(4,128)S(1)}, f32[4,128]{1,0:T(4,128)S(1)}, u32[]{:S(2)}, u32[]{:S(2)}) collective-permute-start(f32[4,128]{1,0:T(4,128)S(1)} %pad_maximum_fusion.4), channel_id=1, source_target_pairs={{0,1},{1,0},{2,3},{3,2},{4,5},{5,4},{6,7},{7,6},{8,9},{9,8},{10,11... | collective-permute-start | bytes 6152 | tf_op jit(solution)/shard_map/ppermute | solution.py:18
  20.6 2.1 %collective-permute-done.7 = f32[4,128]{1,0:T(4,128)S(1)} collective-permute-done((f32[4,128]{1,0:T(4,128)S(1)}, f32[4,128]{1,0:T(4,128)S(1)}, u32[]{:S(2)}, u32[]{:S(2)}) %collective-permute-start.7) | collective-permute-done | bytes 2080 | tf_op jit(solution)/shard_map/ppermute | solution.py:18
  22.7 2.1 %collective-permute-start.3 = (bf16[128,2048]{1,0:T(8,128)(2,1)S(1)}, bf16[128,2048]{1,0:T(8,128)(2,1)}, u32[]{:S(2)}, u32[]{:S(2)}) collective-permute-start(bf16[128,2048]{1,0:T(8,128)(2,1)S(1)} %collective-permute-done.refs_4_), channel_id=1, source_target_pairs={{0,16},{2,10},{4,20},{6,14},{8,0},{10,26},{12,4},{14,30},{16,24},{... | collective-permute-start | bytes 1572872 | tf_op jit(solution)/shard_map/ppermute | solution.py:69
  24.8 1.5 %collective-permute-start.4 = (bf16[128,2048]{1,0:T(8,128)(2,1)S(1)}, bf16[128,2048]{1,0:T(8,128)(2,1)S(1)}, u32[]{:S(2)}, u32[]{:S(2)}) collective-permute-start(bf16[128,2048]{1,0:T(8,128)(2,1)S(1)} %collective-permute-done.refs_4_), channel_id=1, source_target_pairs={{0,4},{2,6},{4,0},{6,2},{8,12},{10,14},{12,8},{14,10},{16,20},{18,... | collective-permute-start | bytes 1572872 | tf_op jit(solution)/shard_map/ppermute | solution.py:69
  26.3 0.0 collective-permute-done.8
  26.3 11.6 %collective-permute-done.5.refs_5_ = bf16[128,2048]{1,0:T(8,128)(2,1)S(1)} collective-permute-done((bf16[128,2048]{1,0:T(8,128)(2,1)}, bf16[128,2048]{1,0:T(8,128)(2,1)S(1)}, u32[]{:S(2)}, u32[]{:S(2)}) %collective-permute-start.5) | collective-permute-done | bytes 524320 | tf_op jit(solution)/shard_map/ppermute | solution.py:69
  37.9 0.0 collective-permute-start.9
  38.0 0.1 collective-permute-start.12
  38.0 2.0 %collective-permute-start.13 = (bf16[128,2048]{1,0:T(8,128)(2,1)S(1)}, bf16[128,2048]{1,0:T(8,128)(2,1)}, u32[]{:S(2)}, u32[]{:S(2)}) collective-permute-start(bf16[128,2048]{1,0:T(8,128)(2,1)S(1)} %collective-permute-done.5.refs_5_), channel_id=1, source_target_pairs={{0,4},{2,6},{4,0},{6,2},{8,12},{10,14},{12,8},{14,10},{16,20},{18,... | collective-permute-start | bytes 1572872 | tf_op jit(solution)/shard_map/ppermute | solution.py:69
  40.0 4.4 %collective-permute-done.9 = f32[2,4,128]{2,0,1:T(2,128)S(1)} collective-permute-done((f32[2,4,128]{2,0,1:T(2,128)S(1)}, f32[2,4,128]{2,0,1:T(2,128)S(1)}, u32[]{:S(2)}, u32[]{:S(2)}) %collective-permute-start.9) | collective-permute-done | bytes 4128 | tf_op jit(solution)/shard_map/ppermute | solution.py:28
  44.4 1.6 %collective-permute-done.3.refs_8_ = bf16[128,2048]{1,0:T(8,128)(2,1)} collective-permute-done((bf16[128,2048]{1,0:T(8,128)(2,1)S(1)}, bf16[128,2048]{1,0:T(8,128)(2,1)}, u32[]{:S(2)}, u32[]{:S(2)}) %collective-permute-start.3) | collective-permute-done | bytes 524320 | tf_op jit(solution)/shard_map/ppermute | solution.py:69
  46.0 0.0 collective-permute-done.4.refs_6_
  46.0 0.0 collective-permute-start.14
  46.0 0.8 copy-done.16
  46.9 0.5 collective-permute-start.10
  47.4 2.8 %collective-permute-start.11 = (bf16[128,2048]{1,0:T(8,128)(2,1)}, bf16[128,2048]{1,0:T(8,128)(2,1)S(1)}, u32[]{:S(2)}, u32[]{:S(2)}) collective-permute-start(bf16[128,2048]{1,0:T(8,128)(2,1)} %collective-permute-done.3.refs_8_), channel_id=1, source_target_pairs={{0,4},{2,6},{4,0},{6,2},{8,12},{10,14},{12,8},{14,10},{16,20},{18,... | collective-permute-start | bytes 1572872 | tf_op jit(solution)/shard_map/ppermute | solution.py:69
  50.2 2.7 %collective-permute-done.14 = f32[4,4,128]{2,0,1:T(4,128)S(1)} collective-permute-done((f32[4,4,128]{2,0,1:T(4,128)S(1)}, f32[4,4,128]{2,0,1:T(4,128)S(1)}, u32[]{:S(2)}, u32[]{:S(2)}) %collective-permute-start.14) | collective-permute-done | bytes 8224 | tf_op jit(solution)/shard_map/ppermute | solution.py:28
  52.9 7.2 %collective-permute-done.12.refs_9_ = bf16[128,2048]{1,0:T(8,128)(2,1)} collective-permute-done((bf16[128,2048]{1,0:T(8,128)(2,1)S(1)}, bf16[128,2048]{1,0:T(8,128)(2,1)}, u32[]{:S(2)}, u32[]{:S(2)}) %collective-permute-start.12) | collective-permute-done | bytes 524320 | tf_op jit(solution)/shard_map/ppermute | solution.py:69
  60.1 0.0 collective-permute-done.13.refs_7_
  60.1 0.0 collective-permute-start.15
  60.2 0.6 dynamic_slice.25
  60.8 1.6 %collective-permute-start.16 = (bf16[128,2048]{1,0:T(8,128)(2,1)}, bf16[128,2048]{1,0:T(8,128)(2,1)S(1)}, u32[]{:S(2)}, u32[]{:S(2)}) collective-permute-start(bf16[128,2048]{1,0:T(8,128)(2,1)} %collective-permute-done.12.refs_9_), channel_id=1, source_target_pairs={{0,8},{2,18},{4,12},{6,22},{8,24},{10,2},{12,28},{14,6},{16,0},{18... | collective-permute-start | bytes 1572872 | tf_op jit(solution)/shard_map/ppermute | solution.py:69
  62.4 1.5 %collective-permute-start.17 = (bf16[128,2048]{1,0:T(8,128)(2,1)}, bf16[128,2048]{1,0:T(8,128)(2,1)S(1)}, u32[]{:S(2)}, u32[]{:S(2)}) collective-permute-start(bf16[128,2048]{1,0:T(8,128)(2,1)} %collective-permute-done.12.refs_9_), channel_id=1, source_target_pairs={{0,4},{2,6},{4,0},{6,2},{8,12},{10,14},{12,8},{14,10},{16,20},{18,... | collective-permute-start | bytes 1572872 | tf_op jit(solution)/shard_map/ppermute | solution.py:69
  63.9 1.5 %collective-permute-done.15 = f32[8,4,128]{2,0,1:T(8,128)S(1)} collective-permute-done((f32[8,4,128]{2,0,1:T(8,128)S(1)}, f32[8,4,128]{2,0,1:T(8,128)S(1)}, u32[]{:S(2)}, u32[]{:S(2)}) %collective-permute-start.15) | collective-permute-done | bytes 16416 | tf_op jit(solution)/shard_map/ppermute | solution.py:28
  65.4 2.7 %collective-permute-start.18 = (bf16[896,2048]{1,0:T(8,128)(2,1)}, bf16[896,2048]{1,0:T(8,128)(2,1)}, u32[]{:S(2)}, u32[]{:S(2)}) collective-permute-start(bf16[896,2048]{1,0:T(8,128)(2,1)} %get-tuple-element.57), channel_id=1, source_target_pairs={{0,2},{2,0},{4,6},{6,4},{8,10},{10,8},{12,14},{14,12},{16,18},{18,... | collective-permute-start | bytes 11010056 | tf_op jit(solution)/shard_map/ppermute | solution.py:69
  68.2 0.9 collective-permute-done.10.refs_2_
  69.1 0.1 fusion.15
  69.2 0.3 reduce_window_sum.22
  69.5 0.1 broadcast_compare_fusion
  69.6 0.7 select_reduce_fusion
  70.2 0.1 slice_reduce_fusion
  70.4 0.1 fusion.7
  70.5 0.1 reduce.1
  70.6 0.2 select_reduce_fusion.1
  70.8 0.1 broadcast_in_dim.86
  70.9 0.1 eq.90
  71.0 0.1 collective-permute-start.19
  71.1 0.6 select_maximum_fusion.coefs
  71.8 12.7 %shard_map.112 = (f32[896,2048]{1,0:T(8,128)}, bf16[1280,2048]{1,0:T(8,128)(2,1)}, f32[16,2048]{1,0:T(8,128)}) custom-call(s32[32]{0:T(128)} %fusion.8.owners, bf16[896,2048]{1,0:T(8,128)(2,1)} %get-tuple-element.58.picked, f32[8,2048]{1,0:T(8,128)} %select_maximum_fusion.coefs, f32[1,2048]{1,0:T(1,128)} %bitcast.48, bf16[128,2048]{1,0:T(8,128)(2,1)} %copy-done.1, ...), custom_call_target="tpu_custom_call" | custom-call | flops 46976204800 | bytes 86376448 | tf_op jit(solution)/shard_map/pallas_call | solution.py:215
  84.5 0.4 collective-permute-start.20
  85.0 9.8 %shard_map.113.refs_6_ = f32[896,2048]{1,0:T(8,128)} custom-call(s32[1]{0:T(128)} %constant.66.clone.1.where, bf16[896,2048]{1,0:T(8,128)(2,1)} %collective-permute-done.18.picked, bf16[1280,2048]{1,0:T(8,128)(2,1)} %get-tuple-element.69.dstream), custom_call_target="tpu_custom_call" | custom-call | flops 4697620480 | bytes 18546688 | tf_op jit(solution)/shard_map/pallas_call | solution.py:259
  94.8 2.8 %collective-permute-done.20.refs_5_ = bf16[128,2048]{1,0:T(8,128)(2,1)S(1)} collective-permute-done((bf16[128,2048]{1,0:T(8,128)(2,1)S(1)}, bf16[128,2048]{1,0:T(8,128)(2,1)S(1)}, u32[]{:S(2)}, u32[]{:S(2)}) %collective-permute-start.20) | collective-permute-done | bytes 524320 | tf_op jit(solution)/shard_map/ppermute | solution.py:69
  97.7 0.8 copy-done.7
  98.4 10.8 %shard_map.114 = (bf16[896,2048]{1,0:T(8,128)(2,1)}, bf16[768,2048]{1,0:T(8,128)(2,1)}, f32[16,2048]{1,0:T(8,128)}) custom-call(s32[32]{0:T(128)} %fusion.8.owners, bf16[896,2048]{1,0:T(8,128)(2,1)} %collective-permute-done.18.picked, f32[8,2048]{1,0:T(8,128)} %select_maximum_fusion.coefs, f32[1,2048]{1,0:T(1,128)} %bitcast.49, bf16[128,2048]{1,0:T(8,128)(2,1)} %copy-done.3, ...), custom_call_target="tpu_custom_call" | custom-call | flops 2818572288 | bytes 15532032 | tf_op jit(solution)/shard_map/pallas_call | solution.py:215
  109.2 0.1 collective-permute-start.22
  109.3 0.6 dynamic-slice.1
  109.9 0.5 fusion.10
  110.4 1.2 fusion.12
  111.6 0.9 add_reduce_fusion
  112.5 0.5 collective-permute-start.21
  113.1 8.2 %shard_map.115.whole = bf16[896,4096]{1,0:T(8,128)(2,1)} custom-call(s32[1]{0:T(128)} %bitcast.20.where, bf16[896,2048]{1,0:T(8,128)(2,1)} %get-tuple-element.58.picked, bf16[768,2048]{1,0:T(8,128)(2,1)} %get-tuple-element.76.dstream, f32[896,2048]{1,0:T(8,128)} %get-tuple-element.77.refs_0_), custom_call_target="tpu_custom_call" | custom-call | flops 2818572288 | bytes 15532032 | tf_op jit(solution)/shard_map/pallas_call | solution.py:259
  121.2 0.6 convert_multiply_fusion.2
  121.8 3.0 %shard_map.116 = bf16[896,4096]{1,0:T(8,128)(2,1)} custom-call(s32[1]{0:T(128)S(6)} %sub.64.where, bf16[896,2048]{1,0:T(8,128)(2,1)} %collective-permute-done.22.part, bf16[896,4096]{1,0:T(8,128)(2,1)} %shard_map.115.whole), custom_call_target="tpu_custom_call", output_to_operand_aliasing={{}: (2, {})} | custom-call | bytes 7340032 | tf_op jit(solution)/shard_map/pallas_call | solution.py:294
  (60 shorter events, 0.3 us)
Async XLA Ops:
  0.6 17.9 %copy-start = (bf16[128,4096]{1,0:T(8,128)(2,1)S(1)}, bf16[128,4096]{1,0:T(8,128)(2,1)}, u32[]{:S(2)}) copy-start(bf16[128,4096]{1,0:T(8,128)(2,1)} %param.8) | copy-start | bytes 3145732
  0.6 16.4 %copy-start.9 = (bf16[4096]{0:T(1024)(128)(2,1)S(1)}, bf16[4096]{0:T(1024)(128)(2,1)}, u32[]{:S(2)}) copy-start(bf16[4096]{0:T(1024)(128)(2,1)} %param.10) | copy-start | bytes 24580
  0.7 16.4 %copy-start.10 = (bf16[4096]{0:T(1024)(128)(2,1)S(1)}, bf16[4096]{0:T(1024)(128)(2,1)}, u32[]{:S(2)}) copy-start(bf16[4096]{0:T(1024)(128)(2,1)} %param.11) | copy-start | bytes 24580
  0.7 16.4 %copy-start.11 = (s32[128]{0:T(128)S(1)}, s32[128]{0:T(128)}, u32[]{:S(2)}) copy-start(s32[128]{0:T(128)} %param.14) | copy-start | bytes 1540
  0.7 16.4 %copy-start.12 = (f32[128]{0:T(128)S(1)}, f32[128]{0:T(128)}, u32[]{:S(2)}) copy-start(f32[128]{0:T(128)} %param.12) | copy-start | bytes 1540
  0.7 16.4 %copy-start.13 = (f32[128]{0:T(128)S(1)}, f32[128]{0:T(128)}, u32[]{:S(2)}) copy-start(f32[128]{0:T(128)} %param.13) | copy-start | bytes 1540
  2.1 69.7 %copy-start.1 = (bf16[128,2048]{1,0:T(8,128)(2,1)}, bf16[128,2048]{1,0:T(8,128)(2,1)S(1)}, u32[]{:S(2)}) copy-start(bf16[128,2048]{1,0:T(8,128)(2,1)S(1)} %get-tuple-element.41.refs_0_) | copy-start | bytes 1572868
  2.1 16.9 %collective-permute-start = (bf16[128,2048]{1,0:T(8,128)(2,1)S(1)}, bf16[128,2048]{1,0:T(8,128)(2,1)S(1)}, u32[]{:S(2)}, u32[]{:S(2)}) collective-permute-start(bf16[128,2048]{1,0:T(8,128)(2,1)S(1)} %get-tuple-element.41.refs_0_), channel_id=1, source_target_pairs={{0,16},{2,10},{4,20},{6,14},{8,0},{10,26},{12,4},{14,30},{16,24},{... | collective-permute-start | bytes 1572872 | tf_op jit(solution)/shard_map/ppermute | solution.py:69
  6.2 12.9 %collective-permute-start.1 = (bf16[128,2048]{1,0:T(8,128)(2,1)S(1)}, bf16[128,2048]{1,0:T(8,128)(2,1)}, u32[]{:S(2)}, u32[]{:S(2)}) collective-permute-start(bf16[128,2048]{1,0:T(8,128)(2,1)S(1)} %get-tuple-element.41.refs_0_), channel_id=1, source_target_pairs={{0,4},{2,6},{4,0},{6,2},{8,12},{10,14},{12,8},{14,10},{16,20},{18,... | collective-permute-start | bytes 1572872 | tf_op jit(solution)/shard_map/ppermute | solution.py:69
  7.7 9.4 %collective-permute-start.2 = (bf16[128,2048]{1,0:T(8,128)(2,1)S(1)}, bf16[128,2048]{1,0:T(8,128)(2,1)}, u32[]{:S(2)}, u32[]{:S(2)}) collective-permute-start(bf16[128,2048]{1,0:T(8,128)(2,1)S(1)} %get-tuple-element.42), channel_id=1, source_target_pairs={{0,2},{2,0},{4,6},{6,4},{8,10},{10,8},{12,14},{14,12},{16,18},{18,... | collective-permute-start | bytes 1572872 | tf_op jit(solution)/shard_map/ppermute | solution.py:69
  17.1 20.8 %collective-permute-start.5 = (bf16[128,2048]{1,0:T(8,128)(2,1)}, bf16[128,2048]{1,0:T(8,128)(2,1)S(1)}, u32[]{:S(2)}, u32[]{:S(2)}) collective-permute-start(bf16[128,2048]{1,0:T(8,128)(2,1)} %collective-permute-done.2.refs_1_), channel_id=1, source_target_pairs={{0,8},{2,18},{4,12},{6,22},{8,24},{10,2},{12,28},{14,6},{16,0},{18... | collective-permute-start | bytes 1572872 | tf_op jit(solution)/shard_map/ppermute | solution.py:69
  18.0 19.9 %collective-permute-start.6 = (bf16[128,2048]{1,0:T(8,128)(2,1)}, bf16[128,2048]{1,0:T(8,128)(2,1)}, u32[]{:S(2)}, u32[]{:S(2)}) collective-permute-start(bf16[128,2048]{1,0:T(8,128)(2,1)} %collective-permute-done.2.refs_1_), channel_id=1, source_target_pairs={{0,4},{2,6},{4,0},{6,2},{8,12},{10,14},{12,8},{14,10},{16,20},{18,... | collective-permute-start | bytes 1572872 | tf_op jit(solution)/shard_map/ppermute | solution.py:69
  19.0 52.7 %copy-start.14 = (bf16[128,2048]{1,0:T(8,128)(2,1)}, bf16[128,2048]{1,0:T(8,128)(2,1)S(1)}, u32[]{:S(2)}) copy-start(bf16[128,2048]{1,0:T(8,128)(2,1)S(1)} %collective-permute-done.refs_4_) | copy-start | bytes 1572868
  19.1 3.7 %collective-permute-start.7 = (f32[4,128]{1,0:T(4,128)S(1)}, f32[4,128]{1,0:T(4,128)S(1)}, u32[]{:S(2)}, u32[]{:S(2)}) collective-permute-start(f32[4,128]{1,0:T(4,128)S(1)} %pad_maximum_fusion.4), channel_id=1, source_target_pairs={{0,1},{1,0},{2,3},{3,2},{4,5},{5,4},{6,7},{7,6},{8,9},{9,8},{10,11... | collective-permute-start | bytes 6152 | tf_op jit(solution)/shard_map/ppermute | solution.py:18
  22.7 3.6 %collective-permute-start.8 = (f32[1,4,128]{2,0,1:T(1,128)S(1)}, f32[1,4,128]{2,0,1:T(1,128)S(1)}, u32[]{:S(2)}, u32[]{:S(2)}) collective-permute-start(f32[1,4,128]{2,0,1:T(1,128)S(1)} %bitcast.59), channel_id=1, source_target_pairs={{0,2},{2,0},{4,6},{6,4},{8,10},{10,8},{12,14},{14,12},{16,18},{18,... | collective-permute-start | bytes 6152 | tf_op jit(solution)/shard_map/ppermute | solution.py:28
  22.7 23.3 %collective-permute-start.3 = (bf16[128,2048]{1,0:T(8,128)(2,1)S(1)}, bf16[128,2048]{1,0:T(8,128)(2,1)}, u32[]{:S(2)}, u32[]{:S(2)}) collective-permute-start(bf16[128,2048]{1,0:T(8,128)(2,1)S(1)} %collective-permute-done.refs_4_), channel_id=1, source_target_pairs={{0,16},{2,10},{4,20},{6,14},{8,0},{10,26},{12,4},{14,30},{16,24},{... | collective-permute-start | bytes 1572872 | tf_op jit(solution)/shard_map/ppermute | solution.py:69
  24.8 21.2 %collective-permute-start.4 = (bf16[128,2048]{1,0:T(8,128)(2,1)S(1)}, bf16[128,2048]{1,0:T(8,128)(2,1)S(1)}, u32[]{:S(2)}, u32[]{:S(2)}) collective-permute-start(bf16[128,2048]{1,0:T(8,128)(2,1)S(1)} %collective-permute-done.refs_4_), channel_id=1, source_target_pairs={{0,4},{2,6},{4,0},{6,2},{8,12},{10,14},{12,8},{14,10},{16,20},{18,... | collective-permute-start | bytes 1572872 | tf_op jit(solution)/shard_map/ppermute | solution.py:69
  37.9 22.8 %copy-start.15 = (bf16[128,2048]{1,0:T(8,128)(2,1)}, bf16[128,2048]{1,0:T(8,128)(2,1)S(1)}, u32[]{:S(2)}) copy-start(bf16[128,2048]{1,0:T(8,128)(2,1)S(1)} %collective-permute-done.5.refs_5_) | copy-start | bytes 1572868
  37.9 6.4 %collective-permute-start.9 = (f32[2,4,128]{2,0,1:T(2,128)S(1)}, f32[2,4,128]{2,0,1:T(2,128)S(1)}, u32[]{:S(2)}, u32[]{:S(2)}) collective-permute-start(f32[2,4,128]{2,0,1:T(2,128)S(1)} %pad_maximum_fusion.3), channel_id=1, source_target_pairs={{0,4},{2,6},{4,0},{6,2},{8,12},{10,14},{12,8},{14,10},{16,20},{18,... | collective-permute-start | bytes 12296 | tf_op jit(solution)/shard_map/ppermute | solution.py:28
  38.0 22.2 %collective-permute-start.12 = (bf16[128,2048]{1,0:T(8,128)(2,1)S(1)}, bf16[128,2048]{1,0:T(8,128)(2,1)}, u32[]{:S(2)}, u32[]{:S(2)}) collective-permute-start(bf16[128,2048]{1,0:T(8,128)(2,1)S(1)} %collective-permute-done.5.refs_5_), channel_id=1, source_target_pairs={{0,8},{2,18},{4,12},{6,22},{8,24},{10,2},{12,28},{14,6},{16,0},{18... | collective-permute-start | bytes 1572872 | tf_op jit(solution)/shard_map/ppermute | solution.py:69
  38.0 22.1 %collective-permute-start.13 = (bf16[128,2048]{1,0:T(8,128)(2,1)S(1)}, bf16[128,2048]{1,0:T(8,128)(2,1)}, u32[]{:S(2)}, u32[]{:S(2)}) collective-permute-start(bf16[128,2048]{1,0:T(8,128)(2,1)S(1)} %collective-permute-done.5.refs_5_), channel_id=1, source_target_pairs={{0,4},{2,6},{4,0},{6,2},{8,12},{10,14},{12,8},{14,10},{16,20},{18,... | collective-permute-start | bytes 1572872 | tf_op jit(solution)/shard_map/ppermute | solution.py:69
  46.0 0.8 copy-start.16
  46.0 6.9 %collective-permute-start.14 = (f32[4,4,128]{2,0,1:T(4,128)S(1)}, f32[4,4,128]{2,0,1:T(4,128)S(1)}, u32[]{:S(2)}, u32[]{:S(2)}) collective-permute-start(f32[4,4,128]{2,0,1:T(4,128)S(1)} %pad_maximum_fusion.2), channel_id=1, source_target_pairs={{0,8},{2,10},{4,12},{6,14},{8,0},{10,2},{12,4},{14,6},{16,24},{18,... | collective-permute-start | bytes 24584 | tf_op jit(solution)/shard_map/ppermute | solution.py:28
  46.9 22.2 %collective-permute-start.10 = (bf16[128,2048]{1,0:T(8,128)(2,1)}, bf16[128,2048]{1,0:T(8,128)(2,1)S(1)}, u32[]{:S(2)}, u32[]{:S(2)}) collective-permute-start(bf16[128,2048]{1,0:T(8,128)(2,1)} %collective-permute-done.3.refs_8_), channel_id=1, source_target_pairs={{0,16},{2,10},{4,20},{6,14},{8,0},{10,26},{12,4},{14,30},{16,24},{... | collective-permute-start | bytes 1572872 | tf_op jit(solution)/shard_map/ppermute | solution.py:69
  47.4 21.7 %collective-permute-start.11 = (bf16[128,2048]{1,0:T(8,128)(2,1)}, bf16[128,2048]{1,0:T(8,128)(2,1)S(1)}, u32[]{:S(2)}, u32[]{:S(2)}) collective-permute-start(bf16[128,2048]{1,0:T(8,128)(2,1)} %collective-permute-done.3.refs_8_), channel_id=1, source_target_pairs={{0,4},{2,6},{4,0},{6,2},{8,12},{10,14},{12,8},{14,10},{16,20},{18,... | collective-permute-start | bytes 1572872 | tf_op jit(solution)/shard_map/ppermute | solution.py:69
  60.1 5.3 %collective-permute-start.15 = (f32[8,4,128]{2,0,1:T(8,128)S(1)}, f32[8,4,128]{2,0,1:T(8,128)S(1)}, u32[]{:S(2)}, u32[]{:S(2)}) collective-permute-start(f32[8,4,128]{2,0,1:T(8,128)S(1)} %pad_maximum_fusion.1), channel_id=1, source_target_pairs={{0,16},{2,18},{4,20},{6,22},{8,24},{10,26},{12,28},{14,30},{16,0},... | collective-permute-start | bytes 49160 | tf_op jit(solution)/shard_map/ppermute | solution.py:28
  60.8 23.7 %collective-permute-start.16 = (bf16[128,2048]{1,0:T(8,128)(2,1)}, bf16[128,2048]{1,0:T(8,128)(2,1)S(1)}, u32[]{:S(2)}, u32[]{:S(2)}) collective-permute-start(bf16[128,2048]{1,0:T(8,128)(2,1)} %collective-permute-done.12.refs_9_), channel_id=1, source_target_pairs={{0,8},{2,18},{4,12},{6,22},{8,24},{10,2},{12,28},{14,6},{16,0},{18... | collective-permute-start | bytes 1572872 | tf_op jit(solution)/shard_map/ppermute | solution.py:69
  62.4 22.1 %collective-permute-start.17 = (bf16[128,2048]{1,0:T(8,128)(2,1)}, bf16[128,2048]{1,0:T(8,128)(2,1)S(1)}, u32[]{:S(2)}, u32[]{:S(2)}) collective-permute-start(bf16[128,2048]{1,0:T(8,128)(2,1)} %collective-permute-done.12.refs_9_), channel_id=1, source_target_pairs={{0,4},{2,6},{4,0},{6,2},{8,12},{10,14},{12,8},{14,10},{16,20},{18,... | collective-permute-start | bytes 1572872 | tf_op jit(solution)/shard_map/ppermute | solution.py:69
  65.4 19.1 %collective-permute-start.18 = (bf16[896,2048]{1,0:T(8,128)(2,1)}, bf16[896,2048]{1,0:T(8,128)(2,1)}, u32[]{:S(2)}, u32[]{:S(2)}) collective-permute-start(bf16[896,2048]{1,0:T(8,128)(2,1)} %get-tuple-element.57), channel_id=1, source_target_pairs={{0,2},{2,0},{4,6},{6,4},{8,10},{10,8},{12,14},{14,12},{16,18},{18,... | collective-permute-start | bytes 11010056 | tf_op jit(solution)/shard_map/ppermute | solution.py:69
  69.1 15.3 %copy-start.2 = (bf16[128,2048]{1,0:T(8,128)(2,1)}, bf16[128,2048]{1,0:T(8,128)(2,1)S(1)}, u32[]{:S(2)}) copy-start(bf16[128,2048]{1,0:T(8,128)(2,1)S(1)} %collective-permute-done.10.refs_2_) | copy-start | bytes 1572868
  69.1 15.3 %copy-start.3 = (bf16[128,2048]{1,0:T(8,128)(2,1)}, bf16[128,2048]{1,0:T(8,128)(2,1)S(1)}, u32[]{:S(2)}) copy-start(bf16[128,2048]{1,0:T(8,128)(2,1)S(1)} %collective-permute-done.11.refs_0_) | copy-start | bytes 1572868
  71.0 23.7 %collective-permute-start.19 = (bf16[128,2048]{1,0:T(8,128)(2,1)S(1)}, bf16[128,2048]{1,0:T(8,128)(2,1)S(1)}, u32[]{:S(2)}, u32[]{:S(2)}) collective-permute-start(bf16[128,2048]{1,0:T(8,128)(2,1)S(1)} %collective-permute-done.11.refs_0_), channel_id=1, source_target_pairs={{0,16},{2,10},{4,20},{6,14},{8,0},{10,26},{12,4},{14,30},{16,24},{... | collective-permute-start | bytes 1572872 | tf_op jit(solution)/shard_map/ppermute | solution.py:69
  84.5 10.3 %copy-start.4 = (bf16[128,2048]{1,0:T(8,128)(2,1)}, bf16[128,2048]{1,0:T(8,128)(2,1)S(1)}, u32[]{:S(2)}) copy-start(bf16[128,2048]{1,0:T(8,128)(2,1)S(1)} %collective-permute-done.16.refs_3_) | copy-start | bytes 1572868
  84.5 10.3 %copy-start.5 = (bf16[128,2048]{1,0:T(8,128)(2,1)}, bf16[128,2048]{1,0:T(8,128)(2,1)S(1)}, u32[]{:S(2)}) copy-start(bf16[128,2048]{1,0:T(8,128)(2,1)S(1)} %collective-permute-done.17.refs_1_) | copy-start | bytes 1572868
  84.5 13.1 %collective-permute-start.20 = (bf16[128,2048]{1,0:T(8,128)(2,1)S(1)}, bf16[128,2048]{1,0:T(8,128)(2,1)S(1)}, u32[]{:S(2)}, u32[]{:S(2)}) collective-permute-start(bf16[128,2048]{1,0:T(8,128)(2,1)S(1)} %collective-permute-done.16.refs_3_), channel_id=1, source_target_pairs={{0,4},{2,6},{4,0},{6,2},{8,12},{10,14},{12,8},{14,10},{16,20},{18,... | collective-permute-start | bytes 1572872 | tf_op jit(solution)/shard_map/ppermute | solution.py:69
  94.8 16.8 %copy-start.8 = (f32[16,2048]{1,0:T(8,128)S(1)}, f32[16,2048]{1,0:T(8,128)}, u32[]{:S(2)}) copy-start(f32[16,2048]{1,0:T(8,128)} %get-tuple-element.74) | copy-start | bytes 393220
  94.8 2.9 %copy-start.6 = (bf16[128,2048]{1,0:T(8,128)(2,1)}, bf16[128,2048]{1,0:T(8,128)(2,1)S(1)}, u32[]{:S(2)}) copy-start(bf16[128,2048]{1,0:T(8,128)(2,1)S(1)} %collective-permute-done.19.refs_4_) | copy-start | bytes 1572868
  97.6 0.8 copy-start.7
  109.2 12.6 %collective-permute-start.22 = (bf16[896,2048]{1,0:T(8,128)(2,1)}, bf16[896,2048]{1,0:T(8,128)(2,1)}, u32[]{:S(2)}, u32[]{:S(2)}) collective-permute-start(bf16[896,2048]{1,0:T(8,128)(2,1)} %get-tuple-element.75), channel_id=1, source_target_pairs={{0,2},{2,0},{4,6},{6,4},{8,10},{10,8},{12,14},{14,12},{16,18},{18,... | collective-permute-start | bytes 11010056 | tf_op jit(solution)/shard_map/ppermute | solution.py:341
  112.5 8.7 %collective-permute-start.21 = (f32[2048]{0:T(1024)S(1)}, f32[2048]{0:T(1024)S(1)}, u32[]{:S(2)}, u32[]{:S(2)}) collective-permute-start(f32[2048]{0:T(1024)S(1)} %add_reduce_fusion), channel_id=1, source_target_pairs={{0,2},{2,0},{4,6},{6,4},{8,10},{10,8},{12,14},{14,12},{16,18},{18,... | collective-permute-start | bytes 24584 | tf_op jit(solution)/shard_map/ppermute | solution.py:341

commit v4 on v3

--- a/solution.py
+++ b/solution.py
@@ -69,12 +69,11 @@
             self.have[name] = lax.ppermute(self.have[source], "seq", pairs)
 
 
-def early_blocks(m):
-    return [(k, a, kind) for k in range(m - 1) for a in range(2) for kind in range(2) if k < m - 2 or a == 0]
-
-
-def late_blocks(m):
-    return [(m - 2, 1, 0), (m - 2, 1, 1)] + [(m - 1, a, kind) for a in range(2) for kind in range(2)]
+def block_groups(m):
+    last = [(m - 1, 1, 0), (m - 1, 1, 1)]
+    middle = [(m - 2, 1, 0), (m - 2, 1, 1), (m - 1, 0, 0), (m - 1, 0, 1)]
+    early = [(k, a, kind) for k in range(m - 1) for a in range(2) for kind in range(2) if k < m - 2 or a == 0]
+    return last, middle, early
 
 
 def run_plan(stream, core_index, own_facts, paths, pick_both, early_own, early_other):
@@ -95,7 +94,10 @@
     )
     have["sums"] = own_facts(have["stream"])
     have["own picks"], have["away picks"] = pick_both()
-    f.event([(1, 0, 0), (0, 1, 0), "sums", "own picks", "away picks"], [((2, 0, 0), (1, 0, 0), ring[0]), ((1, 1, 0), (1, 0, 0), across)])
+    f.event(
+        [(1, 0, 0), (0, 1, 0), "sums", "own picks", "away picks"],
+        [((2, 0, 0), (1, 0, 0), ring[0]), ((1, 1, 0), (1, 0, 0), across)],
+    )
     have["facts"] = butterfly_sum(have["sums"], "tp")[None]
     facts_step()
     f.event([(1, 0, 1), (0, 1, 1), "facts"], [((2, 0, 1), (1, 0, 1), ring[1]), ((1, 1, 1), (1, 0, 1), across)])
@@ -112,17 +114,14 @@
             if k == m - 2 and kind == 1:
                 sends.append(("other picks", "away picks", core))
             if k == m - 1 and kind == 1:
-                waits += ["other picks", "early own"]
+                waits += ["other picks", "early own", "values", "returns"]
             f.event(waits, sends)
             if k == m - 1 and kind == 0:
                 while have["facts"].shape[0] < paths.count:
                     facts_step()
-                blocks = early_blocks(m)
-                have["early own"], have["early dstream"], have["early parts"] = early_own(
-                    have["facts"], have["own picks"], [have[b] for b in blocks]
-                )
-    have["early other"] = early_other(have["early dstream"], have["other picks"])
-    f.event([(m - 1, 1, 0), (m - 1, 1, 1), "early other"])
+                early_own(have)
+    early_other(have)
+    f.event([(m - 1, 1, 0), (m - 1, 1, 1), "other sum"])
     return have
 
 
@@ -166,109 +165,140 @@
         pulls[rows, :] = jnp.broadcast_to(coef[:, 1:2], (tok, 128))
 
 
-def form(owners, first, weights, pulls, head, blocks, dstream, parts):
-    tok, tile = blocks[0].shape
-    parts[...] = jnp.zeros_like(parts)
-    for b, ref in enumerate(blocks):
+def form(tok, owners, first, weights, pulls, head, blocks, dstream, parts, start, chunk):
+    for b in range(blocks.shape[0] // tok):
         rows = slice(b * tok, (b + 1) * tok)
-        sums = []
-        for at in range(0, tile, 128):
-            lanes = slice(at, at + 128)
-            stream_f = ref[:, lanes].astype(jnp.float32)
+        for at in range(0, chunk, 128):
+            lanes = pl.ds(pl.multiple_of(start + at, 128), 128)
+            stream_f = blocks[rows, lanes].astype(jnp.float32)
             weight = weights[rows, :]
             dstream[rows, lanes] = (weight * head[:, lanes] - pulls[rows, :] * stream_f).astype(jnp.bfloat16)
-            sums.append(jnp.sum(weight * stream_f, axis=0, keepdims=True))
-        parts[pl.ds(owners[first + b], 1), :] = jnp.concatenate(sums, axis=1)
-
-
-def form_kernel(count, first, start, added, owners, picked, coefs, head, *refs):
-    blocks, refs = refs[:count], refs[count:]
-    out, dstream, parts, weights, pulls = refs[added:]
-
-    @pl.when(pl.program_id(0) == 0)
-    def _():
-        spread(blocks[0].shape[0], owners, first, coefs, weights, pulls)
-
-    form(owners, first, weights, pulls, head, blocks, dstream, parts)
-    total = jnp.dot(picked[:, start : start + dstream.shape[0]], dstream[...], preferred_element_type=jnp.float32)
+            parts[owners[first + b], :, lanes] = jnp.sum(weight * stream_f, axis=0, keepdims=True)
+
+
+def product_kernel(tok, count, first, given_count, added, chunk, owners, where, *refs):
+    refs = list(refs)
+    take = lambda n: [refs.pop(0) for _ in range(n)]
+    (picked,) = take(1)
+    coefs, head = take(2) if count else (None, None)
+    blocks, given, total = take(count), take(given_count), take(added)
+    (out,) = take(1)
+    dstream, parts = take(2) if count else (None, None)
+    picked_v, dstream_v, sum_v = take(3)
+    blocks_v, weights, pulls = take(3) if count else (None, None, None)
+    out_v = take(1)[0] if added else sum_v
+    sem_picked, sem_blocks, sem_given, sem_total, sem_out, sem_dstream = take(6)
+    half = sum_v.shape[1]
+    steps = half // chunk
+    k = picked_v.shape[1]
+    formed = count * tok
+    base = pl.multiple_of(where[0] * half, half)
+
+    columns = lambda c: pl.ds(pl.multiple_of(c * chunk, chunk), chunk)
+    get_picked = pltpu.make_async_copy(picked.at[:, pl.ds(first * tok, k)], picked_v, sem_picked)
+    get_blocks = [
+        pltpu.make_async_copy(ref, blocks_v.at[pl.ds(b * tok, tok), :], sem_blocks.at[b]) for b, ref in enumerate(blocks)
+    ]
+
+    def get_given(g, c):
+        row = formed + sum(ref.shape[0] for ref in given[:g])
+        rows = pl.ds(row, given[g].shape[0])
+        return pltpu.make_async_copy(given[g].at[:, columns(c)], dstream_v.at[rows, columns(c)], sem_given.at[g, c])
+
+    def get_total(c):
+        return pltpu.make_async_copy(total[0].at[:, columns(c)], sum_v.at[:, columns(c)], sem_total.at[c])
+
+    def put_out(c):
+        there = pl.ds(pl.multiple_of(base + c * chunk, chunk), chunk)
+        return pltpu.make_async_copy(out_v.at[:, columns(c)], out.at[:, there], sem_out.at[c])
+
+    def put_dstream(c):
+        rows = pl.ds(0, formed)
+        return pltpu.make_async_copy(dstream_v.at[rows, columns(c)], dstream.at[:, columns(c)], sem_dstream.at[c])
+
+    for copy in get_blocks:
+        copy.start()
+    get_picked.start()
+    for c in range(steps):
+        for g in range(given_count):
+            get_given(g, c).start()
+        if added:
+            get_total(c).start()
+    if count:
+        parts[...] = jnp.zeros_like(parts)
+        spread(tok, owners, first, coefs, weights, pulls)
+    for copy in get_blocks:
+        copy.wait()
+    get_picked.wait()
+
+    def step(c, carry):
+        if count:
+            form(tok, owners, first, weights, pulls, head, blocks_v, dstream_v, parts, c * chunk, chunk)
+            put_dstream(c).start()
+        for g in range(given_count):
+            get_given(g, c).wait()
+        here = jnp.dot(picked_v[...], dstream_v[:, columns(c)], preferred_element_type=jnp.float32)
+        if added:
+            get_total(c).wait()
+            here += sum_v[:, columns(c)]
+        out_v[:, columns(c)] = here.astype(out_v.dtype)
+        put_out(c).start()
+        return carry
+
+    lax.fori_loop(0, steps, step, 0)
+    for c in range(steps):
+        put_out(c).wait()
+        if count:
+            put_dstream(c).wait()
+
+
+def product(owners, first, picked, formed=None, given=(), total=None, where=None):
+    units, tokens = picked.shape
+    coefs, head, blocks = formed or (None, None, [])
+    half = blocks[0].shape[1] if blocks else given[0].shape[1]
+    count = len(blocks)
+    tok = tokens // owners.shape[0] * 2
+    k = count * tok + sum(g.shape[0] for g in given)
+    chunk = next(t for t in (512 if tokens <= 4096 else 256, 128, half) if half % t == 0)
+    steps = half // chunk
+    added = total is not None
+    anywhere = pl.BlockSpec(memory_space=pl.ANY)
+    inside = pl.BlockSpec(memory_space=pltpu.VMEM)
+    out_type = jnp.bfloat16 if added else jnp.float32
+    out_specs = [anywhere]
+    out_shape = [jax.ShapeDtypeStruct((units, half if where is None else 2 * half), out_type)]
+    scratch = [pltpu.VMEM((units, k), picked.dtype), pltpu.VMEM((k, half), jnp.bfloat16), pltpu.VMEM((units, half), jnp.float32)]
+    if count:
+        out_specs += [anywhere, inside]
+        out_shape += [
+            jax.ShapeDtypeStruct((count * tok, half), jnp.bfloat16),
+            jax.ShapeDtypeStruct((tokens // tok, 1, half), jnp.float32),
+        ]
+        scratch += [pltpu.VMEM((count * tok, half), jnp.bfloat16)] + [pltpu.VMEM((count * tok, 128), jnp.float32)] * 2
     if added:
-        total += refs[0][...]
-    out[...] = total.astype(out.dtype)
-
-
-def tile_of(tokens, width):
-    return next(t for t in (512 if tokens <= 4096 else 256, 128, width) if width % t == 0)
-
-
-def picked_spec(units, start, k):
-    return pl.BlockSpec((units, start + k), lambda i, *_: (0, 0), pipeline_mode=pl.Buffered(1))
-
-
-def form_product(blocks, owners, first, picked, coefs, head, total, out_type):
-    count = len(blocks)
-    tok, half = blocks[0].shape
-    units, tokens = picked.shape
-    k = count * tok
-    tile = tile_of(tokens, half)
-    at = lambda i, *_: (0, i)
-    sums = [] if total is None else [total]
+        scratch += [pltpu.VMEM((units, half), out_type)]
+    sems = [(), (max(count, 1),), (max(len(given), 1), steps), (steps,), (steps,), (steps,)]
     return pl.pallas_call(
-        functools.partial(form_kernel, count, first, first * tok, len(sums)),
+        functools.partial(product_kernel, tok, count, first, len(given), int(added), chunk),
         grid_spec=pltpu.PrefetchScalarGridSpec(
-            num_scalar_prefetch=1,
-            grid=(half // tile,),
-            in_specs=[
-                picked_spec(units, first * tok, k),
-                pl.BlockSpec(coefs.shape, lambda i, *_: (0, 0), pipeline_mode=pl.Buffered(1)),
-                pl.BlockSpec((1, tile), at),
-            ]
-            + [pl.BlockSpec((tok, tile), at)] * count
-            + [pl.BlockSpec((units, tile), at)] * len(sums),
-            out_specs=[
-                pl.BlockSpec((units, tile), at),
-                pl.BlockSpec((k, tile), at),
-                pl.BlockSpec((tokens // tok, tile), at),
-            ],
-            scratch_shapes=[pltpu.VMEM((k, 128), jnp.float32)] * 2,
+            num_scalar_prefetch=2,
+            grid=(),
+            in_specs=[anywhere] + [inside] * 2 * bool(count) + [anywhere] * (count + len(given) + added),
+            out_specs=out_specs,
+            scratch_shapes=scratch + [pltpu.SemaphoreType.DMA(shape) for shape in sems],
         ),
-        out_shape=[
-            jax.ShapeDtypeStruct((units, half), out_type),
-            jax.ShapeDtypeStruct((k, half), jnp.bfloat16),
-            jax.ShapeDtypeStruct((tokens // tok, half), jnp.float32),
-        ],
+        out_shape=out_shape,
         compiler_params=PARAMS,
-        cost_estimate=cost(units, k * (1 if sums else 10), half, 6 * units * half),
-    )(owners, picked, coefs, head, *blocks, *sums)
-
-
-def plain_kernel(start, added, where, picked, dstream, *refs):
-    total = jnp.dot(picked[:, start : start + dstream.shape[0]], dstream[...], preferred_element_type=jnp.float32)
-    if added:
-        total += refs[0][...]
-    refs[-1][...] = total.astype(refs[-1].dtype)
-
-
-def plain_product(picked, start, dstream, total, out_type, where=None):
-    units, tokens = picked.shape
-    k, half = dstream.shape
-    tile = tile_of(tokens, half)
-    steps = half // tile
-    at = lambda i, *_: (0, i)
-    sums = [] if total is None else [total]
-    wide = where is not None
-    return pl.pallas_call(
-        functools.partial(plain_kernel, start, len(sums)),
-        grid_spec=pltpu.PrefetchScalarGridSpec(
-            num_scalar_prefetch=1,
-            grid=(steps,),
-            in_specs=[picked_spec(units, start, k), pl.BlockSpec((k, tile), at)]
-            + [pl.BlockSpec((units, tile), at)] * len(sums),
-            out_specs=pl.BlockSpec((units, tile), lambda i, w: (0, w[0] * steps + i)),
-        ),
-        out_shape=jax.ShapeDtypeStruct((units, half * (2 if wide else 1)), out_type),
-        compiler_params=PARAMS,
-        cost_estimate=cost(units, k, half, 6 * units * half),
-    )(where if wide else jnp.zeros((1,), jnp.int32), picked, dstream, *sums)
+        cost_estimate=cost(units, k * (1 if added or given else 10), half, 6 * units * half),
+    )(
+        owners,
+        jnp.zeros((1,), jnp.int32) if where is None else where,
+        picked,
+        *([coefs, head] if count else []),
+        *blocks,
+        *given,
+        *([total] if added else []),
+    )
 
 
 def put_kernel(pieces, where, part, whole, out, held, sems_in, sems_out):
@@ -339,13 +369,12 @@
         head = gain * value_head.astype(jnp.float32)
         head_half = lax.dynamic_slice_in_dim(head, mine * half, half)[None]
         to_core = lambda x: lax.ppermute(x, "seq", paths.core)
-        early, late = early_blocks(paths.m), late_blocks(paths.m)
-        table = paths.owners(late + early)
+        own = lambda a: lax.dynamic_index_in_dim(a, me, 0, keepdims=False)
+        last, middle, early = block_groups(paths.m)
+        table = paths.owners(last + middle + early)
         both = np.concatenate([table, table[np.arange(shards) ^ 1]], axis=1)
-        owners = lax.dynamic_index_in_dim(jnp.asarray(both), me, 0, keepdims=False)
-        pick_both = lambda: pick(hidden, owners, 2, tok)
-        early_start = len(late) * tok
-        made = {}
+        owners = own(jnp.asarray(both))
+        early_at = len(last + middle)
 
         def own_facts(stream):
             stream_f = stream.astype(jnp.float32)
@@ -359,8 +388,8 @@
                 ]
             )
 
-        def early_own(facts, picked, blocks):
-            sum_squares, along, step_reward, cut = (facts[:, k] for k in range(4))
+        def early_own(have):
+            sum_squares, along, step_reward, cut = (have["facts"][:, k] for k in range(4))
             scale = lax.rsqrt(sum_squares / width + EPSILON)
             values = scale * along
             returns = all_returns(step_reward, cut)
@@ -368,28 +397,36 @@
             pull = scale**3 * along / width
             coefs = jnp.stack([error * scale, error * pull]).reshape(2, shards * tok)
             coefs = jnp.pad(coefs, ((0, 6), (0, 0)))
-            made.update(values=values, returns=returns, coefs=coefs)
-            return form_product(blocks, owners, len(late), picked, coefs, head_half, None, jnp.float32)
-
-        def early_other(dstream, picked):
-            return plain_product(picked, early_start, dstream, None, jnp.float32)
-
-        have = run_plan(stream, mine, own_facts, paths, pick_both, early_own, early_other)
-        blocks = [have[b] for b in late]
-        out, dstream, parts = form_product(
-            blocks, owners, 0, have["other picks"], made["coefs"], head_half, have["early other"], jnp.bfloat16
+            have.update(values=own(values), returns=own(returns), coefs=coefs)
+            have["early own"], have["early dstream"], have["early parts"] = product(
+                owners, early_at, have["own picks"], (coefs, head_half, [have[b] for b in early])
+            )
+
+        def early_other(have):
+            have["other sum"], have["middle dstream"], have["middle parts"] = product(
+                owners,
+                len(last),
+                have["other picks"],
+                (have["coefs"], head_half, [have[b] for b in middle]),
+                [have["early dstream"]],
+            )
+
+        have = run_plan(stream, mine, own_facts, paths, lambda: pick(hidden, owners, 2, tok), early_own, early_other)
+        out, dstream, parts = product(
+            owners, 0, have["other picks"], (have["coefs"], head_half, [have[b] for b in last]), (), have["other sum"]
         )
         swapped = to_core(out)
-        grad_head = jnp.sum(parts + have["early parts"], axis=0)
+        grad_head = jnp.sum(parts + have["middle parts"] + have["early parts"], axis=(0, 1))
         other_head = to_core(grad_head)
         grad_head = gain * jnp.where(
             mine == 0, jnp.concatenate([grad_head, other_head]), jnp.concatenate([other_head, grad_head])
         )
         where = mine[None].astype(jnp.int32)
-        grad_down = plain_product(have["own picks"], 0, dstream, have["early own"], jnp.bfloat16, where)
+        (grad_down,) = product(
+            owners, 0, have["own picks"], None, [dstream, have["middle dstream"]], have["early own"], where
+        )
         grad_down = put(grad_down, swapped, 1 - where)
-        own = lambda a: lax.dynamic_index_in_dim(a, me, 0, keepdims=False)
-        return (own(made["values"]), own(made["returns"]), grad_head, grad_down)
+        return (have["values"], have["returns"], grad_head, grad_down)
 
     return body
 

time: 125 us -> 133 us (1.064)
  Pallas kernels: 52.6 us -> 62.3 us
  waiting for transfers between devices: 35 us -> 33.3 us
    pallas_call x4, Pallas kernels: 41.4 us -> 51.2 us  [product(): pl.pallas_call(functools.partial(product_kernel, tok, count, first, len(g...]
    ppermute x16, waiting for transfers between devices: 24.3 us -> 22.2 us  [event(): self.have[name] = lax.ppermute(self.have[source], 'seq', pairs)]
  transfers between devices with their start and end apart: 23 -> 23, of which waited for: 9 -> 8; matrix products, arithmetic and copies ran while one was open for 7% -> 7% of each run, Pallas kernels for 31% -> 38%
where the time goes in v4:
time: 133 us
  Pallas kernels  62.3 us (47%)
  waiting for transfers between devices  33.3 us (25%)
  starting transfers between devices  24.6 us (18%)
  other arithmetic  6.31 us (5%)
  local copies, waits for them, and re-layouts  5.13 us (4%)
    pallas_call x4, Pallas kernels, product(): pl.pallas_call(functools.partial(product_kernel, tok, count, first, len(g...  51.2 us
    ppermute x16, waiting for transfers between devices, event(): self.have[name] = lax.ppermute(self.have[source], 'seq', pairs)  22.2 us
    ppermute x16, starting transfers between devices, event(): self.have[name] = lax.ppermute(self.have[source], 'seq', pairs)  21.8 us
    ppermute x4, waiting for transfers between devices, butterfly_step(): other = lax.ppermute(x, axis, [(i, i ^ step) for i in range(count)])  9.04 us
    pallas_call x1, Pallas kernels, pick(): pl.pallas_call(functools.partial(pick_kernel, tok), grid_spec=pltpu.Prefe...  8.15 us
    pallas_call x1, Pallas kernels, put(): pl.pallas_call(functools.partial(put_kernel, pieces), grid_spec=pltpu.Pre...  3.02 us
  transfers between devices with their start and end apart: 23, of which 8 were waited for; matrix products, arithmetic and copies ran while one was open for 7% of the time, Pallas kernels for 38%

profile of v4, /device:TPU:0, one launch (start us, length us, event | category | flops | bytes accessed | tf_op | source)
XLA Modules:
  0.0 132.7 jit_solution(9423003420349205132)
XLA Ops:
  0.7 1.3 %constant_dynamic-slice_fusion.4 = (bf16[128,2048]{1,0:T(8,128)(2,1)S(1)}, bf16[128,2048]{1,0:T(8,128)(2,1)S(1)}) fusion(bf16[128,4096]{1,0:T(8,128)(2,1)} %param.8, s32[]{:T(128)S(6)} %select_n.122, s32[]{:T(128)S(6)} %select_n.121), kind=kLoop, calls=%fused_computation.47 | loop fusion | bytes 2097160 | tf_op jit(solution)/shard_map/dynamic_slice | solution.py:82
  2.1 4.1 %collective-permute-start.3 = (bf16[128,2048]{1,0:T(8,128)(2,1)S(1)}, bf16[128,2048]{1,0:T(8,128)(2,1)S(1)}, u32[]{:S(2)}, u32[]{:S(2)}) collective-permute-start(bf16[128,2048]{1,0:T(8,128)(2,1)S(1)} %get-tuple-element.48.refs_3_), channel_id=1, source_target_pairs={{0,16},{2,10},{4,20},{6,14},{8,0},{10,26},{12,4},{14,30},{16,24},{... | collective-permute-start | bytes 1572872 | tf_op jit(solution)/shard_map/ppermute | solution.py:69
  6.2 1.5 %collective-permute-start.4 = (bf16[128,2048]{1,0:T(8,128)(2,1)S(1)}, bf16[128,2048]{1,0:T(8,128)(2,1)S(1)}, u32[]{:S(2)}, u32[]{:S(2)}) collective-permute-start(bf16[128,2048]{1,0:T(8,128)(2,1)S(1)} %get-tuple-element.48.refs_3_), channel_id=1, source_target_pairs={{0,4},{2,6},{4,0},{6,2},{8,12},{10,14},{12,8},{14,10},{16,20},{18,... | collective-permute-start | bytes 1572872 | tf_op jit(solution)/shard_map/ppermute | solution.py:69
  7.7 0.0 collective-permute-start
  7.7 1.2 fusion.8.owners
  8.9 8.1 %shard_map.111 = (bf16[896,2048]{1,0:T(8,128)(2,1)}, bf16[896,2048]{1,0:T(8,128)(2,1)}) custom-call(s32[32]{0:T(128)} %fusion.8.owners, bf16[896,2048]{1,0:T(8,128)(2,1)} %hidden.1), custom_call_target="tpu_custom_call" | custom-call | bytes 11010048 | tf_op jit(solution)/shard_map/pallas_call | solution.py:149
  17.1 0.0 collective-permute-done.refs_4_
  17.1 0.9 collective-permute-start.1
  18.0 0.6 collective-permute-start.2
  18.6 0.4 fusion
  19.0 0.0 collective-permute-done.3.refs_7_
  19.1 0.0 collective-permute-done.4.refs_5_
  19.1 1.6 %collective-permute-start.5 = (f32[4,128]{1,0:T(4,128)S(1)}, f32[4,128]{1,0:T(4,128)S(1)}, u32[]{:S(2)}, u32[]{:S(2)}) collective-permute-start(f32[4,128]{1,0:T(4,128)S(1)} %pad_maximum_fusion.4), channel_id=1, source_target_pairs={{0,1},{1,0},{2,3},{3,2},{4,5},{5,4},{6,7},{7,6},{8,9},{9,8},{10,11... | collective-permute-start | bytes 6152 | tf_op jit(solution)/shard_map/ppermute | solution.py:18
  20.6 2.1 %collective-permute-done.5 = f32[4,128]{1,0:T(4,128)S(1)} collective-permute-done((f32[4,128]{1,0:T(4,128)S(1)}, f32[4,128]{1,0:T(4,128)S(1)}, u32[]{:S(2)}, u32[]{:S(2)}) %collective-permute-start.5) | collective-permute-done | bytes 2080 | tf_op jit(solution)/shard_map/ppermute | solution.py:18
  22.7 1.5 %collective-permute-start.10 = (bf16[128,2048]{1,0:T(8,128)(2,1)S(1)}, bf16[128,2048]{1,0:T(8,128)(2,1)S(1)}, u32[]{:S(2)}, u32[]{:S(2)}) collective-permute-start(bf16[128,2048]{1,0:T(8,128)(2,1)S(1)} %collective-permute-done.3.refs_7_), channel_id=1, source_target_pairs={{0,4},{2,6},{4,0},{6,2},{8,12},{10,14},{12,8},{14,10},{16,20},{18,... | collective-permute-start | bytes 1572872 | tf_op jit(solution)/shard_map/ppermute | solution.py:69
  24.2 2.1 %collective-permute-start.9 = (bf16[128,2048]{1,0:T(8,128)(2,1)S(1)}, bf16[128,2048]{1,0:T(8,128)(2,1)}, u32[]{:S(2)}, u32[]{:S(2)}) collective-permute-start(bf16[128,2048]{1,0:T(8,128)(2,1)S(1)} %collective-permute-done.3.refs_7_), channel_id=1, source_target_pairs={{0,16},{2,10},{4,20},{6,14},{8,0},{10,26},{12,4},{14,30},{16,24},{... | collective-permute-start | bytes 1572872 | tf_op jit(solution)/shard_map/ppermute | solution.py:69
  26.3 0.0 collective-permute-done.6
  26.3 10.4 %collective-permute-done.1.refs_8_ = bf16[128,2048]{1,0:T(8,128)(2,1)S(1)} collective-permute-done((bf16[128,2048]{1,0:T(8,128)(2,1)}, bf16[128,2048]{1,0:T(8,128)(2,1)S(1)}, u32[]{:S(2)}, u32[]{:S(2)}) %collective-permute-start.1) | collective-permute-done | bytes 524320 | tf_op jit(solution)/shard_map/ppermute | solution.py:69
  36.7 0.6 collective-permute-start.11
  37.3 1.5 %collective-permute-start.8 = (bf16[128,2048]{1,0:T(8,128)(2,1)S(1)}, bf16[128,2048]{1,0:T(8,128)(2,1)}, u32[]{:S(2)}, u32[]{:S(2)}) collective-permute-start(bf16[128,2048]{1,0:T(8,128)(2,1)S(1)} %collective-permute-done.1.refs_8_), channel_id=1, source_target_pairs={{0,4},{2,6},{4,0},{6,2},{8,12},{10,14},{12,8},{14,10},{16,20},{18,... | collective-permute-start | bytes 1572872 | tf_op jit(solution)/shard_map/ppermute | solution.py:69
  38.8 5.6 %collective-permute-done.11 = f32[2,4,128]{2,0,1:T(2,128)S(1)} collective-permute-done((f32[2,4,128]{2,0,1:T(2,128)S(1)}, f32[2,4,128]{2,0,1:T(2,128)S(1)}, u32[]{:S(2)}, u32[]{:S(2)}) %collective-permute-start.11) | collective-permute-done | bytes 4128 | tf_op jit(solution)/shard_map/ppermute | solution.py:28
  44.4 0.0 collective-permute-done.10.refs_9_
  44.4 3.1 %collective-permute-done.9.refs_11_ = bf16[128,2048]{1,0:T(8,128)(2,1)} collective-permute-done((bf16[128,2048]{1,0:T(8,128)(2,1)S(1)}, bf16[128,2048]{1,0:T(8,128)(2,1)}, u32[]{:S(2)}, u32[]{:S(2)}) %collective-permute-start.9) | collective-permute-done | bytes 524320 | tf_op jit(solution)/shard_map/ppermute | solution.py:69
  47.5 3.3 %collective-permute-start.16 = (bf16[128,2048]{1,0:T(8,128)(2,1)}, bf16[128,2048]{1,0:T(8,128)(2,1)}, u32[]{:S(2)}, u32[]{:S(2)}) collective-permute-start(bf16[128,2048]{1,0:T(8,128)(2,1)} %collective-permute-done.9.refs_11_), channel_id=1, source_target_pairs={{0,4},{2,6},{4,0},{6,2},{8,12},{10,14},{12,8},{14,10},{16,20},{18,... | collective-permute-start | bytes 1572872 | tf_op jit(solution)/shard_map/ppermute | solution.py:69
  50.8 2.2 %collective-permute-done.12 = f32[4,4,128]{2,0,1:T(4,128)S(1)} collective-permute-done((f32[4,4,128]{2,0,1:T(4,128)S(1)}, f32[4,4,128]{2,0,1:T(4,128)S(1)}, u32[]{:S(2)}, u32[]{:S(2)}) %collective-permute-start.12) | collective-permute-done | bytes 8224 | tf_op jit(solution)/shard_map/ppermute | solution.py:28
  53.0 7.2 %collective-permute-done.7.refs_12_ = bf16[128,2048]{1,0:T(8,128)(2,1)} collective-permute-done((bf16[128,2048]{1,0:T(8,128)(2,1)S(1)}, bf16[128,2048]{1,0:T(8,128)(2,1)}, u32[]{:S(2)}, u32[]{:S(2)}) %collective-permute-start.7) | collective-permute-done | bytes 524320 | tf_op jit(solution)/shard_map/ppermute | solution.py:69
  60.1 0.0 collective-permute-done.8.refs_10_
  60.1 0.0 collective-permute-start.17
  60.2 0.6 dynamic_slice.23
  60.8 1.6 %collective-permute-start.13 = (bf16[128,2048]{1,0:T(8,128)(2,1)}, bf16[128,2048]{1,0:T(8,128)(2,1)}, u32[]{:S(2)}, u32[]{:S(2)}) collective-permute-start(bf16[128,2048]{1,0:T(8,128)(2,1)} %collective-permute-done.7.refs_12_), channel_id=1, source_target_pairs={{0,8},{2,18},{4,12},{6,22},{8,24},{10,2},{12,28},{14,6},{16,0},{18... | collective-permute-start | bytes 1572872 | tf_op jit(solution)/shard_map/ppermute | solution.py:69
  62.4 1.8 %collective-permute-start.14 = (bf16[128,2048]{1,0:T(8,128)(2,1)}, bf16[128,2048]{1,0:T(8,128)(2,1)}, u32[]{:S(2)}, u32[]{:S(2)}) collective-permute-start(bf16[128,2048]{1,0:T(8,128)(2,1)} %collective-permute-done.7.refs_12_), channel_id=1, source_target_pairs={{0,4},{2,6},{4,0},{6,2},{8,12},{10,14},{12,8},{14,10},{16,20},{18,... | collective-permute-start | bytes 1572872 | tf_op jit(solution)/shard_map/ppermute | solution.py:69
  64.1 1.3 collective-permute-done.17
  65.4 2.9 %collective-permute-start.18 = (bf16[896,2048]{1,0:T(8,128)(2,1)}, bf16[896,2048]{1,0:T(8,128)(2,1)}, u32[]{:S(2)}, u32[]{:S(2)}) collective-permute-start(bf16[896,2048]{1,0:T(8,128)(2,1)} %get-tuple-element.62), channel_id=1, source_target_pairs={{0,2},{2,0},{4,6},{6,4},{8,10},{10,8},{12,14},{14,12},{16,18},{18,... | collective-permute-start | bytes 11010056 | tf_op jit(solution)/shard_map/ppermute | solution.py:69
  68.3 1.5 %collective-permute-done.15.refs_5_ = bf16[128,2048]{1,0:T(8,128)(2,1)} collective-permute-done((bf16[128,2048]{1,0:T(8,128)(2,1)}, bf16[128,2048]{1,0:T(8,128)(2,1)}, u32[]{:S(2)}, u32[]{:S(2)}) %collective-permute-start.15) | collective-permute-done | bytes 524320 | tf_op jit(solution)/shard_map/ppermute | solution.py:69
  69.8 0.1 fusion.15
  69.9 0.3 reduce_window_sum.22
  70.2 0.1 broadcast_compare_fusion
  70.3 0.1 fusion.7
  70.5 0.7 select_reduce_fusion
  71.1 0.1 slice_reduce_fusion
  71.2 0.1 reduce.1
  71.4 0.2 select_reduce_fusion.1
  71.5 0.7 dynamic-slice.1
  72.2 0.1 broadcast_in_dim.84
  72.3 0.1 eq.84
  72.4 0.1 collective-permute-start.19
  72.5 0.6 select_maximum_fusion.refs_1_
  73.1 16.2 %shard_map.112 = (f32[896,2048]{1,0:T(8,128)}, bf16[1280,2048]{1,0:T(8,128)(2,1)}, f32[16,1,2048]{2,1,0:T(1,128)}) custom-call(s32[32]{0:T(128)} %fusion.8.owners, s32[1]{0:T(128)} %constant.64.clone.1.where, bf16[896,2048]{1,0:T(8,128)(2,1)} %get-tuple-element.63.refs_0_, f32[8,2048]{1,0:T(8,128)} %select_maximum_fusion.refs_1_, f32[1,2048]{1,0:T(1,128)} %bitcast.54, ...), custom_call_target="tpu_custom_call" | custom-call | flops 46976204800 | bytes 86376448 | tf_op jit(solution)/shard_map/pallas_call | solution.py:281
  89.3 0.5 fusion.10
  89.9 1.2 fusion.12
  91.1 0.0 collective-permute-done.13.refs_6_
  91.1 0.0 collective-permute-done.14.refs_4_
  91.1 0.1 collective-permute-start.20
  91.2 16.3 %shard_map.113 = (f32[896,2048]{1,0:T(8,128)}, bf16[512,2048]{1,0:T(8,128)(2,1)}, f32[16,1,2048]{2,1,0:T(1,128)}) custom-call(s32[32]{0:T(128)} %fusion.8.owners, s32[1]{0:T(128)} %constant.64.clone.1.where, bf16[896,2048]{1,0:T(8,128)(2,1)} %collective-permute-done.18.refs_0_, f32[8,2048]{1,0:T(8,128)} %select_maximum_fusion.refs_1_, f32[1,2048]{1,0:T(1,128)} %bitcast.55, ...), custom_call_target="tpu_custom_call" | custom-call | flops 6576668672 | bytes 21561344 | tf_op jit(solution)/shard_map/pallas_call | solution.py:281
  107.6 0.8 copy-done.1
  108.4 0.2 copy-done.2
  108.6 9.0 %shard_map.114 = (bf16[896,2048]{1,0:T(8,128)(2,1)}, bf16[256,2048]{1,0:T(8,128)(2,1)}, f32[16,1,2048]{2,1,0:T(1,128)}) custom-call(s32[32]{0:T(128)} %fusion.8.owners, s32[1]{0:T(128)} %constant.64.clone.1.where, bf16[896,2048]{1,0:T(8,128)(2,1)} %collective-permute-done.18.refs_0_, f32[8,2048]{1,0:T(8,128)} %select_maximum_fusion.refs_1_, ...), custom_call_target="tpu_custom_call" | custom-call | flops 939524096 | bytes 12517376 | tf_op jit(solution)/shard_map/pallas_call | solution.py:281
  117.5 0.1 collective-permute-start.22
  117.7 1.2 add_reduce_fusion
  118.8 0.5 collective-permute-start.21
  119.4 9.7 %shard_map.115.whole = bf16[896,4096]{1,0:T(8,128)(2,1)} custom-call(s32[32]{0:T(128)} %fusion.8.owners, s32[1]{0:T(128)} %bitcast.20.where, bf16[896,2048]{1,0:T(8,128)(2,1)} %get-tuple-element.63.refs_0_, bf16[256,2048]{1,0:T(8,128)(2,1)} %get-tuple-element.85.refs_1_, bf16[512,2048]{1,0:T(8,128)(2,1)} %get-tuple-element.86.refs_2_, ...), custom_call_target="tpu_custom_call" | custom-call | flops 2818572288 | bytes 15532032 | tf_op jit(solution)/shard_map/pallas_call | solution.py:281
  129.1 0.6 convert_multiply_fusion.2
  129.7 0.0 collective-permute-done.22.part
  129.7 3.0 %shard_map.116 = bf16[896,4096]{1,0:T(8,128)(2,1)} custom-call(s32[1]{0:T(128)S(6)} %sub.64.where, bf16[896,2048]{1,0:T(8,128)(2,1)} %collective-permute-done.22.part, bf16[896,4096]{1,0:T(8,128)(2,1)} %shard_map.115.whole), custom_call_target="tpu_custom_call", output_to_operand_aliasing={{}: (2, {})} | custom-call | bytes 7340032 | tf_op jit(solution)/shard_map/pallas_call | solution.py:324
  (56 shorter events, 0.3 us)
Async XLA Ops:
  0.6 18.0 %copy-start = (bf16[128,4096]{1,0:T(8,128)(2,1)S(1)}, bf16[128,4096]{1,0:T(8,128)(2,1)}, u32[]{:S(2)}) copy-start(bf16[128,4096]{1,0:T(8,128)(2,1)} %param.8) | copy-start | bytes 3145732
  0.6 16.4 %copy-start.6 = (bf16[4096]{0:T(1024)(128)(2,1)S(1)}, bf16[4096]{0:T(1024)(128)(2,1)}, u32[]{:S(2)}) copy-start(bf16[4096]{0:T(1024)(128)(2,1)} %param.10) | copy-start | bytes 24580
  0.7 16.4 %copy-start.7 = (bf16[4096]{0:T(1024)(128)(2,1)S(1)}, bf16[4096]{0:T(1024)(128)(2,1)}, u32[]{:S(2)}) copy-start(bf16[4096]{0:T(1024)(128)(2,1)} %param.11) | copy-start | bytes 24580
  0.7 16.4 %copy-start.9 = (f32[128]{0:T(128)S(1)}, f32[128]{0:T(128)}, u32[]{:S(2)}) copy-start(f32[128]{0:T(128)} %param.12) | copy-start | bytes 1540
  0.7 16.4 %copy-start.10 = (f32[128]{0:T(128)S(1)}, f32[128]{0:T(128)}, u32[]{:S(2)}) copy-start(f32[128]{0:T(128)} %param.13) | copy-start | bytes 1540
  0.7 16.4 %copy-start.8 = (s32[128]{0:T(128)S(1)}, s32[128]{0:T(128)}, u32[]{:S(2)}) copy-start(s32[128]{0:T(128)} %param.14) | copy-start | bytes 1540
  2.1 71.1 %copy-start.3 = (bf16[128,2048]{1,0:T(8,128)(2,1)}, bf16[128,2048]{1,0:T(8,128)(2,1)S(1)}, u32[]{:S(2)}) copy-start(bf16[128,2048]{1,0:T(8,128)(2,1)S(1)} %get-tuple-element.48.refs_3_) | copy-start | bytes 1572868
  2.1 17.0 %collective-permute-start.3 = (bf16[128,2048]{1,0:T(8,128)(2,1)S(1)}, bf16[128,2048]{1,0:T(8,128)(2,1)S(1)}, u32[]{:S(2)}, u32[]{:S(2)}) collective-permute-start(bf16[128,2048]{1,0:T(8,128)(2,1)S(1)} %get-tuple-element.48.refs_3_), channel_id=1, source_target_pairs={{0,16},{2,10},{4,20},{6,14},{8,0},{10,26},{12,4},{14,30},{16,24},{... | collective-permute-start | bytes 1572872 | tf_op jit(solution)/shard_map/ppermute | solution.py:69
  6.2 12.9 %collective-permute-start.4 = (bf16[128,2048]{1,0:T(8,128)(2,1)S(1)}, bf16[128,2048]{1,0:T(8,128)(2,1)S(1)}, u32[]{:S(2)}, u32[]{:S(2)}) collective-permute-start(bf16[128,2048]{1,0:T(8,128)(2,1)S(1)} %get-tuple-element.48.refs_3_), channel_id=1, source_target_pairs={{0,4},{2,6},{4,0},{6,2},{8,12},{10,14},{12,8},{14,10},{16,20},{18,... | collective-permute-start | bytes 1572872 | tf_op jit(solution)/shard_map/ppermute | solution.py:69
  7.7 9.4 %collective-permute-start = (bf16[128,2048]{1,0:T(8,128)(2,1)S(1)}, bf16[128,2048]{1,0:T(8,128)(2,1)}, u32[]{:S(2)}, u32[]{:S(2)}) collective-permute-start(bf16[128,2048]{1,0:T(8,128)(2,1)S(1)} %get-tuple-element.46), channel_id=1, source_target_pairs={{0,2},{2,0},{4,6},{6,4},{8,10},{10,8},{12,14},{14,12},{16,18},{18,... | collective-permute-start | bytes 1572872 | tf_op jit(solution)/shard_map/ppermute | solution.py:69
  17.1 19.6 %collective-permute-start.1 = (bf16[128,2048]{1,0:T(8,128)(2,1)}, bf16[128,2048]{1,0:T(8,128)(2,1)S(1)}, u32[]{:S(2)}, u32[]{:S(2)}) collective-permute-start(bf16[128,2048]{1,0:T(8,128)(2,1)} %collective-permute-done.refs_4_), channel_id=1, source_target_pairs={{0,8},{2,18},{4,12},{6,22},{8,24},{10,2},{12,28},{14,6},{16,0},{18... | collective-permute-start | bytes 1572872 | tf_op jit(solution)/shard_map/ppermute | solution.py:69
  18.0 18.7 %collective-permute-start.2 = (bf16[128,2048]{1,0:T(8,128)(2,1)}, bf16[128,2048]{1,0:T(8,128)(2,1)}, u32[]{:S(2)}, u32[]{:S(2)}) collective-permute-start(bf16[128,2048]{1,0:T(8,128)(2,1)} %collective-permute-done.refs_4_), channel_id=1, source_target_pairs={{0,4},{2,6},{4,0},{6,2},{8,12},{10,14},{12,8},{14,10},{16,20},{18,... | collective-permute-start | bytes 1572872 | tf_op jit(solution)/shard_map/ppermute | solution.py:69
  19.0 54.1 %copy-start.11 = (bf16[128,2048]{1,0:T(8,128)(2,1)}, bf16[128,2048]{1,0:T(8,128)(2,1)S(1)}, u32[]{:S(2)}) copy-start(bf16[128,2048]{1,0:T(8,128)(2,1)S(1)} %collective-permute-done.3.refs_7_) | copy-start | bytes 1572868
  19.1 54.1 %copy-start.12 = (bf16[128,2048]{1,0:T(8,128)(2,1)}, bf16[128,2048]{1,0:T(8,128)(2,1)S(1)}, u32[]{:S(2)}) copy-start(bf16[128,2048]{1,0:T(8,128)(2,1)S(1)} %collective-permute-done.4.refs_5_) | copy-start | bytes 1572868
  19.1 3.7 %collective-permute-start.5 = (f32[4,128]{1,0:T(4,128)S(1)}, f32[4,128]{1,0:T(4,128)S(1)}, u32[]{:S(2)}, u32[]{:S(2)}) collective-permute-start(f32[4,128]{1,0:T(4,128)S(1)} %pad_maximum_fusion.4), channel_id=1, source_target_pairs={{0,1},{1,0},{2,3},{3,2},{4,5},{5,4},{6,7},{7,6},{8,9},{9,8},{10,11... | collective-permute-start | bytes 6152 | tf_op jit(solution)/shard_map/ppermute | solution.py:18
  22.7 3.6 %collective-permute-start.6 = (f32[1,4,128]{2,0,1:T(1,128)S(1)}, f32[1,4,128]{2,0,1:T(1,128)S(1)}, u32[]{:S(2)}, u32[]{:S(2)}) collective-permute-start(f32[1,4,128]{2,0,1:T(1,128)S(1)} %bitcast.60), channel_id=1, source_target_pairs={{0,2},{2,0},{4,6},{6,4},{8,10},{10,8},{12,14},{14,12},{16,18},{18,... | collective-permute-start | bytes 6152 | tf_op jit(solution)/shard_map/ppermute | solution.py:28
  22.7 21.6 %collective-permute-start.10 = (bf16[128,2048]{1,0:T(8,128)(2,1)S(1)}, bf16[128,2048]{1,0:T(8,128)(2,1)S(1)}, u32[]{:S(2)}, u32[]{:S(2)}) collective-permute-start(bf16[128,2048]{1,0:T(8,128)(2,1)S(1)} %collective-permute-done.3.refs_7_), channel_id=1, source_target_pairs={{0,4},{2,6},{4,0},{6,2},{8,12},{10,14},{12,8},{14,10},{16,20},{18,... | collective-permute-start | bytes 1572872 | tf_op jit(solution)/shard_map/ppermute | solution.py:69
  24.2 23.2 %collective-permute-start.9 = (bf16[128,2048]{1,0:T(8,128)(2,1)S(1)}, bf16[128,2048]{1,0:T(8,128)(2,1)}, u32[]{:S(2)}, u32[]{:S(2)}) collective-permute-start(bf16[128,2048]{1,0:T(8,128)(2,1)S(1)} %collective-permute-done.3.refs_7_), channel_id=1, source_target_pairs={{0,16},{2,10},{4,20},{6,14},{8,0},{10,26},{12,4},{14,30},{16,24},{... | collective-permute-start | bytes 1572872 | tf_op jit(solution)/shard_map/ppermute | solution.py:69
  36.7 36.4 %copy-start.13 = (bf16[128,2048]{1,0:T(8,128)(2,1)}, bf16[128,2048]{1,0:T(8,128)(2,1)S(1)}, u32[]{:S(2)}) copy-start(bf16[128,2048]{1,0:T(8,128)(2,1)S(1)} %collective-permute-done.1.refs_8_) | copy-start | bytes 1572868
  36.7 7.6 %collective-permute-start.11 = (f32[2,4,128]{2,0,1:T(2,128)S(1)}, f32[2,4,128]{2,0,1:T(2,128)S(1)}, u32[]{:S(2)}, u32[]{:S(2)}) collective-permute-start(f32[2,4,128]{2,0,1:T(2,128)S(1)} %pad_maximum_fusion.3), channel_id=1, source_target_pairs={{0,4},{2,6},{4,0},{6,2},{8,12},{10,14},{12,8},{14,10},{16,20},{18,... | collective-permute-start | bytes 12296 | tf_op jit(solution)/shard_map/ppermute | solution.py:28
  37.3 22.8 %collective-permute-start.7 = (bf16[128,2048]{1,0:T(8,128)(2,1)S(1)}, bf16[128,2048]{1,0:T(8,128)(2,1)}, u32[]{:S(2)}, u32[]{:S(2)}) collective-permute-start(bf16[128,2048]{1,0:T(8,128)(2,1)S(1)} %collective-permute-done.1.refs_8_), channel_id=1, source_target_pairs={{0,8},{2,18},{4,12},{6,22},{8,24},{10,2},{12,28},{14,6},{16,0},{18... | collective-permute-start | bytes 1572872 | tf_op jit(solution)/shard_map/ppermute | solution.py:69
  37.3 22.8 %collective-permute-start.8 = (bf16[128,2048]{1,0:T(8,128)(2,1)S(1)}, bf16[128,2048]{1,0:T(8,128)(2,1)}, u32[]{:S(2)}, u32[]{:S(2)}) collective-permute-start(bf16[128,2048]{1,0:T(8,128)(2,1)S(1)} %collective-permute-done.1.refs_8_), channel_id=1, source_target_pairs={{0,4},{2,6},{4,0},{6,2},{8,12},{10,14},{12,8},{14,10},{16,20},{18,... | collective-permute-start | bytes 1572872 | tf_op jit(solution)/shard_map/ppermute | solution.py:69
  44.4 28.8 %copy-start.14 = (bf16[128,2048]{1,0:T(8,128)(2,1)}, bf16[128,2048]{1,0:T(8,128)(2,1)S(1)}, u32[]{:S(2)}) copy-start(bf16[128,2048]{1,0:T(8,128)(2,1)S(1)} %collective-permute-done.10.refs_9_) | copy-start | bytes 1572868
  47.4 5.5 %collective-permute-start.12 = (f32[4,4,128]{2,0,1:T(4,128)S(1)}, f32[4,4,128]{2,0,1:T(4,128)S(1)}, u32[]{:S(2)}, u32[]{:S(2)}) collective-permute-start(f32[4,4,128]{2,0,1:T(4,128)S(1)} %pad_maximum_fusion.2), channel_id=1, source_target_pairs={{0,8},{2,10},{4,12},{6,14},{8,0},{10,2},{12,4},{14,6},{16,24},{18,... | collective-permute-start | bytes 24584 | tf_op jit(solution)/shard_map/ppermute | solution.py:28
  47.5 22.4 %collective-permute-start.15 = (bf16[128,2048]{1,0:T(8,128)(2,1)}, bf16[128,2048]{1,0:T(8,128)(2,1)}, u32[]{:S(2)}, u32[]{:S(2)}) collective-permute-start(bf16[128,2048]{1,0:T(8,128)(2,1)} %collective-permute-done.9.refs_11_), channel_id=1, source_target_pairs={{0,16},{2,10},{4,20},{6,14},{8,0},{10,26},{12,4},{14,30},{16,24},{... | collective-permute-start | bytes 1572872 | tf_op jit(solution)/shard_map/ppermute | solution.py:69
  47.5 22.4 %collective-permute-start.16 = (bf16[128,2048]{1,0:T(8,128)(2,1)}, bf16[128,2048]{1,0:T(8,128)(2,1)}, u32[]{:S(2)}, u32[]{:S(2)}) collective-permute-start(bf16[128,2048]{1,0:T(8,128)(2,1)} %collective-permute-done.9.refs_11_), channel_id=1, source_target_pairs={{0,4},{2,6},{4,0},{6,2},{8,12},{10,14},{12,8},{14,10},{16,20},{18,... | collective-permute-start | bytes 1572872 | tf_op jit(solution)/shard_map/ppermute | solution.py:69
  60.1 5.3 %collective-permute-start.17 = (f32[8,4,128]{2,0,1:T(8,128)S(1)}, f32[8,4,128]{2,0,1:T(8,128)S(1)}, u32[]{:S(2)}, u32[]{:S(2)}) collective-permute-start(f32[8,4,128]{2,0,1:T(8,128)S(1)} %pad_maximum_fusion.1), channel_id=1, source_target_pairs={{0,16},{2,18},{4,20},{6,22},{8,24},{10,26},{12,28},{14,30},{16,0},... | collective-permute-start | bytes 49160 | tf_op jit(solution)/shard_map/ppermute | solution.py:28
  60.8 30.3 %collective-permute-start.13 = (bf16[128,2048]{1,0:T(8,128)(2,1)}, bf16[128,2048]{1,0:T(8,128)(2,1)}, u32[]{:S(2)}, u32[]{:S(2)}) collective-permute-start(bf16[128,2048]{1,0:T(8,128)(2,1)} %collective-permute-done.7.refs_12_), channel_id=1, source_target_pairs={{0,8},{2,18},{4,12},{6,22},{8,24},{10,2},{12,28},{14,6},{16,0},{18... | collective-permute-start | bytes 1572872 | tf_op jit(solution)/shard_map/ppermute | solution.py:69
  62.4 28.7 %collective-permute-start.14 = (bf16[128,2048]{1,0:T(8,128)(2,1)}, bf16[128,2048]{1,0:T(8,128)(2,1)}, u32[]{:S(2)}, u32[]{:S(2)}) collective-permute-start(bf16[128,2048]{1,0:T(8,128)(2,1)} %collective-permute-done.7.refs_12_), channel_id=1, source_target_pairs={{0,4},{2,6},{4,0},{6,2},{8,12},{10,14},{12,8},{14,10},{16,20},{18,... | collective-permute-start | bytes 1572872 | tf_op jit(solution)/shard_map/ppermute | solution.py:69
  65.4 25.7 %collective-permute-start.18 = (bf16[896,2048]{1,0:T(8,128)(2,1)}, bf16[896,2048]{1,0:T(8,128)(2,1)}, u32[]{:S(2)}, u32[]{:S(2)}) collective-permute-start(bf16[896,2048]{1,0:T(8,128)(2,1)} %get-tuple-element.62), channel_id=1, source_target_pairs={{0,2},{2,0},{4,6},{6,4},{8,10},{10,8},{12,14},{14,12},{16,18},{18,... | collective-permute-start | bytes 11010056 | tf_op jit(solution)/shard_map/ppermute | solution.py:69
  72.4 35.1 %collective-permute-start.19 = (bf16[128,2048]{1,0:T(8,128)(2,1)}, bf16[128,2048]{1,0:T(8,128)(2,1)S(1)}, u32[]{:S(2)}, u32[]{:S(2)}) collective-permute-start(bf16[128,2048]{1,0:T(8,128)(2,1)} %collective-permute-done.16.refs_3_), channel_id=1, source_target_pairs={{0,16},{2,10},{4,20},{6,14},{8,0},{10,26},{12,4},{14,30},{16,24},{... | collective-permute-start | bytes 1572872 | tf_op jit(solution)/shard_map/ppermute | solution.py:69
  91.1 16.5 %collective-permute-start.20 = (bf16[128,2048]{1,0:T(8,128)(2,1)}, bf16[128,2048]{1,0:T(8,128)(2,1)S(1)}, u32[]{:S(2)}, u32[]{:S(2)}) collective-permute-start(bf16[128,2048]{1,0:T(8,128)(2,1)} %collective-permute-done.13.refs_6_), channel_id=1, source_target_pairs={{0,4},{2,6},{4,0},{6,2},{8,12},{10,14},{12,8},{14,10},{16,20},{18,... | collective-permute-start | bytes 1572872 | tf_op jit(solution)/shard_map/ppermute | solution.py:69
  107.6 0.8 copy-start.1
  107.6 1.0 copy-start.2
  108.6 9.1 %copy-start.4 = (f32[16,1,2048]{2,1,0:T(1,128)S(1)}, f32[16,1,2048]{2,1,0:T(1,128)}, u32[]{:S(2)}) copy-start(f32[16,1,2048]{2,1,0:T(1,128)} %get-tuple-element.83) | copy-start | bytes 393220
  108.6 9.1 %copy-start.5 = (f32[16,1,2048]{2,1,0:T(1,128)S(1)}, f32[16,1,2048]{2,1,0:T(1,128)}, u32[]{:S(2)}) copy-start(f32[16,1,2048]{2,1,0:T(1,128)} %get-tuple-element.82) | copy-start | bytes 393220
  117.5 12.1 %collective-permute-start.22 = (bf16[896,2048]{1,0:T(8,128)(2,1)}, bf16[896,2048]{1,0:T(8,128)(2,1)}, u32[]{:S(2)}, u32[]{:S(2)}) collective-permute-start(bf16[896,2048]{1,0:T(8,128)(2,1)} %get-tuple-element.84), channel_id=1, source_target_pairs={{0,2},{2,0},{4,6},{6,4},{8,10},{10,8},{12,14},{14,12},{16,18},{18,... | collective-permute-start | bytes 11010056 | tf_op jit(solution)/shard_map/ppermute | solution.py:371
  118.8 10.2 %collective-permute-start.21 = (f32[2048]{0:T(1024)S(1)}, f32[2048]{0:T(1024)S(1)}, u32[]{:S(2)}, u32[]{:S(2)}) collective-permute-start(f32[2048]{0:T(1024)S(1)} %add_reduce_fusion), channel_id=1, source_target_pairs={{0,2},{2,0},{4,6},{6,4},{8,10},{10,8},{12,14},{14,12},{16,18},{18,... | collective-permute-start | bytes 24584 | tf_op jit(solution)/shard_map/ppermute | solution.py:371

commit v5 on v4

--- a/solution.py
+++ b/solution.py
@@ -125,7 +125,7 @@
     return have
 
 
-PARAMS = pltpu.CompilerParams(vmem_limit_bytes=60 * 1024 * 1024)
+PARAMS = pltpu.CompilerParams(vmem_limit_bytes=16 * 1024 * 1024)
 
 
 def cost(units, k, width, extra):
@@ -166,93 +166,74 @@
 
 
 def form(tok, owners, first, weights, pulls, head, blocks, dstream, parts, start, chunk):
-    for b in range(blocks.shape[0] // tok):
+    for b in range(len(blocks)):
         rows = slice(b * tok, (b + 1) * tok)
         for at in range(0, chunk, 128):
             lanes = pl.ds(pl.multiple_of(start + at, 128), 128)
-            stream_f = blocks[rows, lanes].astype(jnp.float32)
+            stream_f = blocks[b][:, lanes].astype(jnp.float32)
             weight = weights[rows, :]
             dstream[rows, lanes] = (weight * head[:, lanes] - pulls[rows, :] * stream_f).astype(jnp.bfloat16)
             parts[owners[first + b], :, lanes] = jnp.sum(weight * stream_f, axis=0, keepdims=True)
 
 
-def product_kernel(tok, count, first, given_count, added, chunk, owners, where, *refs):
+def pieces_of(units):
+    return next(n for n in (7, 4, 2, 1) if units % (16 * n) == 0)
+
+
+def product_kernel(tok, count, first, given_count, added, parts_count, wide, chunk, owners, where, *refs):
     refs = list(refs)
     take = lambda n: [refs.pop(0) for _ in range(n)]
     (picked,) = take(1)
     coefs, head = take(2) if count else (None, None)
-    blocks, given, total = take(count), take(given_count), take(added)
+    blocks, given, total, other_parts = take(count), take(given_count), take(added), take(parts_count)
     (out,) = take(1)
-    dstream, parts = take(2) if count else (None, None)
-    picked_v, dstream_v, sum_v = take(3)
-    blocks_v, weights, pulls = take(3) if count else (None, None, None)
-    out_v = take(1)[0] if added else sum_v
-    sem_picked, sem_blocks, sem_given, sem_total, sem_out, sem_dstream = take(6)
-    half = sum_v.shape[1]
+    dstream, parts_out = take(2) if count else (None, None)
+    weights, pulls, parts = take(3) if count else (None, None, None)
+    out_v = take(1)[0] if wide else out
+    (sem_out,) = take(1)
+    half = out_v.shape[1]
     steps = half // chunk
-    k = picked_v.shape[1]
-    formed = count * tok
     base = pl.multiple_of(where[0] * half, half)
 
     columns = lambda c: pl.ds(pl.multiple_of(c * chunk, chunk), chunk)
-    get_picked = pltpu.make_async_copy(picked.at[:, pl.ds(first * tok, k)], picked_v, sem_picked)
-    get_blocks = [
-        pltpu.make_async_copy(ref, blocks_v.at[pl.ds(b * tok, tok), :], sem_blocks.at[b]) for b, ref in enumerate(blocks)
-    ]
-
-    def get_given(g, c):
-        row = formed + sum(ref.shape[0] for ref in given[:g])
-        rows = pl.ds(row, given[g].shape[0])
-        return pltpu.make_async_copy(given[g].at[:, columns(c)], dstream_v.at[rows, columns(c)], sem_given.at[g, c])
-
-    def get_total(c):
-        return pltpu.make_async_copy(total[0].at[:, columns(c)], sum_v.at[:, columns(c)], sem_total.at[c])
 
     def put_out(c):
         there = pl.ds(pl.multiple_of(base + c * chunk, chunk), chunk)
         return pltpu.make_async_copy(out_v.at[:, columns(c)], out.at[:, there], sem_out.at[c])
 
-    def put_dstream(c):
-        rows = pl.ds(0, formed)
-        return pltpu.make_async_copy(dstream_v.at[rows, columns(c)], dstream.at[:, columns(c)], sem_dstream.at[c])
-
-    for copy in get_blocks:
-        copy.start()
-    get_picked.start()
-    for c in range(steps):
-        for g in range(given_count):
-            get_given(g, c).start()
-        if added:
-            get_total(c).start()
     if count:
         parts[...] = jnp.zeros_like(parts)
         spread(tok, owners, first, coefs, weights, pulls)
-    for copy in get_blocks:
-        copy.wait()
-    get_picked.wait()
 
     def step(c, carry):
         if count:
-            form(tok, owners, first, weights, pulls, head, blocks_v, dstream_v, parts, c * chunk, chunk)
-            put_dstream(c).start()
-        for g in range(given_count):
-            get_given(g, c).wait()
-        here = jnp.dot(picked_v[...], dstream_v[:, columns(c)], preferred_element_type=jnp.float32)
-        if added:
-            get_total(c).wait()
-            here += sum_v[:, columns(c)]
+            form(tok, owners, first, weights, pulls, head, blocks, dstream, parts, c * chunk, chunk)
+
+        factors = ([dstream] if count else []) + given
+        here = total[0][:, columns(c)] if added else None
+        at = first * tok
+        for factor in factors:
+            depth = factor.shape[0]
+            term = jnp.dot(picked[:, at : at + depth], factor[:, columns(c)], preferred_element_type=jnp.float32)
+            here = term if here is None else here + term
+            at += depth
         out_v[:, columns(c)] = here.astype(out_v.dtype)
-        put_out(c).start()
+        if wide:
+            put_out(c).start()
         return carry
 
     lax.fori_loop(0, steps, step, 0)
-    for c in range(steps):
-        put_out(c).wait()
-        if count:
-            put_dstream(c).wait()
-
-
-def product(owners, first, picked, formed=None, given=(), total=None, where=None):
+    if count:
+        if other_parts:
+            parts_out[...] = sum([p[...] for p in other_parts], parts[...]).sum(axis=0)
+        else:
+            parts_out[...] = parts[...]
+    if wide:
+        for c in range(steps):
+            put_out(c).wait()
+
+
+def product(owners, first, picked, formed=None, given=(), total=None, parts=(), where=None):
     units, tokens = picked.shape
     coefs, head, blocks = formed or (None, None, [])
     half = blocks[0].shape[1] if blocks else given[0].shape[1]
@@ -261,29 +242,35 @@
     k = count * tok + sum(g.shape[0] for g in given)
     chunk = next(t for t in (512 if tokens <= 4096 else 256, 128, half) if half % t == 0)
     steps = half // chunk
-    added = total is not None
+    added, wide = total is not None, where is not None
     anywhere = pl.BlockSpec(memory_space=pl.ANY)
     inside = pl.BlockSpec(memory_space=pltpu.VMEM)
+    in_vmem = lambda x: pltpu.with_memory_space_constraint(x, pltpu.VMEM)
     out_type = jnp.bfloat16 if added else jnp.float32
-    out_specs = [anywhere]
-    out_shape = [jax.ShapeDtypeStruct((units, half if where is None else 2 * half), out_type)]
-    scratch = [pltpu.VMEM((units, k), picked.dtype), pltpu.VMEM((k, half), jnp.bfloat16), pltpu.VMEM((units, half), jnp.float32)]
+    if wide:
+        out_specs = [anywhere]
+        out_shape = [jax.ShapeDtypeStruct((units, 2 * half), out_type)]
+    else:
+        out_specs = [inside]
+        out_shape = [pltpu.VMEM((units, half), out_type)]
+    scratch = []
+    parts_shape = (tokens // tok, 1, half)
     if count:
-        out_specs += [anywhere, inside]
+        out_specs += [inside, inside]
         out_shape += [
-            jax.ShapeDtypeStruct((count * tok, half), jnp.bfloat16),
-            jax.ShapeDtypeStruct((tokens // tok, 1, half), jnp.float32),
+            pltpu.VMEM((count * tok, half), jnp.bfloat16),
+            jax.ShapeDtypeStruct(parts_shape[1:] if parts else parts_shape, jnp.float32),
         ]
-        scratch += [pltpu.VMEM((count * tok, half), jnp.bfloat16)] + [pltpu.VMEM((count * tok, 128), jnp.float32)] * 2
-    if added:
+        scratch += [pltpu.VMEM((count * tok, 128), jnp.float32)] * 2 + [pltpu.VMEM(parts_shape, jnp.float32)]
+    if wide:
         scratch += [pltpu.VMEM((units, half), out_type)]
-    sems = [(), (max(count, 1),), (max(len(given), 1), steps), (steps,), (steps,), (steps,)]
+    sems = [(steps,)]
     return pl.pallas_call(
-        functools.partial(product_kernel, tok, count, first, len(given), int(added), chunk),
+        functools.partial(product_kernel, tok, count, first, len(given), int(added), len(parts), wide, chunk),
         grid_spec=pltpu.PrefetchScalarGridSpec(
             num_scalar_prefetch=2,
             grid=(),
-            in_specs=[anywhere] + [inside] * 2 * bool(count) + [anywhere] * (count + len(given) + added),
+            in_specs=[inside] * (1 + 2 * bool(count) + count + len(given) + added + len(parts)),
             out_specs=out_specs,
             scratch_shapes=scratch + [pltpu.SemaphoreType.DMA(shape) for shape in sems],
         ),
@@ -292,12 +279,13 @@
         cost_estimate=cost(units, k * (1 if added or given else 10), half, 6 * units * half),
     )(
         owners,
-        jnp.zeros((1,), jnp.int32) if where is None else where,
-        picked,
+        where if wide else jnp.zeros((1,), jnp.int32),
+        in_vmem(picked),
         *([coefs, head] if count else []),
-        *blocks,
-        *given,
-        *([total] if added else []),
+        *[in_vmem(x) for x in blocks],
+        *[in_vmem(x) for x in given],
+        *([in_vmem(total)] if added else []),
+        *parts,
     )
 
 
@@ -320,7 +308,7 @@
 
 def put(whole, part, where):
     units, width = part.shape
-    pieces = next(n for n in (7, 4, 2, 1) if units % (16 * n) == 0)
+    pieces = pieces_of(units)
     return pl.pallas_call(
         functools.partial(put_kernel, pieces),
         grid_spec=pltpu.PrefetchScalarGridSpec(
@@ -412,18 +400,24 @@
             )
 
         have = run_plan(stream, mine, own_facts, paths, lambda: pick(hidden, owners, 2, tok), early_own, early_other)
-        out, dstream, parts = product(
-            owners, 0, have["other picks"], (have["coefs"], head_half, [have[b] for b in last]), (), have["other sum"]
+        out, dstream, grad_head = product(
+            owners,
+            0,
+            have["other picks"],
+            (have["coefs"], head_half, [have[b] for b in last]),
+            (),
+            have["other sum"],
+            [have["early parts"], have["middle parts"]],
         )
         swapped = to_core(out)
-        grad_head = jnp.sum(parts + have["middle parts"] + have["early parts"], axis=(0, 1))
+        grad_head = grad_head[0]
         other_head = to_core(grad_head)
         grad_head = gain * jnp.where(
             mine == 0, jnp.concatenate([grad_head, other_head]), jnp.concatenate([other_head, grad_head])
         )
         where = mine[None].astype(jnp.int32)
         (grad_down,) = product(
-            owners, 0, have["own picks"], None, [dstream, have["middle dstream"]], have["early own"], where
+            owners, 0, have["own picks"], None, [dstream, have["middle dstream"]], have["early own"], (), where
         )
         grad_down = put(grad_down, swapped, 1 - where)
         return (have["values"], have["returns"], grad_head, grad_down)

time: 133 us -> 128 us (0.962)
  Pallas kernels: 62.3 us -> 42.4 us
  local copies, waits for them, and re-layouts: 5.13 us -> 18.7 us
  starting transfers between devices: 24.6 us -> 28.7 us
  waiting for transfers between devices: 33.3 us -> 30.7 us
    unnamed x30 -> x24, local copies, waits for them, and re-layouts: 1.03 us -> 15.9 us
    pallas_call x4, Pallas kernels: 51.2 us -> 36.9 us  [product(): pl.pallas_call(functools.partial(product_kernel, tok, count, first, len(g...]
    pallas_call x1, Pallas kernels: 8.15 us -> 2.55 us  [pick(): pl.pallas_call(functools.partial(pick_kernel, tok), grid_spec=pltpu.Prefe...]
    ppermute x16, waiting for transfers between devices: 22.2 us -> 17.6 us  [event(): self.have[name] = lax.ppermute(self.have[source], 'seq', pairs)]
    ppermute x16, starting transfers between devices: 21.8 us -> 25.9 us  [event(): self.have[name] = lax.ppermute(self.have[source], 'seq', pairs)]
    ppermute x4, waiting for transfers between devices: 9.04 us -> 11 us  [butterfly_step(): other = lax.ppermute(x, axis, [(i, i ^ step) for i in range(count)])]
  transfers between devices with their start and end apart: 23 -> 23, of which waited for: 8 -> 7; matrix products, arithmetic and copies ran while one was open for 7% -> 6% of each run, Pallas kernels for 38% -> 25%
where the time goes in v5:
time: 128 us; the launch traced here: 127 us
  Pallas kernels  42.4 us (33%)
  waiting for transfers between devices  30.7 us (24%)
  starting transfers between devices  28.7 us (22%)
  local copies, waits for them, and re-layouts  18.7 us (15%)
  other arithmetic  5.71 us (4%)
    pallas_call x4, Pallas kernels, product(): pl.pallas_call(functools.partial(product_kernel, tok, count, first, len(g...  36.9 us
    ppermute x16, starting transfers between devices, event(): self.have[name] = lax.ppermute(self.have[source], 'seq', pairs)  25.9 us
    ppermute x16, waiting for transfers between devices, event(): self.have[name] = lax.ppermute(self.have[source], 'seq', pairs)  17.6 us
    unnamed x24, local copies, waits for them, and re-layouts  15.9 us
    ppermute x4, waiting for transfers between devices, butterfly_step(): other = lax.ppermute(x, axis, [(i, i ^ step) for i in range(count)])  11 us
    pallas_call x1, Pallas kernels, put(): pl.pallas_call(functools.partial(put_kernel, pieces), grid_spec=pltpu.Pre...  3.02 us
  transfers between devices with their start and end apart: 23, of which 7 were waited for; matrix products, arithmetic and copies ran while one was open for 6% of the time, Pallas kernels for 25%

profile of v5, /device:TPU:0, one launch (start us, length us, event | category | flops | bytes accessed | tf_op | source)
XLA Modules:
  0.0 127.2 jit_solution(10524573004118249503)
XLA Ops:
  0.7 1.3 %constant_dynamic-slice_fusion.4 = (bf16[128,2048]{1,0:T(8,128)(2,1)S(1)}, bf16[128,2048]{1,0:T(8,128)(2,1)S(1)}) fusion(bf16[128,4096]{1,0:T(8,128)(2,1)} %param.8, s32[]{:T(128)S(6)} %select_n.122, s32[]{:T(128)S(6)} %select_n.121), kind=kLoop, calls=%fused_computation.46 | loop fusion | bytes 2097160 | tf_op jit(solution)/shard_map/dynamic_slice | solution.py:82
  2.0 4.1 %collective-permute-start.3 = (bf16[128,2048]{1,0:T(8,128)(2,1)S(1)}, bf16[128,2048]{1,0:T(8,128)(2,1)S(1)}, u32[]{:S(2)}, u32[]{:S(2)}) collective-permute-start(bf16[128,2048]{1,0:T(8,128)(2,1)S(1)} %get-tuple-element.48.refs_3_), channel_id=1, source_target_pairs={{0,16},{2,10},{4,20},{6,14},{8,0},{10,26},{12,4},{14,30},{16,24},{... | collective-permute-start | bytes 1572872 | tf_op jit(solution)/shard_map/ppermute | solution.py:69
  6.1 1.5 %collective-permute-start.4 = (bf16[128,2048]{1,0:T(8,128)(2,1)S(1)}, bf16[128,2048]{1,0:T(8,128)(2,1)S(1)}, u32[]{:S(2)}, u32[]{:S(2)}) collective-permute-start(bf16[128,2048]{1,0:T(8,128)(2,1)S(1)} %get-tuple-element.48.refs_3_), channel_id=1, source_target_pairs={{0,4},{2,6},{4,0},{6,2},{8,12},{10,14},{12,8},{14,10},{16,20},{18,... | collective-permute-start | bytes 1572872 | tf_op jit(solution)/shard_map/ppermute | solution.py:69
  7.6 0.7 fusion.8.owners
  8.3 2.0 %copy-done.2 = bf16[896,2048]{1,0:T(8,128)(2,1)S(1)} copy-done((bf16[896,2048]{1,0:T(8,128)(2,1)S(1)}, bf16[896,2048]{1,0:T(8,128)(2,1)}, u32[]{:S(2)}) %copy-start.2) | copy-done | bytes 3670040
  10.3 2.6 %shard_map.111 = (bf16[896,2048]{1,0:T(8,128)(2,1)S(1)}, bf16[896,2048]{1,0:T(8,128)(2,1)S(1)}) custom-call(s32[32]{0:T(128)S(1)} %fusion.8.owners, bf16[896,2048]{1,0:T(8,128)(2,1)S(1)} %copy-done.2), custom_call_target="tpu_custom_call" | custom-call | bytes 11010048 | tf_op jit(solution)/shard_map/pallas_call | solution.py:149
  12.9 1.8 %copy-done.3 = bf16[896,2048]{1,0:T(8,128)(2,1)} copy-done((bf16[896,2048]{1,0:T(8,128)(2,1)}, bf16[896,2048]{1,0:T(8,128)(2,1)S(1)}, u32[]{:S(2)}) %copy-start.3) | copy-done | bytes 3670040
  14.7 1.8 %copy-done.6 = bf16[896,2048]{1,0:T(8,128)(2,1)} copy-done((bf16[896,2048]{1,0:T(8,128)(2,1)}, bf16[896,2048]{1,0:T(8,128)(2,1)S(1)}, u32[]{:S(2)}) %copy-start.6) | copy-done | bytes 3670040
  16.6 0.0 collective-permute-done.refs_4_
  16.6 0.9 collective-permute-start.1
  17.5 0.6 collective-permute-start.2
  18.0 1.7 %fusion = (f32[128]{0:T(128)S(1)}, f32[128]{0:T(128)S(1)}) fusion(bf16[128,4096]{1,0:T(8,128)(2,1)} %param.8, f32[4096]{0:T(1024)S(1)} %convert_multiply_fusion.3), kind=kLoop, calls=%fused_computation.2 | loop fusion | flops 2621184 | bytes 1065984 | tf_op jit(solution)/shard_map/reduce_sum | solution.py:372
  19.7 0.0 collective-permute-done.3.refs_7_
  19.7 1.6 %collective-permute-start.5 = (f32[4,128]{1,0:T(4,128)S(1)}, f32[4,128]{1,0:T(4,128)S(1)}, u32[]{:S(2)}, u32[]{:S(2)}) collective-permute-start(f32[4,128]{1,0:T(4,128)S(1)} %pad_maximum_fusion.4), channel_id=1, source_target_pairs={{0,1},{1,0},{2,3},{3,2},{4,5},{5,4},{6,7},{7,6},{8,9},{9,8},{10,11... | collective-permute-start | bytes 6152 | tf_op jit(solution)/shard_map/ppermute | solution.py:18
  21.3 2.1 %collective-permute-done.5 = f32[4,128]{1,0:T(4,128)S(1)} collective-permute-done((f32[4,128]{1,0:T(4,128)S(1)}, f32[4,128]{1,0:T(4,128)S(1)}, u32[]{:S(2)}, u32[]{:S(2)}) %collective-permute-start.5) | collective-permute-done | bytes 2080 | tf_op jit(solution)/shard_map/ppermute | solution.py:18
  23.4 0.0 collective-permute-start.6
  23.4 1.4 %collective-permute-start.10 = (bf16[128,2048]{1,0:T(8,128)(2,1)S(1)}, bf16[128,2048]{1,0:T(8,128)(2,1)}, u32[]{:S(2)}, u32[]{:S(2)}) collective-permute-start(bf16[128,2048]{1,0:T(8,128)(2,1)S(1)} %collective-permute-done.3.refs_7_), channel_id=1, source_target_pairs={{0,4},{2,6},{4,0},{6,2},{8,12},{10,14},{12,8},{14,10},{16,20},{18,... | collective-permute-start | bytes 1572872 | tf_op jit(solution)/shard_map/ppermute | solution.py:69
  24.8 2.1 %collective-permute-start.9 = (bf16[128,2048]{1,0:T(8,128)(2,1)S(1)}, bf16[128,2048]{1,0:T(8,128)(2,1)}, u32[]{:S(2)}, u32[]{:S(2)}) collective-permute-start(bf16[128,2048]{1,0:T(8,128)(2,1)S(1)} %collective-permute-done.3.refs_7_), channel_id=1, source_target_pairs={{0,16},{2,10},{4,20},{6,14},{8,0},{10,26},{12,4},{14,30},{16,24},{... | collective-permute-start | bytes 1572872 | tf_op jit(solution)/shard_map/ppermute | solution.py:69
  27.0 7.6 %collective-permute-done.1.refs_8_ = bf16[128,2048]{1,0:T(8,128)(2,1)S(1)} collective-permute-done((bf16[128,2048]{1,0:T(8,128)(2,1)S(1)}, bf16[128,2048]{1,0:T(8,128)(2,1)S(1)}, u32[]{:S(2)}, u32[]{:S(2)}) %collective-permute-start.1) | collective-permute-done | bytes 524320 | tf_op jit(solution)/shard_map/ppermute | solution.py:69
  34.6 0.0 collective-permute-done.2.refs_6_
  34.6 0.6 collective-permute-start.11
  35.2 0.0 collective-permute-start.7
  35.2 1.4 %collective-permute-start.8 = (bf16[128,2048]{1,0:T(8,128)(2,1)S(1)}, bf16[128,2048]{1,0:T(8,128)(2,1)}, u32[]{:S(2)}, u32[]{:S(2)}) collective-permute-start(bf16[128,2048]{1,0:T(8,128)(2,1)S(1)} %collective-permute-done.1.refs_8_), channel_id=1, source_target_pairs={{0,4},{2,6},{4,0},{6,2},{8,12},{10,14},{12,8},{14,10},{16,20},{18,... | collective-permute-start | bytes 1572872 | tf_op jit(solution)/shard_map/ppermute | solution.py:69
  36.6 7.0 %collective-permute-done.11 = f32[2,4,128]{2,0,1:T(2,128)S(1)} collective-permute-done((f32[2,4,128]{2,0,1:T(2,128)S(1)}, f32[2,4,128]{2,0,1:T(2,128)S(1)}, u32[]{:S(2)}, u32[]{:S(2)}) %collective-permute-start.11) | collective-permute-done | bytes 4128 | tf_op jit(solution)/shard_map/ppermute | solution.py:28
  43.6 0.0 collective-permute-done.10.refs_9_
  43.6 4.1 %collective-permute-done.9.refs_11_ = bf16[128,2048]{1,0:T(8,128)(2,1)} collective-permute-done((bf16[128,2048]{1,0:T(8,128)(2,1)S(1)}, bf16[128,2048]{1,0:T(8,128)(2,1)}, u32[]{:S(2)}, u32[]{:S(2)}) %collective-permute-start.9) | collective-permute-done | bytes 524320 | tf_op jit(solution)/shard_map/ppermute | solution.py:69
  47.7 0.0 collective-permute-start.12
  47.7 0.4 collective-permute-start.15
  48.1 4.0 %collective-permute-start.16 = (bf16[128,2048]{1,0:T(8,128)(2,1)}, bf16[128,2048]{1,0:T(8,128)(2,1)}, u32[]{:S(2)}, u32[]{:S(2)}) collective-permute-start(bf16[128,2048]{1,0:T(8,128)(2,1)} %collective-permute-done.9.refs_11_), channel_id=1, source_target_pairs={{0,4},{2,6},{4,0},{6,2},{8,12},{10,14},{12,8},{14,10},{16,20},{18,... | collective-permute-start | bytes 1572872 | tf_op jit(solution)/shard_map/ppermute | solution.py:69
  52.1 0.1 collective-permute-done.12
  52.2 5.9 %collective-permute-done.7.refs_12_ = bf16[128,2048]{1,0:T(8,128)(2,1)} collective-permute-done((bf16[128,2048]{1,0:T(8,128)(2,1)S(1)}, bf16[128,2048]{1,0:T(8,128)(2,1)}, u32[]{:S(2)}, u32[]{:S(2)}) %collective-permute-start.7) | collective-permute-done | bytes 524320 | tf_op jit(solution)/shard_map/ppermute | solution.py:69
  58.1 0.0 collective-permute-done.8.refs_10_
  58.1 0.0 collective-permute-start.17
  58.1 1.7 %collective-permute-start.13 = (bf16[128,2048]{1,0:T(8,128)(2,1)}, bf16[128,2048]{1,0:T(8,128)(2,1)}, u32[]{:S(2)}, u32[]{:S(2)}) collective-permute-start(bf16[128,2048]{1,0:T(8,128)(2,1)} %collective-permute-done.7.refs_12_), channel_id=1, source_target_pairs={{0,8},{2,18},{4,12},{6,22},{8,24},{10,2},{12,28},{14,6},{16,0},{18... | collective-permute-start | bytes 1572872 | tf_op jit(solution)/shard_map/ppermute | solution.py:69
  59.8 3.9 %collective-permute-done.17 = f32[8,4,128]{2,0,1:T(8,128)S(1)} collective-permute-done((f32[8,4,128]{2,0,1:T(8,128)S(1)}, f32[8,4,128]{2,0,1:T(8,128)S(1)}, u32[]{:S(2)}, u32[]{:S(2)}) %collective-permute-start.17) | collective-permute-done | bytes 16416 | tf_op jit(solution)/shard_map/ppermute | solution.py:28
  63.7 5.2 %collective-permute-start.18 = (bf16[896,2048]{1,0:T(8,128)(2,1)}, bf16[896,2048]{1,0:T(8,128)(2,1)}, u32[]{:S(2)}, u32[]{:S(2)}) collective-permute-start(bf16[896,2048]{1,0:T(8,128)(2,1)} %copy-done.6), channel_id=1, source_target_pairs={{0,2},{2,0},{4,6},{6,4},{8,10},{10,8},{12,14},{14,12},{16,18},{18,... | collective-permute-start | bytes 11010056 | tf_op jit(solution)/shard_map/ppermute | solution.py:69
  69.0 0.1 fusion.15
  69.1 0.3 reduce_window_sum.22
  69.4 0.1 broadcast_compare_fusion
  69.5 0.1 fusion.7
  69.6 0.7 select_reduce_fusion
  70.3 0.1 slice_reduce_fusion
  70.4 0.1 reduce.1
  70.5 0.2 select_reduce_fusion.1
  70.7 0.6 dynamic-slice.1
  71.3 0.1 broadcast_in_dim.84
  71.4 0.1 eq.84
  71.5 0.1 collective-permute-start.19
  71.6 2.0 %copy-done.4 = bf16[896,2048]{1,0:T(8,128)(2,1)S(1)} copy-done((bf16[896,2048]{1,0:T(8,128)(2,1)S(1)}, bf16[896,2048]{1,0:T(8,128)(2,1)}, u32[]{:S(2)}) %copy-start.4) | copy-done | bytes 3670040
  73.6 12.3 %shard_map.112 = (f32[896,2048]{1,0:T(8,128)S(1)}, bf16[1280,2048]{1,0:T(8,128)(2,1)S(1)}, f32[16,1,2048]{2,1,0:T(1,128)S(1)}) custom-call(s32[32]{0:T(128)S(1)} %fusion.8.owners, s32[1]{0:T(128)} %constant.64.clone.1.where, bf16[896,2048]{1,0:T(8,128)(2,1)S(1)} %copy-done.4, f32[8,2048]{1,0:T(8,128)S(1)} %select_maximum_fusion.refs_1_, ...), custom_call_target="tpu_custom_call" | custom-call | flops 46976204800 | bytes 86376448 | tf_op jit(solution)/shard_map/pallas_call | solution.py:268
  86.0 0.0 copy-start
  86.0 3.0 %copy-done = f32[896,2048]{1,0:T(8,128)} copy-done((f32[896,2048]{1,0:T(8,128)}, f32[896,2048]{1,0:T(8,128)S(1)}, u32[]{:S(2)}) %copy-start) | copy-done | bytes 7340056
  89.0 0.5 fusion.10
  89.6 1.2 fusion.12
  90.7 2.5 %collective-permute-start.20 = (bf16[128,2048]{1,0:T(8,128)(2,1)}, bf16[128,2048]{1,0:T(8,128)(2,1)S(1)}, u32[]{:S(2)}, u32[]{:S(2)}) collective-permute-start(bf16[128,2048]{1,0:T(8,128)(2,1)} %collective-permute-done.13.refs_6_), channel_id=1, source_target_pairs={{0,4},{2,6},{4,0},{6,2},{8,12},{10,14},{12,8},{14,10},{16,20},{18,... | collective-permute-start | bytes 1572872 | tf_op jit(solution)/shard_map/ppermute | solution.py:69
  93.3 12.3 %shard_map.113 = (f32[896,2048]{1,0:T(8,128)S(1)}, bf16[512,2048]{1,0:T(8,128)(2,1)S(1)}, f32[16,1,2048]{2,1,0:T(1,128)S(1)}) custom-call(s32[32]{0:T(128)S(1)} %fusion.8.owners, s32[1]{0:T(128)} %constant.64.clone.1.where, bf16[896,2048]{1,0:T(8,128)(2,1)} %collective-permute-done.18.refs_0_, f32[8,2048]{1,0:T(8,128)S(1)} %select_maximum_fusion.refs_1_, ...), custom_call_target="tpu_custom_call" | custom-call | flops 6576668672 | bytes 21561344 | tf_op jit(solution)/shard_map/pallas_call | solution.py:268
  105.6 7.2 %shard_map.114 = (bf16[896,2048]{1,0:T(8,128)(2,1)}, bf16[256,2048]{1,0:T(8,128)(2,1)S(1)}, f32[1,2048]{1,0:T(1,128)S(1)}) custom-call(s32[32]{0:T(128)S(1)} %fusion.8.owners, s32[1]{0:T(128)} %constant.64.clone.1.where, bf16[896,2048]{1,0:T(8,128)(2,1)} %collective-permute-done.18.refs_0_, f32[8,2048]{1,0:T(8,128)S(1)} %select_maximum_fusion.refs_1_, ...), custom_call_target="tpu_custom_call" | custom-call | flops 939524096 | bytes 12517376 | tf_op jit(solution)/shard_map/pallas_call | solution.py:268
  112.8 0.1 collective-permute-start.22
  112.9 0.5 collective-permute-start.21
  113.4 3.1 %copy-done.1 = f32[896,2048]{1,0:T(8,128)S(1)} copy-done((f32[896,2048]{1,0:T(8,128)S(1)}, f32[896,2048]{1,0:T(8,128)}, u32[]{:S(2)}) %copy-start.1) | copy-done | bytes 7340056
  116.5 2.0 %copy-done.5 = bf16[896,2048]{1,0:T(8,128)(2,1)S(1)} copy-done((bf16[896,2048]{1,0:T(8,128)(2,1)S(1)}, bf16[896,2048]{1,0:T(8,128)(2,1)}, u32[]{:S(2)}) %copy-start.5) | copy-done | bytes 3670040
  118.5 5.0 %shard_map.115.whole = bf16[896,4096]{1,0:T(8,128)(2,1)} custom-call(s32[32]{0:T(128)S(1)} %fusion.8.owners, s32[1]{0:T(128)} %bitcast.21.where, bf16[896,2048]{1,0:T(8,128)(2,1)S(1)} %copy-done.5, bf16[256,2048]{1,0:T(8,128)(2,1)S(1)} %get-tuple-element.85.refs_1_, bf16[512,2048]{1,0:T(8,128)(2,1)S(1)} %get-tuple-element.86.refs_2_, f32[896,2048]{1,0:T(8,128)S(1)} %copy-done.1), custom_call_target="tpu_custom_call" | custom-call | flops 2818572288 | bytes 15532032 | tf_op jit(solution)/shard_map/pallas_call | solution.py:268
  123.5 0.6 convert_multiply_fusion.2
  124.2 3.0 %shard_map.116 = bf16[896,4096]{1,0:T(8,128)(2,1)} custom-call(s32[1]{0:T(128)S(6)} %sub.64.where, bf16[896,2048]{1,0:T(8,128)(2,1)} %collective-permute-done.22.part, bf16[896,4096]{1,0:T(8,128)(2,1)} %shard_map.115.whole), custom_call_target="tpu_custom_call", output_to_operand_aliasing={{}: (2, {})} | custom-call | bytes 7340032 | tf_op jit(solution)/shard_map/pallas_call | solution.py:312
  (49 shorter events, 0.3 us)
Async XLA Ops:
  0.6 15.9 %copy-start.7 = (bf16[4096]{0:T(1024)(128)(2,1)S(1)}, bf16[4096]{0:T(1024)(128)(2,1)}, u32[]{:S(2)}) copy-start(bf16[4096]{0:T(1024)(128)(2,1)} %param.10) | copy-start | bytes 24580
  0.6 15.9 %copy-start.8 = (bf16[4096]{0:T(1024)(128)(2,1)S(1)}, bf16[4096]{0:T(1024)(128)(2,1)}, u32[]{:S(2)}) copy-start(bf16[4096]{0:T(1024)(128)(2,1)} %param.11) | copy-start | bytes 24580
  0.7 15.9 %copy-start.10 = (f32[128]{0:T(128)S(1)}, f32[128]{0:T(128)}, u32[]{:S(2)}) copy-start(f32[128]{0:T(128)} %param.12) | copy-start | bytes 1540
  0.7 15.9 %copy-start.11 = (f32[128]{0:T(128)S(1)}, f32[128]{0:T(128)}, u32[]{:S(2)}) copy-start(f32[128]{0:T(128)} %param.13) | copy-start | bytes 1540
  0.7 15.9 %copy-start.9 = (s32[128]{0:T(128)S(1)}, s32[128]{0:T(128)}, u32[]{:S(2)}) copy-start(s32[128]{0:T(128)} %param.14) | copy-start | bytes 1540
  2.0 17.7 %collective-permute-start.3 = (bf16[128,2048]{1,0:T(8,128)(2,1)S(1)}, bf16[128,2048]{1,0:T(8,128)(2,1)S(1)}, u32[]{:S(2)}, u32[]{:S(2)}) collective-permute-start(bf16[128,2048]{1,0:T(8,128)(2,1)S(1)} %get-tuple-element.48.refs_3_), channel_id=1, source_target_pairs={{0,16},{2,10},{4,20},{6,14},{8,0},{10,26},{12,4},{14,30},{16,24},{... | collective-permute-start | bytes 1572872 | tf_op jit(solution)/shard_map/ppermute | solution.py:69
  6.1 13.7 %collective-permute-start.4 = (bf16[128,2048]{1,0:T(8,128)(2,1)S(1)}, bf16[128,2048]{1,0:T(8,128)(2,1)S(1)}, u32[]{:S(2)}, u32[]{:S(2)}) collective-permute-start(bf16[128,2048]{1,0:T(8,128)(2,1)S(1)} %get-tuple-element.48.refs_3_), channel_id=1, source_target_pairs={{0,4},{2,6},{4,0},{6,2},{8,12},{10,14},{12,8},{14,10},{16,20},{18,... | collective-permute-start | bytes 1572872 | tf_op jit(solution)/shard_map/ppermute | solution.py:69
  7.6 9.0 %collective-permute-start = (bf16[128,2048]{1,0:T(8,128)(2,1)S(1)}, bf16[128,2048]{1,0:T(8,128)(2,1)S(1)}, u32[]{:S(2)}, u32[]{:S(2)}) collective-permute-start(bf16[128,2048]{1,0:T(8,128)(2,1)S(1)} %get-tuple-element.46), channel_id=1, source_target_pairs={{0,2},{2,0},{4,6},{6,4},{8,10},{10,8},{12,14},{14,12},{16,18},{18,... | collective-permute-start | bytes 1572872 | tf_op jit(solution)/shard_map/ppermute | solution.py:69
  8.3 2.0 %copy-start.2 = (bf16[896,2048]{1,0:T(8,128)(2,1)S(1)}, bf16[896,2048]{1,0:T(8,128)(2,1)}, u32[]{:S(2)}) copy-start(bf16[896,2048]{1,0:T(8,128)(2,1)} %hidden.1) | copy-start | bytes 11010052
  12.9 1.8 %copy-start.3 = (bf16[896,2048]{1,0:T(8,128)(2,1)}, bf16[896,2048]{1,0:T(8,128)(2,1)S(1)}, u32[]{:S(2)}) copy-start(bf16[896,2048]{1,0:T(8,128)(2,1)S(1)} %get-tuple-element.63.refs_0_) | copy-start | bytes 11010052
  14.7 1.8 %copy-start.6 = (bf16[896,2048]{1,0:T(8,128)(2,1)}, bf16[896,2048]{1,0:T(8,128)(2,1)S(1)}, u32[]{:S(2)}) copy-start(bf16[896,2048]{1,0:T(8,128)(2,1)S(1)} %get-tuple-element.62) | copy-start | bytes 11010052
  16.6 18.0 %collective-permute-start.1 = (bf16[128,2048]{1,0:T(8,128)(2,1)S(1)}, bf16[128,2048]{1,0:T(8,128)(2,1)S(1)}, u32[]{:S(2)}, u32[]{:S(2)}) collective-permute-start(bf16[128,2048]{1,0:T(8,128)(2,1)S(1)} %collective-permute-done.refs_4_), channel_id=1, source_target_pairs={{0,8},{2,18},{4,12},{6,22},{8,24},{10,2},{12,28},{14,6},{16,0},{18... | collective-permute-start | bytes 1572872 | tf_op jit(solution)/shard_map/ppermute | solution.py:69
  17.5 17.1 %collective-permute-start.2 = (bf16[128,2048]{1,0:T(8,128)(2,1)S(1)}, bf16[128,2048]{1,0:T(8,128)(2,1)S(1)}, u32[]{:S(2)}, u32[]{:S(2)}) collective-permute-start(bf16[128,2048]{1,0:T(8,128)(2,1)S(1)} %collective-permute-done.refs_4_), channel_id=1, source_target_pairs={{0,4},{2,6},{4,0},{6,2},{8,12},{10,14},{12,8},{14,10},{16,20},{18,... | collective-permute-start | bytes 1572872 | tf_op jit(solution)/shard_map/ppermute | solution.py:69
  19.7 3.7 %collective-permute-start.5 = (f32[4,128]{1,0:T(4,128)S(1)}, f32[4,128]{1,0:T(4,128)S(1)}, u32[]{:S(2)}, u32[]{:S(2)}) collective-permute-start(f32[4,128]{1,0:T(4,128)S(1)} %pad_maximum_fusion.4), channel_id=1, source_target_pairs={{0,1},{1,0},{2,3},{3,2},{4,5},{5,4},{6,7},{7,6},{8,9},{9,8},{10,11... | collective-permute-start | bytes 6152 | tf_op jit(solution)/shard_map/ppermute | solution.py:18
  23.4 3.5 %collective-permute-start.6 = (f32[1,4,128]{2,0,1:T(1,128)S(1)}, f32[1,4,128]{2,0,1:T(1,128)S(1)}, u32[]{:S(2)}, u32[]{:S(2)}) collective-permute-start(f32[1,4,128]{2,0,1:T(1,128)S(1)} %bitcast.63), channel_id=1, source_target_pairs={{0,2},{2,0},{4,6},{6,4},{8,10},{10,8},{12,14},{14,12},{16,18},{18,... | collective-permute-start | bytes 6152 | tf_op jit(solution)/shard_map/ppermute | solution.py:28
  23.4 20.2 %collective-permute-start.10 = (bf16[128,2048]{1,0:T(8,128)(2,1)S(1)}, bf16[128,2048]{1,0:T(8,128)(2,1)}, u32[]{:S(2)}, u32[]{:S(2)}) collective-permute-start(bf16[128,2048]{1,0:T(8,128)(2,1)S(1)} %collective-permute-done.3.refs_7_), channel_id=1, source_target_pairs={{0,4},{2,6},{4,0},{6,2},{8,12},{10,14},{12,8},{14,10},{16,20},{18,... | collective-permute-start | bytes 1572872 | tf_op jit(solution)/shard_map/ppermute | solution.py:69
  24.8 22.8 %collective-permute-start.9 = (bf16[128,2048]{1,0:T(8,128)(2,1)S(1)}, bf16[128,2048]{1,0:T(8,128)(2,1)}, u32[]{:S(2)}, u32[]{:S(2)}) collective-permute-start(bf16[128,2048]{1,0:T(8,128)(2,1)S(1)} %collective-permute-done.3.refs_7_), channel_id=1, source_target_pairs={{0,16},{2,10},{4,20},{6,14},{8,0},{10,26},{12,4},{14,30},{16,24},{... | collective-permute-start | bytes 1572872 | tf_op jit(solution)/shard_map/ppermute | solution.py:69
  34.6 9.0 %collective-permute-start.11 = (f32[2,4,128]{2,0,1:T(2,128)S(1)}, f32[2,4,128]{2,0,1:T(2,128)S(1)}, u32[]{:S(2)}, u32[]{:S(2)}) collective-permute-start(f32[2,4,128]{2,0,1:T(2,128)S(1)} %pad_maximum_fusion.3), channel_id=1, source_target_pairs={{0,4},{2,6},{4,0},{6,2},{8,12},{10,14},{12,8},{14,10},{16,20},{18,... | collective-permute-start | bytes 12296 | tf_op jit(solution)/shard_map/ppermute | solution.py:28
  35.2 22.9 %collective-permute-start.7 = (bf16[128,2048]{1,0:T(8,128)(2,1)S(1)}, bf16[128,2048]{1,0:T(8,128)(2,1)}, u32[]{:S(2)}, u32[]{:S(2)}) collective-permute-start(bf16[128,2048]{1,0:T(8,128)(2,1)S(1)} %collective-permute-done.1.refs_8_), channel_id=1, source_target_pairs={{0,8},{2,18},{4,12},{6,22},{8,24},{10,2},{12,28},{14,6},{16,0},{18... | collective-permute-start | bytes 1572872 | tf_op jit(solution)/shard_map/ppermute | solution.py:69
  35.2 22.9 %collective-permute-start.8 = (bf16[128,2048]{1,0:T(8,128)(2,1)S(1)}, bf16[128,2048]{1,0:T(8,128)(2,1)}, u32[]{:S(2)}, u32[]{:S(2)}) collective-permute-start(bf16[128,2048]{1,0:T(8,128)(2,1)S(1)} %collective-permute-done.1.refs_8_), channel_id=1, source_target_pairs={{0,4},{2,6},{4,0},{6,2},{8,12},{10,14},{12,8},{14,10},{16,20},{18,... | collective-permute-start | bytes 1572872 | tf_op jit(solution)/shard_map/ppermute | solution.py:69
  47.7 4.5 %collective-permute-start.12 = (f32[4,4,128]{2,0,1:T(4,128)S(1)}, f32[4,4,128]{2,0,1:T(4,128)S(1)}, u32[]{:S(2)}, u32[]{:S(2)}) collective-permute-start(f32[4,4,128]{2,0,1:T(4,128)S(1)} %pad_maximum_fusion.2), channel_id=1, source_target_pairs={{0,8},{2,10},{4,12},{6,14},{8,0},{10,2},{12,4},{14,6},{16,24},{18,... | collective-permute-start | bytes 24584 | tf_op jit(solution)/shard_map/ppermute | solution.py:28
  47.7 21.3 %collective-permute-start.15 = (bf16[128,2048]{1,0:T(8,128)(2,1)}, bf16[128,2048]{1,0:T(8,128)(2,1)}, u32[]{:S(2)}, u32[]{:S(2)}) collective-permute-start(bf16[128,2048]{1,0:T(8,128)(2,1)} %collective-permute-done.9.refs_11_), channel_id=1, source_target_pairs={{0,16},{2,10},{4,20},{6,14},{8,0},{10,26},{12,4},{14,30},{16,24},{... | collective-permute-start | bytes 1572872 | tf_op jit(solution)/shard_map/ppermute | solution.py:69
  48.1 20.9 %collective-permute-start.16 = (bf16[128,2048]{1,0:T(8,128)(2,1)}, bf16[128,2048]{1,0:T(8,128)(2,1)}, u32[]{:S(2)}, u32[]{:S(2)}) collective-permute-start(bf16[128,2048]{1,0:T(8,128)(2,1)} %collective-permute-done.9.refs_11_), channel_id=1, source_target_pairs={{0,4},{2,6},{4,0},{6,2},{8,12},{10,14},{12,8},{14,10},{16,20},{18,... | collective-permute-start | bytes 1572872 | tf_op jit(solution)/shard_map/ppermute | solution.py:69
  58.1 5.7 %collective-permute-start.17 = (f32[8,4,128]{2,0,1:T(8,128)S(1)}, f32[8,4,128]{2,0,1:T(8,128)S(1)}, u32[]{:S(2)}, u32[]{:S(2)}) collective-permute-start(f32[8,4,128]{2,0,1:T(8,128)S(1)} %pad_maximum_fusion.1), channel_id=1, source_target_pairs={{0,16},{2,18},{4,20},{6,22},{8,24},{10,26},{12,28},{14,30},{16,0},... | collective-permute-start | bytes 49160 | tf_op jit(solution)/shard_map/ppermute | solution.py:28
  58.1 32.6 %collective-permute-start.13 = (bf16[128,2048]{1,0:T(8,128)(2,1)}, bf16[128,2048]{1,0:T(8,128)(2,1)}, u32[]{:S(2)}, u32[]{:S(2)}) collective-permute-start(bf16[128,2048]{1,0:T(8,128)(2,1)} %collective-permute-done.7.refs_12_), channel_id=1, source_target_pairs={{0,8},{2,18},{4,12},{6,22},{8,24},{10,2},{12,28},{14,6},{16,0},{18... | collective-permute-start | bytes 1572872 | tf_op jit(solution)/shard_map/ppermute | solution.py:69
  59.8 30.9 %collective-permute-start.14 = (bf16[128,2048]{1,0:T(8,128)(2,1)}, bf16[128,2048]{1,0:T(8,128)(2,1)}, u32[]{:S(2)}, u32[]{:S(2)}) collective-permute-start(bf16[128,2048]{1,0:T(8,128)(2,1)} %collective-permute-done.7.refs_12_), channel_id=1, source_target_pairs={{0,4},{2,6},{4,0},{6,2},{8,12},{10,14},{12,8},{14,10},{16,20},{18,... | collective-permute-start | bytes 1572872 | tf_op jit(solution)/shard_map/ppermute | solution.py:69
  63.7 27.0 %collective-permute-start.18 = (bf16[896,2048]{1,0:T(8,128)(2,1)}, bf16[896,2048]{1,0:T(8,128)(2,1)}, u32[]{:S(2)}, u32[]{:S(2)}) collective-permute-start(bf16[896,2048]{1,0:T(8,128)(2,1)} %copy-done.6), channel_id=1, source_target_pairs={{0,2},{2,0},{4,6},{6,4},{8,10},{10,8},{12,14},{14,12},{16,18},{18,... | collective-permute-start | bytes 11010056 | tf_op jit(solution)/shard_map/ppermute | solution.py:69
  71.5 34.1 %collective-permute-start.19 = (bf16[128,2048]{1,0:T(8,128)(2,1)}, bf16[128,2048]{1,0:T(8,128)(2,1)S(1)}, u32[]{:S(2)}, u32[]{:S(2)}) collective-permute-start(bf16[128,2048]{1,0:T(8,128)(2,1)} %collective-permute-done.16.refs_3_), channel_id=1, source_target_pairs={{0,16},{2,10},{4,20},{6,14},{8,0},{10,26},{12,4},{14,30},{16,24},{... | collective-permute-start | bytes 1572872 | tf_op jit(solution)/shard_map/ppermute | solution.py:69
  71.6 2.0 %copy-start.4 = (bf16[896,2048]{1,0:T(8,128)(2,1)S(1)}, bf16[896,2048]{1,0:T(8,128)(2,1)}, u32[]{:S(2)}) copy-start(bf16[896,2048]{1,0:T(8,128)(2,1)} %copy-done.3) | copy-start | bytes 11010052
  86.0 3.1 %copy-start = (f32[896,2048]{1,0:T(8,128)}, f32[896,2048]{1,0:T(8,128)S(1)}, u32[]{:S(2)}) copy-start(f32[896,2048]{1,0:T(8,128)S(1)} %get-tuple-element.87.refs_3_) | copy-start | bytes 22020100
  90.7 14.9 %collective-permute-start.20 = (bf16[128,2048]{1,0:T(8,128)(2,1)}, bf16[128,2048]{1,0:T(8,128)(2,1)S(1)}, u32[]{:S(2)}, u32[]{:S(2)}) collective-permute-start(bf16[128,2048]{1,0:T(8,128)(2,1)} %collective-permute-done.13.refs_6_), channel_id=1, source_target_pairs={{0,4},{2,6},{4,0},{6,2},{8,12},{10,14},{12,8},{14,10},{16,20},{18,... | collective-permute-start | bytes 1572872 | tf_op jit(solution)/shard_map/ppermute | solution.py:69
  112.8 11.4 %collective-permute-start.22 = (bf16[896,2048]{1,0:T(8,128)(2,1)}, bf16[896,2048]{1,0:T(8,128)(2,1)}, u32[]{:S(2)}, u32[]{:S(2)}) collective-permute-start(bf16[896,2048]{1,0:T(8,128)(2,1)} %get-tuple-element.84), channel_id=1, source_target_pairs={{0,2},{2,0},{4,6},{6,4},{8,10},{10,8},{12,14},{14,12},{16,18},{18,... | collective-permute-start | bytes 11010056 | tf_op jit(solution)/shard_map/ppermute | solution.py:359
  112.9 10.7 %collective-permute-start.21 = (f32[2048]{0:T(1024)S(1)}, f32[2048]{0:T(1024)S(1)}, u32[]{:S(2)}, u32[]{:S(2)}) collective-permute-start(f32[2048]{0:T(1024)S(1)} %bitcast.46), channel_id=1, source_target_pairs={{0,2},{2,0},{4,6},{6,4},{8,10},{10,8},{12,14},{14,12},{16,18},{18,... | collective-permute-start | bytes 24584 | tf_op jit(solution)/shard_map/ppermute | solution.py:359
  113.4 3.1 %copy-start.1 = (f32[896,2048]{1,0:T(8,128)S(1)}, f32[896,2048]{1,0:T(8,128)}, u32[]{:S(2)}) copy-start(f32[896,2048]{1,0:T(8,128)} %copy-done) | copy-start | bytes 22020100
  116.5 2.0 %copy-start.5 = (bf16[896,2048]{1,0:T(8,128)(2,1)S(1)}, bf16[896,2048]{1,0:T(8,128)(2,1)}, u32[]{:S(2)}) copy-start(bf16[896,2048]{1,0:T(8,128)(2,1)} %copy-done.3) | copy-start | bytes 11010052

commit v6 on v5

--- a/solution.py
+++ b/solution.py
@@ -20,14 +20,16 @@
     return x
 
 
-def butterfly_step(x, axis):
+def butterfly_step(x, axis, low):
     count = lax.axis_size(axis)
     step = x.shape[0]
     if step >= count:
         return x
     other = lax.ppermute(x, axis, [(i, i ^ step) for i in range(count)])
-    low = (lax.axis_index(axis) & step) == 0
-    return jnp.concatenate([jnp.where(low, x, other), jnp.where(low, other, x)])
+    if step > 1:
+        return jnp.concatenate([jnp.where(low[step], x, other), jnp.where(low[step], other, x)])
+    first = lax.broadcasted_iota(jnp.int32, (2, *x.shape), 0) == 0
+    return jnp.where(first == low[step], x[None], other[None]).reshape(2 * step, *x.shape[1:])
 
 
 class Paths:
@@ -76,20 +78,23 @@
     return last, middle, early
 
 
-def run_plan(stream, core_index, own_facts, paths, pick_both, early_own, early_other):
+def run_plan(stream, scalars, own_facts, paths, pick_both, early_own, early_other):
     half = stream.shape[1] // 2
     m, ring, across, core = paths.m, paths.ring, paths.across, paths.core
     cut = lambda c: lax.dynamic_slice_in_dim(stream, c * half, half, 1)
-    f = Flights(stream=stream, away=cut(1 - core_index))
+    core_index = scalars["core"]
+    f = Flights(stream=stream, away=cut(1 - core_index), **scalars)
     f.have[0, 0, 0] = cut(core_index)
     have = f.have
+    names = list(scalars)
+    low = lambda: {1 << n: have["low %d" % n] for n in range(paths.count.bit_length() - 1)}
 
     def facts_step():
-        have["facts"] = butterfly_step(have["facts"], "seq")
+        have["facts"] = butterfly_step(have["facts"], "seq", low())
 
     f.event([], [((1, 0, 0), (0, 0, 0), ring[0]), ((0, 1, 0), (0, 0, 0), across), ((0, 0, 1), "away", core)])
     f.event(
-        [(0, 0, 1), "stream"],
+        [(0, 0, 1), "stream", *names],
         [((1, 0, 1), (0, 0, 1), ring[1]), ((0, 1, 1), (0, 0, 1), across)],
     )
     have["sums"] = own_facts(have["stream"])
@@ -332,15 +337,17 @@
 def all_returns(step_reward, resets):
     shards, tok = step_reward.shape
     position = jnp.arange(tok)
-    before = jnp.cumsum(resets, axis=1) - resets
+    earlier = position[None, :] < position[:, None]
+    before = jnp.sum(jnp.where(earlier[None], resets[:, None, :], 0.0), axis=2)
     total = jnp.sum(resets, axis=1, keepdims=True)
     reach = (position[None, :] >= position[:, None])[None] & (before[:, None, :] == before[:, :, None])
     local = jnp.sum(jnp.where(reach, step_reward[:, None, :], 0.0), axis=2)
     passing = before == total
     blocked = jnp.where(passing[:, 0], 0.0, 1.0)
-    upto = jnp.cumsum(blocked)
     ids = jnp.arange(shards)
-    open_path = (ids[None, :] > ids[:, None]) & ((upto - blocked)[None, :] == upto[:, None])
+    later = ids[None, :] > ids[:, None]
+    between = later[:, None, :] & (ids[None, :] < ids[:, None])[None]
+    open_path = later & (jnp.sum(jnp.where(between, blocked[None, None, :], 0.0), axis=2) == 0.0)
     incoming = jnp.sum(jnp.where(open_path, local[None, :, 0], 0.0), axis=1)
     return local + jnp.where(passing, incoming[:, None], 0.0)
 
@@ -357,7 +364,7 @@
         head = gain * value_head.astype(jnp.float32)
         head_half = lax.dynamic_slice_in_dim(head, mine * half, half)[None]
         to_core = lambda x: lax.ppermute(x, "seq", paths.core)
-        own = lambda a: lax.dynamic_index_in_dim(a, me, 0, keepdims=False)
+        own = lambda a, me=me: lax.dynamic_index_in_dim(a, me, 0, keepdims=False)
         last, middle, early = block_groups(paths.m)
         table = paths.owners(last + middle + early)
         both = np.concatenate([table, table[np.arange(shards) ^ 1]], axis=1)
@@ -385,23 +392,27 @@
             pull = scale**3 * along / width
             coefs = jnp.stack([error * scale, error * pull]).reshape(2, shards * tok)
             coefs = jnp.pad(coefs, ((0, 6), (0, 0)))
-            have.update(values=own(values), returns=own(returns), coefs=coefs)
+            have.update(values=own(values, have["me"]), returns=own(returns, have["me"]), coefs=coefs)
             have["early own"], have["early dstream"], have["early parts"] = product(
-                owners, early_at, have["own picks"], (coefs, head_half, [have[b] for b in early])
+                have["owners"], early_at, have["own picks"], (coefs, head_half, [have[b] for b in early])
             )
 
         def early_other(have):
             have["other sum"], have["middle dstream"], have["middle parts"] = product(
-                owners,
+                have["owners"],
                 len(last),
                 have["other picks"],
                 (have["coefs"], head_half, [have[b] for b in middle]),
                 [have["early dstream"]],
             )
 
-        have = run_plan(stream, mine, own_facts, paths, lambda: pick(hidden, owners, 2, tok), early_own, early_other)
+        where = mine[None].astype(jnp.int32)
+        scalars = {"core": mine, "me": me, "first core": mine == 0, "where": where, "elsewhere": 1 - where}
+        scalars.update({"low %d" % n: (me >> n) % 2 == 0 for n in range(shards.bit_length() - 1)})
+        scalars["owners"] = owners
+        have = run_plan(stream, scalars, own_facts, paths, lambda: pick(hidden, owners, 2, tok), early_own, early_other)
         out, dstream, grad_head = product(
-            owners,
+            have["owners"],
             0,
             have["other picks"],
             (have["coefs"], head_half, [have[b] for b in last]),
@@ -413,13 +424,12 @@
         grad_head = grad_head[0]
         other_head = to_core(grad_head)
         grad_head = gain * jnp.where(
-            mine == 0, jnp.concatenate([grad_head, other_head]), jnp.concatenate([other_head, grad_head])
+            have["first core"], jnp.concatenate([grad_head, other_head]), jnp.concatenate([other_head, grad_head])
         )
-        where = mine[None].astype(jnp.int32)
         (grad_down,) = product(
-            owners, 0, have["own picks"], None, [dstream, have["middle dstream"]], have["early own"], (), where
+            have["owners"], 0, have["own picks"], None, [dstream, have["middle dstream"]], have["early own"], (), have["where"]
         )
-        grad_down = put(grad_down, swapped, 1 - where)
+        grad_down = put(grad_down, swapped, have["elsewhere"])
         return (have["values"], have["returns"], grad_head, grad_down)
 
     return body

time: 128 us -> 116 us (0.906)
  Pallas kernels: 42.4 us -> 35.9 us
  starting transfers between devices: 28.7 us -> 23.6 us
  local copies, waits for them, and re-layouts: 18.7 us -> 15.4 us
  waiting for transfers between devices: 30.7 us -> 33.8 us
    pallas_call x4, Pallas kernels: 36.9 us -> 31.1 us  [product(): pl.pallas_call(functools.partial(product_kernel, tok, count, first, len(g...]
    ppermute x16, starting transfers between devices: 25.9 us -> 20.8 us  [event(): self.have[name] = lax.ppermute(self.have[source], 'seq', pairs)]
    ppermute x16, waiting for transfers between devices: 17.6 us -> 22.1 us  [event(): self.have[name] = lax.ppermute(self.have[source], 'seq', pairs)]
    unnamed x24 -> x32, local copies, waits for them, and re-layouts: 15.9 us -> 12.6 us
    ppermute x1, waiting for transfers between devices: 2.09 us -> 0.01 us  [butterfly_sum(): x = x + lax.ppermute(x, axis, [(i, i ^ step) for i in range(count)])]
  transfers between devices with their start and end apart: 23 -> 23, of which waited for: 7 -> 10; matrix products, arithmetic and copies ran while one was open for 6% -> 6% of each run, Pallas kernels for 25% -> 26%
where the time goes in v6:
time: 116 us; the launch traced here: 115 us
  Pallas kernels  35.9 us (31%)
  waiting for transfers between devices  33.8 us (29%)
  starting transfers between devices  23.6 us (20%)
  local copies, waits for them, and re-layouts  15.4 us (13%)
  other arithmetic  5.83 us (5%)
    pallas_call x4, Pallas kernels, product(): pl.pallas_call(functools.partial(product_kernel, tok, count, first, len(g...  31.1 us
    ppermute x16, waiting for transfers between devices, event(): self.have[name] = lax.ppermute(self.have[source], 'seq', pairs)  22.1 us
    ppermute x16, starting transfers between devices, event(): self.have[name] = lax.ppermute(self.have[source], 'seq', pairs)  20.8 us
    unnamed x32, local copies, waits for them, and re-layouts  12.6 us
    ppermute x4, waiting for transfers between devices, butterfly_step(): other = lax.ppermute(x, axis, [(i, i ^ step) for i in range(count)])  10.8 us
    pallas_call x1, Pallas kernels, pick(): pl.pallas_call(functools.partial(pick_kernel, tok), grid_spec=pltpu.Prefe...  2.55 us
  transfers between devices with their start and end apart: 23, of which 10 were waited for; matrix products, arithmetic and copies ran while one was open for 6% of the time, Pallas kernels for 26%

profile of v6, /device:TPU:0, one launch (start us, length us, event | category | flops | bytes accessed | tf_op | source)
XLA Modules:
  0.0 115.5 jit_solution(11453613951853567878)
XLA Ops:
  0.7 1.3 %constant_dynamic-slice_fusion.4 = (bf16[128,2048]{1,0:T(8,128)(2,1)S(1)}, bf16[128,2048]{1,0:T(8,128)(2,1)S(1)}) fusion(bf16[128,4096]{1,0:T(8,128)(2,1)} %param.8, s32[]{:T(128)S(6)} %select_n.142, s32[]{:T(128)S(6)} %select_n.141), kind=kLoop, calls=%fused_computation.46 | loop fusion | bytes 2097160 | tf_op jit(solution)/shard_map/dynamic_slice | solution.py:84
  2.0 4.1 %collective-permute-start.3 = (bf16[128,2048]{1,0:T(8,128)(2,1)S(1)}, bf16[128,2048]{1,0:T(8,128)(2,1)S(1)}, u32[]{:S(2)}, u32[]{:S(2)}) collective-permute-start(bf16[128,2048]{1,0:T(8,128)(2,1)S(1)} %get-tuple-element.58.refs_3_), channel_id=1, source_target_pairs={{0,16},{2,10},{4,20},{6,14},{8,0},{10,26},{12,4},{14,30},{16,24},{... | collective-permute-start | bytes 1572872 | tf_op jit(solution)/shard_map/ppermute | solution.py:71
  6.1 1.5 %collective-permute-start.4 = (bf16[128,2048]{1,0:T(8,128)(2,1)S(1)}, bf16[128,2048]{1,0:T(8,128)(2,1)S(1)}, u32[]{:S(2)}, u32[]{:S(2)}) collective-permute-start(bf16[128,2048]{1,0:T(8,128)(2,1)S(1)} %get-tuple-element.58.refs_3_), channel_id=1, source_target_pairs={{0,4},{2,6},{4,0},{6,2},{8,12},{10,14},{12,8},{14,10},{16,20},{18,... | collective-permute-start | bytes 1572872 | tf_op jit(solution)/shard_map/ppermute | solution.py:71
  7.6 0.0 collective-permute-start
  7.6 0.7 fusion.5.owners
  8.3 2.0 %copy-done = bf16[896,2048]{1,0:T(8,128)(2,1)S(1)} copy-done((bf16[896,2048]{1,0:T(8,128)(2,1)S(1)}, bf16[896,2048]{1,0:T(8,128)(2,1)}, u32[]{:S(2)}) %copy-start) | copy-done | bytes 3670040
  10.3 2.6 %shard_map.111 = (bf16[896,2048]{1,0:T(8,128)(2,1)S(1)}, bf16[896,2048]{1,0:T(8,128)(2,1)S(1)}) custom-call(s32[32]{0:T(128)S(1)} %fusion.5.owners, bf16[896,2048]{1,0:T(8,128)(2,1)S(1)} %copy-done), custom_call_target="tpu_custom_call" | custom-call | bytes 11010048 | tf_op jit(solution)/shard_map/pallas_call | solution.py:154
  12.9 1.8 %copy-done.1 = bf16[896,2048]{1,0:T(8,128)(2,1)} copy-done((bf16[896,2048]{1,0:T(8,128)(2,1)}, bf16[896,2048]{1,0:T(8,128)(2,1)S(1)}, u32[]{:S(2)}) %copy-start.1) | copy-done | bytes 3670040
  14.7 1.8 %copy-done.4 = bf16[896,2048]{1,0:T(8,128)(2,1)} copy-done((bf16[896,2048]{1,0:T(8,128)(2,1)}, bf16[896,2048]{1,0:T(8,128)(2,1)S(1)}, u32[]{:S(2)}) %copy-start.4) | copy-done | bytes 3670040
  16.6 0.0 collective-permute-done.refs_4_
  16.6 0.9 collective-permute-start.1
  17.5 0.6 collective-permute-start.2
  18.1 1.7 %fusion = (f32[128]{0:T(128)S(1)}, f32[128]{0:T(128)S(1)}) fusion(bf16[128,4096]{1,0:T(8,128)(2,1)} %param.8, f32[4096]{0:T(1024)S(1)} %convert_multiply_fusion.3), kind=kLoop, calls=%fused_computation.2 | loop fusion | flops 2621184 | bytes 1065984 | tf_op jit(solution)/shard_map/reduce_sum | solution.py:379
  19.8 1.6 %collective-permute-start.5 = (f32[4,128]{1,0:T(4,128)S(1)}, f32[4,128]{1,0:T(4,128)S(1)}, u32[]{:S(2)}, u32[]{:S(2)}) collective-permute-start(f32[4,128]{1,0:T(4,128)S(1)} %pad_maximum_fusion.3), channel_id=1, source_target_pairs={{0,1},{1,0},{2,3},{3,2},{4,5},{5,4},{6,7},{7,6},{8,9},{9,8},{10,11... | collective-permute-start | bytes 6152 | tf_op jit(solution)/shard_map/ppermute | solution.py:18
  21.3 1.4 %collective-permute-start.10 = (bf16[128,2048]{1,0:T(8,128)(2,1)S(1)}, bf16[128,2048]{1,0:T(8,128)(2,1)S(1)}, u32[]{:S(2)}, u32[]{:S(2)}) collective-permute-start(bf16[128,2048]{1,0:T(8,128)(2,1)S(1)} %collective-permute-done.3.refs_7_), channel_id=1, source_target_pairs={{0,4},{2,6},{4,0},{6,2},{8,12},{10,14},{12,8},{14,10},{16,20},{18,... | collective-permute-start | bytes 1572872 | tf_op jit(solution)/shard_map/ppermute | solution.py:71
  22.8 2.1 %collective-permute-start.9 = (bf16[128,2048]{1,0:T(8,128)(2,1)S(1)}, bf16[128,2048]{1,0:T(8,128)(2,1)}, u32[]{:S(2)}, u32[]{:S(2)}) collective-permute-start(bf16[128,2048]{1,0:T(8,128)(2,1)S(1)} %collective-permute-done.3.refs_7_), channel_id=1, source_target_pairs={{0,16},{2,10},{4,20},{6,14},{8,0},{10,26},{12,4},{14,30},{16,24},{... | collective-permute-start | bytes 1572872 | tf_op jit(solution)/shard_map/ppermute | solution.py:71
  24.9 1.1 collective-permute-done.6
  26.0 0.1 broadcast_select_fusion.4
  26.1 10.7 %collective-permute-done.1.refs_8_ = bf16[128,2048]{1,0:T(8,128)(2,1)S(1)} collective-permute-done((bf16[128,2048]{1,0:T(8,128)(2,1)S(1)}, bf16[128,2048]{1,0:T(8,128)(2,1)S(1)}, u32[]{:S(2)}, u32[]{:S(2)}) %collective-permute-start.1) | collective-permute-done | bytes 524320 | tf_op jit(solution)/shard_map/ppermute | solution.py:71
  36.8 0.6 collective-permute-start.11
  37.4 0.1 collective-permute-start.7
  37.5 1.5 %collective-permute-start.8 = (bf16[128,2048]{1,0:T(8,128)(2,1)S(1)}, bf16[128,2048]{1,0:T(8,128)(2,1)S(1)}, u32[]{:S(2)}, u32[]{:S(2)}) collective-permute-start(bf16[128,2048]{1,0:T(8,128)(2,1)S(1)} %collective-permute-done.1.refs_8_), channel_id=1, source_target_pairs={{0,4},{2,6},{4,0},{6,2},{8,12},{10,14},{12,8},{14,10},{16,20},{18,... | collective-permute-start | bytes 1572872 | tf_op jit(solution)/shard_map/ppermute | solution.py:71
  39.0 4.7 %collective-permute-done.11 = f32[2,4,128]{2,1,0:T(4,128)S(1)} collective-permute-done((f32[2,4,128]{2,1,0:T(4,128)S(1)}, f32[2,4,128]{2,1,0:T(4,128)S(1)}, u32[]{:S(2)}, u32[]{:S(2)}) %collective-permute-start.11) | collective-permute-done | bytes 4128 | tf_op jit(solution)/shard_map/ppermute | solution.py:28
  43.6 0.8 copy-done.5
  44.4 1.6 %collective-permute-done.9.refs_11_ = bf16[128,2048]{1,0:T(8,128)(2,1)} collective-permute-done((bf16[128,2048]{1,0:T(8,128)(2,1)S(1)}, bf16[128,2048]{1,0:T(8,128)(2,1)}, u32[]{:S(2)}, u32[]{:S(2)}) %collective-permute-start.9) | collective-permute-done | bytes 524320 | tf_op jit(solution)/shard_map/ppermute | solution.py:71
  46.0 1.2 %collective-permute-start.15 = (bf16[128,2048]{1,0:T(8,128)(2,1)}, bf16[128,2048]{1,0:T(8,128)(2,1)}, u32[]{:S(2)}, u32[]{:S(2)}) collective-permute-start(bf16[128,2048]{1,0:T(8,128)(2,1)} %collective-permute-done.9.refs_11_), channel_id=1, source_target_pairs={{0,16},{2,10},{4,20},{6,14},{8,0},{10,26},{12,4},{14,30},{16,24},{... | collective-permute-start | bytes 1572872 | tf_op jit(solution)/shard_map/ppermute | solution.py:71
  47.3 2.7 %collective-permute-start.16 = (bf16[128,2048]{1,0:T(8,128)(2,1)}, bf16[128,2048]{1,0:T(8,128)(2,1)}, u32[]{:S(2)}, u32[]{:S(2)}) collective-permute-start(bf16[128,2048]{1,0:T(8,128)(2,1)} %collective-permute-done.9.refs_11_), channel_id=1, source_target_pairs={{0,4},{2,6},{4,0},{6,2},{8,12},{10,14},{12,8},{14,10},{16,20},{18,... | collective-permute-start | bytes 1572872 | tf_op jit(solution)/shard_map/ppermute | solution.py:71
  49.9 2.2 %collective-permute-done.12 = f32[4,4,128]{2,1,0:T(4,128)S(1)} collective-permute-done((f32[4,4,128]{2,1,0:T(4,128)S(1)}, f32[4,4,128]{2,1,0:T(4,128)S(1)}, u32[]{:S(2)}, u32[]{:S(2)}) %collective-permute-start.12) | collective-permute-done | bytes 8224 | tf_op jit(solution)/shard_map/ppermute | solution.py:28
  52.2 7.3 %collective-permute-done.7.refs_12_ = bf16[128,2048]{1,0:T(8,128)(2,1)S(1)} collective-permute-done((bf16[128,2048]{1,0:T(8,128)(2,1)S(1)}, bf16[128,2048]{1,0:T(8,128)(2,1)S(1)}, u32[]{:S(2)}, u32[]{:S(2)}) %collective-permute-start.7) | collective-permute-done | bytes 524320 | tf_op jit(solution)/shard_map/ppermute | solution.py:71
  59.5 0.8 copy-done.9
  60.4 0.1 copy-done.7
  60.5 2.5 %collective-permute-start.13 = (bf16[128,2048]{1,0:T(8,128)(2,1)}, bf16[128,2048]{1,0:T(8,128)(2,1)S(1)}, u32[]{:S(2)}, u32[]{:S(2)}) collective-permute-start(bf16[128,2048]{1,0:T(8,128)(2,1)} %copy-done.7), channel_id=1, source_target_pairs={{0,8},{2,18},{4,12},{6,22},{8,24},{10,2},{12,28},{14,6},{16,0},{18... | collective-permute-start | bytes 1572872 | tf_op jit(solution)/shard_map/ppermute | solution.py:71
  63.0 1.2 %collective-permute-start.14 = (bf16[128,2048]{1,0:T(8,128)(2,1)}, bf16[128,2048]{1,0:T(8,128)(2,1)S(1)}, u32[]{:S(2)}, u32[]{:S(2)}) collective-permute-start(bf16[128,2048]{1,0:T(8,128)(2,1)} %copy-done.7), channel_id=1, source_target_pairs={{0,4},{2,6},{4,0},{6,2},{8,12},{10,14},{12,8},{14,10},{16,20},{18,... | collective-permute-start | bytes 1572872 | tf_op jit(solution)/shard_map/ppermute | solution.py:71
  64.2 2.8 %collective-permute-done.17 = f32[8,4,128]{2,1,0:T(4,128)S(1)} collective-permute-done((f32[8,4,128]{2,1,0:T(4,128)S(1)}, f32[8,4,128]{2,1,0:T(4,128)S(1)}, u32[]{:S(2)}, u32[]{:S(2)}) %collective-permute-start.17) | collective-permute-done | bytes 16416 | tf_op jit(solution)/shard_map/ppermute | solution.py:28
  67.0 0.3 collective-permute-done.15.refs_5_
  67.3 0.2 fusion.11
  67.5 0.3 select_reduce_fusion.1
  67.8 0.1 broadcast_compare_fusion
  67.9 0.1 select_reduce_fusion.4
  68.0 0.7 select_reduce_fusion
  68.7 0.1 slice_reduce_fusion
  68.8 0.9 collective-permute-start.19
  69.7 0.1 select_reduce_fusion.2
  69.9 0.1 select_reduce_fusion.3
  70.0 0.1 broadcast_in_dim.147
  70.0 0.1 eq.100
  70.2 2.0 %copy-done.2 = bf16[896,2048]{1,0:T(8,128)(2,1)S(1)} copy-done((bf16[896,2048]{1,0:T(8,128)(2,1)S(1)}, bf16[896,2048]{1,0:T(8,128)(2,1)}, u32[]{:S(2)}) %copy-start.2) | copy-done | bytes 3670040
  72.3 1.0 copy-done.6
  73.3 1.0 copy-done.8
  74.3 1.0 copy-done.10
  75.4 11.8 %shard_map.112 = (f32[896,2048]{1,0:T(8,128)S(1)}, bf16[1280,2048]{1,0:T(8,128)(2,1)S(1)}, f32[16,1,2048]{2,1,0:T(1,128)S(1)}) custom-call(s32[32]{0:T(128)S(1)} %fusion.5.owners, s32[1]{0:T(128)} %constant.75.clone.1.where, bf16[896,2048]{1,0:T(8,128)(2,1)S(1)} %copy-done.2, f32[8,2048]{1,0:T(8,128)S(1)} %select_maximum_fusion.refs_1_, ...), custom_call_target="tpu_custom_call" | custom-call | flops 46976204800 | bytes 86376448 | tf_op jit(solution)/shard_map/pallas_call | solution.py:273
  87.2 0.6 dynamic-slice.1
  87.8 1.2 %fusion.9 = f32[128]{0:T(128)} fusion(f32[16,128]{1,0:T(8,128)S(1)} %select_reduce_fusion, s32[]{:T(128)S(6)} %select_n.166, pred[16,128]{1,0:T(8,128)(4,1)S(1)} %broadcast_compare_fusion, f32[1]{0:T(128)} %dynamic-slice.1), kind=kLoop, calls=%fused_computation.52 | loop fusion | flops 256 | bytes 1160 | tf_op jit(solution)/shard_map/jit(dynamic_index_in_dim)/squeeze | solution.py:367
  88.9 0.5 fusion.7
  89.5 0.2 collective-permute-start.20
  89.6 10.9 %shard_map.113 = (f32[896,2048]{1,0:T(8,128)S(1)}, bf16[512,2048]{1,0:T(8,128)(2,1)S(1)}, f32[16,1,2048]{2,1,0:T(1,128)S(1)}) custom-call(s32[32]{0:T(128)S(1)} %fusion.5.owners, s32[1]{0:T(128)} %constant.75.clone.1.where, bf16[896,2048]{1,0:T(8,128)(2,1)S(1)} %collective-permute-done.18.refs_0_, f32[8,2048]{1,0:T(8,128)S(1)} %select_maximum_fusion.refs_1_, ...), custom_call_target="tpu_custom_call" | custom-call | flops 6576668672 | bytes 21561344 | tf_op jit(solution)/shard_map/pallas_call | solution.py:273
  100.6 2.2 %collective-permute-done.20.refs_4_ = bf16[128,2048]{1,0:T(8,128)(2,1)S(1)} collective-permute-done((bf16[128,2048]{1,0:T(8,128)(2,1)S(1)}, bf16[128,2048]{1,0:T(8,128)(2,1)S(1)}, u32[]{:S(2)}, u32[]{:S(2)}) %collective-permute-start.20) | collective-permute-done | bytes 524320 | tf_op jit(solution)/shard_map/ppermute | solution.py:71
  102.8 3.4 %shard_map.114 = (bf16[896,2048]{1,0:T(8,128)(2,1)S(1)}, bf16[256,2048]{1,0:T(8,128)(2,1)S(1)}, f32[1,2048]{1,0:T(1,128)S(1)}) custom-call(s32[32]{0:T(128)S(1)} %fusion.5.owners, s32[1]{0:T(128)} %constant.75.clone.1.where, bf16[896,2048]{1,0:T(8,128)(2,1)S(1)} %collective-permute-done.18.refs_0_, f32[8,2048]{1,0:T(8,128)S(1)} %select_maximum_fusion.refs_1_, ...), custom_call_target="tpu_custom_call" | custom-call | flops 939524096 | bytes 12517376 | tf_op jit(solution)/shard_map/pallas_call | solution.py:273
  106.2 0.1 collective-permute-start.22
  106.3 0.5 collective-permute-start.21
  106.8 5.0 %shard_map.115.whole = bf16[896,4096]{1,0:T(8,128)(2,1)} custom-call(s32[32]{0:T(128)S(1)} %fusion.5.owners, s32[1]{0:T(128)} %bitcast.where, bf16[896,2048]{1,0:T(8,128)(2,1)S(1)} %copy-done.3, bf16[256,2048]{1,0:T(8,128)(2,1)S(1)} %get-tuple-element.103.refs_1_, bf16[512,2048]{1,0:T(8,128)(2,1)S(1)} %get-tuple-element.104.refs_2_, ...), custom_call_target="tpu_custom_call" | custom-call | flops 2818572288 | bytes 15532032 | tf_op jit(solution)/shard_map/pallas_call | solution.py:273
  111.8 0.9 collective-permute-done.21
  112.7 0.6 convert_multiply_fusion.2
  113.3 2.2 %shard_map.116 = bf16[896,4096]{1,0:T(8,128)(2,1)} custom-call(s32[1]{0:T(128)S(6)} %sub.26.where, bf16[896,2048]{1,0:T(8,128)(2,1)S(1)} %collective-permute-done.22.part, bf16[896,4096]{1,0:T(8,128)(2,1)} %shard_map.115.whole), custom_call_target="tpu_custom_call", output_to_operand_aliasing={{}: (2, {})} | custom-call | bytes 7340032 | tf_op jit(solution)/shard_map/pallas_call | solution.py:317
  (56 shorter events, 0.3 us)
Async XLA Ops:
  0.6 15.9 %copy-start.11 = (bf16[4096]{0:T(1024)(128)(2,1)S(1)}, bf16[4096]{0:T(1024)(128)(2,1)}, u32[]{:S(2)}) copy-start(bf16[4096]{0:T(1024)(128)(2,1)} %param.10) | copy-start | bytes 24580
  0.6 15.9 %copy-start.12 = (bf16[4096]{0:T(1024)(128)(2,1)S(1)}, bf16[4096]{0:T(1024)(128)(2,1)}, u32[]{:S(2)}) copy-start(bf16[4096]{0:T(1024)(128)(2,1)} %param.11) | copy-start | bytes 24580
  0.7 15.9 %copy-start.14 = (f32[128]{0:T(128)S(1)}, f32[128]{0:T(128)}, u32[]{:S(2)}) copy-start(f32[128]{0:T(128)} %param.12) | copy-start | bytes 1540
  0.7 15.9 %copy-start.15 = (f32[128]{0:T(128)S(1)}, f32[128]{0:T(128)}, u32[]{:S(2)}) copy-start(f32[128]{0:T(128)} %param.13) | copy-start | bytes 1540
  0.7 15.9 %copy-start.13 = (s32[128]{0:T(128)S(1)}, s32[128]{0:T(128)}, u32[]{:S(2)}) copy-start(s32[128]{0:T(128)} %param.14) | copy-start | bytes 1540
  2.0 17.7 %collective-permute-start.3 = (bf16[128,2048]{1,0:T(8,128)(2,1)S(1)}, bf16[128,2048]{1,0:T(8,128)(2,1)S(1)}, u32[]{:S(2)}, u32[]{:S(2)}) collective-permute-start(bf16[128,2048]{1,0:T(8,128)(2,1)S(1)} %get-tuple-element.58.refs_3_), channel_id=1, source_target_pairs={{0,16},{2,10},{4,20},{6,14},{8,0},{10,26},{12,4},{14,30},{16,24},{... | collective-permute-start | bytes 1572872 | tf_op jit(solution)/shard_map/ppermute | solution.py:71
  6.1 13.7 %collective-permute-start.4 = (bf16[128,2048]{1,0:T(8,128)(2,1)S(1)}, bf16[128,2048]{1,0:T(8,128)(2,1)S(1)}, u32[]{:S(2)}, u32[]{:S(2)}) collective-permute-start(bf16[128,2048]{1,0:T(8,128)(2,1)S(1)} %get-tuple-element.58.refs_3_), channel_id=1, source_target_pairs={{0,4},{2,6},{4,0},{6,2},{8,12},{10,14},{12,8},{14,10},{16,20},{18,... | collective-permute-start | bytes 1572872 | tf_op jit(solution)/shard_map/ppermute | solution.py:71
  7.6 9.0 %collective-permute-start = (bf16[128,2048]{1,0:T(8,128)(2,1)S(1)}, bf16[128,2048]{1,0:T(8,128)(2,1)S(1)}, u32[]{:S(2)}, u32[]{:S(2)}) collective-permute-start(bf16[128,2048]{1,0:T(8,128)(2,1)S(1)} %get-tuple-element.55), channel_id=1, source_target_pairs={{0,2},{2,0},{4,6},{6,4},{8,10},{10,8},{12,14},{14,12},{16,18},{18,... | collective-permute-start | bytes 1572872 | tf_op jit(solution)/shard_map/ppermute | solution.py:71
  8.3 2.0 %copy-start = (bf16[896,2048]{1,0:T(8,128)(2,1)S(1)}, bf16[896,2048]{1,0:T(8,128)(2,1)}, u32[]{:S(2)}) copy-start(bf16[896,2048]{1,0:T(8,128)(2,1)} %hidden.1) | copy-start | bytes 11010052
  12.9 1.8 %copy-start.1 = (bf16[896,2048]{1,0:T(8,128)(2,1)}, bf16[896,2048]{1,0:T(8,128)(2,1)S(1)}, u32[]{:S(2)}) copy-start(bf16[896,2048]{1,0:T(8,128)(2,1)S(1)} %get-tuple-element.77.refs_0_) | copy-start | bytes 11010052
  14.7 1.8 %copy-start.4 = (bf16[896,2048]{1,0:T(8,128)(2,1)}, bf16[896,2048]{1,0:T(8,128)(2,1)S(1)}, u32[]{:S(2)}) copy-start(bf16[896,2048]{1,0:T(8,128)(2,1)S(1)} %get-tuple-element.75) | copy-start | bytes 11010052
  16.6 20.2 %collective-permute-start.1 = (bf16[128,2048]{1,0:T(8,128)(2,1)S(1)}, bf16[128,2048]{1,0:T(8,128)(2,1)S(1)}, u32[]{:S(2)}, u32[]{:S(2)}) collective-permute-start(bf16[128,2048]{1,0:T(8,128)(2,1)S(1)} %collective-permute-done.refs_4_), channel_id=1, source_target_pairs={{0,8},{2,18},{4,12},{6,22},{8,24},{10,2},{12,28},{14,6},{16,0},{18... | collective-permute-start | bytes 1572872 | tf_op jit(solution)/shard_map/ppermute | solution.py:71
  17.5 19.3 %collective-permute-start.2 = (bf16[128,2048]{1,0:T(8,128)(2,1)S(1)}, bf16[128,2048]{1,0:T(8,128)(2,1)S(1)}, u32[]{:S(2)}, u32[]{:S(2)}) collective-permute-start(bf16[128,2048]{1,0:T(8,128)(2,1)S(1)} %collective-permute-done.refs_4_), channel_id=1, source_target_pairs={{0,4},{2,6},{4,0},{6,2},{8,12},{10,14},{12,8},{14,10},{16,20},{18,... | collective-permute-start | bytes 1572872 | tf_op jit(solution)/shard_map/ppermute | solution.py:71
  19.8 5.1 %collective-permute-start.5 = (f32[4,128]{1,0:T(4,128)S(1)}, f32[4,128]{1,0:T(4,128)S(1)}, u32[]{:S(2)}, u32[]{:S(2)}) collective-permute-start(f32[4,128]{1,0:T(4,128)S(1)} %pad_maximum_fusion.3), channel_id=1, source_target_pairs={{0,1},{1,0},{2,3},{3,2},{4,5},{5,4},{6,7},{7,6},{8,9},{9,8},{10,11... | collective-permute-start | bytes 6152 | tf_op jit(solution)/shard_map/ppermute | solution.py:18
  21.3 22.3 %collective-permute-start.10 = (bf16[128,2048]{1,0:T(8,128)(2,1)S(1)}, bf16[128,2048]{1,0:T(8,128)(2,1)S(1)}, u32[]{:S(2)}, u32[]{:S(2)}) collective-permute-start(bf16[128,2048]{1,0:T(8,128)(2,1)S(1)} %collective-permute-done.3.refs_7_), channel_id=1, source_target_pairs={{0,4},{2,6},{4,0},{6,2},{8,12},{10,14},{12,8},{14,10},{16,20},{18,... | collective-permute-start | bytes 1572872 | tf_op jit(solution)/shard_map/ppermute | solution.py:71
  22.8 23.2 %collective-permute-start.9 = (bf16[128,2048]{1,0:T(8,128)(2,1)S(1)}, bf16[128,2048]{1,0:T(8,128)(2,1)}, u32[]{:S(2)}, u32[]{:S(2)}) collective-permute-start(bf16[128,2048]{1,0:T(8,128)(2,1)S(1)} %collective-permute-done.3.refs_7_), channel_id=1, source_target_pairs={{0,16},{2,10},{4,20},{6,14},{8,0},{10,26},{12,4},{14,30},{16,24},{... | collective-permute-start | bytes 1572872 | tf_op jit(solution)/shard_map/ppermute | solution.py:71
  24.9 1.2 %collective-permute-start.6 = (f32[1,4,128]{2,1,0:T(4,128)S(1)}, f32[1,4,128]{2,1,0:T(4,128)S(1)}, u32[]{:S(2)}, u32[]{:S(2)}) collective-permute-start(f32[1,4,128]{2,1,0:T(4,128)S(1)} %bitcast.71), channel_id=1, source_target_pairs={{0,2},{2,0},{4,6},{6,4},{8,10},{10,8},{12,14},{14,12},{16,18},{18,... | collective-permute-start | bytes 6152 | tf_op jit(solution)/shard_map/ppermute | solution.py:28
  36.8 6.8 %collective-permute-start.11 = (f32[2,4,128]{2,1,0:T(4,128)S(1)}, f32[2,4,128]{2,1,0:T(4,128)S(1)}, u32[]{:S(2)}, u32[]{:S(2)}) collective-permute-start(f32[2,4,128]{2,1,0:T(4,128)S(1)} %broadcast_select_fusion.4), channel_id=1, source_target_pairs={{0,4},{2,6},{4,0},{6,2},{8,12},{10,14},{12,8},{14,10},{16,20},{18,... | collective-permute-start | bytes 12296 | tf_op jit(solution)/shard_map/ppermute | solution.py:28
  37.4 22.1 %collective-permute-start.7 = (bf16[128,2048]{1,0:T(8,128)(2,1)S(1)}, bf16[128,2048]{1,0:T(8,128)(2,1)S(1)}, u32[]{:S(2)}, u32[]{:S(2)}) collective-permute-start(bf16[128,2048]{1,0:T(8,128)(2,1)S(1)} %collective-permute-done.1.refs_8_), channel_id=1, source_target_pairs={{0,8},{2,18},{4,12},{6,22},{8,24},{10,2},{12,28},{14,6},{16,0},{18... | collective-permute-start | bytes 1572872 | tf_op jit(solution)/shard_map/ppermute | solution.py:71
  37.5 22.1 %collective-permute-start.8 = (bf16[128,2048]{1,0:T(8,128)(2,1)S(1)}, bf16[128,2048]{1,0:T(8,128)(2,1)S(1)}, u32[]{:S(2)}, u32[]{:S(2)}) collective-permute-start(bf16[128,2048]{1,0:T(8,128)(2,1)S(1)} %collective-permute-done.1.refs_8_), channel_id=1, source_target_pairs={{0,4},{2,6},{4,0},{6,2},{8,12},{10,14},{12,8},{14,10},{16,20},{18,... | collective-permute-start | bytes 1572872 | tf_op jit(solution)/shard_map/ppermute | solution.py:71
  43.6 0.8 copy-start.5
  46.0 6.2 %collective-permute-start.12 = (f32[4,4,128]{2,1,0:T(4,128)S(1)}, f32[4,4,128]{2,1,0:T(4,128)S(1)}, u32[]{:S(2)}, u32[]{:S(2)}) collective-permute-start(f32[4,4,128]{2,1,0:T(4,128)S(1)} %pad_maximum_fusion.2), channel_id=1, source_target_pairs={{0,8},{2,10},{4,12},{6,14},{8,0},{10,2},{12,4},{14,6},{16,24},{18,... | collective-permute-start | bytes 24584 | tf_op jit(solution)/shard_map/ppermute | solution.py:28
  46.0 21.3 %collective-permute-start.15 = (bf16[128,2048]{1,0:T(8,128)(2,1)}, bf16[128,2048]{1,0:T(8,128)(2,1)}, u32[]{:S(2)}, u32[]{:S(2)}) collective-permute-start(bf16[128,2048]{1,0:T(8,128)(2,1)} %collective-permute-done.9.refs_11_), channel_id=1, source_target_pairs={{0,16},{2,10},{4,20},{6,14},{8,0},{10,26},{12,4},{14,30},{16,24},{... | collective-permute-start | bytes 1572872 | tf_op jit(solution)/shard_map/ppermute | solution.py:71
  47.3 20.0 %collective-permute-start.16 = (bf16[128,2048]{1,0:T(8,128)(2,1)}, bf16[128,2048]{1,0:T(8,128)(2,1)}, u32[]{:S(2)}, u32[]{:S(2)}) collective-permute-start(bf16[128,2048]{1,0:T(8,128)(2,1)} %collective-permute-done.9.refs_11_), channel_id=1, source_target_pairs={{0,4},{2,6},{4,0},{6,2},{8,12},{10,14},{12,8},{14,10},{16,20},{18,... | collective-permute-start | bytes 1572872 | tf_op jit(solution)/shard_map/ppermute | solution.py:71
  59.5 1.0 copy-start.7
  59.5 0.8 copy-start.9
  60.4 6.6 %collective-permute-start.17 = (f32[8,4,128]{2,1,0:T(4,128)S(1)}, f32[8,4,128]{2,1,0:T(4,128)S(1)}, u32[]{:S(2)}, u32[]{:S(2)}) collective-permute-start(f32[8,4,128]{2,1,0:T(4,128)S(1)} %pad_maximum_fusion.1), channel_id=1, source_target_pairs={{0,16},{2,18},{4,20},{6,22},{8,24},{10,26},{12,28},{14,30},{16,0},... | collective-permute-start | bytes 49160 | tf_op jit(solution)/shard_map/ppermute | solution.py:28
  60.5 28.9 %collective-permute-start.13 = (bf16[128,2048]{1,0:T(8,128)(2,1)}, bf16[128,2048]{1,0:T(8,128)(2,1)S(1)}, u32[]{:S(2)}, u32[]{:S(2)}) collective-permute-start(bf16[128,2048]{1,0:T(8,128)(2,1)} %copy-done.7), channel_id=1, source_target_pairs={{0,8},{2,18},{4,12},{6,22},{8,24},{10,2},{12,28},{14,6},{16,0},{18... | collective-permute-start | bytes 1572872 | tf_op jit(solution)/shard_map/ppermute | solution.py:71
  63.0 26.5 %collective-permute-start.14 = (bf16[128,2048]{1,0:T(8,128)(2,1)}, bf16[128,2048]{1,0:T(8,128)(2,1)S(1)}, u32[]{:S(2)}, u32[]{:S(2)}) collective-permute-start(bf16[128,2048]{1,0:T(8,128)(2,1)} %copy-done.7), channel_id=1, source_target_pairs={{0,4},{2,6},{4,0},{6,2},{8,12},{10,14},{12,8},{14,10},{16,20},{18,... | collective-permute-start | bytes 1572872 | tf_op jit(solution)/shard_map/ppermute | solution.py:71
  67.0 22.5 %collective-permute-start.18 = (bf16[896,2048]{1,0:T(8,128)(2,1)}, bf16[896,2048]{1,0:T(8,128)(2,1)S(1)}, u32[]{:S(2)}, u32[]{:S(2)}) collective-permute-start(bf16[896,2048]{1,0:T(8,128)(2,1)} %copy-done.4), channel_id=1, source_target_pairs={{0,2},{2,0},{4,6},{6,4},{8,10},{10,8},{12,14},{14,12},{16,18},{18,... | collective-permute-start | bytes 11010056 | tf_op jit(solution)/shard_map/ppermute | solution.py:71
  68.8 31.8 %collective-permute-start.19 = (bf16[128,2048]{1,0:T(8,128)(2,1)}, bf16[128,2048]{1,0:T(8,128)(2,1)S(1)}, u32[]{:S(2)}, u32[]{:S(2)}) collective-permute-start(bf16[128,2048]{1,0:T(8,128)(2,1)} %collective-permute-done.16.refs_3_), channel_id=1, source_target_pairs={{0,16},{2,10},{4,20},{6,14},{8,0},{10,26},{12,4},{14,30},{16,24},{... | collective-permute-start | bytes 1572872 | tf_op jit(solution)/shard_map/ppermute | solution.py:71
  70.2 2.0 %copy-start.2 = (bf16[896,2048]{1,0:T(8,128)(2,1)S(1)}, bf16[896,2048]{1,0:T(8,128)(2,1)}, u32[]{:S(2)}) copy-start(bf16[896,2048]{1,0:T(8,128)(2,1)} %copy-done.1) | copy-start | bytes 11010052
  72.3 1.0 copy-start.6
  73.3 1.0 copy-start.8
  74.3 1.0 copy-start.10
  89.5 13.4 %collective-permute-start.20 = (bf16[128,2048]{1,0:T(8,128)(2,1)S(1)}, bf16[128,2048]{1,0:T(8,128)(2,1)S(1)}, u32[]{:S(2)}, u32[]{:S(2)}) collective-permute-start(bf16[128,2048]{1,0:T(8,128)(2,1)S(1)} %collective-permute-done.13.refs_6_), channel_id=1, source_target_pairs={{0,4},{2,6},{4,0},{6,2},{8,12},{10,14},{12,8},{14,10},{16,20},{18,... | collective-permute-start | bytes 1572872 | tf_op jit(solution)/shard_map/ppermute | solution.py:71
  102.8 3.9 %copy-start.3 = (bf16[896,2048]{1,0:T(8,128)(2,1)S(1)}, bf16[896,2048]{1,0:T(8,128)(2,1)}, u32[]{:S(2)}) copy-start(bf16[896,2048]{1,0:T(8,128)(2,1)} %copy-done.1) | copy-start | bytes 11010052
  106.2 7.1 %collective-permute-start.22 = (bf16[896,2048]{1,0:T(8,128)(2,1)S(1)}, bf16[896,2048]{1,0:T(8,128)(2,1)S(1)}, u32[]{:S(2)}, u32[]{:S(2)}) collective-permute-start(bf16[896,2048]{1,0:T(8,128)(2,1)S(1)} %get-tuple-element.101), channel_id=1, source_target_pairs={{0,2},{2,0},{4,6},{6,4},{8,10},{10,8},{12,14},{14,12},{16,18},{18,... | collective-permute-start | bytes 11010056 | tf_op jit(solution)/shard_map/ppermute | solution.py:366
  106.3 6.4 %collective-permute-start.21 = (f32[2048]{0:T(1024)S(1)}, f32[2048]{0:T(1024)S(1)}, u32[]{:S(2)}, u32[]{:S(2)}) collective-permute-start(f32[2048]{0:T(1024)S(1)} %bitcast.53), channel_id=1, source_target_pairs={{0,2},{2,0},{4,6},{6,4},{8,10},{10,8},{12,14},{14,12},{16,18},{18,... | collective-permute-start | bytes 24584 | tf_op jit(solution)/shard_map/ppermute | solution.py:366

commit v7 on v6

--- a/solution.py
+++ b/solution.py
@@ -26,7 +26,7 @@
     if step >= count:
         return x
     other = lax.ppermute(x, axis, [(i, i ^ step) for i in range(count)])
-    if step > 1:
+    if step > 2:
         return jnp.concatenate([jnp.where(low[step], x, other), jnp.where(low[step], other, x)])
     first = lax.broadcasted_iota(jnp.int32, (2, *x.shape), 0) == 0
     return jnp.where(first == low[step], x[None], other[None]).reshape(2 * step, *x.shape[1:])
@@ -97,13 +97,13 @@
         [(0, 0, 1), "stream", *names],
         [((1, 0, 1), (0, 0, 1), ring[1]), ((0, 1, 1), (0, 0, 1), across)],
     )
-    have["sums"] = own_facts(have["stream"])
+    have["facts"] = butterfly_sum(own_facts(have["stream"]), "tp")[None]
     have["own picks"], have["away picks"] = pick_both()
     f.event(
-        [(1, 0, 0), (0, 1, 0), "sums", "own picks", "away picks"],
+        [(1, 0, 0), (0, 1, 0), "facts", "own picks", "away picks"],
         [((2, 0, 0), (1, 0, 0), ring[0]), ((1, 1, 0), (1, 0, 0), across)],
     )
-    have["facts"] = butterfly_sum(have["sums"], "tp")[None]
+    facts_step()
     facts_step()
     f.event([(1, 0, 1), (0, 1, 1), "facts"], [((2, 0, 1), (1, 0, 1), ring[1]), ((1, 1, 1), (1, 0, 1), across)])
     for k in range(2, m):
@@ -121,7 +121,7 @@
             if k == m - 1 and kind == 1:
                 waits += ["other picks", "early own", "values", "returns"]
             f.event(waits, sends)
-            if k == m - 1 and kind == 0:
+            if k == m - 2 and kind == 1:
                 while have["facts"].shape[0] < paths.count:
                     facts_step()
                 early_own(have)
@@ -364,7 +364,7 @@
         head = gain * value_head.astype(jnp.float32)
         head_half = lax.dynamic_slice_in_dim(head, mine * half, half)[None]
         to_core = lambda x: lax.ppermute(x, "seq", paths.core)
-        own = lambda a, me=me: lax.dynamic_index_in_dim(a, me, 0, keepdims=False)
+        own = lambda a: lax.dynamic_index_in_dim(a, me, 0, keepdims=False)
         last, middle, early = block_groups(paths.m)
         table = paths.owners(last + middle + early)
         both = np.concatenate([table, table[np.arange(shards) ^ 1]], axis=1)
@@ -392,7 +392,9 @@
             pull = scale**3 * along / width
             coefs = jnp.stack([error * scale, error * pull]).reshape(2, shards * tok)
             coefs = jnp.pad(coefs, ((0, 6), (0, 0)))
-            have.update(values=own(values, have["me"]), returns=own(returns, have["me"]), coefs=coefs)
+            mask = jnp.arange(shards)[:, None] == have["me"]
+            row = lambda a: jnp.sum(jnp.where(mask, a, 0.0), axis=0)
+            have.update(values=row(values), returns=row(returns), coefs=coefs)
             have["early own"], have["early dstream"], have["early parts"] = product(
                 have["owners"], early_at, have["own picks"], (coefs, head_half, [have[b] for b in early])
             )

time: 116 us -> 112 us (0.966)
  local copies, waits for them, and re-layouts: 15.4 us -> 10.1 us
  Pallas kernels: 35.9 us -> 33.6 us
  waiting for transfers between devices: 33.8 us -> 35.5 us
  starting transfers between devices: 23.6 us -> 24.9 us
    ppermute x4, waiting for transfers between devices: 10.8 us -> 27.3 us  [butterfly_step(): other = lax.ppermute(x, axis, [(i, i ^ step) for i in range(count)])]
    ppermute x16, waiting for transfers between devices: 22.1 us -> 7.35 us  [event(): self.have[name] = lax.ppermute(self.have[source], 'seq', pairs)]
    unnamed x32 -> x12, local copies, waits for them, and re-layouts: 12.6 us -> 7.69 us
    pallas_call x4, Pallas kernels: 31.1 us -> 28.8 us  [product(): pl.pallas_call(functools.partial(product_kernel, tok, count, first, len(g...]
    ppermute x4, starting transfers between devices: 0.62 us -> 2.88 us  [butterfly_step(): other = lax.ppermute(x, axis, [(i, i ^ step) for i in range(count)])]
    squeeze x2 -> x0, other arithmetic: 1.68 us -> none  [body(): own = lambda a, me=me: lax.dynamic_index_in_dim(a, me, 0, keepdims=False)]
  transfers between devices with their start and end apart: 23 -> 23, of which waited for: 10 -> 8; matrix products, arithmetic and copies ran while one was open for 6% -> 7% of each run, Pallas kernels for 26% -> 25%
where the time goes in v7:
time: 112 us; the launch traced here: 111 us
  waiting for transfers between devices  35.5 us (32%)
  Pallas kernels  33.6 us (30%)
  starting transfers between devices  24.9 us (22%)
  local copies, waits for them, and re-layouts  10.1 us (9%)
  other arithmetic  6.14 us (5%)
    pallas_call x4, Pallas kernels, product(): pl.pallas_call(functools.partial(product_kernel, tok, count, first, len(g...  28.8 us
    ppermute x4, waiting for transfers between devices, butterfly_step(): other = lax.ppermute(x, axis, [(i, i ^ step) for i in range(count)])  27.3 us
    ppermute x16, starting transfers between devices, event(): self.have[name] = lax.ppermute(self.have[source], 'seq', pairs)  19.9 us
    unnamed x12, local copies, waits for them, and re-layouts  7.69 us
    ppermute x16, waiting for transfers between devices, event(): self.have[name] = lax.ppermute(self.have[source], 'seq', pairs)  7.35 us
    ppermute x4, starting transfers between devices, butterfly_step(): other = lax.ppermute(x, axis, [(i, i ^ step) for i in range(count)])  2.88 us
    pallas_call x1, Pallas kernels, pick(): pl.pallas_call(functools.partial(pick_kernel, tok), grid_spec=pltpu.Prefe...  2.55 us
  transfers between devices with their start and end apart: 23, of which 8 were waited for; matrix products, arithmetic and copies ran while one was open for 7% of the time, Pallas kernels for 25%

profile of v7, /device:TPU:0, one launch (start us, length us, event | category | flops | bytes accessed | tf_op | source)
XLA Modules:
  0.0 111.2 jit_solution(11045362860197758261)
XLA Ops:
  0.7 1.3 %constant_dynamic-slice_fusion.1 = (bf16[128,2048]{1,0:T(8,128)(2,1)S(1)}, bf16[128,2048]{1,0:T(8,128)(2,1)S(1)}) fusion(bf16[128,4096]{1,0:T(8,128)(2,1)} %param.8, s32[]{:T(128)S(6)} %select_n.141, s32[]{:T(128)S(6)} %select_n.140), kind=kLoop, calls=%fused_computation.46 | loop fusion | bytes 2097160 | tf_op jit(solution)/shard_map/dynamic_slice | solution.py:84
  2.0 4.1 %collective-permute-start.3 = (bf16[128,2048]{1,0:T(8,128)(2,1)S(1)}, bf16[128,2048]{1,0:T(8,128)(2,1)S(1)}, u32[]{:S(2)}, u32[]{:S(2)}) collective-permute-start(bf16[128,2048]{1,0:T(8,128)(2,1)S(1)} %get-tuple-element.58.refs_3_), channel_id=1, source_target_pairs={{0,16},{2,10},{4,20},{6,14},{8,0},{10,26},{12,4},{14,30},{16,24},{... | collective-permute-start | bytes 1572872 | tf_op jit(solution)/shard_map/ppermute | solution.py:71
  6.0 1.5 %collective-permute-start.4 = (bf16[128,2048]{1,0:T(8,128)(2,1)S(1)}, bf16[128,2048]{1,0:T(8,128)(2,1)S(1)}, u32[]{:S(2)}, u32[]{:S(2)}) collective-permute-start(bf16[128,2048]{1,0:T(8,128)(2,1)S(1)} %get-tuple-element.58.refs_3_), channel_id=1, source_target_pairs={{0,4},{2,6},{4,0},{6,2},{8,12},{10,14},{12,8},{14,10},{16,20},{18,... | collective-permute-start | bytes 1572872 | tf_op jit(solution)/shard_map/ppermute | solution.py:71
  7.6 0.0 collective-permute-start
  7.6 0.7 fusion.6.owners
  8.3 0.7 multiply_bitcast_fusion
  9.0 0.7 convert_multiply_fusion.3
  9.7 1.7 %fusion = (f32[128]{0:T(128)S(1)}, f32[128]{0:T(128)S(1)}) fusion(bf16[128,4096]{1,0:T(8,128)(2,1)} %param.8, f32[4096]{0:T(1024)S(1)} %convert_multiply_fusion.3), kind=kLoop, calls=%fused_computation.2 | loop fusion | flops 2621184 | bytes 1065984 | tf_op jit(solution)/shard_map/reduce_sum | solution.py:379
  11.4 1.6 %collective-permute-start.5 = (f32[4,128]{1,0:T(4,128)S(1)}, f32[4,128]{1,0:T(4,128)S(1)}, u32[]{:S(2)}, u32[]{:S(2)}) collective-permute-start(f32[4,128]{1,0:T(4,128)S(1)} %pad_maximum_fusion.2), channel_id=1, source_target_pairs={{0,1},{1,0},{2,3},{3,2},{4,5},{5,4},{6,7},{7,6},{8,9},{9,8},{10,11... | collective-permute-start | bytes 6152 | tf_op jit(solution)/shard_map/ppermute | solution.py:18
  13.0 0.0 copy-start
  13.0 2.0 %copy-done = bf16[896,2048]{1,0:T(8,128)(2,1)S(1)} copy-done((bf16[896,2048]{1,0:T(8,128)(2,1)S(1)}, bf16[896,2048]{1,0:T(8,128)(2,1)}, u32[]{:S(2)}) %copy-start) | copy-done | bytes 3670040
  15.0 2.6 %shard_map.111 = (bf16[896,2048]{1,0:T(8,128)(2,1)S(1)}, bf16[896,2048]{1,0:T(8,128)(2,1)S(1)}) custom-call(s32[32]{0:T(128)S(1)} %fusion.6.owners, bf16[896,2048]{1,0:T(8,128)(2,1)S(1)} %copy-done), custom_call_target="tpu_custom_call" | custom-call | bytes 11010048 | tf_op jit(solution)/shard_map/pallas_call | solution.py:154
  17.6 1.8 %copy-done.1 = bf16[896,2048]{1,0:T(8,128)(2,1)} copy-done((bf16[896,2048]{1,0:T(8,128)(2,1)}, bf16[896,2048]{1,0:T(8,128)(2,1)S(1)}, u32[]{:S(2)}) %copy-start.1) | copy-done | bytes 3670040
  19.4 1.8 %copy-done.4 = bf16[896,2048]{1,0:T(8,128)(2,1)} copy-done((bf16[896,2048]{1,0:T(8,128)(2,1)}, bf16[896,2048]{1,0:T(8,128)(2,1)S(1)}, u32[]{:S(2)}) %copy-start.4) | copy-done | bytes 3670040
  21.2 0.8 collective-permute-start.1
  22.1 0.6 collective-permute-start.2
  22.6 0.0 collective-permute-done.5
  22.7 0.0 collective-permute-done.3.refs_7_
  22.7 0.5 collective-permute-start.6
  23.1 0.8 collective-permute-done.6
  24.0 0.1 broadcast_select_fusion.4
  24.0 1.5 %collective-permute-start.7 = (f32[2,4,128]{2,1,0:T(4,128)S(1)}, f32[2,4,128]{2,1,0:T(4,128)S(1)}, u32[]{:S(2)}, u32[]{:S(2)}) collective-permute-start(f32[2,4,128]{2,1,0:T(4,128)S(1)} %broadcast_select_fusion.4), channel_id=1, source_target_pairs={{0,4},{2,6},{4,0},{6,2},{8,12},{10,14},{12,8},{14,10},{16,20},{18,... | collective-permute-start | bytes 12296 | tf_op jit(solution)/shard_map/ppermute | solution.py:28
  25.5 0.1 iota.66
  25.6 0.1 eq.126
  25.7 2.0 %collective-permute-start.10 = (bf16[128,2048]{1,0:T(8,128)(2,1)S(1)}, bf16[128,2048]{1,0:T(8,128)(2,1)S(1)}, u32[]{:S(2)}, u32[]{:S(2)}) collective-permute-start(bf16[128,2048]{1,0:T(8,128)(2,1)S(1)} %collective-permute-done.3.refs_7_), channel_id=1, source_target_pairs={{0,16},{2,10},{4,20},{6,14},{8,0},{10,26},{12,4},{14,30},{16,24},{... | collective-permute-start | bytes 1572872 | tf_op jit(solution)/shard_map/ppermute | solution.py:71
  27.7 0.5 collective-permute-start.11
  28.2 8.7 %collective-permute-done.7 = f32[2,4,128]{2,1,0:T(4,128)S(1)} collective-permute-done((f32[2,4,128]{2,1,0:T(4,128)S(1)}, f32[2,4,128]{2,1,0:T(4,128)S(1)}, u32[]{:S(2)}, u32[]{:S(2)}) %collective-permute-start.7) | collective-permute-done | bytes 4128 | tf_op jit(solution)/shard_map/ppermute | solution.py:28
  37.0 0.1 copy_select_fusion
  37.0 5.6 %collective-permute-done.1.refs_8_ = bf16[128,2048]{1,0:T(8,128)(2,1)S(1)} collective-permute-done((bf16[128,2048]{1,0:T(8,128)(2,1)S(1)}, bf16[128,2048]{1,0:T(8,128)(2,1)S(1)}, u32[]{:S(2)}, u32[]{:S(2)}) %collective-permute-start.1) | collective-permute-done | bytes 524320 | tf_op jit(solution)/shard_map/ppermute | solution.py:71
  42.7 2.1 %collective-permute-start.8 = (bf16[128,2048]{1,0:T(8,128)(2,1)S(1)}, bf16[128,2048]{1,0:T(8,128)(2,1)S(1)}, u32[]{:S(2)}, u32[]{:S(2)}) collective-permute-start(bf16[128,2048]{1,0:T(8,128)(2,1)S(1)} %collective-permute-done.1.refs_8_), channel_id=1, source_target_pairs={{0,8},{2,18},{4,12},{6,22},{8,24},{10,2},{12,28},{14,6},{16,0},{18... | collective-permute-start | bytes 1572872 | tf_op jit(solution)/shard_map/ppermute | solution.py:71
  44.7 0.6 collective-permute-start.9
  45.3 4.0 %collective-permute-done.12 = f32[4,4,128]{2,0,1:T(4,128)S(1)} collective-permute-done((f32[4,4,128]{2,0,1:T(4,128)S(1)}, f32[4,4,128]{2,0,1:T(4,128)S(1)}, u32[]{:S(2)}, u32[]{:S(2)}) %collective-permute-start.12) | collective-permute-done | bytes 8224 | tf_op jit(solution)/shard_map/ppermute | solution.py:28
  49.4 1.0 collective-permute-start.13
  50.3 2.0 %collective-permute-start.17 = (bf16[128,2048]{1,0:T(8,128)(2,1)S(1)}, bf16[128,2048]{1,0:T(8,128)(2,1)S(1)}, u32[]{:S(2)}, u32[]{:S(2)}) collective-permute-start(bf16[128,2048]{1,0:T(8,128)(2,1)S(1)} %collective-permute-done.10.refs_11_), channel_id=1, source_target_pairs={{0,16},{2,10},{4,20},{6,14},{8,0},{10,26},{12,4},{14,30},{16,24},{... | collective-permute-start | bytes 1572872 | tf_op jit(solution)/shard_map/ppermute | solution.py:71
  52.4 0.6 collective-permute-start.18
  52.9 13.7 %collective-permute-done.13 = f32[8,4,128]{2,0,1:T(8,128)S(1)} collective-permute-done((f32[8,4,128]{2,0,1:T(8,128)S(1)}, f32[8,4,128]{2,0,1:T(8,128)S(1)}, u32[]{:S(2)}, u32[]{:S(2)}) %collective-permute-start.13) | collective-permute-done | bytes 16416 | tf_op jit(solution)/shard_map/ppermute | solution.py:28
  66.7 0.1 collective-permute-start.14
  66.8 0.6 collective-permute-start.15
  67.4 0.1 fusion.9
  67.5 0.3 select_reduce_fusion.1
  67.9 0.1 broadcast_compare_fusion
  67.9 0.1 select_reduce_fusion.5
  68.0 0.7 select_reduce_fusion
  68.7 0.1 slice_reduce_fusion
  68.8 0.1 select_reduce_fusion.2
  68.9 0.1 select_reduce_fusion.4
  69.1 0.1 broadcast_in_dim.191
  69.1 0.1 eq.133
  69.3 0.1 collective-permute-start.16
  69.4 2.0 %copy-done.2 = bf16[896,2048]{1,0:T(8,128)(2,1)S(1)} copy-done((bf16[896,2048]{1,0:T(8,128)(2,1)S(1)}, bf16[896,2048]{1,0:T(8,128)(2,1)}, u32[]{:S(2)}) %copy-start.2) | copy-done | bytes 3670040
  71.4 10.8 %shard_map.112 = (f32[896,2048]{1,0:T(8,128)S(1)}, bf16[1280,2048]{1,0:T(8,128)(2,1)S(1)}, f32[16,1,2048]{2,1,0:T(1,128)S(1)}) custom-call(s32[32]{0:T(128)S(1)} %fusion.6.owners, s32[1]{0:T(128)} %constant.69.clone.1.where, bf16[896,2048]{1,0:T(8,128)(2,1)S(1)} %copy-done.2, f32[8,2048]{1,0:T(8,128)S(1)} %select_maximum_fusion.refs_1_, ...), custom_call_target="tpu_custom_call" | custom-call | flops 46976204800 | bytes 86376448 | tf_op jit(solution)/shard_map/pallas_call | solution.py:273
  82.2 0.6 select_reduce_fusion.3
  82.8 2.9 %collective-permute-start.19 = (bf16[128,2048]{1,0:T(8,128)(2,1)S(1)}, bf16[128,2048]{1,0:T(8,128)(2,1)S(1)}, u32[]{:S(2)}, u32[]{:S(2)}) collective-permute-start(bf16[128,2048]{1,0:T(8,128)(2,1)S(1)} %collective-permute-done.18.refs_3_), channel_id=1, source_target_pairs={{0,16},{2,10},{4,20},{6,14},{8,0},{10,26},{12,4},{14,30},{16,24},{... | collective-permute-start | bytes 1572872 | tf_op jit(solution)/shard_map/ppermute | solution.py:71
  85.7 1.5 %collective-permute-start.20 = (bf16[128,2048]{1,0:T(8,128)(2,1)S(1)}, bf16[128,2048]{1,0:T(8,128)(2,1)S(1)}, u32[]{:S(2)}, u32[]{:S(2)}) collective-permute-start(bf16[128,2048]{1,0:T(8,128)(2,1)S(1)} %collective-permute-done.14.refs_6_), channel_id=1, source_target_pairs={{0,4},{2,6},{4,0},{6,2},{8,12},{10,14},{12,8},{14,10},{16,20},{18,... | collective-permute-start | bytes 1572872 | tf_op jit(solution)/shard_map/ppermute | solution.py:71
  87.2 9.7 %shard_map.113 = (f32[896,2048]{1,0:T(8,128)S(1)}, bf16[512,2048]{1,0:T(8,128)(2,1)S(1)}, f32[16,1,2048]{2,1,0:T(1,128)S(1)}) custom-call(s32[32]{0:T(128)S(1)} %fusion.6.owners, s32[1]{0:T(128)} %constant.69.clone.1.where, bf16[896,2048]{1,0:T(8,128)(2,1)S(1)} %collective-permute-done.16.refs_0_, f32[8,2048]{1,0:T(8,128)S(1)} %select_maximum_fusion.refs_1_, ...), custom_call_target="tpu_custom_call" | custom-call | flops 6576668672 | bytes 21561344 | tf_op jit(solution)/shard_map/pallas_call | solution.py:273
  96.9 0.7 collective-permute-done.19.refs_3_
  97.6 1.0 collective-permute-done.20.refs_4_
  98.6 3.4 %shard_map.114 = (bf16[896,2048]{1,0:T(8,128)(2,1)S(1)}, bf16[256,2048]{1,0:T(8,128)(2,1)S(1)}, f32[1,2048]{1,0:T(1,128)S(1)}) custom-call(s32[32]{0:T(128)S(1)} %fusion.6.owners, s32[1]{0:T(128)} %constant.69.clone.1.where, bf16[896,2048]{1,0:T(8,128)(2,1)S(1)} %collective-permute-done.16.refs_0_, f32[8,2048]{1,0:T(8,128)S(1)} %select_maximum_fusion.refs_1_, ...), custom_call_target="tpu_custom_call" | custom-call | flops 939524096 | bytes 12517376 | tf_op jit(solution)/shard_map/pallas_call | solution.py:273
  101.9 0.1 collective-permute-start.22
  102.0 0.5 collective-permute-start.21
  102.5 5.0 %shard_map.115.whole = bf16[896,4096]{1,0:T(8,128)(2,1)} custom-call(s32[32]{0:T(128)S(1)} %fusion.6.owners, s32[1]{0:T(128)} %bitcast.where, bf16[896,2048]{1,0:T(8,128)(2,1)S(1)} %copy-done.3, bf16[256,2048]{1,0:T(8,128)(2,1)S(1)} %get-tuple-element.101.refs_1_, bf16[512,2048]{1,0:T(8,128)(2,1)S(1)} %get-tuple-element.102.refs_2_, ...), custom_call_target="tpu_custom_call" | custom-call | flops 2818572288 | bytes 15532032 | tf_op jit(solution)/shard_map/pallas_call | solution.py:273
  107.6 0.9 collective-permute-done.21
  108.4 0.6 convert_multiply_fusion.2
  109.1 2.2 %shard_map.116 = bf16[896,4096]{1,0:T(8,128)(2,1)} custom-call(s32[1]{0:T(128)S(6)} %sub.26.where, bf16[896,2048]{1,0:T(8,128)(2,1)S(1)} %collective-permute-done.22.part, bf16[896,4096]{1,0:T(8,128)(2,1)} %shard_map.115.whole), custom_call_target="tpu_custom_call", output_to_operand_aliasing={{}: (2, {})} | custom-call | bytes 7340032 | tf_op jit(solution)/shard_map/pallas_call | solution.py:317
  (39 shorter events, 0.2 us)
Async XLA Ops:
  2.0 20.7 %collective-permute-start.3 = (bf16[128,2048]{1,0:T(8,128)(2,1)S(1)}, bf16[128,2048]{1,0:T(8,128)(2,1)S(1)}, u32[]{:S(2)}, u32[]{:S(2)}) collective-permute-start(bf16[128,2048]{1,0:T(8,128)(2,1)S(1)} %get-tuple-element.58.refs_3_), channel_id=1, source_target_pairs={{0,16},{2,10},{4,20},{6,14},{8,0},{10,26},{12,4},{14,30},{16,24},{... | collective-permute-start | bytes 1572872 | tf_op jit(solution)/shard_map/ppermute | solution.py:71
  6.0 16.6 %collective-permute-start.4 = (bf16[128,2048]{1,0:T(8,128)(2,1)S(1)}, bf16[128,2048]{1,0:T(8,128)(2,1)S(1)}, u32[]{:S(2)}, u32[]{:S(2)}) collective-permute-start(bf16[128,2048]{1,0:T(8,128)(2,1)S(1)} %get-tuple-element.58.refs_3_), channel_id=1, source_target_pairs={{0,4},{2,6},{4,0},{6,2},{8,12},{10,14},{12,8},{14,10},{16,20},{18,... | collective-permute-start | bytes 1572872 | tf_op jit(solution)/shard_map/ppermute | solution.py:71
  7.6 2.2 %collective-permute-start = (bf16[128,2048]{1,0:T(8,128)(2,1)S(1)}, bf16[128,2048]{1,0:T(8,128)(2,1)S(1)}, u32[]{:S(2)}, u32[]{:S(2)}) collective-permute-start(bf16[128,2048]{1,0:T(8,128)(2,1)S(1)} %get-tuple-element.54), channel_id=1, source_target_pairs={{0,2},{2,0},{4,6},{6,4},{8,10},{10,8},{12,14},{14,12},{16,18},{18,... | collective-permute-start | bytes 1572872 | tf_op jit(solution)/shard_map/ppermute | solution.py:71
  11.4 11.2 %collective-permute-start.5 = (f32[4,128]{1,0:T(4,128)S(1)}, f32[4,128]{1,0:T(4,128)S(1)}, u32[]{:S(2)}, u32[]{:S(2)}) collective-permute-start(f32[4,128]{1,0:T(4,128)S(1)} %pad_maximum_fusion.2), channel_id=1, source_target_pairs={{0,1},{1,0},{2,3},{3,2},{4,5},{5,4},{6,7},{7,6},{8,9},{9,8},{10,11... | collective-permute-start | bytes 6152 | tf_op jit(solution)/shard_map/ppermute | solution.py:18
  13.0 2.0 %copy-start = (bf16[896,2048]{1,0:T(8,128)(2,1)S(1)}, bf16[896,2048]{1,0:T(8,128)(2,1)}, u32[]{:S(2)}) copy-start(bf16[896,2048]{1,0:T(8,128)(2,1)} %hidden.1) | copy-start | bytes 11010052
  17.6 1.8 %copy-start.1 = (bf16[896,2048]{1,0:T(8,128)(2,1)}, bf16[896,2048]{1,0:T(8,128)(2,1)S(1)}, u32[]{:S(2)}) copy-start(bf16[896,2048]{1,0:T(8,128)(2,1)S(1)} %get-tuple-element.73.refs_0_) | copy-start | bytes 11010052
  19.4 1.8 %copy-start.4 = (bf16[896,2048]{1,0:T(8,128)(2,1)}, bf16[896,2048]{1,0:T(8,128)(2,1)S(1)}, u32[]{:S(2)}) copy-start(bf16[896,2048]{1,0:T(8,128)(2,1)S(1)} %get-tuple-element.71) | copy-start | bytes 11010052
  21.2 21.4 %collective-permute-start.1 = (bf16[128,2048]{1,0:T(8,128)(2,1)S(1)}, bf16[128,2048]{1,0:T(8,128)(2,1)S(1)}, u32[]{:S(2)}, u32[]{:S(2)}) collective-permute-start(bf16[128,2048]{1,0:T(8,128)(2,1)S(1)} %collective-permute-done.refs_4_), channel_id=1, source_target_pairs={{0,8},{2,18},{4,12},{6,22},{8,24},{10,2},{12,28},{14,6},{16,0},{18... | collective-permute-start | bytes 1572872 | tf_op jit(solution)/shard_map/ppermute | solution.py:71
  22.1 20.6 %collective-permute-start.2 = (bf16[128,2048]{1,0:T(8,128)(2,1)S(1)}, bf16[128,2048]{1,0:T(8,128)(2,1)S(1)}, u32[]{:S(2)}, u32[]{:S(2)}) collective-permute-start(bf16[128,2048]{1,0:T(8,128)(2,1)S(1)} %collective-permute-done.refs_4_), channel_id=1, source_target_pairs={{0,4},{2,6},{4,0},{6,2},{8,12},{10,14},{12,8},{14,10},{16,20},{18,... | collective-permute-start | bytes 1572872 | tf_op jit(solution)/shard_map/ppermute | solution.py:71
  22.7 1.3 %collective-permute-start.6 = (f32[1,4,128]{2,1,0:T(4,128)S(1)}, f32[1,4,128]{2,1,0:T(4,128)S(1)}, u32[]{:S(2)}, u32[]{:S(2)}) collective-permute-start(f32[1,4,128]{2,1,0:T(4,128)S(1)} %add_bitcast_fusion), channel_id=1, source_target_pairs={{0,2},{2,0},{4,6},{6,4},{8,10},{10,8},{12,14},{14,12},{16,18},{18,... | collective-permute-start | bytes 6152 | tf_op jit(solution)/shard_map/ppermute | solution.py:28
  24.0 12.9 %collective-permute-start.7 = (f32[2,4,128]{2,1,0:T(4,128)S(1)}, f32[2,4,128]{2,1,0:T(4,128)S(1)}, u32[]{:S(2)}, u32[]{:S(2)}) collective-permute-start(f32[2,4,128]{2,1,0:T(4,128)S(1)} %broadcast_select_fusion.4), channel_id=1, source_target_pairs={{0,4},{2,6},{4,0},{6,2},{8,12},{10,14},{12,8},{14,10},{16,20},{18,... | collective-permute-start | bytes 12296 | tf_op jit(solution)/shard_map/ppermute | solution.py:28
  25.7 23.7 %collective-permute-start.10 = (bf16[128,2048]{1,0:T(8,128)(2,1)S(1)}, bf16[128,2048]{1,0:T(8,128)(2,1)S(1)}, u32[]{:S(2)}, u32[]{:S(2)}) collective-permute-start(bf16[128,2048]{1,0:T(8,128)(2,1)S(1)} %collective-permute-done.3.refs_7_), channel_id=1, source_target_pairs={{0,16},{2,10},{4,20},{6,14},{8,0},{10,26},{12,4},{14,30},{16,24},{... | collective-permute-start | bytes 1572872 | tf_op jit(solution)/shard_map/ppermute | solution.py:71
  27.7 21.7 %collective-permute-start.11 = (bf16[128,2048]{1,0:T(8,128)(2,1)S(1)}, bf16[128,2048]{1,0:T(8,128)(2,1)S(1)}, u32[]{:S(2)}, u32[]{:S(2)}) collective-permute-start(bf16[128,2048]{1,0:T(8,128)(2,1)S(1)} %collective-permute-done.3.refs_7_), channel_id=1, source_target_pairs={{0,4},{2,6},{4,0},{6,2},{8,12},{10,14},{12,8},{14,10},{16,20},{18,... | collective-permute-start | bytes 1572872 | tf_op jit(solution)/shard_map/ppermute | solution.py:71
  42.7 6.7 %collective-permute-start.12 = (f32[4,4,128]{2,0,1:T(4,128)S(1)}, f32[4,4,128]{2,0,1:T(4,128)S(1)}, u32[]{:S(2)}, u32[]{:S(2)}) collective-permute-start(f32[4,4,128]{2,0,1:T(4,128)S(1)} %copy_select_fusion), channel_id=1, source_target_pairs={{0,8},{2,10},{4,12},{6,14},{8,0},{10,2},{12,4},{14,6},{16,24},{18,... | collective-permute-start | bytes 24584 | tf_op jit(solution)/shard_map/ppermute | solution.py:28
  42.7 24.0 %collective-permute-start.8 = (bf16[128,2048]{1,0:T(8,128)(2,1)S(1)}, bf16[128,2048]{1,0:T(8,128)(2,1)S(1)}, u32[]{:S(2)}, u32[]{:S(2)}) collective-permute-start(bf16[128,2048]{1,0:T(8,128)(2,1)S(1)} %collective-permute-done.1.refs_8_), channel_id=1, source_target_pairs={{0,8},{2,18},{4,12},{6,22},{8,24},{10,2},{12,28},{14,6},{16,0},{18... | collective-permute-start | bytes 1572872 | tf_op jit(solution)/shard_map/ppermute | solution.py:71
  44.7 21.9 %collective-permute-start.9 = (bf16[128,2048]{1,0:T(8,128)(2,1)S(1)}, bf16[128,2048]{1,0:T(8,128)(2,1)S(1)}, u32[]{:S(2)}, u32[]{:S(2)}) collective-permute-start(bf16[128,2048]{1,0:T(8,128)(2,1)S(1)} %collective-permute-done.1.refs_8_), channel_id=1, source_target_pairs={{0,4},{2,6},{4,0},{6,2},{8,12},{10,14},{12,8},{14,10},{16,20},{18,... | collective-permute-start | bytes 1572872 | tf_op jit(solution)/shard_map/ppermute | solution.py:71
  49.4 17.3 %collective-permute-start.13 = (f32[8,4,128]{2,0,1:T(8,128)S(1)}, f32[8,4,128]{2,0,1:T(8,128)S(1)}, u32[]{:S(2)}, u32[]{:S(2)}) collective-permute-start(f32[8,4,128]{2,0,1:T(8,128)S(1)} %pad_maximum_fusion.1), channel_id=1, source_target_pairs={{0,16},{2,18},{4,20},{6,22},{8,24},{10,26},{12,28},{14,30},{16,0},... | collective-permute-start | bytes 49160 | tf_op jit(solution)/shard_map/ppermute | solution.py:28
  50.3 32.5 %collective-permute-start.17 = (bf16[128,2048]{1,0:T(8,128)(2,1)S(1)}, bf16[128,2048]{1,0:T(8,128)(2,1)S(1)}, u32[]{:S(2)}, u32[]{:S(2)}) collective-permute-start(bf16[128,2048]{1,0:T(8,128)(2,1)S(1)} %collective-permute-done.10.refs_11_), channel_id=1, source_target_pairs={{0,16},{2,10},{4,20},{6,14},{8,0},{10,26},{12,4},{14,30},{16,24},{... | collective-permute-start | bytes 1572872 | tf_op jit(solution)/shard_map/ppermute | solution.py:71
  52.4 30.4 %collective-permute-start.18 = (bf16[128,2048]{1,0:T(8,128)(2,1)S(1)}, bf16[128,2048]{1,0:T(8,128)(2,1)S(1)}, u32[]{:S(2)}, u32[]{:S(2)}) collective-permute-start(bf16[128,2048]{1,0:T(8,128)(2,1)S(1)} %collective-permute-done.10.refs_11_), channel_id=1, source_target_pairs={{0,4},{2,6},{4,0},{6,2},{8,12},{10,14},{12,8},{14,10},{16,20},{18,... | collective-permute-start | bytes 1572872 | tf_op jit(solution)/shard_map/ppermute | solution.py:71
  66.7 19.0 %collective-permute-start.14 = (bf16[128,2048]{1,0:T(8,128)(2,1)S(1)}, bf16[128,2048]{1,0:T(8,128)(2,1)S(1)}, u32[]{:S(2)}, u32[]{:S(2)}) collective-permute-start(bf16[128,2048]{1,0:T(8,128)(2,1)S(1)} %collective-permute-done.8.refs_12_), channel_id=1, source_target_pairs={{0,8},{2,18},{4,12},{6,22},{8,24},{10,2},{12,28},{14,6},{16,0},{18... | collective-permute-start | bytes 1572872 | tf_op jit(solution)/shard_map/ppermute | solution.py:71
  66.8 18.9 %collective-permute-start.15 = (bf16[128,2048]{1,0:T(8,128)(2,1)S(1)}, bf16[128,2048]{1,0:T(8,128)(2,1)S(1)}, u32[]{:S(2)}, u32[]{:S(2)}) collective-permute-start(bf16[128,2048]{1,0:T(8,128)(2,1)S(1)} %collective-permute-done.8.refs_12_), channel_id=1, source_target_pairs={{0,4},{2,6},{4,0},{6,2},{8,12},{10,14},{12,8},{14,10},{16,20},{18,... | collective-permute-start | bytes 1572872 | tf_op jit(solution)/shard_map/ppermute | solution.py:71
  69.3 16.4 %collective-permute-start.16 = (bf16[896,2048]{1,0:T(8,128)(2,1)}, bf16[896,2048]{1,0:T(8,128)(2,1)S(1)}, u32[]{:S(2)}, u32[]{:S(2)}) collective-permute-start(bf16[896,2048]{1,0:T(8,128)(2,1)} %copy-done.4), channel_id=1, source_target_pairs={{0,2},{2,0},{4,6},{6,4},{8,10},{10,8},{12,14},{14,12},{16,18},{18,... | collective-permute-start | bytes 11010056 | tf_op jit(solution)/shard_map/ppermute | solution.py:71
  69.4 2.0 %copy-start.2 = (bf16[896,2048]{1,0:T(8,128)(2,1)S(1)}, bf16[896,2048]{1,0:T(8,128)(2,1)}, u32[]{:S(2)}) copy-start(bf16[896,2048]{1,0:T(8,128)(2,1)} %copy-done.1) | copy-start | bytes 11010052
  82.8 14.8 %collective-permute-start.19 = (bf16[128,2048]{1,0:T(8,128)(2,1)S(1)}, bf16[128,2048]{1,0:T(8,128)(2,1)S(1)}, u32[]{:S(2)}, u32[]{:S(2)}) collective-permute-start(bf16[128,2048]{1,0:T(8,128)(2,1)S(1)} %collective-permute-done.18.refs_3_), channel_id=1, source_target_pairs={{0,16},{2,10},{4,20},{6,14},{8,0},{10,26},{12,4},{14,30},{16,24},{... | collective-permute-start | bytes 1572872 | tf_op jit(solution)/shard_map/ppermute | solution.py:71
  85.7 12.9 %collective-permute-start.20 = (bf16[128,2048]{1,0:T(8,128)(2,1)S(1)}, bf16[128,2048]{1,0:T(8,128)(2,1)S(1)}, u32[]{:S(2)}, u32[]{:S(2)}) collective-permute-start(bf16[128,2048]{1,0:T(8,128)(2,1)S(1)} %collective-permute-done.14.refs_6_), channel_id=1, source_target_pairs={{0,4},{2,6},{4,0},{6,2},{8,12},{10,14},{12,8},{14,10},{16,20},{18,... | collective-permute-start | bytes 1572872 | tf_op jit(solution)/shard_map/ppermute | solution.py:71
  98.6 4.0 %copy-start.3 = (bf16[896,2048]{1,0:T(8,128)(2,1)S(1)}, bf16[896,2048]{1,0:T(8,128)(2,1)}, u32[]{:S(2)}) copy-start(bf16[896,2048]{1,0:T(8,128)(2,1)} %copy-done.1) | copy-start | bytes 11010052
  101.9 7.1 %collective-permute-start.22 = (bf16[896,2048]{1,0:T(8,128)(2,1)S(1)}, bf16[896,2048]{1,0:T(8,128)(2,1)S(1)}, u32[]{:S(2)}, u32[]{:S(2)}) collective-permute-start(bf16[896,2048]{1,0:T(8,128)(2,1)S(1)} %get-tuple-element.99), channel_id=1, source_target_pairs={{0,2},{2,0},{4,6},{6,4},{8,10},{10,8},{12,14},{14,12},{16,18},{18,... | collective-permute-start | bytes 11010056 | tf_op jit(solution)/shard_map/ppermute | solution.py:366
  102.0 6.4 %collective-permute-start.21 = (f32[2048]{0:T(1024)S(1)}, f32[2048]{0:T(1024)S(1)}, u32[]{:S(2)}, u32[]{:S(2)}) collective-permute-start(f32[2048]{0:T(1024)S(1)} %bitcast.38), channel_id=1, source_target_pairs={{0,2},{2,0},{4,6},{6,4},{8,10},{10,8},{12,14},{14,12},{16,18},{18,... | collective-permute-start | bytes 24584 | tf_op jit(solution)/shard_map/ppermute | solution.py:366
  102.5 5.9 %copy-start.5 = (bf16[4096]{0:T(1024)(128)(2,1)S(1)}, bf16[4096]{0:T(1024)(128)(2,1)}, u32[]{:S(2)}) copy-start(bf16[4096]{0:T(1024)(128)(2,1)} %param.10) | copy-start | bytes 24580

commit v8 on v7

--- a/solution.py
+++ b/solution.py
@@ -20,16 +20,15 @@
     return x
 
 
-def butterfly_step(x, axis, low):
-    count = lax.axis_size(axis)
-    step = x.shape[0]
-    if step >= count:
-        return x
-    other = lax.ppermute(x, axis, [(i, i ^ step) for i in range(count)])
-    if step > 2:
-        return jnp.concatenate([jnp.where(low[step], x, other), jnp.where(low[step], other, x)])
-    first = lax.broadcasted_iota(jnp.int32, (2, *x.shape), 0) == 0
-    return jnp.where(first == low[step], x[None], other[None]).reshape(2 * step, *x.shape[1:])
+def butterfly_send(x, axis):
+    return lax.ppermute(x, axis, [(i, i ^ x.shape[0]) for i in range(lax.axis_size(axis))])
+
+
+def butterfly_merge(x, other, low):
+    low = low[x.shape[0]]
+    if low.ndim:
+        return jnp.where(low[:, None, None], jnp.concatenate([x, x]), jnp.concatenate([other, other]))
+    return jnp.concatenate([jnp.where(low, x, other), jnp.where(low, other, x)])
 
 
 class Paths:
@@ -89,8 +88,16 @@
     names = list(scalars)
     low = lambda: {1 << n: have["low %d" % n] for n in range(paths.count.bit_length() - 1)}
 
+    def facts_send():
+        have["other facts"] = butterfly_send(have["facts"], "seq")
+
+    def facts_merge():
+        have["facts"] = butterfly_merge(have["facts"], have["other facts"], low())
+
     def facts_step():
-        have["facts"] = butterfly_step(have["facts"], "seq", low())
+        if have["facts"].shape[0] < paths.count:
+            facts_send()
+            facts_merge()
 
     f.event([], [((1, 0, 0), (0, 0, 0), ring[0]), ((0, 1, 0), (0, 0, 0), across), ((0, 0, 1), "away", core)])
     f.event(
@@ -98,23 +105,24 @@
         [((1, 0, 1), (0, 0, 1), ring[1]), ((0, 1, 1), (0, 0, 1), across)],
     )
     have["facts"] = butterfly_sum(own_facts(have["stream"]), "tp")[None]
-    have["own picks"], have["away picks"] = pick_both()
     f.event(
-        [(1, 0, 0), (0, 1, 0), "facts", "own picks", "away picks"],
+        [(1, 0, 0), (0, 1, 0), "facts"],
         [((2, 0, 0), (1, 0, 0), ring[0]), ((1, 1, 0), (1, 0, 0), across)],
     )
+    have["own picks"], have["away picks"] = pick_both()
     facts_step()
-    facts_step()
-    f.event([(1, 0, 1), (0, 1, 1), "facts"], [((2, 0, 1), (1, 0, 1), ring[1]), ((1, 1, 1), (1, 0, 1), across)])
+    facts_send()
+    f.event([(1, 0, 1), (0, 1, 1), "facts", "other facts", "own picks", "away picks"], [((2, 0, 1), (1, 0, 1), ring[1]), ((1, 1, 1), (1, 0, 1), across)])
+    facts_merge()
     for k in range(2, m):
         for kind in range(2):
             facts_step()
             if k < m - 1:
                 sends = [((k + 1, 0, kind), (k, 0, kind), ring[kind]), ((k, 1, kind), (k, 0, kind), across)]
             elif kind == 0:
-                sends = [((k, 1, kind), (k - 1, 1, kind), ring[kind])]
+                sends = []
             else:
-                sends = [((k, 1, kind), (k, 0, kind), across)]
+                sends = [((k, 1, 0), (k - 1, 1, 0), ring[0]), ((k, 1, 1), (k, 0, 1), across)]
             waits = [(k, 0, kind), (k - 1, 1, kind), "facts"]
             if k == m - 2 and kind == 1:
                 sends.append(("other picks", "away picks", core))
@@ -130,7 +138,8 @@
     return have
 
 
-PARAMS = pltpu.CompilerParams(vmem_limit_bytes=16 * 1024 * 1024)
+def params(tokens):
+    return pltpu.CompilerParams(vmem_limit_bytes=(16 if tokens <= 4096 else 40) * 1024 * 1024)
 
 
 def cost(units, k, width, extra):
@@ -147,7 +156,8 @@
             out[:, b * tok : (b + 1) * tok] = hidden[:, columns]
 
 
-def pick(hidden, owners, orders, tok):
+def pick(hidden, owners, tok):
+    orders = 2
     units, tokens = hidden.shape
     rows = next(r for r in range(128, 0, -16) if units % r == 0)
     spec = pl.BlockSpec((rows, tokens), lambda i, *_: (i, 0))
@@ -156,10 +166,10 @@
         grid_spec=pltpu.PrefetchScalarGridSpec(
             num_scalar_prefetch=1, grid=(units // rows,), in_specs=[spec], out_specs=[spec] * orders
         ),
-        out_shape=[jax.ShapeDtypeStruct(hidden.shape, hidden.dtype)] * orders,
-        compiler_params=PARAMS,
-        cost_estimate=cost(units, 0, 0, 2 * (1 + orders) * units * tokens),
-    )(owners, hidden)
+        out_shape=[pltpu.VMEM(hidden.shape, hidden.dtype), pltpu.HBM(hidden.shape, hidden.dtype)],
+        compiler_params=params(tokens),
+        cost_estimate=cost(0, 0, 0, 1),
+    )(owners, pltpu.with_memory_space_constraint(hidden, pltpu.HBM))
 
 
 def spread(tok, owners, first, coefs, weights, pulls):
@@ -174,7 +184,7 @@
     for b in range(len(blocks)):
         rows = slice(b * tok, (b + 1) * tok)
         for at in range(0, chunk, 128):
-            lanes = pl.ds(pl.multiple_of(start + at, 128), 128)
+            lanes = slice(start + at, start + at + 128)
             stream_f = blocks[b][:, lanes].astype(jnp.float32)
             weight = weights[rows, :]
             dstream[rows, lanes] = (weight * head[:, lanes] - pulls[rows, :] * stream_f).astype(jnp.bfloat16)
@@ -200,7 +210,7 @@
     steps = half // chunk
     base = pl.multiple_of(where[0] * half, half)
 
-    columns = lambda c: pl.ds(pl.multiple_of(c * chunk, chunk), chunk)
+    columns = lambda c: pl.ds(c * chunk, chunk)
 
     def put_out(c):
         there = pl.ds(pl.multiple_of(base + c * chunk, chunk), chunk)
@@ -210,11 +220,14 @@
         parts[...] = jnp.zeros_like(parts)
         spread(tok, owners, first, coefs, weights, pulls)
 
-    def step(c, carry):
-        if count:
+    def form_chunk(c):
+        if count and c < steps:
             form(tok, owners, first, weights, pulls, head, blocks, dstream, parts, c * chunk, chunk)
 
-        factors = ([dstream] if count else []) + given
+    factors = ([dstream] if count else []) + given
+    form_chunk(0)
+    for c in range(steps):
+        form_chunk(c + 1)
         here = total[0][:, columns(c)] if added else None
         at = first * tok
         for factor in factors:
@@ -225,9 +238,6 @@
         out_v[:, columns(c)] = here.astype(out_v.dtype)
         if wide:
             put_out(c).start()
-        return carry
-
-    lax.fori_loop(0, steps, step, 0)
     if count:
         if other_parts:
             parts_out[...] = sum([p[...] for p in other_parts], parts[...]).sum(axis=0)
@@ -280,7 +290,7 @@
             scratch_shapes=scratch + [pltpu.SemaphoreType.DMA(shape) for shape in sems],
         ),
         out_shape=out_shape,
-        compiler_params=PARAMS,
+        compiler_params=params(tokens),
         cost_estimate=cost(units, k * (1 if added or given else 10), half, 6 * units * half),
     )(
         owners,
@@ -329,7 +339,7 @@
         ),
         out_shape=jax.ShapeDtypeStruct(whole.shape, whole.dtype),
         input_output_aliases={2: 0},
-        compiler_params=PARAMS,
+        compiler_params=params(0),
         cost_estimate=cost(0, 0, 0, 4 * units * width),
     )(where, part, whole)
 
@@ -410,9 +420,11 @@
 
         where = mine[None].astype(jnp.int32)
         scalars = {"core": mine, "me": me, "first core": mine == 0, "where": where, "elsewhere": 1 - where}
-        scalars.update({"low %d" % n: (me >> n) % 2 == 0 for n in range(shards.bit_length() - 1)})
+        for n in range(shards.bit_length() - 1):
+            low = (me >> n) % 2 == 0
+            scalars["low %d" % n] = low if n > 1 else (jnp.arange(2 << n) < 1 << n) == low
         scalars["owners"] = owners
-        have = run_plan(stream, scalars, own_facts, paths, lambda: pick(hidden, owners, 2, tok), early_own, early_other)
+        have = run_plan(stream, scalars, own_facts, paths, lambda: pick(hidden, owners, tok), early_own, early_other)
         out, dstream, grad_head = product(
             have["owners"],
             0,

time: 112 us -> 122 us (1.089)
  the two profiles are of different devices: /device:TPU:0 before, /device:TPU:11 now
where the time goes in v8:
time: 122 us
  starting transfers between devices  42.1 us (35%)
  waiting for transfers between devices  33 us (27%)
  Pallas kernels  32.3 us (26%)
  local copies, waits for them, and re-layouts  7.08 us (6%)
  other arithmetic  6.12 us (5%)
    ppermute x16, starting transfers between devices, event(): self.have[name] = lax.ppermute(self.have[source], 'seq', pairs)  35 us
    pallas_call x4, Pallas kernels, product(): pl.pallas_call(functools.partial(product_kernel, tok, count, first, len(g...  22.8 us
    ppermute x16, waiting for transfers between devices, event(): self.have[name] = lax.ppermute(self.have[source], 'seq', pairs)  21.2 us
    ppermute x4, waiting for transfers between devices, butterfly_send(): lax.ppermute(x, axis, [(i, i ^ x.shape[0]) for i in range(lax.axis_size(a...  9.53 us
    pallas_call x1, Pallas kernels, pick(): pl.pallas_call(functools.partial(pick_kernel, tok), grid_spec=pltpu.Prefe...  7.39 us
    ppermute x4, starting transfers between devices, butterfly_send(): lax.ppermute(x, axis, [(i, i ^ x.shape[0]) for i in range(lax.axis_size(a...  5.87 us
    unnamed x6, local copies, waits for them, and re-layouts  4.84 us
  transfers between devices with their start and end apart: 23, of which 8 were waited for; matrix products, arithmetic and copies ran while one was open for 6% of the time, Pallas kernels for 23%

profile of v8, /device:TPU:11, one launch (start us, length us, event | category | flops | bytes accessed | tf_op | source)
XLA Modules:
  0.0 121.7 jit_solution(13807498421848282911)
XLA Ops:
  0.7 1.3 %constant_dynamic-slice_fusion.1 = (bf16[128,2048]{1,0:T(8,128)(2,1)S(1)}, bf16[128,2048]{1,0:T(8,128)(2,1)S(1)}) fusion(bf16[128,4096]{1,0:T(8,128)(2,1)} %param.8, s32[]{:T(128)S(6)} %select_n.133, s32[]{:T(128)S(6)} %select_n.132), kind=kLoop, calls=%fused_computation.45 | loop fusion | bytes 2097160 | tf_op jit(solution)/shard_map/dynamic_slice | solution.py:83
  1.9 2.4 %collective-permute-start.3 = (bf16[128,2048]{1,0:T(8,128)(2,1)S(1)}, bf16[128,2048]{1,0:T(8,128)(2,1)S(1)}, u32[]{:S(2)}, u32[]{:S(2)}) collective-permute-start(bf16[128,2048]{1,0:T(8,128)(2,1)S(1)} %get-tuple-element.59.refs_3_), channel_id=1, source_target_pairs={{0,16},{2,10},{4,20},{6,14},{8,0},{10,26},{12,4},{14,30},{16,24},{... | collective-permute-start | bytes 1572872 | tf_op jit(solution)/shard_map/ppermute | solution.py:70
  4.3 1.2 %collective-permute-start.4 = (bf16[128,2048]{1,0:T(8,128)(2,1)S(1)}, bf16[128,2048]{1,0:T(8,128)(2,1)S(1)}, u32[]{:S(2)}, u32[]{:S(2)}) collective-permute-start(bf16[128,2048]{1,0:T(8,128)(2,1)S(1)} %get-tuple-element.59.refs_3_), channel_id=1, source_target_pairs={{0,4},{2,6},{4,0},{6,2},{8,12},{10,14},{12,8},{14,10},{16,20},{18,... | collective-permute-start | bytes 1572872 | tf_op jit(solution)/shard_map/ppermute | solution.py:70
  5.6 0.7 fusion.6.owners
  6.3 0.7 multiply_bitcast_fusion
  7.0 0.7 convert_multiply_fusion.3
  7.7 0.0 collective-permute-done.refs_4_
  7.7 1.7 %fusion = (f32[128]{0:T(128)S(1)}, f32[128]{0:T(128)S(1)}) fusion(bf16[128,4096]{1,0:T(8,128)(2,1)} %param.8, f32[4096]{0:T(1024)S(1)} %convert_multiply_fusion.3), kind=kLoop, calls=%fused_computation.2 | loop fusion | flops 2621184 | bytes 1065984 | tf_op jit(solution)/shard_map/reduce_sum | solution.py:389
  9.4 0.3 collective-permute-start.5
  9.7 1.4 %collective-permute-start.1 = (bf16[128,2048]{1,0:T(8,128)(2,1)S(1)}, bf16[128,2048]{1,0:T(8,128)(2,1)S(1)}, u32[]{:S(2)}, u32[]{:S(2)}) collective-permute-start(bf16[128,2048]{1,0:T(8,128)(2,1)S(1)} %collective-permute-done.refs_4_), channel_id=1, source_target_pairs={{0,8},{2,18},{4,12},{6,22},{8,24},{10,2},{12,28},{14,6},{16,0},{18... | collective-permute-start | bytes 1572872 | tf_op jit(solution)/shard_map/ppermute | solution.py:70
  11.1 0.2 collective-permute-start.2
  11.3 0.9 collective-permute-done.5
  12.2 9.2 %collective-permute-done.3.refs_7_ = bf16[128,2048]{1,0:T(8,128)(2,1)S(1)} collective-permute-done((bf16[128,2048]{1,0:T(8,128)(2,1)S(1)}, bf16[128,2048]{1,0:T(8,128)(2,1)S(1)}, u32[]{:S(2)}, u32[]{:S(2)}) %collective-permute-start.3) | collective-permute-done | bytes 524320 | tf_op jit(solution)/shard_map/ppermute | solution.py:70
  21.4 0.0 collective-permute-done.4.refs_5_
  21.4 0.0 collective-permute-start.6
  21.4 1.1 collective-permute-done.6
  22.6 0.1 maximum_select_fusion.2
  22.6 2.3 %collective-permute-start.7 = (f32[2,4,128]{2,0,1:T(2,128)S(1)}, f32[2,4,128]{2,0,1:T(2,128)S(1)}, u32[]{:S(2)}, u32[]{:S(2)}) collective-permute-start(f32[2,4,128]{2,0,1:T(2,128)S(1)} %maximum_select_fusion.2), channel_id=1, source_target_pairs={{0,4},{2,6},{4,0},{6,2},{8,12},{10,14},{12,8},{14,10},{16,20},{18,... | collective-permute-start | bytes 12296 | tf_op jit(solution)/shard_map/ppermute | solution.py:24
  24.9 7.4 %shard_map.111 = (bf16[896,2048]{1,0:T(8,128)(2,1)S(1)}, bf16[896,2048]{1,0:T(8,128)(2,1)}) custom-call(s32[32]{0:T(128)S(1)} %fusion.6.owners, bf16[896,2048]{1,0:T(8,128)(2,1)} %hidden.1), custom_call_target="tpu_custom_call" | custom-call | bytes 1 | tf_op jit(solution)/shard_map/pallas_call | solution.py:164
  32.3 3.6 %collective-permute-start.10 = (bf16[128,2048]{1,0:T(8,128)(2,1)S(1)}, bf16[128,2048]{1,0:T(8,128)(2,1)S(1)}, u32[]{:S(2)}, u32[]{:S(2)}) collective-permute-start(bf16[128,2048]{1,0:T(8,128)(2,1)S(1)} %collective-permute-done.3.refs_7_), channel_id=1, source_target_pairs={{0,16},{2,10},{4,20},{6,14},{8,0},{10,26},{12,4},{14,30},{16,24},{... | collective-permute-start | bytes 1572872 | tf_op jit(solution)/shard_map/ppermute | solution.py:70
  35.9 0.0 collective-permute-start.11
  35.9 0.1 maximum_select_fusion.1
  36.0 0.0 collective-permute-start.12
  36.1 1.5 %collective-permute-start.8 = (bf16[128,2048]{1,0:T(8,128)(2,1)S(1)}, bf16[128,2048]{1,0:T(8,128)(2,1)S(1)}, u32[]{:S(2)}, u32[]{:S(2)}) collective-permute-start(bf16[128,2048]{1,0:T(8,128)(2,1)S(1)} %collective-permute-done.1.refs_8_), channel_id=1, source_target_pairs={{0,8},{2,18},{4,12},{6,22},{8,24},{10,2},{12,28},{14,6},{16,0},{18... | collective-permute-start | bytes 1572872 | tf_op jit(solution)/shard_map/ppermute | solution.py:70
  37.6 1.4 %collective-permute-start.9 = (bf16[128,2048]{1,0:T(8,128)(2,1)S(1)}, bf16[128,2048]{1,0:T(8,128)(2,1)S(1)}, u32[]{:S(2)}, u32[]{:S(2)}) collective-permute-start(bf16[128,2048]{1,0:T(8,128)(2,1)S(1)} %collective-permute-done.1.refs_8_), channel_id=1, source_target_pairs={{0,4},{2,6},{4,0},{6,2},{8,12},{10,14},{12,8},{14,10},{16,20},{18,... | collective-permute-start | bytes 1572872 | tf_op jit(solution)/shard_map/ppermute | solution.py:70
  39.0 7.2 %collective-permute-done.12 = f32[4,4,128]{2,0,1:T(4,128)S(1)} collective-permute-done((f32[4,4,128]{2,0,1:T(4,128)S(1)}, f32[4,4,128]{2,0,1:T(4,128)S(1)}, u32[]{:S(2)}, u32[]{:S(2)}) %collective-permute-start.12) | collective-permute-done | bytes 8224 | tf_op jit(solution)/shard_map/ppermute | solution.py:24
  46.3 9.1 %collective-permute-done.10.refs_11_ = bf16[128,2048]{1,0:T(8,128)(2,1)S(1)} collective-permute-done((bf16[128,2048]{1,0:T(8,128)(2,1)S(1)}, bf16[128,2048]{1,0:T(8,128)(2,1)S(1)}, u32[]{:S(2)}, u32[]{:S(2)}) %collective-permute-start.10) | collective-permute-done | bytes 524320 | tf_op jit(solution)/shard_map/ppermute | solution.py:70
  55.3 0.0 collective-permute-done.11.refs_9_
  55.3 3.6 %collective-permute-start.13 = (f32[8,4,128]{2,0,1:T(8,128)S(1)}, f32[8,4,128]{2,0,1:T(8,128)S(1)}, u32[]{:S(2)}, u32[]{:S(2)}) collective-permute-start(f32[8,4,128]{2,0,1:T(8,128)S(1)} %pad_maximum_fusion.1), channel_id=1, source_target_pairs={{0,16},{2,18},{4,20},{6,22},{8,24},{10,26},{12,28},{14,30},{16,0},... | collective-permute-start | bytes 49160 | tf_op jit(solution)/shard_map/ppermute | solution.py:24
  58.9 0.1 collective-permute-start.17
  59.0 0.0 collective-permute-start.18
  59.0 1.1 collective-permute-done.13
  60.2 0.0 collective-permute-done.8.refs_12_
  60.2 1.1 collective-permute-start.14
  61.3 0.7 collective-permute-start.15
  62.0 0.1 fusion.10
  62.1 0.3 select_reduce_fusion.1
  62.4 0.1 broadcast_compare_fusion
  62.5 0.1 select_reduce_fusion.5
  62.6 0.7 select_reduce_fusion
  63.3 0.1 slice_reduce_fusion
  63.4 0.1 select_reduce_fusion.2
  63.5 0.1 select_reduce_fusion.4
  63.6 0.1 broadcast_in_dim.160
  63.7 0.1 eq.106
  63.8 21.1 %collective-permute-start.16 = (bf16[896,2048]{1,0:T(8,128)(2,1)}, bf16[896,2048]{1,0:T(8,128)(2,1)S(1)}, u32[]{:S(2)}, u32[]{:S(2)}) collective-permute-start(bf16[896,2048]{1,0:T(8,128)(2,1)} %get-tuple-element.74), channel_id=1, source_target_pairs={{0,2},{2,0},{4,6},{6,4},{8,10},{10,8},{12,14},{14,12},{16,18},{18,... | collective-permute-start | bytes 11010056 | tf_op jit(solution)/shard_map/ppermute | solution.py:70
  84.9 7.6 %shard_map.112 = (f32[896,2048]{1,0:T(8,128)S(1)}, bf16[1280,2048]{1,0:T(8,128)(2,1)S(1)}, f32[16,1,2048]{2,1,0:T(1,128)S(1)}) custom-call(s32[32]{0:T(128)S(1)} %fusion.6.owners, s32[1]{0:T(128)} %constant.69.clone.1.where, bf16[896,2048]{1,0:T(8,128)(2,1)S(1)} %get-tuple-element.76.refs_0_, f32[8,2048]{1,0:T(8,128)S(1)} %select_maximum_fusion.refs_1_, ...), custom_call_target="tpu_custom_call" | custom-call | flops 46976204800 | bytes 86376448 | tf_op jit(solution)/shard_map/pallas_call | solution.py:283
  92.5 0.0 copy-start
  92.6 2.3 %copy-done = bf16[1280,2048]{1,0:T(8,128)(2,1)} copy-done((bf16[1280,2048]{1,0:T(8,128)(2,1)}, bf16[1280,2048]{1,0:T(8,128)(2,1)S(1)}, u32[]{:S(2)}) %copy-start) | copy-done | bytes 5242904
  94.9 0.6 select_reduce_fusion.3
  95.5 0.0 collective-permute-done.17.refs_5_
  95.5 0.2 collective-permute-start.19
  95.8 0.1 collective-permute-start.20
  95.9 0.0 copy-start.1
  95.9 2.5 %copy-done.1 = bf16[1280,2048]{1,0:T(8,128)(2,1)S(1)} copy-done((bf16[1280,2048]{1,0:T(8,128)(2,1)S(1)}, bf16[1280,2048]{1,0:T(8,128)(2,1)}, u32[]{:S(2)}) %copy-start.1) | copy-done | bytes 5242904
  98.4 8.1 %shard_map.113 = (f32[896,2048]{1,0:T(8,128)S(1)}, bf16[512,2048]{1,0:T(8,128)(2,1)S(1)}, f32[16,1,2048]{2,1,0:T(1,128)S(1)}) custom-call(s32[32]{0:T(128)S(1)} %fusion.6.owners, s32[1]{0:T(128)} %constant.69.clone.1.where, bf16[896,2048]{1,0:T(8,128)(2,1)S(1)} %collective-permute-done.16.refs_0_, f32[8,2048]{1,0:T(8,128)S(1)} %select_maximum_fusion.refs_1_, ...), custom_call_target="tpu_custom_call" | custom-call | flops 6576668672 | bytes 21561344 | tf_op jit(solution)/shard_map/pallas_call | solution.py:283
  106.5 2.9 %collective-permute-done.20.refs_4_ = bf16[128,2048]{1,0:T(8,128)(2,1)S(1)} collective-permute-done((bf16[128,2048]{1,0:T(8,128)(2,1)S(1)}, bf16[128,2048]{1,0:T(8,128)(2,1)S(1)}, u32[]{:S(2)}, u32[]{:S(2)}) %collective-permute-start.20) | collective-permute-done | bytes 524320 | tf_op jit(solution)/shard_map/ppermute | solution.py:70
  109.4 2.4 %shard_map.114 = (bf16[896,2048]{1,0:T(8,128)(2,1)S(1)}, bf16[256,2048]{1,0:T(8,128)(2,1)S(1)}, f32[1,2048]{1,0:T(1,128)S(1)}) custom-call(s32[32]{0:T(128)S(1)} %fusion.6.owners, s32[1]{0:T(128)} %constant.69.clone.1.where, bf16[896,2048]{1,0:T(8,128)(2,1)S(1)} %collective-permute-done.16.refs_0_, f32[8,2048]{1,0:T(8,128)S(1)} %select_maximum_fusion.refs_1_, ...), custom_call_target="tpu_custom_call" | custom-call | flops 939524096 | bytes 12517376 | tf_op jit(solution)/shard_map/pallas_call | solution.py:283
  111.8 0.9 collective-permute-start.22
  112.7 0.1 collective-permute-start.21
  112.8 4.5 %shard_map.115.whole = bf16[896,4096]{1,0:T(8,128)(2,1)} custom-call(s32[32]{0:T(128)S(1)} %fusion.6.owners, s32[1]{0:T(128)} %bitcast.where, bf16[896,2048]{1,0:T(8,128)(2,1)S(1)} %get-tuple-element.76.refs_0_, bf16[256,2048]{1,0:T(8,128)(2,1)S(1)} %get-tuple-element.105.refs_1_, bf16[512,2048]{1,0:T(8,128)(2,1)S(1)} %get-tuple-element.106.refs_2_, ...), custom_call_target="tpu_custom_call" | custom-call | flops 2818572288 | bytes 15532032 | tf_op jit(solution)/shard_map/pallas_call | solution.py:283
  117.3 1.4 %collective-permute-done.21 = f32[2048]{0:T(1024)S(1)} collective-permute-done((f32[2048]{0:T(1024)S(1)}, f32[2048]{0:T(1024)S(1)}, u32[]{:S(2)}, u32[]{:S(2)}) %collective-permute-start.21) | collective-permute-done | bytes 8224 | tf_op jit(solution)/shard_map/ppermute | solution.py:376
  118.8 0.6 convert_multiply_fusion.2
  119.4 2.2 %shard_map.116 = bf16[896,4096]{1,0:T(8,128)(2,1)} custom-call(s32[1]{0:T(128)S(6)} %sub.26.where, bf16[896,2048]{1,0:T(8,128)(2,1)S(1)} %collective-permute-done.22.part, bf16[896,4096]{1,0:T(8,128)(2,1)} %shard_map.115.whole), custom_call_target="tpu_custom_call", output_to_operand_aliasing={{}: (2, {})} | custom-call | bytes 7340032 | tf_op jit(solution)/shard_map/pallas_call | solution.py:327
  (29 shorter events, 0.2 us)
Async XLA Ops:
  1.9 19.5 %collective-permute-start.3 = (bf16[128,2048]{1,0:T(8,128)(2,1)S(1)}, bf16[128,2048]{1,0:T(8,128)(2,1)S(1)}, u32[]{:S(2)}, u32[]{:S(2)}) collective-permute-start(bf16[128,2048]{1,0:T(8,128)(2,1)S(1)} %get-tuple-element.59.refs_3_), channel_id=1, source_target_pairs={{0,16},{2,10},{4,20},{6,14},{8,0},{10,26},{12,4},{14,30},{16,24},{... | collective-permute-start | bytes 1572872 | tf_op jit(solution)/shard_map/ppermute | solution.py:70
  4.3 17.1 %collective-permute-start.4 = (bf16[128,2048]{1,0:T(8,128)(2,1)S(1)}, bf16[128,2048]{1,0:T(8,128)(2,1)S(1)}, u32[]{:S(2)}, u32[]{:S(2)}) collective-permute-start(bf16[128,2048]{1,0:T(8,128)(2,1)S(1)} %get-tuple-element.59.refs_3_), channel_id=1, source_target_pairs={{0,4},{2,6},{4,0},{6,2},{8,12},{10,14},{12,8},{14,10},{16,20},{18,... | collective-permute-start | bytes 1572872 | tf_op jit(solution)/shard_map/ppermute | solution.py:70
  5.5 2.2 %collective-permute-start = (bf16[128,2048]{1,0:T(8,128)(2,1)S(1)}, bf16[128,2048]{1,0:T(8,128)(2,1)S(1)}, u32[]{:S(2)}, u32[]{:S(2)}) collective-permute-start(bf16[128,2048]{1,0:T(8,128)(2,1)S(1)} %get-tuple-element.56), channel_id=1, source_target_pairs={{0,2},{2,0},{4,6},{6,4},{8,10},{10,8},{12,14},{14,12},{16,18},{18,... | collective-permute-start | bytes 1572872 | tf_op jit(solution)/shard_map/ppermute | solution.py:70
  9.4 2.8 %collective-permute-start.5 = (f32[4,128]{1,0:T(4,128)S(1)}, f32[4,128]{1,0:T(4,128)S(1)}, u32[]{:S(2)}, u32[]{:S(2)}) collective-permute-start(f32[4,128]{1,0:T(4,128)S(1)} %pad_maximum_fusion.2), channel_id=1, source_target_pairs={{0,1},{1,0},{2,3},{3,2},{4,5},{5,4},{6,7},{7,6},{8,9},{9,8},{10,11... | collective-permute-start | bytes 6152 | tf_op jit(solution)/shard_map/ppermute | solution.py:18
  9.7 26.2 %collective-permute-start.1 = (bf16[128,2048]{1,0:T(8,128)(2,1)S(1)}, bf16[128,2048]{1,0:T(8,128)(2,1)S(1)}, u32[]{:S(2)}, u32[]{:S(2)}) collective-permute-start(bf16[128,2048]{1,0:T(8,128)(2,1)S(1)} %collective-permute-done.refs_4_), channel_id=1, source_target_pairs={{0,8},{2,18},{4,12},{6,22},{8,24},{10,2},{12,28},{14,6},{16,0},{18... | collective-permute-start | bytes 1572872 | tf_op jit(solution)/shard_map/ppermute | solution.py:70
  11.1 24.9 %collective-permute-start.2 = (bf16[128,2048]{1,0:T(8,128)(2,1)S(1)}, bf16[128,2048]{1,0:T(8,128)(2,1)S(1)}, u32[]{:S(2)}, u32[]{:S(2)}) collective-permute-start(bf16[128,2048]{1,0:T(8,128)(2,1)S(1)} %collective-permute-done.refs_4_), channel_id=1, source_target_pairs={{0,4},{2,6},{4,0},{6,2},{8,12},{10,14},{12,8},{14,10},{16,20},{18,... | collective-permute-start | bytes 1572872 | tf_op jit(solution)/shard_map/ppermute | solution.py:70
  21.4 1.2 collective-permute-start.6
  22.6 13.3 %collective-permute-start.7 = (f32[2,4,128]{2,0,1:T(2,128)S(1)}, f32[2,4,128]{2,0,1:T(2,128)S(1)}, u32[]{:S(2)}, u32[]{:S(2)}) collective-permute-start(f32[2,4,128]{2,0,1:T(2,128)S(1)} %maximum_select_fusion.2), channel_id=1, source_target_pairs={{0,4},{2,6},{4,0},{6,2},{8,12},{10,14},{12,8},{14,10},{16,20},{18,... | collective-permute-start | bytes 12296 | tf_op jit(solution)/shard_map/ppermute | solution.py:24
  32.3 23.0 %collective-permute-start.10 = (bf16[128,2048]{1,0:T(8,128)(2,1)S(1)}, bf16[128,2048]{1,0:T(8,128)(2,1)S(1)}, u32[]{:S(2)}, u32[]{:S(2)}) collective-permute-start(bf16[128,2048]{1,0:T(8,128)(2,1)S(1)} %collective-permute-done.3.refs_7_), channel_id=1, source_target_pairs={{0,16},{2,10},{4,20},{6,14},{8,0},{10,26},{12,4},{14,30},{16,24},{... | collective-permute-start | bytes 1572872 | tf_op jit(solution)/shard_map/ppermute | solution.py:70
  35.9 19.4 %collective-permute-start.11 = (bf16[128,2048]{1,0:T(8,128)(2,1)S(1)}, bf16[128,2048]{1,0:T(8,128)(2,1)S(1)}, u32[]{:S(2)}, u32[]{:S(2)}) collective-permute-start(bf16[128,2048]{1,0:T(8,128)(2,1)S(1)} %collective-permute-done.3.refs_7_), channel_id=1, source_target_pairs={{0,4},{2,6},{4,0},{6,2},{8,12},{10,14},{12,8},{14,10},{16,20},{18,... | collective-permute-start | bytes 1572872 | tf_op jit(solution)/shard_map/ppermute | solution.py:70
  36.0 10.2 %collective-permute-start.12 = (f32[4,4,128]{2,0,1:T(4,128)S(1)}, f32[4,4,128]{2,0,1:T(4,128)S(1)}, u32[]{:S(2)}, u32[]{:S(2)}) collective-permute-start(f32[4,4,128]{2,0,1:T(4,128)S(1)} %maximum_select_fusion.1), channel_id=1, source_target_pairs={{0,8},{2,10},{4,12},{6,14},{8,0},{10,2},{12,4},{14,6},{16,24},{18,... | collective-permute-start | bytes 24584 | tf_op jit(solution)/shard_map/ppermute | solution.py:24
  36.1 24.1 %collective-permute-start.8 = (bf16[128,2048]{1,0:T(8,128)(2,1)S(1)}, bf16[128,2048]{1,0:T(8,128)(2,1)S(1)}, u32[]{:S(2)}, u32[]{:S(2)}) collective-permute-start(bf16[128,2048]{1,0:T(8,128)(2,1)S(1)} %collective-permute-done.1.refs_8_), channel_id=1, source_target_pairs={{0,8},{2,18},{4,12},{6,22},{8,24},{10,2},{12,28},{14,6},{16,0},{18... | collective-permute-start | bytes 1572872 | tf_op jit(solution)/shard_map/ppermute | solution.py:70
  37.6 22.6 %collective-permute-start.9 = (bf16[128,2048]{1,0:T(8,128)(2,1)S(1)}, bf16[128,2048]{1,0:T(8,128)(2,1)S(1)}, u32[]{:S(2)}, u32[]{:S(2)}) collective-permute-start(bf16[128,2048]{1,0:T(8,128)(2,1)S(1)} %collective-permute-done.1.refs_8_), channel_id=1, source_target_pairs={{0,4},{2,6},{4,0},{6,2},{8,12},{10,14},{12,8},{14,10},{16,20},{18,... | collective-permute-start | bytes 1572872 | tf_op jit(solution)/shard_map/ppermute | solution.py:70
  55.3 4.8 %collective-permute-start.13 = (f32[8,4,128]{2,0,1:T(8,128)S(1)}, f32[8,4,128]{2,0,1:T(8,128)S(1)}, u32[]{:S(2)}, u32[]{:S(2)}) collective-permute-start(f32[8,4,128]{2,0,1:T(8,128)S(1)} %pad_maximum_fusion.1), channel_id=1, source_target_pairs={{0,16},{2,18},{4,20},{6,22},{8,24},{10,26},{12,28},{14,30},{16,0},... | collective-permute-start | bytes 49160 | tf_op jit(solution)/shard_map/ppermute | solution.py:24
  58.9 36.6 %collective-permute-start.17 = (bf16[128,2048]{1,0:T(8,128)(2,1)S(1)}, bf16[128,2048]{1,0:T(8,128)(2,1)S(1)}, u32[]{:S(2)}, u32[]{:S(2)}) collective-permute-start(bf16[128,2048]{1,0:T(8,128)(2,1)S(1)} %collective-permute-done.10.refs_11_), channel_id=1, source_target_pairs={{0,16},{2,10},{4,20},{6,14},{8,0},{10,26},{12,4},{14,30},{16,24},{... | collective-permute-start | bytes 1572872 | tf_op jit(solution)/shard_map/ppermute | solution.py:70
  59.0 36.5 %collective-permute-start.18 = (bf16[128,2048]{1,0:T(8,128)(2,1)S(1)}, bf16[128,2048]{1,0:T(8,128)(2,1)S(1)}, u32[]{:S(2)}, u32[]{:S(2)}) collective-permute-start(bf16[128,2048]{1,0:T(8,128)(2,1)S(1)} %collective-permute-done.10.refs_11_), channel_id=1, source_target_pairs={{0,4},{2,6},{4,0},{6,2},{8,12},{10,14},{12,8},{14,10},{16,20},{18,... | collective-permute-start | bytes 1572872 | tf_op jit(solution)/shard_map/ppermute | solution.py:70
  60.2 35.3 %collective-permute-start.14 = (bf16[128,2048]{1,0:T(8,128)(2,1)S(1)}, bf16[128,2048]{1,0:T(8,128)(2,1)S(1)}, u32[]{:S(2)}, u32[]{:S(2)}) collective-permute-start(bf16[128,2048]{1,0:T(8,128)(2,1)S(1)} %collective-permute-done.8.refs_12_), channel_id=1, source_target_pairs={{0,8},{2,18},{4,12},{6,22},{8,24},{10,2},{12,28},{14,6},{16,0},{18... | collective-permute-start | bytes 1572872 | tf_op jit(solution)/shard_map/ppermute | solution.py:70
  61.3 34.2 %collective-permute-start.15 = (bf16[128,2048]{1,0:T(8,128)(2,1)S(1)}, bf16[128,2048]{1,0:T(8,128)(2,1)S(1)}, u32[]{:S(2)}, u32[]{:S(2)}) collective-permute-start(bf16[128,2048]{1,0:T(8,128)(2,1)S(1)} %collective-permute-done.8.refs_12_), channel_id=1, source_target_pairs={{0,4},{2,6},{4,0},{6,2},{8,12},{10,14},{12,8},{14,10},{16,20},{18,... | collective-permute-start | bytes 1572872 | tf_op jit(solution)/shard_map/ppermute | solution.py:70
  63.8 31.7 %collective-permute-start.16 = (bf16[896,2048]{1,0:T(8,128)(2,1)}, bf16[896,2048]{1,0:T(8,128)(2,1)S(1)}, u32[]{:S(2)}, u32[]{:S(2)}) collective-permute-start(bf16[896,2048]{1,0:T(8,128)(2,1)} %get-tuple-element.74), channel_id=1, source_target_pairs={{0,2},{2,0},{4,6},{6,4},{8,10},{10,8},{12,14},{14,12},{16,18},{18,... | collective-permute-start | bytes 11010056 | tf_op jit(solution)/shard_map/ppermute | solution.py:70
  92.5 2.4 %copy-start = (bf16[1280,2048]{1,0:T(8,128)(2,1)}, bf16[1280,2048]{1,0:T(8,128)(2,1)S(1)}, u32[]{:S(2)}) copy-start(bf16[1280,2048]{1,0:T(8,128)(2,1)S(1)} %get-tuple-element.94.refs_7_) | copy-start | bytes 15728644
  95.5 11.0 %collective-permute-start.19 = (bf16[128,2048]{1,0:T(8,128)(2,1)S(1)}, bf16[128,2048]{1,0:T(8,128)(2,1)S(1)}, u32[]{:S(2)}, u32[]{:S(2)}) collective-permute-start(bf16[128,2048]{1,0:T(8,128)(2,1)S(1)} %collective-permute-done.18.refs_3_), channel_id=1, source_target_pairs={{0,16},{2,10},{4,20},{6,14},{8,0},{10,26},{12,4},{14,30},{16,24},{... | collective-permute-start | bytes 1572872 | tf_op jit(solution)/shard_map/ppermute | solution.py:70
  95.8 13.6 %collective-permute-start.20 = (bf16[128,2048]{1,0:T(8,128)(2,1)S(1)}, bf16[128,2048]{1,0:T(8,128)(2,1)S(1)}, u32[]{:S(2)}, u32[]{:S(2)}) collective-permute-start(bf16[128,2048]{1,0:T(8,128)(2,1)S(1)} %collective-permute-done.14.refs_6_), channel_id=1, source_target_pairs={{0,4},{2,6},{4,0},{6,2},{8,12},{10,14},{12,8},{14,10},{16,20},{18,... | collective-permute-start | bytes 1572872 | tf_op jit(solution)/shard_map/ppermute | solution.py:70
  95.9 2.5 %copy-start.1 = (bf16[1280,2048]{1,0:T(8,128)(2,1)S(1)}, bf16[1280,2048]{1,0:T(8,128)(2,1)}, u32[]{:S(2)}) copy-start(bf16[1280,2048]{1,0:T(8,128)(2,1)} %copy-done) | copy-start | bytes 15728644
  111.8 7.5 %collective-permute-start.22 = (bf16[896,2048]{1,0:T(8,128)(2,1)S(1)}, bf16[896,2048]{1,0:T(8,128)(2,1)S(1)}, u32[]{:S(2)}, u32[]{:S(2)}) collective-permute-start(bf16[896,2048]{1,0:T(8,128)(2,1)S(1)} %get-tuple-element.103), channel_id=1, source_target_pairs={{0,2},{2,0},{4,6},{6,4},{8,10},{10,8},{12,14},{14,12},{16,18},{18,... | collective-permute-start | bytes 11010056 | tf_op jit(solution)/shard_map/ppermute | solution.py:376
  112.7 6.0 %collective-permute-start.21 = (f32[2048]{0:T(1024)S(1)}, f32[2048]{0:T(1024)S(1)}, u32[]{:S(2)}, u32[]{:S(2)}) collective-permute-start(f32[2048]{0:T(1024)S(1)} %bitcast.33), channel_id=1, source_target_pairs={{0,2},{2,0},{4,6},{6,4},{8,10},{10,8},{12,14},{14,12},{16,18},{18,... | collective-permute-start | bytes 24584 | tf_op jit(solution)/shard_map/ppermute | solution.py:376
  112.8 6.0 %copy-start.2 = (bf16[4096]{0:T(1024)(128)(2,1)S(1)}, bf16[4096]{0:T(1024)(128)(2,1)}, u32[]{:S(2)}) copy-start(bf16[4096]{0:T(1024)(128)(2,1)} %param.10) | copy-start | bytes 24580

commit v9 on v8

--- a/solution.py
+++ b/solution.py
@@ -77,12 +77,12 @@
     return last, middle, early
 
 
-def run_plan(stream, scalars, own_facts, paths, pick_both, early_own, early_other):
+def run_plan(stream, hidden, scalars, own_facts, paths, pick_both, early_own, early_other):
     half = stream.shape[1] // 2
     m, ring, across, core = paths.m, paths.ring, paths.across, paths.core
     cut = lambda c: lax.dynamic_slice_in_dim(stream, c * half, half, 1)
     core_index = scalars["core"]
-    f = Flights(stream=stream, away=cut(1 - core_index), **scalars)
+    f = Flights(stream=stream, hidden=hidden, away=cut(1 - core_index), **scalars)
     f.have[0, 0, 0] = cut(core_index)
     have = f.have
     names = list(scalars)
@@ -105,14 +105,15 @@
         [((1, 0, 1), (0, 0, 1), ring[1]), ((0, 1, 1), (0, 0, 1), across)],
     )
     have["facts"] = butterfly_sum(own_facts(have["stream"]), "tp")[None]
+    f.event(["facts", "hidden"])
+    have["own picks"], have["away picks"] = pick_both(have["hidden"])
     f.event(
-        [(1, 0, 0), (0, 1, 0), "facts"],
+        [(1, 0, 0), (0, 1, 0), "facts", "own picks", "away picks"],
         [((2, 0, 0), (1, 0, 0), ring[0]), ((1, 1, 0), (1, 0, 0), across)],
     )
-    have["own picks"], have["away picks"] = pick_both()
     facts_step()
     facts_send()
-    f.event([(1, 0, 1), (0, 1, 1), "facts", "other facts", "own picks", "away picks"], [((2, 0, 1), (1, 0, 1), ring[1]), ((1, 1, 1), (1, 0, 1), across)])
+    f.event([(1, 0, 1), (0, 1, 1), "facts", "other facts"], [((2, 0, 1), (1, 0, 1), ring[1]), ((1, 1, 1), (1, 0, 1), across)])
     facts_merge()
     for k in range(2, m):
         for kind in range(2):
@@ -139,7 +140,7 @@
 
 
 def params(tokens):
-    return pltpu.CompilerParams(vmem_limit_bytes=(16 if tokens <= 4096 else 40) * 1024 * 1024)
+    return pltpu.CompilerParams(vmem_limit_bytes=(9 if tokens <= 4096 else 40) * 1024 * 1024)
 
 
 def cost(units, k, width, extra):
@@ -148,26 +149,46 @@
     )
 
 
-def pick_kernel(tok, owners, hidden, *picked):
-    count = hidden.shape[1] // tok
-    for n, out in enumerate(picked):
-        for b in range(count):
-            columns = pl.ds(pl.multiple_of(owners[n * count + b] * tok, tok), tok)
-            out[:, b * tok : (b + 1) * tok] = hidden[:, columns]
+def pieces_of(units):
+    return next(n for n in (7, 4, 2, 1) if units % (16 * n) == 0)
+
+
+def pick_kernel(tok, owners, hidden, own, away, held, turned, sems_in, sems_out):
+    units, tokens = hidden.shape
+    count = tokens // tok
+    pieces = pieces_of(units)
+    size = units // pieces
+    rows = [pl.ds(n * size, size) for n in range(pieces)]
+    fetch = [pltpu.make_async_copy(hidden.at[r, :], held.at[r, :], sems_in.at[n]) for n, r in enumerate(rows)]
+    place = [pltpu.make_async_copy(turned.at[r, :], away.at[r, :], sems_out.at[n]) for n, r in enumerate(rows)]
+    for copy in fetch:
+        copy.start()
+    for n, r in enumerate(rows):
+        fetch[n].wait()
+        for m, out in enumerate((own, turned)):
+            for b in range(count):
+                columns = pl.ds(pl.multiple_of(owners[m * count + b] * tok, tok), tok)
+                out[r, b * tok : (b + 1) * tok] = held[r, columns]
+        place[n].start()
+    for copy in place:
+        copy.wait()
 
 
 def pick(hidden, owners, tok):
-    orders = 2
-    units, tokens = hidden.shape
-    rows = next(r for r in range(128, 0, -16) if units % r == 0)
-    spec = pl.BlockSpec((rows, tokens), lambda i, *_: (i, 0))
+    inside = pl.BlockSpec(memory_space=pltpu.VMEM)
+    anywhere = pl.BlockSpec(memory_space=pl.ANY)
+    pieces = pieces_of(hidden.shape[0])
     return pl.pallas_call(
         functools.partial(pick_kernel, tok),
         grid_spec=pltpu.PrefetchScalarGridSpec(
-            num_scalar_prefetch=1, grid=(units // rows,), in_specs=[spec], out_specs=[spec] * orders
+            num_scalar_prefetch=1,
+            grid=(),
+            in_specs=[anywhere],
+            out_specs=[inside, anywhere],
+            scratch_shapes=[pltpu.VMEM(hidden.shape, hidden.dtype)] * 2 + [pltpu.SemaphoreType.DMA((pieces,))] * 2,
         ),
         out_shape=[pltpu.VMEM(hidden.shape, hidden.dtype), pltpu.HBM(hidden.shape, hidden.dtype)],
-        compiler_params=params(tokens),
+        compiler_params=params(hidden.shape[1]),
         cost_estimate=cost(0, 0, 0, 1),
     )(owners, pltpu.with_memory_space_constraint(hidden, pltpu.HBM))
 
@@ -189,10 +210,6 @@
             weight = weights[rows, :]
             dstream[rows, lanes] = (weight * head[:, lanes] - pulls[rows, :] * stream_f).astype(jnp.bfloat16)
             parts[owners[first + b], :, lanes] = jnp.sum(weight * stream_f, axis=0, keepdims=True)
-
-
-def pieces_of(units):
-    return next(n for n in (7, 4, 2, 1) if units % (16 * n) == 0)
 
 
 def product_kernel(tok, count, first, given_count, added, parts_count, wide, chunk, owners, where, *refs):
@@ -424,7 +441,7 @@
             low = (me >> n) % 2 == 0
             scalars["low %d" % n] = low if n > 1 else (jnp.arange(2 << n) < 1 << n) == low
         scalars["owners"] = owners
-        have = run_plan(stream, scalars, own_facts, paths, lambda: pick(hidden, owners, tok), early_own, early_other)
+        have = run_plan(stream, hidden, scalars, own_facts, paths, lambda hidden: pick(hidden, owners, tok), early_own, early_other)
         out, dstream, grad_head = product(
             have["owners"],
             0,

time: 122 us -> 104 us (0.85)
  the two profiles are of different devices: /device:TPU:11 before, /device:TPU:0 now
where the time goes in v9:
time: 104 us; the launch traced here: 102 us
  waiting for transfers between devices  34 us (33%)
  starting transfers between devices  29.7 us (29%)
  Pallas kernels  29.3 us (28%)
  other arithmetic  6.13 us (6%)
  local copies, waits for them, and re-layouts  2.24 us (2%)
  between operations  1.06 us (1%)
    ppermute x4, waiting for transfers between devices, butterfly_send(): lax.ppermute(x, axis, [(i, i ^ x.shape[0]) for i in range(lax.axis_size(a...  23.5 us
    pallas_call x4, Pallas kernels, product(): pl.pallas_call(functools.partial(product_kernel, tok, count, first, len(g...  22.7 us
    ppermute x16, starting transfers between devices, event(): self.have[name] = lax.ppermute(self.have[source], 'seq', pairs)  20.1 us
    ppermute x16, waiting for transfers between devices, event(): self.have[name] = lax.ppermute(self.have[source], 'seq', pairs)  8.33 us
    ppermute x4, starting transfers between devices, butterfly_send(): lax.ppermute(x, axis, [(i, i ^ x.shape[0]) for i in range(lax.axis_size(a...  7.39 us
    pallas_call x1, Pallas kernels, pick(): pl.pallas_call(functools.partial(pick_kernel, tok), grid_spec=pltpu.Prefe...  4.35 us
    pallas_call x1, Pallas kernels, put(): pl.pallas_call(functools.partial(put_kernel, pieces), grid_spec=pltpu.Pre...  2.2 us
  transfers between devices with their start and end apart: 23, of which 11 were waited for; matrix products, arithmetic and copies ran while one was open for 7% of the time, Pallas kernels for 24%

profile of v9, /device:TPU:0, one launch (start us, length us, event | category | flops | bytes accessed | tf_op | source)
XLA Modules:
  0.0 102.4 jit_solution(17463241024237175701)
XLA Ops:
  0.7 1.3 %constant_dynamic-slice_fusion.1 = (bf16[128,2048]{1,0:T(8,128)(2,1)S(1)}, bf16[128,2048]{1,0:T(8,128)(2,1)S(1)}) fusion(bf16[128,4096]{1,0:T(8,128)(2,1)} %param.8, s32[]{:T(128)S(6)} %select_n.133, s32[]{:T(128)S(6)} %select_n.132), kind=kLoop, calls=%fused_computation.45 | loop fusion | bytes 2097160 | tf_op jit(solution)/shard_map/dynamic_slice | solution.py:83
  1.9 4.1 %collective-permute-start.3 = (bf16[128,2048]{1,0:T(8,128)(2,1)S(1)}, bf16[128,2048]{1,0:T(8,128)(2,1)S(1)}, u32[]{:S(2)}, u32[]{:S(2)}) collective-permute-start(bf16[128,2048]{1,0:T(8,128)(2,1)S(1)} %get-tuple-element.61.refs_3_), channel_id=1, source_target_pairs={{0,16},{2,10},{4,20},{6,14},{8,0},{10,26},{12,4},{14,30},{16,24},{... | collective-permute-start | bytes 1572872 | tf_op jit(solution)/shard_map/ppermute | solution.py:70
  6.0 1.5 %collective-permute-start.4 = (bf16[128,2048]{1,0:T(8,128)(2,1)S(1)}, bf16[128,2048]{1,0:T(8,128)(2,1)S(1)}, u32[]{:S(2)}, u32[]{:S(2)}) collective-permute-start(bf16[128,2048]{1,0:T(8,128)(2,1)S(1)} %get-tuple-element.61.refs_3_), channel_id=1, source_target_pairs={{0,4},{2,6},{4,0},{6,2},{8,12},{10,14},{12,8},{14,10},{16,20},{18,... | collective-permute-start | bytes 1572872 | tf_op jit(solution)/shard_map/ppermute | solution.py:70
  7.6 0.7 fusion.6.owners
  8.3 0.7 multiply_bitcast_fusion
  9.0 0.7 convert_multiply_fusion.3
  9.7 1.7 %fusion = (f32[128]{0:T(128)S(1)}, f32[128]{0:T(128)S(1)}) fusion(bf16[128,4096]{1,0:T(8,128)(2,1)} %param.8, f32[4096]{0:T(1024)S(1)} %convert_multiply_fusion.3), kind=kLoop, calls=%fused_computation.2 | loop fusion | flops 2621184 | bytes 1065984 | tf_op jit(solution)/shard_map/reduce_sum | solution.py:406
  11.4 1.6 %collective-permute-start.5 = (f32[4,128]{1,0:T(4,128)S(1)}, f32[4,128]{1,0:T(4,128)S(1)}, u32[]{:S(2)}, u32[]{:S(2)}) collective-permute-start(f32[4,128]{1,0:T(4,128)S(1)} %pad_maximum_fusion.2), channel_id=1, source_target_pairs={{0,1},{1,0},{2,3},{3,2},{4,5},{5,4},{6,7},{7,6},{8,9},{9,8},{10,11... | collective-permute-start | bytes 6152 | tf_op jit(solution)/shard_map/ppermute | solution.py:18
  12.9 0.8 collective-permute-start.1
  13.8 0.5 collective-permute-start.2
  14.3 0.8 collective-permute-done.5
  15.0 4.3 %shard_map.111 = (bf16[896,2048]{1,0:T(8,128)(2,1)S(1)}, bf16[896,2048]{1,0:T(8,128)(2,1)}) custom-call(s32[32]{0:T(128)S(1)} %fusion.6.owners, bf16[896,2048]{1,0:T(8,128)(2,1)} %hidden), custom_call_target="tpu_custom_call" | custom-call | bytes 1 | tf_op jit(solution)/shard_map/pallas_call | solution.py:181
  19.4 0.8 collective-permute-done.3.refs_7_
  20.2 0.0 collective-permute-done.4.refs_5_
  20.2 0.0 collective-permute-start.6
  20.2 1.1 %collective-permute-done.6 = f32[1,4,128]{2,0,1:T(1,128)S(1)} collective-permute-done((f32[1,4,128]{2,0,1:T(1,128)S(1)}, f32[1,4,128]{2,0,1:T(1,128)S(1)}, u32[]{:S(2)}, u32[]{:S(2)}) %collective-permute-start.6) | collective-permute-done | bytes 2080 | tf_op jit(solution)/shard_map/ppermute | solution.py:24
  21.3 0.1 maximum_select_fusion.2
  21.4 4.2 %collective-permute-start.7 = (f32[2,4,128]{2,0,1:T(2,128)S(1)}, f32[2,4,128]{2,0,1:T(2,128)S(1)}, u32[]{:S(2)}, u32[]{:S(2)}) collective-permute-start(f32[2,4,128]{2,0,1:T(2,128)S(1)} %maximum_select_fusion.2), channel_id=1, source_target_pairs={{0,4},{2,6},{4,0},{6,2},{8,12},{10,14},{12,8},{14,10},{16,20},{18,... | collective-permute-start | bytes 12296 | tf_op jit(solution)/shard_map/ppermute | solution.py:24
  25.6 0.1 collective-permute-start.10
  25.6 0.1 collective-permute-start.11
  25.7 4.7 %collective-permute-done.7 = f32[2,4,128]{2,0,1:T(2,128)S(1)} collective-permute-done((f32[2,4,128]{2,0,1:T(2,128)S(1)}, f32[2,4,128]{2,0,1:T(2,128)S(1)}, u32[]{:S(2)}, u32[]{:S(2)}) %collective-permute-start.7) | collective-permute-done | bytes 4128 | tf_op jit(solution)/shard_map/ppermute | solution.py:24
  30.4 0.4 collective-permute-done.1.refs_8_
  30.9 0.0 collective-permute-done.2.refs_6_
  30.9 0.1 maximum_select_fusion.1
  30.9 0.0 collective-permute-start.12
  31.0 2.0 %collective-permute-start.8 = (bf16[128,2048]{1,0:T(8,128)(2,1)S(1)}, bf16[128,2048]{1,0:T(8,128)(2,1)S(1)}, u32[]{:S(2)}, u32[]{:S(2)}) collective-permute-start(bf16[128,2048]{1,0:T(8,128)(2,1)S(1)} %collective-permute-done.1.refs_8_), channel_id=1, source_target_pairs={{0,8},{2,18},{4,12},{6,22},{8,24},{10,2},{12,28},{14,6},{16,0},{18... | collective-permute-start | bytes 1572872 | tf_op jit(solution)/shard_map/ppermute | solution.py:70
  33.0 2.1 %collective-permute-start.9 = (bf16[128,2048]{1,0:T(8,128)(2,1)S(1)}, bf16[128,2048]{1,0:T(8,128)(2,1)S(1)}, u32[]{:S(2)}, u32[]{:S(2)}) collective-permute-start(bf16[128,2048]{1,0:T(8,128)(2,1)S(1)} %collective-permute-done.1.refs_8_), channel_id=1, source_target_pairs={{0,4},{2,6},{4,0},{6,2},{8,12},{10,14},{12,8},{14,10},{16,20},{18,... | collective-permute-start | bytes 1572872 | tf_op jit(solution)/shard_map/ppermute | solution.py:70
  35.1 15.8 %collective-permute-done.12 = f32[4,4,128]{2,0,1:T(4,128)S(1)} collective-permute-done((f32[4,4,128]{2,0,1:T(4,128)S(1)}, f32[4,4,128]{2,0,1:T(4,128)S(1)}, u32[]{:S(2)}, u32[]{:S(2)}) %collective-permute-start.12) | collective-permute-done | bytes 8224 | tf_op jit(solution)/shard_map/ppermute | solution.py:24
  50.9 0.0 collective-permute-done.10.refs_11_
  50.9 0.0 collective-permute-done.11.refs_9_
  50.9 3.2 %collective-permute-start.13 = (f32[8,4,128]{2,0,1:T(8,128)S(1)}, f32[8,4,128]{2,0,1:T(8,128)S(1)}, u32[]{:S(2)}, u32[]{:S(2)}) collective-permute-start(f32[8,4,128]{2,0,1:T(8,128)S(1)} %pad_maximum_fusion.1), channel_id=1, source_target_pairs={{0,16},{2,18},{4,20},{6,22},{8,24},{10,26},{12,28},{14,30},{16,0},... | collective-permute-start | bytes 49160 | tf_op jit(solution)/shard_map/ppermute | solution.py:24
  54.1 0.1 collective-permute-start.17
  54.2 0.0 collective-permute-start.18
  54.2 1.9 %collective-permute-done.13 = f32[8,4,128]{2,0,1:T(8,128)S(1)} collective-permute-done((f32[8,4,128]{2,0,1:T(8,128)S(1)}, f32[8,4,128]{2,0,1:T(8,128)S(1)}, u32[]{:S(2)}, u32[]{:S(2)}) %collective-permute-start.13) | collective-permute-done | bytes 16416 | tf_op jit(solution)/shard_map/ppermute | solution.py:24
  56.1 0.0 collective-permute-done.9.refs_10_
  56.1 6.5 %collective-permute-start.14 = (bf16[128,2048]{1,0:T(8,128)(2,1)S(1)}, bf16[128,2048]{1,0:T(8,128)(2,1)S(1)}, u32[]{:S(2)}, u32[]{:S(2)}) collective-permute-start(bf16[128,2048]{1,0:T(8,128)(2,1)S(1)} %collective-permute-done.8.refs_12_), channel_id=1, source_target_pairs={{0,8},{2,18},{4,12},{6,22},{8,24},{10,2},{12,28},{14,6},{16,0},{18... | collective-permute-start | bytes 1572872 | tf_op jit(solution)/shard_map/ppermute | solution.py:70
  62.7 0.3 collective-permute-start.15
  62.9 0.1 fusion.10
  63.1 0.3 select_reduce_fusion.1
  63.4 0.1 broadcast_compare_fusion
  63.5 0.1 select_reduce_fusion.5
  63.6 0.7 select_reduce_fusion
  64.3 0.1 slice_reduce_fusion
  64.4 0.1 select_reduce_fusion.2
  64.5 0.1 select_reduce_fusion.4
  64.6 0.1 broadcast_in_dim.160
  64.7 0.1 eq.106
  64.8 0.1 collective-permute-start.16
  64.9 7.6 %shard_map.112 = (f32[896,2048]{1,0:T(8,128)S(1)}, bf16[1280,2048]{1,0:T(8,128)(2,1)S(1)}, f32[16,1,2048]{2,1,0:T(1,128)S(1)}) custom-call(s32[32]{0:T(128)S(1)} %fusion.6.owners, s32[1]{0:T(128)} %constant.69.clone.1.where, bf16[896,2048]{1,0:T(8,128)(2,1)S(1)} %get-tuple-element.80.refs_0_, f32[8,2048]{1,0:T(8,128)S(1)} %select_maximum_fusion.refs_1_, ...), custom_call_target="tpu_custom_call" | custom-call | flops 46976204800 | bytes 86376448 | tf_op jit(solution)/shard_map/pallas_call | solution.py:300
  72.5 0.6 select_reduce_fusion.3
  73.2 0.0 collective-permute-done.17.refs_5_
  73.2 5.3 %collective-permute-done.14.refs_6_ = bf16[128,2048]{1,0:T(8,128)(2,1)S(1)} collective-permute-done((bf16[128,2048]{1,0:T(8,128)(2,1)S(1)}, bf16[128,2048]{1,0:T(8,128)(2,1)S(1)}, u32[]{:S(2)}, u32[]{:S(2)}) %collective-permute-start.14) | collective-permute-done | bytes 524320 | tf_op jit(solution)/shard_map/ppermute | solution.py:70
  78.4 2.0 %collective-permute-start.19 = (bf16[128,2048]{1,0:T(8,128)(2,1)S(1)}, bf16[128,2048]{1,0:T(8,128)(2,1)S(1)}, u32[]{:S(2)}, u32[]{:S(2)}) collective-permute-start(bf16[128,2048]{1,0:T(8,128)(2,1)S(1)} %collective-permute-done.18.refs_3_), channel_id=1, source_target_pairs={{0,16},{2,10},{4,20},{6,14},{8,0},{10,26},{12,4},{14,30},{16,24},{... | collective-permute-start | bytes 1572872 | tf_op jit(solution)/shard_map/ppermute | solution.py:70
  80.4 0.1 collective-permute-start.20
  80.4 8.1 %shard_map.113 = (f32[896,2048]{1,0:T(8,128)S(1)}, bf16[512,2048]{1,0:T(8,128)(2,1)S(1)}, f32[16,1,2048]{2,1,0:T(1,128)S(1)}) custom-call(s32[32]{0:T(128)S(1)} %fusion.6.owners, s32[1]{0:T(128)} %constant.69.clone.1.where, bf16[896,2048]{1,0:T(8,128)(2,1)S(1)} %collective-permute-done.16.refs_0_, f32[8,2048]{1,0:T(8,128)S(1)} %select_maximum_fusion.refs_1_, ...), custom_call_target="tpu_custom_call" | custom-call | flops 6576668672 | bytes 21561344 | tf_op jit(solution)/shard_map/pallas_call | solution.py:300
  88.6 0.9 collective-permute-done.19.refs_3_
  89.5 0.9 collective-permute-done.20.refs_4_
  90.4 2.4 %shard_map.114 = (bf16[896,2048]{1,0:T(8,128)(2,1)S(1)}, bf16[256,2048]{1,0:T(8,128)(2,1)S(1)}, f32[1,2048]{1,0:T(1,128)S(1)}) custom-call(s32[32]{0:T(128)S(1)} %fusion.6.owners, s32[1]{0:T(128)} %constant.69.clone.1.where, bf16[896,2048]{1,0:T(8,128)(2,1)S(1)} %collective-permute-done.16.refs_0_, f32[8,2048]{1,0:T(8,128)S(1)} %select_maximum_fusion.refs_1_, ...), custom_call_target="tpu_custom_call" | custom-call | flops 939524096 | bytes 12517376 | tf_op jit(solution)/shard_map/pallas_call | solution.py:300
  92.9 0.1 collective-permute-start.22
  93.0 0.5 collective-permute-start.21
  93.5 4.5 %shard_map.115.whole = bf16[896,4096]{1,0:T(8,128)(2,1)} custom-call(s32[32]{0:T(128)S(1)} %fusion.6.owners, s32[1]{0:T(128)} %bitcast.where, bf16[896,2048]{1,0:T(8,128)(2,1)S(1)} %get-tuple-element.80.refs_0_, bf16[256,2048]{1,0:T(8,128)(2,1)S(1)} %get-tuple-element.109.refs_1_, bf16[512,2048]{1,0:T(8,128)(2,1)S(1)} %get-tuple-element.110.refs_2_, ...), custom_call_target="tpu_custom_call" | custom-call | flops 2818572288 | bytes 15532032 | tf_op jit(solution)/shard_map/pallas_call | solution.py:300
  98.0 1.4 %collective-permute-done.21 = f32[2048]{0:T(1024)S(1)} collective-permute-done((f32[2048]{0:T(1024)S(1)}, f32[2048]{0:T(1024)S(1)}, u32[]{:S(2)}, u32[]{:S(2)}) %collective-permute-start.21) | collective-permute-done | bytes 8224 | tf_op jit(solution)/shard_map/ppermute | solution.py:393
  99.4 0.6 convert_multiply_fusion.2
  100.0 2.2 %shard_map.116 = bf16[896,4096]{1,0:T(8,128)(2,1)} custom-call(s32[1]{0:T(128)S(6)} %sub.26.where, bf16[896,2048]{1,0:T(8,128)(2,1)S(1)} %collective-permute-done.22.part, bf16[896,4096]{1,0:T(8,128)(2,1)} %shard_map.115.whole), custom_call_target="tpu_custom_call", output_to_operand_aliasing={{}: (2, {})} | custom-call | bytes 7340032 | tf_op jit(solution)/shard_map/pallas_call | solution.py:344
  (25 shorter events, 0.2 us)
Async XLA Ops:
  1.9 18.2 %collective-permute-start.3 = (bf16[128,2048]{1,0:T(8,128)(2,1)S(1)}, bf16[128,2048]{1,0:T(8,128)(2,1)S(1)}, u32[]{:S(2)}, u32[]{:S(2)}) collective-permute-start(bf16[128,2048]{1,0:T(8,128)(2,1)S(1)} %get-tuple-element.61.refs_3_), channel_id=1, source_target_pairs={{0,16},{2,10},{4,20},{6,14},{8,0},{10,26},{12,4},{14,30},{16,24},{... | collective-permute-start | bytes 1572872 | tf_op jit(solution)/shard_map/ppermute | solution.py:70
  6.0 14.2 %collective-permute-start.4 = (bf16[128,2048]{1,0:T(8,128)(2,1)S(1)}, bf16[128,2048]{1,0:T(8,128)(2,1)S(1)}, u32[]{:S(2)}, u32[]{:S(2)}) collective-permute-start(bf16[128,2048]{1,0:T(8,128)(2,1)S(1)} %get-tuple-element.61.refs_3_), channel_id=1, source_target_pairs={{0,4},{2,6},{4,0},{6,2},{8,12},{10,14},{12,8},{14,10},{16,20},{18,... | collective-permute-start | bytes 1572872 | tf_op jit(solution)/shard_map/ppermute | solution.py:70
  7.5 2.2 %collective-permute-start = (bf16[128,2048]{1,0:T(8,128)(2,1)S(1)}, bf16[128,2048]{1,0:T(8,128)(2,1)S(1)}, u32[]{:S(2)}, u32[]{:S(2)}) collective-permute-start(bf16[128,2048]{1,0:T(8,128)(2,1)S(1)} %get-tuple-element.58), channel_id=1, source_target_pairs={{0,2},{2,0},{4,6},{6,4},{8,10},{10,8},{12,14},{14,12},{16,18},{18,... | collective-permute-start | bytes 1572872 | tf_op jit(solution)/shard_map/ppermute | solution.py:70
  11.4 3.7 %collective-permute-start.5 = (f32[4,128]{1,0:T(4,128)S(1)}, f32[4,128]{1,0:T(4,128)S(1)}, u32[]{:S(2)}, u32[]{:S(2)}) collective-permute-start(f32[4,128]{1,0:T(4,128)S(1)} %pad_maximum_fusion.2), channel_id=1, source_target_pairs={{0,1},{1,0},{2,3},{3,2},{4,5},{5,4},{6,7},{7,6},{8,9},{9,8},{10,11... | collective-permute-start | bytes 6152 | tf_op jit(solution)/shard_map/ppermute | solution.py:18
  12.9 17.9 %collective-permute-start.1 = (bf16[128,2048]{1,0:T(8,128)(2,1)S(1)}, bf16[128,2048]{1,0:T(8,128)(2,1)S(1)}, u32[]{:S(2)}, u32[]{:S(2)}) collective-permute-start(bf16[128,2048]{1,0:T(8,128)(2,1)S(1)} %collective-permute-done.refs_4_), channel_id=1, source_target_pairs={{0,8},{2,18},{4,12},{6,22},{8,24},{10,2},{12,28},{14,6},{16,0},{18... | collective-permute-start | bytes 1572872 | tf_op jit(solution)/shard_map/ppermute | solution.py:70
  13.8 17.1 %collective-permute-start.2 = (bf16[128,2048]{1,0:T(8,128)(2,1)S(1)}, bf16[128,2048]{1,0:T(8,128)(2,1)S(1)}, u32[]{:S(2)}, u32[]{:S(2)}) collective-permute-start(bf16[128,2048]{1,0:T(8,128)(2,1)S(1)} %collective-permute-done.refs_4_), channel_id=1, source_target_pairs={{0,4},{2,6},{4,0},{6,2},{8,12},{10,14},{12,8},{14,10},{16,20},{18,... | collective-permute-start | bytes 1572872 | tf_op jit(solution)/shard_map/ppermute | solution.py:70
  20.2 1.2 %collective-permute-start.6 = (f32[1,4,128]{2,0,1:T(1,128)S(1)}, f32[1,4,128]{2,0,1:T(1,128)S(1)}, u32[]{:S(2)}, u32[]{:S(2)}) collective-permute-start(f32[1,4,128]{2,0,1:T(1,128)S(1)} %bitcast.46), channel_id=1, source_target_pairs={{0,2},{2,0},{4,6},{6,4},{8,10},{10,8},{12,14},{14,12},{16,18},{18,... | collective-permute-start | bytes 6152 | tf_op jit(solution)/shard_map/ppermute | solution.py:24
  21.4 9.0 %collective-permute-start.7 = (f32[2,4,128]{2,0,1:T(2,128)S(1)}, f32[2,4,128]{2,0,1:T(2,128)S(1)}, u32[]{:S(2)}, u32[]{:S(2)}) collective-permute-start(f32[2,4,128]{2,0,1:T(2,128)S(1)} %maximum_select_fusion.2), channel_id=1, source_target_pairs={{0,4},{2,6},{4,0},{6,2},{8,12},{10,14},{12,8},{14,10},{16,20},{18,... | collective-permute-start | bytes 12296 | tf_op jit(solution)/shard_map/ppermute | solution.py:24
  25.6 25.3 %collective-permute-start.10 = (bf16[128,2048]{1,0:T(8,128)(2,1)S(1)}, bf16[128,2048]{1,0:T(8,128)(2,1)S(1)}, u32[]{:S(2)}, u32[]{:S(2)}) collective-permute-start(bf16[128,2048]{1,0:T(8,128)(2,1)S(1)} %collective-permute-done.3.refs_7_), channel_id=1, source_target_pairs={{0,16},{2,10},{4,20},{6,14},{8,0},{10,26},{12,4},{14,30},{16,24},{... | collective-permute-start | bytes 1572872 | tf_op jit(solution)/shard_map/ppermute | solution.py:70
  25.6 25.3 %collective-permute-start.11 = (bf16[128,2048]{1,0:T(8,128)(2,1)S(1)}, bf16[128,2048]{1,0:T(8,128)(2,1)S(1)}, u32[]{:S(2)}, u32[]{:S(2)}) collective-permute-start(bf16[128,2048]{1,0:T(8,128)(2,1)S(1)} %collective-permute-done.3.refs_7_), channel_id=1, source_target_pairs={{0,4},{2,6},{4,0},{6,2},{8,12},{10,14},{12,8},{14,10},{16,20},{18,... | collective-permute-start | bytes 1572872 | tf_op jit(solution)/shard_map/ppermute | solution.py:70
  30.9 19.9 %collective-permute-start.12 = (f32[4,4,128]{2,0,1:T(4,128)S(1)}, f32[4,4,128]{2,0,1:T(4,128)S(1)}, u32[]{:S(2)}, u32[]{:S(2)}) collective-permute-start(f32[4,4,128]{2,0,1:T(4,128)S(1)} %maximum_select_fusion.1), channel_id=1, source_target_pairs={{0,8},{2,10},{4,12},{6,14},{8,0},{10,2},{12,4},{14,6},{16,24},{18,... | collective-permute-start | bytes 24584 | tf_op jit(solution)/shard_map/ppermute | solution.py:24
  31.0 25.1 %collective-permute-start.8 = (bf16[128,2048]{1,0:T(8,128)(2,1)S(1)}, bf16[128,2048]{1,0:T(8,128)(2,1)S(1)}, u32[]{:S(2)}, u32[]{:S(2)}) collective-permute-start(bf16[128,2048]{1,0:T(8,128)(2,1)S(1)} %collective-permute-done.1.refs_8_), channel_id=1, source_target_pairs={{0,8},{2,18},{4,12},{6,22},{8,24},{10,2},{12,28},{14,6},{16,0},{18... | collective-permute-start | bytes 1572872 | tf_op jit(solution)/shard_map/ppermute | solution.py:70
  33.0 23.1 %collective-permute-start.9 = (bf16[128,2048]{1,0:T(8,128)(2,1)S(1)}, bf16[128,2048]{1,0:T(8,128)(2,1)S(1)}, u32[]{:S(2)}, u32[]{:S(2)}) collective-permute-start(bf16[128,2048]{1,0:T(8,128)(2,1)S(1)} %collective-permute-done.1.refs_8_), channel_id=1, source_target_pairs={{0,4},{2,6},{4,0},{6,2},{8,12},{10,14},{12,8},{14,10},{16,20},{18,... | collective-permute-start | bytes 1572872 | tf_op jit(solution)/shard_map/ppermute | solution.py:70
  50.9 5.2 %collective-permute-start.13 = (f32[8,4,128]{2,0,1:T(8,128)S(1)}, f32[8,4,128]{2,0,1:T(8,128)S(1)}, u32[]{:S(2)}, u32[]{:S(2)}) collective-permute-start(f32[8,4,128]{2,0,1:T(8,128)S(1)} %pad_maximum_fusion.1), channel_id=1, source_target_pairs={{0,16},{2,18},{4,20},{6,22},{8,24},{10,26},{12,28},{14,30},{16,0},... | collective-permute-start | bytes 49160 | tf_op jit(solution)/shard_map/ppermute | solution.py:24
  54.1 19.0 %collective-permute-start.17 = (bf16[128,2048]{1,0:T(8,128)(2,1)S(1)}, bf16[128,2048]{1,0:T(8,128)(2,1)S(1)}, u32[]{:S(2)}, u32[]{:S(2)}) collective-permute-start(bf16[128,2048]{1,0:T(8,128)(2,1)S(1)} %collective-permute-done.10.refs_11_), channel_id=1, source_target_pairs={{0,16},{2,10},{4,20},{6,14},{8,0},{10,26},{12,4},{14,30},{16,24},{... | collective-permute-start | bytes 1572872 | tf_op jit(solution)/shard_map/ppermute | solution.py:70
  54.2 19.0 %collective-permute-start.18 = (bf16[128,2048]{1,0:T(8,128)(2,1)S(1)}, bf16[128,2048]{1,0:T(8,128)(2,1)S(1)}, u32[]{:S(2)}, u32[]{:S(2)}) collective-permute-start(bf16[128,2048]{1,0:T(8,128)(2,1)S(1)} %collective-permute-done.10.refs_11_), channel_id=1, source_target_pairs={{0,4},{2,6},{4,0},{6,2},{8,12},{10,14},{12,8},{14,10},{16,20},{18,... | collective-permute-start | bytes 1572872 | tf_op jit(solution)/shard_map/ppermute | solution.py:70
  56.1 22.3 %collective-permute-start.14 = (bf16[128,2048]{1,0:T(8,128)(2,1)S(1)}, bf16[128,2048]{1,0:T(8,128)(2,1)S(1)}, u32[]{:S(2)}, u32[]{:S(2)}) collective-permute-start(bf16[128,2048]{1,0:T(8,128)(2,1)S(1)} %collective-permute-done.8.refs_12_), channel_id=1, source_target_pairs={{0,8},{2,18},{4,12},{6,22},{8,24},{10,2},{12,28},{14,6},{16,0},{18... | collective-permute-start | bytes 1572872 | tf_op jit(solution)/shard_map/ppermute | solution.py:70
  62.7 15.8 %collective-permute-start.15 = (bf16[128,2048]{1,0:T(8,128)(2,1)S(1)}, bf16[128,2048]{1,0:T(8,128)(2,1)S(1)}, u32[]{:S(2)}, u32[]{:S(2)}) collective-permute-start(bf16[128,2048]{1,0:T(8,128)(2,1)S(1)} %collective-permute-done.8.refs_12_), channel_id=1, source_target_pairs={{0,4},{2,6},{4,0},{6,2},{8,12},{10,14},{12,8},{14,10},{16,20},{18,... | collective-permute-start | bytes 1572872 | tf_op jit(solution)/shard_map/ppermute | solution.py:70
  64.8 13.6 %collective-permute-start.16 = (bf16[896,2048]{1,0:T(8,128)(2,1)}, bf16[896,2048]{1,0:T(8,128)(2,1)S(1)}, u32[]{:S(2)}, u32[]{:S(2)}) collective-permute-start(bf16[896,2048]{1,0:T(8,128)(2,1)} %get-tuple-element.78), channel_id=1, source_target_pairs={{0,2},{2,0},{4,6},{6,4},{8,10},{10,8},{12,14},{14,12},{16,18},{18,... | collective-permute-start | bytes 11010056 | tf_op jit(solution)/shard_map/ppermute | solution.py:70
  78.4 11.1 %collective-permute-start.19 = (bf16[128,2048]{1,0:T(8,128)(2,1)S(1)}, bf16[128,2048]{1,0:T(8,128)(2,1)S(1)}, u32[]{:S(2)}, u32[]{:S(2)}) collective-permute-start(bf16[128,2048]{1,0:T(8,128)(2,1)S(1)} %collective-permute-done.18.refs_3_), channel_id=1, source_target_pairs={{0,16},{2,10},{4,20},{6,14},{8,0},{10,26},{12,4},{14,30},{16,24},{... | collective-permute-start | bytes 1572872 | tf_op jit(solution)/shard_map/ppermute | solution.py:70
  80.4 10.1 %collective-permute-start.20 = (bf16[128,2048]{1,0:T(8,128)(2,1)S(1)}, bf16[128,2048]{1,0:T(8,128)(2,1)S(1)}, u32[]{:S(2)}, u32[]{:S(2)}) collective-permute-start(bf16[128,2048]{1,0:T(8,128)(2,1)S(1)} %collective-permute-done.14.refs_6_), channel_id=1, source_target_pairs={{0,4},{2,6},{4,0},{6,2},{8,12},{10,14},{12,8},{14,10},{16,20},{18,... | collective-permute-start | bytes 1572872 | tf_op jit(solution)/shard_map/ppermute | solution.py:70
  92.9 7.1 %collective-permute-start.22 = (bf16[896,2048]{1,0:T(8,128)(2,1)S(1)}, bf16[896,2048]{1,0:T(8,128)(2,1)S(1)}, u32[]{:S(2)}, u32[]{:S(2)}) collective-permute-start(bf16[896,2048]{1,0:T(8,128)(2,1)S(1)} %get-tuple-element.107), channel_id=1, source_target_pairs={{0,2},{2,0},{4,6},{6,4},{8,10},{10,8},{12,14},{14,12},{16,18},{18,... | collective-permute-start | bytes 11010056 | tf_op jit(solution)/shard_map/ppermute | solution.py:393
  93.0 6.4 %collective-permute-start.21 = (f32[2048]{0:T(1024)S(1)}, f32[2048]{0:T(1024)S(1)}, u32[]{:S(2)}, u32[]{:S(2)}) collective-permute-start(f32[2048]{0:T(1024)S(1)} %bitcast.33), channel_id=1, source_target_pairs={{0,2},{2,0},{4,6},{6,4},{8,10},{10,8},{12,14},{14,12},{16,18},{18,... | collective-permute-start | bytes 24584 | tf_op jit(solution)/shard_map/ppermute | solution.py:393
  93.5 5.9 %copy-start = (bf16[4096]{0:T(1024)(128)(2,1)S(1)}, bf16[4096]{0:T(1024)(128)(2,1)}, u32[]{:S(2)}) copy-start(bf16[4096]{0:T(1024)(128)(2,1)} %param.10) | copy-start | bytes 24580

commit v10 on v9

--- a/solution.py
+++ b/solution.py
@@ -20,14 +20,19 @@
     return x
 
 
-def butterfly_send(x, axis):
-    return lax.ppermute(x, axis, [(i, i ^ x.shape[0]) for i in range(lax.axis_size(axis))])
-
-
-def butterfly_merge(x, other, low):
-    low = low[x.shape[0]]
-    if low.ndim:
-        return jnp.where(low[:, None, None], jnp.concatenate([x, x]), jnp.concatenate([other, other]))
+def butterfly_send(x, axis, bit):
+    return lax.ppermute(x, axis, [(i, i ^ bit) for i in range(lax.axis_size(axis))])
+
+
+def butterfly_merge(x, other, bit, low):
+    low = low[bit]
+    if bit == 1:
+        return jnp.where(low[:, None, None], x, other)
+    if bit == 4:
+        return jnp.where(low[:, None, None, None], x[None], other[None])
+    if bit == 2:
+        both = jnp.stack([jnp.where(low, x, other), jnp.where(low, other, x)], axis=1)
+        return both.reshape(-1, *x.shape[2:])
     return jnp.concatenate([jnp.where(low, x, other), jnp.where(low, other, x)])
 
 
@@ -88,14 +93,16 @@
     names = list(scalars)
     low = lambda: {1 << n: have["low %d" % n] for n in range(paths.count.bit_length() - 1)}
 
+    bits = [1, 4, 2] + [8 << n for n in range(paths.count.bit_length() - 4)]
+
     def facts_send():
-        have["other facts"] = butterfly_send(have["facts"], "seq")
+        have["other facts"] = butterfly_send(have["facts"], "seq", bits[0])
 
     def facts_merge():
-        have["facts"] = butterfly_merge(have["facts"], have["other facts"], low())
+        have["facts"] = butterfly_merge(have["facts"], have["other facts"], bits.pop(0), low())
 
     def facts_step():
-        if have["facts"].shape[0] < paths.count:
+        if bits:
             facts_send()
             facts_merge()
 
@@ -131,7 +138,7 @@
                 waits += ["other picks", "early own", "values", "returns"]
             f.event(waits, sends)
             if k == m - 2 and kind == 1:
-                while have["facts"].shape[0] < paths.count:
+                while bits:
                     facts_step()
                 early_own(have)
     early_other(have)
@@ -321,19 +328,15 @@
     )
 
 
-def put_kernel(pieces, where, part, whole, out, held, sems_in, sems_out):
+def put_kernel(pieces, where, part, whole, out, sems):
     units, width = part.shape
     start = pl.multiple_of(where[0] * width, width)
     rows = [pl.ds(n * (units // pieces), units // pieces) for n in range(pieces)]
-    fetch = [pltpu.make_async_copy(part.at[r, :], held.at[r, :], sems_in.at[n]) for n, r in enumerate(rows)]
     place = [
-        pltpu.make_async_copy(held.at[r, :], out.at[r, pl.ds(start, width)], sems_out.at[n]) for n, r in enumerate(rows)
+        pltpu.make_async_copy(part.at[r, :], out.at[r, pl.ds(start, width)], sems.at[n]) for n, r in enumerate(rows)
     ]
-    for copy in fetch:
+    for copy in place:
         copy.start()
-    for n in range(pieces):
-        fetch[n].wait()
-        place[n].start()
     for copy in place:
         copy.wait()
 
@@ -341,24 +344,21 @@
 def put(whole, part, where):
     units, width = part.shape
     pieces = pieces_of(units)
+    anywhere = pl.BlockSpec(memory_space=pl.ANY)
     return pl.pallas_call(
         functools.partial(put_kernel, pieces),
         grid_spec=pltpu.PrefetchScalarGridSpec(
             num_scalar_prefetch=1,
             grid=(),
-            in_specs=[pl.BlockSpec(memory_space=pl.ANY)] * 2,
-            out_specs=pl.BlockSpec(memory_space=pl.ANY),
-            scratch_shapes=[
-                pltpu.VMEM(part.shape, part.dtype),
-                pltpu.SemaphoreType.DMA((pieces,)),
-                pltpu.SemaphoreType.DMA((pieces,)),
-            ],
+            in_specs=[pl.BlockSpec(memory_space=pltpu.VMEM), anywhere],
+            out_specs=anywhere,
+            scratch_shapes=[pltpu.SemaphoreType.DMA((pieces,))],
         ),
         out_shape=jax.ShapeDtypeStruct(whole.shape, whole.dtype),
         input_output_aliases={2: 0},
         compiler_params=params(0),
         cost_estimate=cost(0, 0, 0, 4 * units * width),
-    )(where, part, whole)
+    )(where, pltpu.with_memory_space_constraint(part, pltpu.VMEM), whole)
 
 
 def all_returns(step_reward, resets):
@@ -439,7 +439,7 @@
         scalars = {"core": mine, "me": me, "first core": mine == 0, "where": where, "elsewhere": 1 - where}
         for n in range(shards.bit_length() - 1):
             low = (me >> n) % 2 == 0
-            scalars["low %d" % n] = low if n > 1 else (jnp.arange(2 << n) < 1 << n) == low
+            scalars["low %d" % n] = (jnp.arange(2) == 0) == low if n in (0, 2) else low
         scalars["owners"] = owners
         have = run_plan(stream, hidden, scalars, own_facts, paths, lambda hidden: pick(hidden, owners, tok), early_own, early_other)
         out, dstream, grad_head = product(

time: 104 us -> 102 us (0.981)
  waiting for transfers between devices: 34 us -> 27.5 us
  starting transfers between devices: 29.7 us -> 34.7 us
    ppermute x4, waiting for transfers between devices: 23.5 us -> 14.5 us  [butterfly_send(): lax.ppermute(x, axis, [(i, i ^ bit) for i in range(lax.axis_size(axis))])]
    ppermute x16, starting transfers between devices: 20.1 us -> 26.8 us  [event(): self.have[name] = lax.ppermute(self.have[source], 'seq', pairs)]
    ppermute x16, waiting for transfers between devices: 8.33 us -> 10.9 us  [event(): self.have[name] = lax.ppermute(self.have[source], 'seq', pairs)]
    ppermute x4, starting transfers between devices: 7.39 us -> 5.84 us  [butterfly_send(): lax.ppermute(x, axis, [(i, i ^ bit) for i in range(lax.axis_size(axis))])]
where the time goes in v10:
time: 102 us; the launch traced here: 101 us
  starting transfers between devices  34.7 us (34%)
  Pallas kernels  28.9 us (28%)
  waiting for transfers between devices  27.5 us (27%)
  other arithmetic  6.19 us (6%)
  local copies, waits for them, and re-layouts  2.23 us (2%)
    ppermute x16, starting transfers between devices, event(): self.have[name] = lax.ppermute(self.have[source], 'seq', pairs)  26.8 us
    pallas_call x4, Pallas kernels, product(): pl.pallas_call(functools.partial(product_kernel, tok, count, first, len(g...  22.7 us
    ppermute x4, waiting for transfers between devices, butterfly_send(): lax.ppermute(x, axis, [(i, i ^ bit) for i in range(lax.axis_size(axis))])  14.5 us
    ppermute x16, waiting for transfers between devices, event(): self.have[name] = lax.ppermute(self.have[source], 'seq', pairs)  10.9 us
    ppermute x4, starting transfers between devices, butterfly_send(): lax.ppermute(x, axis, [(i, i ^ bit) for i in range(lax.axis_size(axis))])  5.84 us
    pallas_call x1, Pallas kernels, pick(): pl.pallas_call(functools.partial(pick_kernel, tok), grid_spec=pltpu.Prefe...  4.35 us
  transfers between devices with their start and end apart: 23, of which 11 were waited for; matrix products, arithmetic and copies ran while one was open for 7% of the time, Pallas kernels for 24%

profile of v10, /device:TPU:0, one launch (start us, length us, event | category | flops | bytes accessed | tf_op | source)
XLA Modules:
  0.0 100.6 jit_solution(9127665225211866781)
XLA Ops:
  0.7 1.3 %constant_dynamic-slice_fusion.1 = (bf16[128,2048]{1,0:T(8,128)(2,1)S(1)}, bf16[128,2048]{1,0:T(8,128)(2,1)S(1)}) fusion(bf16[128,4096]{1,0:T(8,128)(2,1)} %param.8, s32[]{:T(128)S(6)} %select_n.133, s32[]{:T(128)S(6)} %select_n.132), kind=kLoop, calls=%fused_computation.46 | loop fusion | bytes 2097160 | tf_op jit(solution)/shard_map/dynamic_slice | solution.py:88
  1.9 4.1 %collective-permute-start.3 = (bf16[128,2048]{1,0:T(8,128)(2,1)S(1)}, bf16[128,2048]{1,0:T(8,128)(2,1)S(1)}, u32[]{:S(2)}, u32[]{:S(2)}) collective-permute-start(bf16[128,2048]{1,0:T(8,128)(2,1)S(1)} %get-tuple-element.61.refs_3_), channel_id=1, source_target_pairs={{0,16},{2,10},{4,20},{6,14},{8,0},{10,26},{12,4},{14,30},{16,24},{... | collective-permute-start | bytes 1572872 | tf_op jit(solution)/shard_map/ppermute | solution.py:75
  6.0 1.5 %collective-permute-start.4 = (bf16[128,2048]{1,0:T(8,128)(2,1)S(1)}, bf16[128,2048]{1,0:T(8,128)(2,1)S(1)}, u32[]{:S(2)}, u32[]{:S(2)}) collective-permute-start(bf16[128,2048]{1,0:T(8,128)(2,1)S(1)} %get-tuple-element.61.refs_3_), channel_id=1, source_target_pairs={{0,4},{2,6},{4,0},{6,2},{8,12},{10,14},{12,8},{14,10},{16,20},{18,... | collective-permute-start | bytes 1572872 | tf_op jit(solution)/shard_map/ppermute | solution.py:75
  7.6 0.7 fusion.6.owners
  8.3 0.7 multiply_bitcast_fusion
  9.0 0.7 convert_multiply_fusion.3
  9.7 0.0 collective-permute-done.refs_4_
  9.7 1.7 %fusion = (f32[128]{0:T(128)S(1)}, f32[128]{0:T(128)S(1)}) fusion(bf16[128,4096]{1,0:T(8,128)(2,1)} %param.8, f32[4096]{0:T(1024)S(1)} %convert_multiply_fusion.3), kind=kLoop, calls=%fused_computation.2 | loop fusion | flops 2621184 | bytes 1065984 | tf_op jit(solution)/shard_map/reduce_sum | solution.py:406
  11.3 1.6 %collective-permute-start.5 = (f32[4,128]{1,0:T(4,128)S(1)}, f32[4,128]{1,0:T(4,128)S(1)}, u32[]{:S(2)}, u32[]{:S(2)}) collective-permute-start(f32[4,128]{1,0:T(4,128)S(1)} %pad_maximum_fusion.2), channel_id=1, source_target_pairs={{0,1},{1,0},{2,3},{3,2},{4,5},{5,4},{6,7},{7,6},{8,9},{9,8},{10,11... | collective-permute-start | bytes 6152 | tf_op jit(solution)/shard_map/ppermute | solution.py:18
  12.9 0.8 collective-permute-start.1
  13.7 0.5 collective-permute-start.2
  14.2 0.8 collective-permute-done.5
  15.0 4.3 %shard_map.111 = (bf16[896,2048]{1,0:T(8,128)(2,1)S(1)}, bf16[896,2048]{1,0:T(8,128)(2,1)}) custom-call(s32[32]{0:T(128)S(1)} %fusion.6.owners, bf16[896,2048]{1,0:T(8,128)(2,1)} %hidden), custom_call_target="tpu_custom_call" | custom-call | bytes 1 | tf_op jit(solution)/shard_map/pallas_call | solution.py:188
  19.4 0.8 collective-permute-done.3.refs_7_
  20.2 0.0 collective-permute-done.4.refs_5_
  20.2 1.1 %collective-permute-done.6 = f32[1,4,128]{2,1,0:T(4,128)S(1)} collective-permute-done((f32[1,4,128]{2,1,0:T(4,128)S(1)}, f32[1,4,128]{2,1,0:T(4,128)S(1)}, u32[]{:S(2)}, u32[]{:S(2)}) %collective-permute-start.6) | collective-permute-done | bytes 2080 | tf_op jit(solution)/shard_map/ppermute | solution.py:24
  21.4 0.1 broadcast_select_fusion.3
  21.4 2.2 %collective-permute-start.7 = (f32[2,4,128]{2,0,1:T(2,128)S(1)}, f32[2,4,128]{2,0,1:T(2,128)S(1)}, u32[]{:S(2)}, u32[]{:S(2)}) collective-permute-start(f32[2,4,128]{2,0,1:T(2,128)S(1)} %broadcast_select_fusion.3), channel_id=1, source_target_pairs={{0,8},{2,10},{4,12},{6,14},{8,0},{10,2},{12,4},{14,6},{16,24},{18,... | collective-permute-start | bytes 12296 | tf_op jit(solution)/shard_map/ppermute | solution.py:24
  23.6 3.9 %collective-permute-start.10 = (bf16[128,2048]{1,0:T(8,128)(2,1)S(1)}, bf16[128,2048]{1,0:T(8,128)(2,1)S(1)}, u32[]{:S(2)}, u32[]{:S(2)}) collective-permute-start(bf16[128,2048]{1,0:T(8,128)(2,1)S(1)} %collective-permute-done.3.refs_7_), channel_id=1, source_target_pairs={{0,16},{2,10},{4,20},{6,14},{8,0},{10,26},{12,4},{14,30},{16,24},{... | collective-permute-start | bytes 1572872 | tf_op jit(solution)/shard_map/ppermute | solution.py:75
  27.6 3.2 %collective-permute-start.11 = (bf16[128,2048]{1,0:T(8,128)(2,1)S(1)}, bf16[128,2048]{1,0:T(8,128)(2,1)S(1)}, u32[]{:S(2)}, u32[]{:S(2)}) collective-permute-start(bf16[128,2048]{1,0:T(8,128)(2,1)S(1)} %collective-permute-done.3.refs_7_), channel_id=1, source_target_pairs={{0,4},{2,6},{4,0},{6,2},{8,12},{10,14},{12,8},{14,10},{16,20},{18,... | collective-permute-start | bytes 1572872 | tf_op jit(solution)/shard_map/ppermute | solution.py:75
  30.7 0.0 collective-permute-done.7
  30.7 0.3 collective-permute-done.1.refs_8_
  31.1 0.0 collective-permute-done.2.refs_6_
  31.1 0.1 broadcast_select_fusion
  31.2 1.2 %collective-permute-start.12 = (f32[2,2,4,128]{3,1,0,2:T(2,128)S(1)}, f32[2,2,4,128]{3,1,0,2:T(2,128)S(1)}, u32[]{:S(2)}, u32[]{:S(2)}) collective-permute-start(f32[2,2,4,128]{3,1,0,2:T(2,128)S(1)} %broadcast_select_fusion), channel_id=1, source_target_pairs={{0,4},{2,6},{4,0},{6,2},{8,12},{10,14},{12,8},{14,10},{16,20},{18,... | collective-permute-start | bytes 24584 | tf_op jit(solution)/shard_map/ppermute | solution.py:24
  32.4 0.9 collective-permute-start.8
  33.3 2.0 %collective-permute-start.9 = (bf16[128,2048]{1,0:T(8,128)(2,1)S(1)}, bf16[128,2048]{1,0:T(8,128)(2,1)S(1)}, u32[]{:S(2)}, u32[]{:S(2)}) collective-permute-start(bf16[128,2048]{1,0:T(8,128)(2,1)S(1)} %collective-permute-done.1.refs_8_), channel_id=1, source_target_pairs={{0,4},{2,6},{4,0},{6,2},{8,12},{10,14},{12,8},{14,10},{16,20},{18,... | collective-permute-start | bytes 1572872 | tf_op jit(solution)/shard_map/ppermute | solution.py:75
  35.3 8.5 %collective-permute-done.12 = f32[2,2,4,128]{3,1,0,2:T(2,128)S(1)} collective-permute-done((f32[2,2,4,128]{3,1,0,2:T(2,128)S(1)}, f32[2,2,4,128]{3,1,0,2:T(2,128)S(1)}, u32[]{:S(2)}, u32[]{:S(2)}) %collective-permute-start.12) | collective-permute-done | bytes 8224 | tf_op jit(solution)/shard_map/ppermute | solution.py:24
  43.7 0.1 select_bitcast_fusion.1
  43.8 1.5 %collective-permute-done.10.refs_11_ = bf16[128,2048]{1,0:T(8,128)(2,1)S(1)} collective-permute-done((bf16[128,2048]{1,0:T(8,128)(2,1)S(1)}, bf16[128,2048]{1,0:T(8,128)(2,1)S(1)}, u32[]{:S(2)}, u32[]{:S(2)}) %collective-permute-start.10) | collective-permute-done | bytes 524320 | tf_op jit(solution)/shard_map/ppermute | solution.py:75
  45.3 0.0 collective-permute-done.11.refs_9_
  45.3 2.4 %collective-permute-start.13 = (f32[8,4,128]{2,0,1:T(8,128)S(1)}, f32[8,4,128]{2,0,1:T(8,128)S(1)}, u32[]{:S(2)}, u32[]{:S(2)}) collective-permute-start(f32[8,4,128]{2,0,1:T(8,128)S(1)} %bitcast.47), channel_id=1, source_target_pairs={{0,16},{2,18},{4,20},{6,22},{8,24},{10,26},{12,28},{14,30},{16,0},... | collective-permute-start | bytes 49160 | tf_op jit(solution)/shard_map/ppermute | solution.py:24
  47.8 0.5 collective-permute-start.17
  48.3 3.1 %collective-permute-start.18 = (bf16[128,2048]{1,0:T(8,128)(2,1)S(1)}, bf16[128,2048]{1,0:T(8,128)(2,1)S(1)}, u32[]{:S(2)}, u32[]{:S(2)}) collective-permute-start(bf16[128,2048]{1,0:T(8,128)(2,1)S(1)} %collective-permute-done.10.refs_11_), channel_id=1, source_target_pairs={{0,4},{2,6},{4,0},{6,2},{8,12},{10,14},{12,8},{14,10},{16,20},{18,... | collective-permute-start | bytes 1572872 | tf_op jit(solution)/shard_map/ppermute | solution.py:75
  51.3 4.9 %collective-permute-done.13 = f32[8,4,128]{2,0,1:T(8,128)S(1)} collective-permute-done((f32[8,4,128]{2,0,1:T(8,128)S(1)}, f32[8,4,128]{2,0,1:T(8,128)S(1)}, u32[]{:S(2)}, u32[]{:S(2)}) %collective-permute-start.13) | collective-permute-done | bytes 16416 | tf_op jit(solution)/shard_map/ppermute | solution.py:24
  56.3 0.0 collective-permute-done.8.refs_12_
  56.3 2.0 %collective-permute-start.14 = (bf16[128,2048]{1,0:T(8,128)(2,1)S(1)}, bf16[128,2048]{1,0:T(8,128)(2,1)S(1)}, u32[]{:S(2)}, u32[]{:S(2)}) collective-permute-start(bf16[128,2048]{1,0:T(8,128)(2,1)S(1)} %collective-permute-done.8.refs_12_), channel_id=1, source_target_pairs={{0,8},{2,18},{4,12},{6,22},{8,24},{10,2},{12,28},{14,6},{16,0},{18... | collective-permute-start | bytes 1572872 | tf_op jit(solution)/shard_map/ppermute | solution.py:75
  58.2 1.4 %collective-permute-start.15 = (bf16[128,2048]{1,0:T(8,128)(2,1)S(1)}, bf16[128,2048]{1,0:T(8,128)(2,1)S(1)}, u32[]{:S(2)}, u32[]{:S(2)}) collective-permute-start(bf16[128,2048]{1,0:T(8,128)(2,1)S(1)} %collective-permute-done.8.refs_12_), channel_id=1, source_target_pairs={{0,4},{2,6},{4,0},{6,2},{8,12},{10,14},{12,8},{14,10},{16,20},{18,... | collective-permute-start | bytes 1572872 | tf_op jit(solution)/shard_map/ppermute | solution.py:75
  59.6 0.1 fusion.9
  59.7 0.3 select_reduce_fusion.1
  60.1 0.1 broadcast_compare_fusion
  60.2 0.1 select_reduce_fusion.5
  60.3 0.7 select_reduce_fusion
  60.9 0.1 slice_reduce_fusion
  61.1 0.1 select_reduce_fusion.2
  61.2 0.1 select_reduce_fusion.4
  61.3 0.1 broadcast_in_dim.204
  61.4 0.1 eq.113
  61.5 0.1 collective-permute-start.16
  61.6 7.6 %shard_map.112 = (f32[896,2048]{1,0:T(8,128)S(1)}, bf16[1280,2048]{1,0:T(8,128)(2,1)S(1)}, f32[16,1,2048]{2,1,0:T(1,128)S(1)}) custom-call(s32[32]{0:T(128)S(1)} %fusion.6.owners, s32[1]{0:T(128)} %constant.68.clone.1.where, bf16[896,2048]{1,0:T(8,128)(2,1)S(1)} %get-tuple-element.80.refs_0_, f32[8,2048]{1,0:T(8,128)S(1)} %select_maximum_fusion.refs_1_, ...), custom_call_target="tpu_custom_call" | custom-call | flops 46976204800 | bytes 86376448 | tf_op jit(solution)/shard_map/pallas_call | solution.py:307
  69.2 0.6 select_reduce_fusion.3
  69.8 3.0 %collective-permute-done.17.refs_5_ = bf16[128,2048]{1,0:T(8,128)(2,1)S(1)} collective-permute-done((bf16[128,2048]{1,0:T(8,128)(2,1)S(1)}, bf16[128,2048]{1,0:T(8,128)(2,1)S(1)}, u32[]{:S(2)}, u32[]{:S(2)}) %collective-permute-start.17) | collective-permute-done | bytes 524320 | tf_op jit(solution)/shard_map/ppermute | solution.py:75
  72.9 2.9 %collective-permute-done.14.refs_6_ = bf16[128,2048]{1,0:T(8,128)(2,1)S(1)} collective-permute-done((bf16[128,2048]{1,0:T(8,128)(2,1)S(1)}, bf16[128,2048]{1,0:T(8,128)(2,1)S(1)}, u32[]{:S(2)}, u32[]{:S(2)}) %collective-permute-start.14) | collective-permute-done | bytes 524320 | tf_op jit(solution)/shard_map/ppermute | solution.py:75
  75.7 1.1 %collective-permute-start.19 = (bf16[128,2048]{1,0:T(8,128)(2,1)S(1)}, bf16[128,2048]{1,0:T(8,128)(2,1)S(1)}, u32[]{:S(2)}, u32[]{:S(2)}) collective-permute-start(bf16[128,2048]{1,0:T(8,128)(2,1)S(1)} %collective-permute-done.18.refs_3_), channel_id=1, source_target_pairs={{0,16},{2,10},{4,20},{6,14},{8,0},{10,26},{12,4},{14,30},{16,24},{... | collective-permute-start | bytes 1572872 | tf_op jit(solution)/shard_map/ppermute | solution.py:75
  76.8 1.7 %collective-permute-start.20 = (bf16[128,2048]{1,0:T(8,128)(2,1)S(1)}, bf16[128,2048]{1,0:T(8,128)(2,1)S(1)}, u32[]{:S(2)}, u32[]{:S(2)}) collective-permute-start(bf16[128,2048]{1,0:T(8,128)(2,1)S(1)} %collective-permute-done.14.refs_6_), channel_id=1, source_target_pairs={{0,4},{2,6},{4,0},{6,2},{8,12},{10,14},{12,8},{14,10},{16,20},{18,... | collective-permute-start | bytes 1572872 | tf_op jit(solution)/shard_map/ppermute | solution.py:75
  78.6 8.1 %shard_map.113 = (f32[896,2048]{1,0:T(8,128)S(1)}, bf16[512,2048]{1,0:T(8,128)(2,1)S(1)}, f32[16,1,2048]{2,1,0:T(1,128)S(1)}) custom-call(s32[32]{0:T(128)S(1)} %fusion.6.owners, s32[1]{0:T(128)} %constant.68.clone.1.where, bf16[896,2048]{1,0:T(8,128)(2,1)S(1)} %collective-permute-done.16.refs_0_, f32[8,2048]{1,0:T(8,128)S(1)} %select_maximum_fusion.refs_1_, ...), custom_call_target="tpu_custom_call" | custom-call | flops 6576668672 | bytes 21561344 | tf_op jit(solution)/shard_map/pallas_call | solution.py:307
  86.7 2.3 %collective-permute-done.19.refs_3_ = bf16[128,2048]{1,0:T(8,128)(2,1)S(1)} collective-permute-done((bf16[128,2048]{1,0:T(8,128)(2,1)S(1)}, bf16[128,2048]{1,0:T(8,128)(2,1)S(1)}, u32[]{:S(2)}, u32[]{:S(2)}) %collective-permute-start.19) | collective-permute-done | bytes 524320 | tf_op jit(solution)/shard_map/ppermute | solution.py:75
  89.0 2.4 %shard_map.114 = (bf16[896,2048]{1,0:T(8,128)(2,1)S(1)}, bf16[256,2048]{1,0:T(8,128)(2,1)S(1)}, f32[1,2048]{1,0:T(1,128)S(1)}) custom-call(s32[32]{0:T(128)S(1)} %fusion.6.owners, s32[1]{0:T(128)} %constant.68.clone.1.where, bf16[896,2048]{1,0:T(8,128)(2,1)S(1)} %collective-permute-done.16.refs_0_, f32[8,2048]{1,0:T(8,128)S(1)} %select_maximum_fusion.refs_1_, ...), custom_call_target="tpu_custom_call" | custom-call | flops 939524096 | bytes 12517376 | tf_op jit(solution)/shard_map/pallas_call | solution.py:307
  91.5 0.1 collective-permute-start.22
  91.6 0.5 collective-permute-start.21
  92.1 4.5 %shard_map.115.whole = bf16[896,4096]{1,0:T(8,128)(2,1)} custom-call(s32[32]{0:T(128)S(1)} %fusion.6.owners, s32[1]{0:T(128)} %bitcast.where, bf16[896,2048]{1,0:T(8,128)(2,1)S(1)} %get-tuple-element.80.refs_0_, bf16[256,2048]{1,0:T(8,128)(2,1)S(1)} %get-tuple-element.109.refs_1_, bf16[512,2048]{1,0:T(8,128)(2,1)S(1)} %get-tuple-element.110.refs_2_, ...), custom_call_target="tpu_custom_call" | custom-call | flops 2818572288 | bytes 15532032 | tf_op jit(solution)/shard_map/pallas_call | solution.py:307
  96.6 1.4 %collective-permute-done.21 = f32[2048]{0:T(1024)S(1)} collective-permute-done((f32[2048]{0:T(1024)S(1)}, f32[2048]{0:T(1024)S(1)}, u32[]{:S(2)}, u32[]{:S(2)}) %collective-permute-start.21) | collective-permute-done | bytes 8224 | tf_op jit(solution)/shard_map/ppermute | solution.py:393
  98.0 0.6 convert_multiply_fusion.2
  98.6 1.9 %shard_map.116 = bf16[896,4096]{1,0:T(8,128)(2,1)} custom-call(s32[1]{0:T(128)S(6)} %sub.26.where, bf16[896,2048]{1,0:T(8,128)(2,1)S(1)} %collective-permute-done.22.part, bf16[896,4096]{1,0:T(8,128)(2,1)} %shard_map.115.whole), custom_call_target="tpu_custom_call", output_to_operand_aliasing={{}: (2, {})} | custom-call | bytes 7340032 | tf_op jit(solution)/shard_map/pallas_call | solution.py:348
  (24 shorter events, 0.2 us)
Async XLA Ops:
  1.9 18.3 %collective-permute-start.3 = (bf16[128,2048]{1,0:T(8,128)(2,1)S(1)}, bf16[128,2048]{1,0:T(8,128)(2,1)S(1)}, u32[]{:S(2)}, u32[]{:S(2)}) collective-permute-start(bf16[128,2048]{1,0:T(8,128)(2,1)S(1)} %get-tuple-element.61.refs_3_), channel_id=1, source_target_pairs={{0,16},{2,10},{4,20},{6,14},{8,0},{10,26},{12,4},{14,30},{16,24},{... | collective-permute-start | bytes 1572872 | tf_op jit(solution)/shard_map/ppermute | solution.py:75
  6.0 14.2 %collective-permute-start.4 = (bf16[128,2048]{1,0:T(8,128)(2,1)S(1)}, bf16[128,2048]{1,0:T(8,128)(2,1)S(1)}, u32[]{:S(2)}, u32[]{:S(2)}) collective-permute-start(bf16[128,2048]{1,0:T(8,128)(2,1)S(1)} %get-tuple-element.61.refs_3_), channel_id=1, source_target_pairs={{0,4},{2,6},{4,0},{6,2},{8,12},{10,14},{12,8},{14,10},{16,20},{18,... | collective-permute-start | bytes 1572872 | tf_op jit(solution)/shard_map/ppermute | solution.py:75
  7.5 2.1 %collective-permute-start = (bf16[128,2048]{1,0:T(8,128)(2,1)S(1)}, bf16[128,2048]{1,0:T(8,128)(2,1)S(1)}, u32[]{:S(2)}, u32[]{:S(2)}) collective-permute-start(bf16[128,2048]{1,0:T(8,128)(2,1)S(1)} %get-tuple-element.58), channel_id=1, source_target_pairs={{0,2},{2,0},{4,6},{6,4},{8,10},{10,8},{12,14},{14,12},{16,18},{18,... | collective-permute-start | bytes 1572872 | tf_op jit(solution)/shard_map/ppermute | solution.py:75
  11.3 3.7 %collective-permute-start.5 = (f32[4,128]{1,0:T(4,128)S(1)}, f32[4,128]{1,0:T(4,128)S(1)}, u32[]{:S(2)}, u32[]{:S(2)}) collective-permute-start(f32[4,128]{1,0:T(4,128)S(1)} %pad_maximum_fusion.2), channel_id=1, source_target_pairs={{0,1},{1,0},{2,3},{3,2},{4,5},{5,4},{6,7},{7,6},{8,9},{9,8},{10,11... | collective-permute-start | bytes 6152 | tf_op jit(solution)/shard_map/ppermute | solution.py:18
  12.9 18.2 %collective-permute-start.1 = (bf16[128,2048]{1,0:T(8,128)(2,1)S(1)}, bf16[128,2048]{1,0:T(8,128)(2,1)S(1)}, u32[]{:S(2)}, u32[]{:S(2)}) collective-permute-start(bf16[128,2048]{1,0:T(8,128)(2,1)S(1)} %collective-permute-done.refs_4_), channel_id=1, source_target_pairs={{0,8},{2,18},{4,12},{6,22},{8,24},{10,2},{12,28},{14,6},{16,0},{18... | collective-permute-start | bytes 1572872 | tf_op jit(solution)/shard_map/ppermute | solution.py:75
  13.7 17.4 %collective-permute-start.2 = (bf16[128,2048]{1,0:T(8,128)(2,1)S(1)}, bf16[128,2048]{1,0:T(8,128)(2,1)S(1)}, u32[]{:S(2)}, u32[]{:S(2)}) collective-permute-start(bf16[128,2048]{1,0:T(8,128)(2,1)S(1)} %collective-permute-done.refs_4_), channel_id=1, source_target_pairs={{0,4},{2,6},{4,0},{6,2},{8,12},{10,14},{12,8},{14,10},{16,20},{18,... | collective-permute-start | bytes 1572872 | tf_op jit(solution)/shard_map/ppermute | solution.py:75
  20.2 1.2 %collective-permute-start.6 = (f32[1,4,128]{2,1,0:T(4,128)S(1)}, f32[1,4,128]{2,1,0:T(4,128)S(1)}, u32[]{:S(2)}, u32[]{:S(2)}) collective-permute-start(f32[1,4,128]{2,1,0:T(4,128)S(1)} %add_bitcast_fusion), channel_id=1, source_target_pairs={{0,2},{2,0},{4,6},{6,4},{8,10},{10,8},{12,14},{14,12},{16,18},{18,... | collective-permute-start | bytes 6152 | tf_op jit(solution)/shard_map/ppermute | solution.py:24
  21.4 9.3 %collective-permute-start.7 = (f32[2,4,128]{2,0,1:T(2,128)S(1)}, f32[2,4,128]{2,0,1:T(2,128)S(1)}, u32[]{:S(2)}, u32[]{:S(2)}) collective-permute-start(f32[2,4,128]{2,0,1:T(2,128)S(1)} %broadcast_select_fusion.3), channel_id=1, source_target_pairs={{0,8},{2,10},{4,12},{6,14},{8,0},{10,2},{12,4},{14,6},{16,24},{18,... | collective-permute-start | bytes 12296 | tf_op jit(solution)/shard_map/ppermute | solution.py:24
  23.6 21.7 %collective-permute-start.10 = (bf16[128,2048]{1,0:T(8,128)(2,1)S(1)}, bf16[128,2048]{1,0:T(8,128)(2,1)S(1)}, u32[]{:S(2)}, u32[]{:S(2)}) collective-permute-start(bf16[128,2048]{1,0:T(8,128)(2,1)S(1)} %collective-permute-done.3.refs_7_), channel_id=1, source_target_pairs={{0,16},{2,10},{4,20},{6,14},{8,0},{10,26},{12,4},{14,30},{16,24},{... | collective-permute-start | bytes 1572872 | tf_op jit(solution)/shard_map/ppermute | solution.py:75
  27.6 17.8 %collective-permute-start.11 = (bf16[128,2048]{1,0:T(8,128)(2,1)S(1)}, bf16[128,2048]{1,0:T(8,128)(2,1)S(1)}, u32[]{:S(2)}, u32[]{:S(2)}) collective-permute-start(bf16[128,2048]{1,0:T(8,128)(2,1)S(1)} %collective-permute-done.3.refs_7_), channel_id=1, source_target_pairs={{0,4},{2,6},{4,0},{6,2},{8,12},{10,14},{12,8},{14,10},{16,20},{18,... | collective-permute-start | bytes 1572872 | tf_op jit(solution)/shard_map/ppermute | solution.py:75
  31.2 12.6 %collective-permute-start.12 = (f32[2,2,4,128]{3,1,0,2:T(2,128)S(1)}, f32[2,2,4,128]{3,1,0,2:T(2,128)S(1)}, u32[]{:S(2)}, u32[]{:S(2)}) collective-permute-start(f32[2,2,4,128]{3,1,0,2:T(2,128)S(1)} %broadcast_select_fusion), channel_id=1, source_target_pairs={{0,4},{2,6},{4,0},{6,2},{8,12},{10,14},{12,8},{14,10},{16,20},{18,... | collective-permute-start | bytes 24584 | tf_op jit(solution)/shard_map/ppermute | solution.py:24
  32.4 23.9 %collective-permute-start.8 = (bf16[128,2048]{1,0:T(8,128)(2,1)S(1)}, bf16[128,2048]{1,0:T(8,128)(2,1)S(1)}, u32[]{:S(2)}, u32[]{:S(2)}) collective-permute-start(bf16[128,2048]{1,0:T(8,128)(2,1)S(1)} %collective-permute-done.1.refs_8_), channel_id=1, source_target_pairs={{0,8},{2,18},{4,12},{6,22},{8,24},{10,2},{12,28},{14,6},{16,0},{18... | collective-permute-start | bytes 1572872 | tf_op jit(solution)/shard_map/ppermute | solution.py:75
  33.3 23.0 %collective-permute-start.9 = (bf16[128,2048]{1,0:T(8,128)(2,1)S(1)}, bf16[128,2048]{1,0:T(8,128)(2,1)S(1)}, u32[]{:S(2)}, u32[]{:S(2)}) collective-permute-start(bf16[128,2048]{1,0:T(8,128)(2,1)S(1)} %collective-permute-done.1.refs_8_), channel_id=1, source_target_pairs={{0,4},{2,6},{4,0},{6,2},{8,12},{10,14},{12,8},{14,10},{16,20},{18,... | collective-permute-start | bytes 1572872 | tf_op jit(solution)/shard_map/ppermute | solution.py:75
  45.3 10.9 %collective-permute-start.13 = (f32[8,4,128]{2,0,1:T(8,128)S(1)}, f32[8,4,128]{2,0,1:T(8,128)S(1)}, u32[]{:S(2)}, u32[]{:S(2)}) collective-permute-start(f32[8,4,128]{2,0,1:T(8,128)S(1)} %bitcast.47), channel_id=1, source_target_pairs={{0,16},{2,18},{4,20},{6,22},{8,24},{10,26},{12,28},{14,30},{16,0},... | collective-permute-start | bytes 49160 | tf_op jit(solution)/shard_map/ppermute | solution.py:24
  47.8 25.1 %collective-permute-start.17 = (bf16[128,2048]{1,0:T(8,128)(2,1)S(1)}, bf16[128,2048]{1,0:T(8,128)(2,1)S(1)}, u32[]{:S(2)}, u32[]{:S(2)}) collective-permute-start(bf16[128,2048]{1,0:T(8,128)(2,1)S(1)} %collective-permute-done.10.refs_11_), channel_id=1, source_target_pairs={{0,16},{2,10},{4,20},{6,14},{8,0},{10,26},{12,4},{14,30},{16,24},{... | collective-permute-start | bytes 1572872 | tf_op jit(solution)/shard_map/ppermute | solution.py:75
  48.3 24.6 %collective-permute-start.18 = (bf16[128,2048]{1,0:T(8,128)(2,1)S(1)}, bf16[128,2048]{1,0:T(8,128)(2,1)S(1)}, u32[]{:S(2)}, u32[]{:S(2)}) collective-permute-start(bf16[128,2048]{1,0:T(8,128)(2,1)S(1)} %collective-permute-done.10.refs_11_), channel_id=1, source_target_pairs={{0,4},{2,6},{4,0},{6,2},{8,12},{10,14},{12,8},{14,10},{16,20},{18,... | collective-permute-start | bytes 1572872 | tf_op jit(solution)/shard_map/ppermute | solution.py:75
  56.3 19.4 %collective-permute-start.14 = (bf16[128,2048]{1,0:T(8,128)(2,1)S(1)}, bf16[128,2048]{1,0:T(8,128)(2,1)S(1)}, u32[]{:S(2)}, u32[]{:S(2)}) collective-permute-start(bf16[128,2048]{1,0:T(8,128)(2,1)S(1)} %collective-permute-done.8.refs_12_), channel_id=1, source_target_pairs={{0,8},{2,18},{4,12},{6,22},{8,24},{10,2},{12,28},{14,6},{16,0},{18... | collective-permute-start | bytes 1572872 | tf_op jit(solution)/shard_map/ppermute | solution.py:75
  58.2 17.5 %collective-permute-start.15 = (bf16[128,2048]{1,0:T(8,128)(2,1)S(1)}, bf16[128,2048]{1,0:T(8,128)(2,1)S(1)}, u32[]{:S(2)}, u32[]{:S(2)}) collective-permute-start(bf16[128,2048]{1,0:T(8,128)(2,1)S(1)} %collective-permute-done.8.refs_12_), channel_id=1, source_target_pairs={{0,4},{2,6},{4,0},{6,2},{8,12},{10,14},{12,8},{14,10},{16,20},{18,... | collective-permute-start | bytes 1572872 | tf_op jit(solution)/shard_map/ppermute | solution.py:75
  61.5 14.2 %collective-permute-start.16 = (bf16[896,2048]{1,0:T(8,128)(2,1)}, bf16[896,2048]{1,0:T(8,128)(2,1)S(1)}, u32[]{:S(2)}, u32[]{:S(2)}) collective-permute-start(bf16[896,2048]{1,0:T(8,128)(2,1)} %get-tuple-element.78), channel_id=1, source_target_pairs={{0,2},{2,0},{4,6},{6,4},{8,10},{10,8},{12,14},{14,12},{16,18},{18,... | collective-permute-start | bytes 11010056 | tf_op jit(solution)/shard_map/ppermute | solution.py:75
  75.7 13.3 %collective-permute-start.19 = (bf16[128,2048]{1,0:T(8,128)(2,1)S(1)}, bf16[128,2048]{1,0:T(8,128)(2,1)S(1)}, u32[]{:S(2)}, u32[]{:S(2)}) collective-permute-start(bf16[128,2048]{1,0:T(8,128)(2,1)S(1)} %collective-permute-done.18.refs_3_), channel_id=1, source_target_pairs={{0,16},{2,10},{4,20},{6,14},{8,0},{10,26},{12,4},{14,30},{16,24},{... | collective-permute-start | bytes 1572872 | tf_op jit(solution)/shard_map/ppermute | solution.py:75
  76.8 12.2 %collective-permute-start.20 = (bf16[128,2048]{1,0:T(8,128)(2,1)S(1)}, bf16[128,2048]{1,0:T(8,128)(2,1)S(1)}, u32[]{:S(2)}, u32[]{:S(2)}) collective-permute-start(bf16[128,2048]{1,0:T(8,128)(2,1)S(1)} %collective-permute-done.14.refs_6_), channel_id=1, source_target_pairs={{0,4},{2,6},{4,0},{6,2},{8,12},{10,14},{12,8},{14,10},{16,20},{18,... | collective-permute-start | bytes 1572872 | tf_op jit(solution)/shard_map/ppermute | solution.py:75
  91.5 7.1 %collective-permute-start.22 = (bf16[896,2048]{1,0:T(8,128)(2,1)S(1)}, bf16[896,2048]{1,0:T(8,128)(2,1)S(1)}, u32[]{:S(2)}, u32[]{:S(2)}) collective-permute-start(bf16[896,2048]{1,0:T(8,128)(2,1)S(1)} %get-tuple-element.107), channel_id=1, source_target_pairs={{0,2},{2,0},{4,6},{6,4},{8,10},{10,8},{12,14},{14,12},{16,18},{18,... | collective-permute-start | bytes 11010056 | tf_op jit(solution)/shard_map/ppermute | solution.py:393
  91.6 6.4 %collective-permute-start.21 = (f32[2048]{0:T(1024)S(1)}, f32[2048]{0:T(1024)S(1)}, u32[]{:S(2)}, u32[]{:S(2)}) collective-permute-start(f32[2048]{0:T(1024)S(1)} %bitcast.39), channel_id=1, source_target_pairs={{0,2},{2,0},{4,6},{6,4},{8,10},{10,8},{12,14},{14,12},{16,18},{18,... | collective-permute-start | bytes 24584 | tf_op jit(solution)/shard_map/ppermute | solution.py:393
  92.1 5.9 %copy-start = (bf16[4096]{0:T(1024)(128)(2,1)S(1)}, bf16[4096]{0:T(1024)(128)(2,1)}, u32[]{:S(2)}) copy-start(bf16[4096]{0:T(1024)(128)(2,1)} %param.10) | copy-start | bytes 24580

commit v11 on v10

--- a/solution.py
+++ b/solution.py
@@ -24,16 +24,34 @@
     return lax.ppermute(x, axis, [(i, i ^ bit) for i in range(lax.axis_size(axis))])
 
 
-def butterfly_merge(x, other, bit, low):
-    low = low[bit]
+def butterfly_merge(x, others, bit, low):
+    if bit == 4:
+        out = others[2][None]
+        for mask, part in zip(low[4], (x, *others[:2])):
+            out = jnp.where(mask[:, None, None, None], part[None], out)
+        return out
+    (other,) = others
     if bit == 1:
-        return jnp.where(low[:, None, None], x, other)
-    if bit == 4:
-        return jnp.where(low[:, None, None, None], x[None], other[None])
+        return jnp.where(low[1][:, None, None], x, other)
+    first, second = jnp.where(low[bit], x, other), jnp.where(low[bit], other, x)
     if bit == 2:
-        both = jnp.stack([jnp.where(low, x, other), jnp.where(low, other, x)], axis=1)
-        return both.reshape(-1, *x.shape[2:])
-    return jnp.concatenate([jnp.where(low, x, other), jnp.where(low, other, x)])
+        return jnp.stack([first, second], axis=1).reshape(-1, *x.shape[2:])
+    return jnp.concatenate([first, second])
+
+
+def settle_kernel(x, out):
+    out[...] = x[...]
+
+
+def settle(x):
+    inside = pl.BlockSpec(memory_space=pltpu.VMEM)
+    return pl.pallas_call(
+        settle_kernel,
+        in_specs=[inside],
+        out_specs=inside,
+        out_shape=jax.ShapeDtypeStruct(x.shape, x.dtype),
+        cost_estimate=pl.CostEstimate(flops=2 * 10**9, bytes_accessed=1, transcendentals=0),
+    )(x)
 
 
 class Paths:
@@ -91,20 +109,22 @@
     f.have[0, 0, 0] = cut(core_index)
     have = f.have
     names = list(scalars)
-    low = lambda: {1 << n: have["low %d" % n] for n in range(paths.count.bit_length() - 1)}
-
-    bits = [1, 4, 2] + [8 << n for n in range(paths.count.bit_length() - 4)]
+    bits = [1, 4, 2] + [16 << n for n in range(paths.count.bit_length() - 5)]
 
     def facts_send():
-        have["other facts"] = butterfly_send(have["facts"], "seq", bits[0])
-
-    def facts_merge():
-        have["facts"] = butterfly_merge(have["facts"], have["other facts"], bits.pop(0), low())
+        steps = (4, 8, 12) if bits[0] == 4 else (bits[0],)
+        for n, step in enumerate(steps):
+            have["facts %d" % n] = butterfly_send(have["facts"], "seq", step)
+        return ["facts %d" % n for n in range(len(steps))]
+
+    def facts_merge(arrived):
+        bit = bits.pop(0)
+        low = {bit: [have["ring %d" % n] for n in range(3)] if bit == 4 else have["low %d" % bit]}
+        have["facts"] = butterfly_merge(have["facts"], [have[name] for name in arrived], bit, low)
 
     def facts_step():
         if bits:
-            facts_send()
-            facts_merge()
+            facts_merge(facts_send())
 
     f.event([], [((1, 0, 0), (0, 0, 0), ring[0]), ((0, 1, 0), (0, 0, 0), across), ((0, 0, 1), "away", core)])
     f.event(
@@ -119,12 +139,15 @@
         [((2, 0, 0), (1, 0, 0), ring[0]), ((1, 1, 0), (1, 0, 0), across)],
     )
     facts_step()
-    facts_send()
-    f.event([(1, 0, 1), (0, 1, 1), "facts", "other facts"], [((2, 0, 1), (1, 0, 1), ring[1]), ((1, 1, 1), (1, 0, 1), across)])
-    facts_merge()
+    arriving = facts_send()
+    f.event([(1, 0, 1), (0, 1, 1), "facts", *arriving], [((2, 0, 1), (1, 0, 1), ring[1]), ((1, 1, 1), (1, 0, 1), across)])
+    facts_merge(arriving)
     for k in range(2, m):
         for kind in range(2):
-            facts_step()
+            if bits:
+                facts_step()
+            elif k < m - 1:
+                have["facts"] = settle(have["facts"])
             if k < m - 1:
                 sends = [((k + 1, 0, kind), (k, 0, kind), ring[kind]), ((k, 1, kind), (k, 0, kind), across)]
             elif kind == 0:
@@ -439,7 +462,9 @@
         scalars = {"core": mine, "me": me, "first core": mine == 0, "where": where, "elsewhere": 1 - where}
         for n in range(shards.bit_length() - 1):
             low = (me >> n) % 2 == 0
-            scalars["low %d" % n] = (jnp.arange(2) == 0) == low if n in (0, 2) else low
+            scalars["low %d" % (1 << n)] = (jnp.arange(2) == 0) == low if n == 0 else low
+        for n in range(3):
+            scalars["ring %d" % n] = (jnp.arange(4) ^ (me >> 2) % 4) == n
         scalars["owners"] = owners
         have = run_plan(stream, hidden, scalars, own_facts, paths, lambda hidden: pick(hidden, owners, tok), early_own, early_other)
         out, dstream, grad_head = product(

time: 102 us -> 108 us (1.059)
  waiting for transfers between devices: 27.5 us -> 21.5 us
  local copies, waits for them, and re-layouts: 2.23 us -> 7.94 us
  Pallas kernels: 28.9 us -> 33.1 us
  other arithmetic: 6.19 us -> 9.51 us
  starting transfers between devices: 34.7 us -> 33.6 us
    unnamed x2 -> x12, local copies, waits for them, and re-layouts: 0.01 us -> 5.7 us
    ppermute x16, starting transfers between devices: 26.8 us -> 23.4 us  [event(): self.have[name] = lax.ppermute(self.have[source], 'seq', pairs)]
    ppermute x4 -> x5, waiting for transfers between devices: 14.5 us -> 11.5 us  [butterfly_send(): lax.ppermute(x, axis, [(i, i ^ bit) for i in range(lax.axis_size(axis))])]
    ppermute x16, waiting for transfers between devices: 10.9 us -> 8.03 us  [event(): self.have[name] = lax.ppermute(self.have[source], 'seq', pairs)]
    pallas_call x4, Pallas kernels: 22.7 us -> 25.5 us  [product(): pl.pallas_call(functools.partial(product_kernel, tok, count, first, len(g...]
    ppermute x4 -> x5, starting transfers between devices: 5.84 us -> 8.16 us  [butterfly_send(): lax.ppermute(x, axis, [(i, i ^ bit) for i in range(lax.axis_size(axis))])]
    mul x2, other arithmetic: 0.05 us -> 1.74 us  [early_own(): coefs = jnp.stack([error * scale, error * pull]).reshape(2, shards * tok)]
    pallas_call x0 -> x1, Pallas kernels: none -> 1.36 us  [settle(): pl.pallas_call(settle_kernel, in_specs=[inside], out_specs=inside, out_sh...]
  transfers between devices with their start and end apart: 23 -> 24, of which waited for: 11 -> 11; matrix products, arithmetic and copies ran while one was open for 7% -> 10% of each run, Pallas kernels for 24% -> 27%
where the time goes in v11:
time: 108 us; the launch traced here: 107 us
  starting transfers between devices  33.6 us (31%)
  Pallas kernels  33.1 us (31%)
  waiting for transfers between devices  21.5 us (20%)
  other arithmetic  9.51 us (9%)
  local copies, waits for them, and re-layouts  7.94 us (7%)
    pallas_call x4, Pallas kernels, product(): pl.pallas_call(functools.partial(product_kernel, tok, count, first, len(g...  25.5 us
    ppermute x16, starting transfers between devices, event(): self.have[name] = lax.ppermute(self.have[source], 'seq', pairs)  23.4 us
    ppermute x5, waiting for transfers between devices, butterfly_send(): lax.ppermute(x, axis, [(i, i ^ bit) for i in range(lax.axis_size(axis))])  11.5 us
    ppermute x5, starting transfers between devices, butterfly_send(): lax.ppermute(x, axis, [(i, i ^ bit) for i in range(lax.axis_size(axis))])  8.16 us
    ppermute x16, waiting for transfers between devices, event(): self.have[name] = lax.ppermute(self.have[source], 'seq', pairs)  8.03 us
    unnamed x12, local copies, waits for them, and re-layouts  5.7 us
    pallas_call x1, Pallas kernels, pick(): pl.pallas_call(functools.partial(pick_kernel, tok), grid_spec=pltpu.Prefe...  4.35 us
  transfers between devices with their start and end apart: 24, of which 11 were waited for; matrix products, arithmetic and copies ran while one was open for 10% of the time, Pallas kernels for 27%

profile of v11, /device:TPU:0, one launch (start us, length us, event | category | flops | bytes accessed | tf_op | source)
XLA Modules:
  0.0 106.8 jit_solution(9778584950411886432)
XLA Ops:
  0.7 1.3 %constant_dynamic-slice_fusion.1 = (bf16[128,2048]{1,0:T(8,128)(2,1)S(1)}, bf16[128,2048]{1,0:T(8,128)(2,1)S(1)}) fusion(bf16[128,4096]{1,0:T(8,128)(2,1)} %param.8, s32[]{:T(128)S(6)} %select_n.132, s32[]{:T(128)S(6)} %select_n.131), kind=kLoop, calls=%fused_computation.40 | loop fusion | bytes 2097160 | tf_op jit(solution)/shard_map/dynamic_slice | solution.py:106
  1.9 4.1 %collective-permute-start.3 = (bf16[128,2048]{1,0:T(8,128)(2,1)S(1)}, bf16[128,2048]{1,0:T(8,128)(2,1)S(1)}, u32[]{:S(2)}, u32[]{:S(2)}) collective-permute-start(bf16[128,2048]{1,0:T(8,128)(2,1)S(1)} %get-tuple-element.64.refs_3_), channel_id=1, source_target_pairs={{0,16},{2,10},{4,20},{6,14},{8,0},{10,26},{12,4},{14,30},{16,24},{... | collective-permute-start | bytes 1572872 | tf_op jit(solution)/shard_map/ppermute | solution.py:93
  6.0 1.5 %collective-permute-start.4 = (bf16[128,2048]{1,0:T(8,128)(2,1)S(1)}, bf16[128,2048]{1,0:T(8,128)(2,1)S(1)}, u32[]{:S(2)}, u32[]{:S(2)}) collective-permute-start(bf16[128,2048]{1,0:T(8,128)(2,1)S(1)} %get-tuple-element.64.refs_3_), channel_id=1, source_target_pairs={{0,4},{2,6},{4,0},{6,2},{8,12},{10,14},{12,8},{14,10},{16,20},{18,... | collective-permute-start | bytes 1572872 | tf_op jit(solution)/shard_map/ppermute | solution.py:93
  7.5 0.0 collective-permute-start
  7.6 0.7 fusion.5.owners
  8.3 0.7 multiply_bitcast_fusion
  9.0 0.7 convert_multiply_fusion.3
  9.7 1.7 %fusion = (f32[128]{0:T(128)S(1)}, f32[128]{0:T(128)S(1)}) fusion(bf16[128,4096]{1,0:T(8,128)(2,1)} %param.8, f32[4096]{0:T(1024)S(1)} %convert_multiply_fusion.3), kind=kLoop, calls=%fused_computation.2 | loop fusion | flops 2621184 | bytes 1065984 | tf_op jit(solution)/shard_map/reduce_sum | solution.py:429
  11.4 1.6 %collective-permute-start.5 = (f32[4,128]{1,0:T(4,128)S(1)}, f32[4,128]{1,0:T(4,128)S(1)}, u32[]{:S(2)}, u32[]{:S(2)}) collective-permute-start(f32[4,128]{1,0:T(4,128)S(1)} %pad_maximum_fusion.1), channel_id=1, source_target_pairs={{0,1},{1,0},{2,3},{3,2},{4,5},{5,4},{6,7},{7,6},{8,9},{9,8},{10,11... | collective-permute-start | bytes 6152 | tf_op jit(solution)/shard_map/ppermute | solution.py:18
  13.0 0.9 collective-permute-start.1
  13.9 0.5 collective-permute-start.2
  14.4 0.7 collective-permute-done.5
  15.1 4.3 %shard_map.111 = (bf16[896,2048]{1,0:T(8,128)(2,1)S(1)}, bf16[896,2048]{1,0:T(8,128)(2,1)}) custom-call(s32[32]{0:T(128)S(1)} %fusion.5.owners, bf16[896,2048]{1,0:T(8,128)(2,1)} %hidden), custom_call_target="tpu_custom_call" | custom-call | bytes 1 | tf_op jit(solution)/shard_map/pallas_call | solution.py:211
  19.4 1.8 %copy-done = bf16[896,2048]{1,0:T(8,128)(2,1)} copy-done((bf16[896,2048]{1,0:T(8,128)(2,1)}, bf16[896,2048]{1,0:T(8,128)(2,1)S(1)}, u32[]{:S(2)}) %copy-start) | copy-done | bytes 3670040
  21.3 1.1 %collective-permute-done.6 = f32[1,4,128]{2,1,0:T(4,128)S(1)} collective-permute-done((f32[1,4,128]{2,1,0:T(4,128)S(1)}, f32[1,4,128]{2,1,0:T(4,128)S(1)}, u32[]{:S(2)}, u32[]{:S(2)}) %collective-permute-start.6) | collective-permute-done | bytes 2080 | tf_op jit(solution)/shard_map/ppermute | solution.py:24
  22.4 0.1 broadcast_select_fusion
  22.5 1.0 collective-permute-start.7
  23.5 3.9 %collective-permute-start.8 = (f32[2,4,128]{2,1,0:T(4,128)S(1)}, f32[2,4,128]{2,1,0:T(4,128)S(1)}, u32[]{:S(2)}, u32[]{:S(2)}) collective-permute-start(f32[2,4,128]{2,1,0:T(4,128)S(1)} %broadcast_select_fusion), channel_id=1, source_target_pairs={{0,16},{2,18},{4,20},{6,22},{8,24},{10,26},{12,28},{14,30},{16,0},... | collective-permute-start | bytes 12296 | tf_op jit(solution)/shard_map/ppermute | solution.py:24
  27.4 0.2 collective-permute-done.7
  27.6 3.5 %collective-permute-start.12 = (bf16[128,2048]{1,0:T(8,128)(2,1)S(1)}, bf16[128,2048]{1,0:T(8,128)(2,1)}, u32[]{:S(2)}, u32[]{:S(2)}) collective-permute-start(bf16[128,2048]{1,0:T(8,128)(2,1)S(1)} %collective-permute-done.3.refs_7_), channel_id=1, source_target_pairs={{0,16},{2,10},{4,20},{6,14},{8,0},{10,26},{12,4},{14,30},{16,24},{... | collective-permute-start | bytes 1572872 | tf_op jit(solution)/shard_map/ppermute | solution.py:93
  31.1 1.5 %collective-permute-start.13 = (bf16[128,2048]{1,0:T(8,128)(2,1)S(1)}, bf16[128,2048]{1,0:T(8,128)(2,1)S(1)}, u32[]{:S(2)}, u32[]{:S(2)}) collective-permute-start(bf16[128,2048]{1,0:T(8,128)(2,1)S(1)} %collective-permute-done.3.refs_7_), channel_id=1, source_target_pairs={{0,4},{2,6},{4,0},{6,2},{8,12},{10,14},{12,8},{14,10},{16,20},{18,... | collective-permute-start | bytes 1572872 | tf_op jit(solution)/shard_map/ppermute | solution.py:93
  32.6 0.4 collective-permute-done.9
  33.0 0.1 select_select_fusion
  33.1 3.2 %collective-permute-start.14 = (f32[4,2,4,128]{3,2,1,0:T(4,128)S(1)}, f32[4,2,4,128]{3,2,1,0:T(4,128)S(1)}, u32[]{:S(2)}, u32[]{:S(2)}) collective-permute-start(f32[4,2,4,128]{3,2,1,0:T(4,128)S(1)} %select_select_fusion), channel_id=1, source_target_pairs={{0,4},{2,6},{4,0},{6,2},{8,12},{10,14},{12,8},{14,10},{16,20},{18,... | collective-permute-start | bytes 49160 | tf_op jit(solution)/shard_map/ppermute | solution.py:24
  36.3 0.1 collective-permute-start.11
  36.5 9.8 %collective-permute-done.14 = f32[4,2,4,128]{3,2,1,0:T(4,128)S(1)} collective-permute-done((f32[4,2,4,128]{3,2,1,0:T(4,128)S(1)}, f32[4,2,4,128]{3,2,1,0:T(4,128)S(1)}, u32[]{:S(2)}, u32[]{:S(2)}) %collective-permute-start.14) | collective-permute-done | bytes 16416 | tf_op jit(solution)/shard_map/ppermute | solution.py:24
  46.3 0.1 select_bitcast_fusion.1
  46.4 0.6 pad_maximum_fusion
  47.0 1.4 %collective-permute-done.12.refs_11_ = bf16[128,2048]{1,0:T(8,128)(2,1)} collective-permute-done((bf16[128,2048]{1,0:T(8,128)(2,1)S(1)}, bf16[128,2048]{1,0:T(8,128)(2,1)}, u32[]{:S(2)}, u32[]{:S(2)}) %collective-permute-start.12) | collective-permute-done | bytes 524320 | tf_op jit(solution)/shard_map/ppermute | solution.py:93
  48.4 0.8 copy-done.3
  49.2 0.8 collective-permute-start.18
  50.0 5.2 %collective-permute-start.19 = (bf16[128,2048]{1,0:T(8,128)(2,1)}, bf16[128,2048]{1,0:T(8,128)(2,1)}, u32[]{:S(2)}, u32[]{:S(2)}) collective-permute-start(bf16[128,2048]{1,0:T(8,128)(2,1)} %collective-permute-done.12.refs_11_), channel_id=1, source_target_pairs={{0,4},{2,6},{4,0},{6,2},{8,12},{10,14},{12,8},{14,10},{16,20},{18,... | collective-permute-start | bytes 1572872 | tf_op jit(solution)/shard_map/ppermute | solution.py:93
  55.2 1.4 %shard_map.112 = f32[16,4,128]{2,1,0:T(4,128)} custom-call(f32[16,4,128]{2,1,0:T(4,128)} %bitcast.52), custom_call_target="tpu_custom_call" | custom-call | flops 2000000000 | bytes 1 | tf_op jit(solution)/shard_map/pallas_call | solution.py:48
  56.6 4.9 %collective-permute-done.10.refs_12_ = bf16[128,2048]{1,0:T(8,128)(2,1)} collective-permute-done((bf16[128,2048]{1,0:T(8,128)(2,1)S(1)}, bf16[128,2048]{1,0:T(8,128)(2,1)}, u32[]{:S(2)}, u32[]{:S(2)}) %collective-permute-start.10) | collective-permute-done | bytes 524320 | tf_op jit(solution)/shard_map/ppermute | solution.py:93
  61.5 1.1 %slice_multiply_fusion = (f32[16,1,128]{2,1,0:T(1,128)S(1)}, f32[16,1,128]{2,1,0:T(1,128)S(1)}, f32[16,1,128]{2,1,0:T(1,128)S(1)}, f32[16]{0:T(128)S(1)}) fusion(f32[16,4,128]{2,1,0:T(4,128)} %shard_map.112), kind=kLoop, calls=%fused_computation.50 | loop fusion | flops 8176 | bytes 57408 | tf_op jit(solution)/shard_map/mul | solution.py:439
  62.6 0.3 select_reduce_fusion.1
  63.0 0.1 broadcast_compare_fusion
  63.1 0.1 select_reduce_fusion.6
  63.2 0.7 select_reduce_fusion
  63.8 0.1 slice_reduce_fusion
  64.0 0.1 select_reduce_fusion.2
  64.1 0.1 select_reduce_fusion.5
  64.2 0.1 broadcast_in_dim.238
  64.3 0.1 eq.111
  64.3 0.9 bitcast_multiply_fusion.1
  65.2 0.9 multiply_multiply_fusion.1
  66.1 0.1 collective-permute-start.17
  66.2 2.0 %copy-done.1 = bf16[896,2048]{1,0:T(8,128)(2,1)S(1)} copy-done((bf16[896,2048]{1,0:T(8,128)(2,1)S(1)}, bf16[896,2048]{1,0:T(8,128)(2,1)}, u32[]{:S(2)}) %copy-start.1) | copy-done | bytes 3670040
  68.2 1.0 copy-done.4
  69.3 9.1 %shard_map.113 = (f32[896,2048]{1,0:T(8,128)S(1)}, bf16[1280,2048]{1,0:T(8,128)(2,1)S(1)}, f32[16,1,2048]{2,1,0:T(1,128)S(1)}) custom-call(s32[32]{0:T(128)S(1)} %fusion.5.owners, s32[1]{0:T(128)} %constant.80.clone.1.where, bf16[896,2048]{1,0:T(8,128)(2,1)S(1)} %copy-done.1, f32[8,2048]{1,0:T(8,128)S(1)} %select_maximum_fusion.refs_1_, ...), custom_call_target="tpu_custom_call" | custom-call | flops 46976204800 | bytes 86376448 | tf_op jit(solution)/shard_map/pallas_call | solution.py:330
  78.3 0.6 select_reduce_fusion.3
  79.0 0.1 collective-permute-done.16.refs_4_
  79.0 3.1 %collective-permute-start.20 = (bf16[128,2048]{1,0:T(8,128)(2,1)}, bf16[128,2048]{1,0:T(8,128)(2,1)S(1)}, u32[]{:S(2)}, u32[]{:S(2)}) collective-permute-start(bf16[128,2048]{1,0:T(8,128)(2,1)} %collective-permute-done.19.refs_3_), channel_id=1, source_target_pairs={{0,16},{2,10},{4,20},{6,14},{8,0},{10,26},{12,4},{14,30},{16,24},{... | collective-permute-start | bytes 1572872 | tf_op jit(solution)/shard_map/ppermute | solution.py:93
  82.1 2.0 %collective-permute-start.21 = (bf16[128,2048]{1,0:T(8,128)(2,1)S(1)}, bf16[128,2048]{1,0:T(8,128)(2,1)S(1)}, u32[]{:S(2)}, u32[]{:S(2)}) collective-permute-start(bf16[128,2048]{1,0:T(8,128)(2,1)S(1)} %collective-permute-done.15.refs_6_), channel_id=1, source_target_pairs={{0,4},{2,6},{4,0},{6,2},{8,12},{10,14},{12,8},{14,10},{16,20},{18,... | collective-permute-start | bytes 1572872 | tf_op jit(solution)/shard_map/ppermute | solution.py:93
  84.2 9.4 %shard_map.114 = (f32[896,2048]{1,0:T(8,128)S(1)}, bf16[512,2048]{1,0:T(8,128)(2,1)S(1)}, f32[16,1,2048]{2,1,0:T(1,128)S(1)}) custom-call(s32[32]{0:T(128)S(1)} %fusion.5.owners, s32[1]{0:T(128)} %constant.80.clone.1.where, bf16[896,2048]{1,0:T(8,128)(2,1)S(1)} %collective-permute-done.17.refs_0_, f32[8,2048]{1,0:T(8,128)S(1)} %select_maximum_fusion.refs_1_, ...), custom_call_target="tpu_custom_call" | custom-call | flops 6576668672 | bytes 21561344 | tf_op jit(solution)/shard_map/pallas_call | solution.py:330
  93.5 0.6 collective-permute-done.20.refs_3_
  94.1 1.0 collective-permute-done.21.refs_4_
  95.1 2.5 %shard_map.115 = (bf16[896,2048]{1,0:T(8,128)(2,1)S(1)}, bf16[256,2048]{1,0:T(8,128)(2,1)S(1)}, f32[1,2048]{1,0:T(1,128)S(1)}) custom-call(s32[32]{0:T(128)S(1)} %fusion.5.owners, s32[1]{0:T(128)} %constant.80.clone.1.where, bf16[896,2048]{1,0:T(8,128)(2,1)S(1)} %collective-permute-done.17.refs_0_, f32[8,2048]{1,0:T(8,128)S(1)} %select_maximum_fusion.refs_1_, ...), custom_call_target="tpu_custom_call" | custom-call | flops 939524096 | bytes 12517376 | tf_op jit(solution)/shard_map/pallas_call | solution.py:330
  97.6 0.1 collective-permute-start.23
  97.7 0.5 collective-permute-start.22
  98.2 4.6 %shard_map.116.whole = bf16[896,4096]{1,0:T(8,128)(2,1)} custom-call(s32[32]{0:T(128)S(1)} %fusion.5.owners, s32[1]{0:T(128)} %bitcast.where, bf16[896,2048]{1,0:T(8,128)(2,1)S(1)} %copy-done.2, bf16[256,2048]{1,0:T(8,128)(2,1)S(1)} %get-tuple-element.115.refs_1_, bf16[512,2048]{1,0:T(8,128)(2,1)S(1)} %get-tuple-element.116.refs_2_, ...), custom_call_target="tpu_custom_call" | custom-call | flops 2818572288 | bytes 15532032 | tf_op jit(solution)/shard_map/pallas_call | solution.py:330
  102.8 1.3 %collective-permute-done.22 = f32[2048]{0:T(1024)S(1)} collective-permute-done((f32[2048]{0:T(1024)S(1)}, f32[2048]{0:T(1024)S(1)}, u32[]{:S(2)}, u32[]{:S(2)}) %collective-permute-start.22) | collective-permute-done | bytes 8224 | tf_op jit(solution)/shard_map/ppermute | solution.py:416
  104.1 0.6 convert_multiply_fusion.2
  104.7 1.9 %shard_map.117 = bf16[896,4096]{1,0:T(8,128)(2,1)} custom-call(s32[1]{0:T(128)S(6)} %sub.26.where, bf16[896,2048]{1,0:T(8,128)(2,1)S(1)} %collective-permute-done.23.part, bf16[896,4096]{1,0:T(8,128)(2,1)} %shard_map.116.whole), custom_call_target="tpu_custom_call", output_to_operand_aliasing={{}: (2, {})} | custom-call | bytes 7340032 | tf_op jit(solution)/shard_map/pallas_call | solution.py:371
  (37 shorter events, 0.2 us)
Async XLA Ops:
  1.9 19.3 %collective-permute-start.3 = (bf16[128,2048]{1,0:T(8,128)(2,1)S(1)}, bf16[128,2048]{1,0:T(8,128)(2,1)S(1)}, u32[]{:S(2)}, u32[]{:S(2)}) collective-permute-start(bf16[128,2048]{1,0:T(8,128)(2,1)S(1)} %get-tuple-element.64.refs_3_), channel_id=1, source_target_pairs={{0,16},{2,10},{4,20},{6,14},{8,0},{10,26},{12,4},{14,30},{16,24},{... | collective-permute-start | bytes 1572872 | tf_op jit(solution)/shard_map/ppermute | solution.py:93
  6.0 15.2 %collective-permute-start.4 = (bf16[128,2048]{1,0:T(8,128)(2,1)S(1)}, bf16[128,2048]{1,0:T(8,128)(2,1)S(1)}, u32[]{:S(2)}, u32[]{:S(2)}) collective-permute-start(bf16[128,2048]{1,0:T(8,128)(2,1)S(1)} %get-tuple-element.64.refs_3_), channel_id=1, source_target_pairs={{0,4},{2,6},{4,0},{6,2},{8,12},{10,14},{12,8},{14,10},{16,20},{18,... | collective-permute-start | bytes 1572872 | tf_op jit(solution)/shard_map/ppermute | solution.py:93
  7.5 2.2 %collective-permute-start = (bf16[128,2048]{1,0:T(8,128)(2,1)S(1)}, bf16[128,2048]{1,0:T(8,128)(2,1)S(1)}, u32[]{:S(2)}, u32[]{:S(2)}) collective-permute-start(bf16[128,2048]{1,0:T(8,128)(2,1)S(1)} %get-tuple-element.61), channel_id=1, source_target_pairs={{0,2},{2,0},{4,6},{6,4},{8,10},{10,8},{12,14},{14,12},{16,18},{18,... | collective-permute-start | bytes 1572872 | tf_op jit(solution)/shard_map/ppermute | solution.py:93
  11.4 3.7 %collective-permute-start.5 = (f32[4,128]{1,0:T(4,128)S(1)}, f32[4,128]{1,0:T(4,128)S(1)}, u32[]{:S(2)}, u32[]{:S(2)}) collective-permute-start(f32[4,128]{1,0:T(4,128)S(1)} %pad_maximum_fusion.1), channel_id=1, source_target_pairs={{0,1},{1,0},{2,3},{3,2},{4,5},{5,4},{6,7},{7,6},{8,9},{9,8},{10,11... | collective-permute-start | bytes 6152 | tf_op jit(solution)/shard_map/ppermute | solution.py:18
  13.0 20.0 %collective-permute-start.1 = (bf16[128,2048]{1,0:T(8,128)(2,1)S(1)}, bf16[128,2048]{1,0:T(8,128)(2,1)S(1)}, u32[]{:S(2)}, u32[]{:S(2)}) collective-permute-start(bf16[128,2048]{1,0:T(8,128)(2,1)S(1)} %collective-permute-done.refs_4_), channel_id=1, source_target_pairs={{0,8},{2,18},{4,12},{6,22},{8,24},{10,2},{12,28},{14,6},{16,0},{18... | collective-permute-start | bytes 1572872 | tf_op jit(solution)/shard_map/ppermute | solution.py:93
  13.9 19.1 %collective-permute-start.2 = (bf16[128,2048]{1,0:T(8,128)(2,1)S(1)}, bf16[128,2048]{1,0:T(8,128)(2,1)S(1)}, u32[]{:S(2)}, u32[]{:S(2)}) collective-permute-start(bf16[128,2048]{1,0:T(8,128)(2,1)S(1)} %collective-permute-done.refs_4_), channel_id=1, source_target_pairs={{0,4},{2,6},{4,0},{6,2},{8,12},{10,14},{12,8},{14,10},{16,20},{18,... | collective-permute-start | bytes 1572872 | tf_op jit(solution)/shard_map/ppermute | solution.py:93
  19.4 1.8 %copy-start = (bf16[896,2048]{1,0:T(8,128)(2,1)}, bf16[896,2048]{1,0:T(8,128)(2,1)S(1)}, u32[]{:S(2)}) copy-start(bf16[896,2048]{1,0:T(8,128)(2,1)S(1)} %get-tuple-element.86.refs_0_) | copy-start | bytes 11010052
  21.2 1.2 %collective-permute-start.6 = (f32[1,4,128]{2,1,0:T(4,128)S(1)}, f32[1,4,128]{2,1,0:T(4,128)S(1)}, u32[]{:S(2)}, u32[]{:S(2)}) collective-permute-start(f32[1,4,128]{2,1,0:T(4,128)S(1)} %add_bitcast_fusion), channel_id=1, source_target_pairs={{0,2},{2,0},{4,6},{6,4},{8,10},{10,8},{12,14},{14,12},{16,18},{18,... | collective-permute-start | bytes 6152 | tf_op jit(solution)/shard_map/ppermute | solution.py:24
  22.5 5.1 %collective-permute-start.7 = (f32[2,4,128]{2,1,0:T(4,128)S(1)}, f32[2,4,128]{2,1,0:T(4,128)S(1)}, u32[]{:S(2)}, u32[]{:S(2)}) collective-permute-start(f32[2,4,128]{2,1,0:T(4,128)S(1)} %broadcast_select_fusion), channel_id=1, source_target_pairs={{0,8},{2,10},{4,12},{6,14},{8,0},{10,2},{12,4},{14,6},{16,24},{18,... | collective-permute-start | bytes 12296 | tf_op jit(solution)/shard_map/ppermute | solution.py:24
  23.5 7.6 %collective-permute-start.8 = (f32[2,4,128]{2,1,0:T(4,128)S(1)}, f32[2,4,128]{2,1,0:T(4,128)S(1)}, u32[]{:S(2)}, u32[]{:S(2)}) collective-permute-start(f32[2,4,128]{2,1,0:T(4,128)S(1)} %broadcast_select_fusion), channel_id=1, source_target_pairs={{0,16},{2,18},{4,20},{6,22},{8,24},{10,26},{12,28},{14,30},{16,0},... | collective-permute-start | bytes 12296 | tf_op jit(solution)/shard_map/ppermute | solution.py:24
  27.4 5.6 %collective-permute-start.9 = (f32[2,4,128]{2,1,0:T(4,128)S(1)}, f32[2,4,128]{2,1,0:T(4,128)S(1)}, u32[]{:S(2)}, u32[]{:S(2)}) collective-permute-start(f32[2,4,128]{2,1,0:T(4,128)S(1)} %broadcast_select_fusion), channel_id=1, source_target_pairs={{0,24},{2,26},{4,28},{6,30},{8,16},{10,18},{12,20},{14,22},{16,8},... | collective-permute-start | bytes 12296 | tf_op jit(solution)/shard_map/ppermute | solution.py:24
  27.6 20.9 %collective-permute-start.12 = (bf16[128,2048]{1,0:T(8,128)(2,1)S(1)}, bf16[128,2048]{1,0:T(8,128)(2,1)}, u32[]{:S(2)}, u32[]{:S(2)}) collective-permute-start(bf16[128,2048]{1,0:T(8,128)(2,1)S(1)} %collective-permute-done.3.refs_7_), channel_id=1, source_target_pairs={{0,16},{2,10},{4,20},{6,14},{8,0},{10,26},{12,4},{14,30},{16,24},{... | collective-permute-start | bytes 1572872 | tf_op jit(solution)/shard_map/ppermute | solution.py:93
  31.1 17.3 %collective-permute-start.13 = (bf16[128,2048]{1,0:T(8,128)(2,1)S(1)}, bf16[128,2048]{1,0:T(8,128)(2,1)S(1)}, u32[]{:S(2)}, u32[]{:S(2)}) collective-permute-start(bf16[128,2048]{1,0:T(8,128)(2,1)S(1)} %collective-permute-done.3.refs_7_), channel_id=1, source_target_pairs={{0,4},{2,6},{4,0},{6,2},{8,12},{10,14},{12,8},{14,10},{16,20},{18,... | collective-permute-start | bytes 1572872 | tf_op jit(solution)/shard_map/ppermute | solution.py:93
  33.1 13.2 %collective-permute-start.14 = (f32[4,2,4,128]{3,2,1,0:T(4,128)S(1)}, f32[4,2,4,128]{3,2,1,0:T(4,128)S(1)}, u32[]{:S(2)}, u32[]{:S(2)}) collective-permute-start(f32[4,2,4,128]{3,2,1,0:T(4,128)S(1)} %select_select_fusion), channel_id=1, source_target_pairs={{0,4},{2,6},{4,0},{6,2},{8,12},{10,14},{12,8},{14,10},{16,20},{18,... | collective-permute-start | bytes 49160 | tf_op jit(solution)/shard_map/ppermute | solution.py:24
  36.3 25.2 %collective-permute-start.10 = (bf16[128,2048]{1,0:T(8,128)(2,1)S(1)}, bf16[128,2048]{1,0:T(8,128)(2,1)}, u32[]{:S(2)}, u32[]{:S(2)}) collective-permute-start(bf16[128,2048]{1,0:T(8,128)(2,1)S(1)} %collective-permute-done.1.refs_8_), channel_id=1, source_target_pairs={{0,8},{2,18},{4,12},{6,22},{8,24},{10,2},{12,28},{14,6},{16,0},{18... | collective-permute-start | bytes 1572872 | tf_op jit(solution)/shard_map/ppermute | solution.py:93
  36.3 25.2 %collective-permute-start.11 = (bf16[128,2048]{1,0:T(8,128)(2,1)S(1)}, bf16[128,2048]{1,0:T(8,128)(2,1)}, u32[]{:S(2)}, u32[]{:S(2)}) collective-permute-start(bf16[128,2048]{1,0:T(8,128)(2,1)S(1)} %collective-permute-done.1.refs_8_), channel_id=1, source_target_pairs={{0,4},{2,6},{4,0},{6,2},{8,12},{10,14},{12,8},{14,10},{16,20},{18,... | collective-permute-start | bytes 1572872 | tf_op jit(solution)/shard_map/ppermute | solution.py:93
  48.4 0.8 copy-start.3
  49.2 29.7 %collective-permute-start.18 = (bf16[128,2048]{1,0:T(8,128)(2,1)}, bf16[128,2048]{1,0:T(8,128)(2,1)}, u32[]{:S(2)}, u32[]{:S(2)}) collective-permute-start(bf16[128,2048]{1,0:T(8,128)(2,1)} %collective-permute-done.12.refs_11_), channel_id=1, source_target_pairs={{0,16},{2,10},{4,20},{6,14},{8,0},{10,26},{12,4},{14,30},{16,24},{... | collective-permute-start | bytes 1572872 | tf_op jit(solution)/shard_map/ppermute | solution.py:93
  50.0 28.9 %collective-permute-start.19 = (bf16[128,2048]{1,0:T(8,128)(2,1)}, bf16[128,2048]{1,0:T(8,128)(2,1)}, u32[]{:S(2)}, u32[]{:S(2)}) collective-permute-start(bf16[128,2048]{1,0:T(8,128)(2,1)} %collective-permute-done.12.refs_11_), channel_id=1, source_target_pairs={{0,4},{2,6},{4,0},{6,2},{8,12},{10,14},{12,8},{14,10},{16,20},{18,... | collective-permute-start | bytes 1572872 | tf_op jit(solution)/shard_map/ppermute | solution.py:93
  61.5 17.4 %collective-permute-start.15 = (bf16[128,2048]{1,0:T(8,128)(2,1)}, bf16[128,2048]{1,0:T(8,128)(2,1)S(1)}, u32[]{:S(2)}, u32[]{:S(2)}) collective-permute-start(bf16[128,2048]{1,0:T(8,128)(2,1)} %collective-permute-done.10.refs_12_), channel_id=1, source_target_pairs={{0,8},{2,18},{4,12},{6,22},{8,24},{10,2},{12,28},{14,6},{16,0},{18... | collective-permute-start | bytes 1572872 | tf_op jit(solution)/shard_map/ppermute | solution.py:93
  61.5 17.5 %collective-permute-start.16 = (bf16[128,2048]{1,0:T(8,128)(2,1)}, bf16[128,2048]{1,0:T(8,128)(2,1)S(1)}, u32[]{:S(2)}, u32[]{:S(2)}) collective-permute-start(bf16[128,2048]{1,0:T(8,128)(2,1)} %collective-permute-done.10.refs_12_), channel_id=1, source_target_pairs={{0,4},{2,6},{4,0},{6,2},{8,12},{10,14},{12,8},{14,10},{16,20},{18,... | collective-permute-start | bytes 1572872 | tf_op jit(solution)/shard_map/ppermute | solution.py:93
  66.1 13.0 %collective-permute-start.17 = (bf16[896,2048]{1,0:T(8,128)(2,1)}, bf16[896,2048]{1,0:T(8,128)(2,1)S(1)}, u32[]{:S(2)}, u32[]{:S(2)}) collective-permute-start(bf16[896,2048]{1,0:T(8,128)(2,1)} %get-tuple-element.84), channel_id=1, source_target_pairs={{0,2},{2,0},{4,6},{6,4},{8,10},{10,8},{12,14},{14,12},{16,18},{18,... | collective-permute-start | bytes 11010056 | tf_op jit(solution)/shard_map/ppermute | solution.py:93
  66.2 2.0 %copy-start.1 = (bf16[896,2048]{1,0:T(8,128)(2,1)S(1)}, bf16[896,2048]{1,0:T(8,128)(2,1)}, u32[]{:S(2)}) copy-start(bf16[896,2048]{1,0:T(8,128)(2,1)} %copy-done) | copy-start | bytes 11010052
  68.2 1.0 copy-start.4
  79.0 15.0 %collective-permute-start.20 = (bf16[128,2048]{1,0:T(8,128)(2,1)}, bf16[128,2048]{1,0:T(8,128)(2,1)S(1)}, u32[]{:S(2)}, u32[]{:S(2)}) collective-permute-start(bf16[128,2048]{1,0:T(8,128)(2,1)} %collective-permute-done.19.refs_3_), channel_id=1, source_target_pairs={{0,16},{2,10},{4,20},{6,14},{8,0},{10,26},{12,4},{14,30},{16,24},{... | collective-permute-start | bytes 1572872 | tf_op jit(solution)/shard_map/ppermute | solution.py:93
  82.1 13.0 %collective-permute-start.21 = (bf16[128,2048]{1,0:T(8,128)(2,1)S(1)}, bf16[128,2048]{1,0:T(8,128)(2,1)S(1)}, u32[]{:S(2)}, u32[]{:S(2)}) collective-permute-start(bf16[128,2048]{1,0:T(8,128)(2,1)S(1)} %collective-permute-done.15.refs_6_), channel_id=1, source_target_pairs={{0,4},{2,6},{4,0},{6,2},{8,12},{10,14},{12,8},{14,10},{16,20},{18,... | collective-permute-start | bytes 1572872 | tf_op jit(solution)/shard_map/ppermute | solution.py:93
  95.1 3.1 %copy-start.2 = (bf16[896,2048]{1,0:T(8,128)(2,1)S(1)}, bf16[896,2048]{1,0:T(8,128)(2,1)}, u32[]{:S(2)}) copy-start(bf16[896,2048]{1,0:T(8,128)(2,1)} %copy-done) | copy-start | bytes 11010052
  97.6 7.1 %collective-permute-start.23 = (bf16[896,2048]{1,0:T(8,128)(2,1)S(1)}, bf16[896,2048]{1,0:T(8,128)(2,1)S(1)}, u32[]{:S(2)}, u32[]{:S(2)}) collective-permute-start(bf16[896,2048]{1,0:T(8,128)(2,1)S(1)} %get-tuple-element.113), channel_id=1, source_target_pairs={{0,2},{2,0},{4,6},{6,4},{8,10},{10,8},{12,14},{14,12},{16,18},{18,... | collective-permute-start | bytes 11010056 | tf_op jit(solution)/shard_map/ppermute | solution.py:416
  97.7 6.4 %collective-permute-start.22 = (f32[2048]{0:T(1024)S(1)}, f32[2048]{0:T(1024)S(1)}, u32[]{:S(2)}, u32[]{:S(2)}) collective-permute-start(f32[2048]{0:T(1024)S(1)} %bitcast.47), channel_id=1, source_target_pairs={{0,2},{2,0},{4,6},{6,4},{8,10},{10,8},{12,14},{14,12},{16,18},{18,... | collective-permute-start | bytes 24584 | tf_op jit(solution)/shard_map/ppermute | solution.py:416
  98.2 5.9 %copy-start.5 = (bf16[4096]{0:T(1024)(128)(2,1)S(1)}, bf16[4096]{0:T(1024)(128)(2,1)}, u32[]{:S(2)}) copy-start(bf16[4096]{0:T(1024)(128)(2,1)} %param.10) | copy-start | bytes 24580

commit v12 on v10

--- a/solution.py
+++ b/solution.py
@@ -128,15 +128,17 @@
             if k < m - 1:
                 sends = [((k + 1, 0, kind), (k, 0, kind), ring[kind]), ((k, 1, kind), (k, 0, kind), across)]
             elif kind == 0:
-                sends = []
+                sends = [((k, 1, 0), (k, 0, 0), across)]
             else:
-                sends = [((k, 1, 0), (k - 1, 1, 0), ring[0]), ((k, 1, 1), (k, 0, 1), across)]
+                sends = [((k, 1, 1), (k - 1, 1, 1), ring[1])]
             waits = [(k, 0, kind), (k - 1, 1, kind), "facts"]
             if k == m - 2 and kind == 1:
                 sends.append(("other picks", "away picks", core))
             if k == m - 1 and kind == 1:
-                waits += ["other picks", "early own", "values", "returns"]
+                waits = [(k - 1, 1, kind), "early own"]
             f.event(waits, sends)
+            if k == m - 1 and kind == 1:
+                f.event([(k, 0, kind), "other picks", "values", "returns"])
             if k == m - 2 and kind == 1:
                 while bits:
                     facts_step()

time: 102 us -> 102 us (level)
  waiting for transfers between devices: 27.5 us -> 26.3 us
  starting transfers between devices: 34.7 us -> 35.9 us
    ppermute x16, waiting for transfers between devices: 10.9 us -> 9.7 us  [event(): self.have[name] = lax.ppermute(self.have[source], 'seq', pairs)]
    ppermute x16, starting transfers between devices: 26.8 us -> 27.9 us  [event(): self.have[name] = lax.ppermute(self.have[source], 'seq', pairs)]
  transfers between devices with their start and end apart: 23 -> 23, of which waited for: 11 -> 12; matrix products, arithmetic and copies ran while one was open for 7% -> 7% of each run, Pallas kernels for 24% -> 24%
where the time goes in v12:
time: 102 us; the launch traced here: 101 us
  starting transfers between devices  35.9 us (35%)
  Pallas kernels  29 us (28%)
  waiting for transfers between devices  26.3 us (26%)
  other arithmetic  6.19 us (6%)
  local copies, waits for them, and re-layouts  2.23 us (2%)
    ppermute x16, starting transfers between devices, event(): self.have[name] = lax.ppermute(self.have[source], 'seq', pairs)  27.9 us
    pallas_call x4, Pallas kernels, product(): pl.pallas_call(functools.partial(product_kernel, tok, count, first, len(g...  22.7 us
    ppermute x4, waiting for transfers between devices, butterfly_send(): lax.ppermute(x, axis, [(i, i ^ bit) for i in range(lax.axis_size(axis))])  14.5 us
    ppermute x16, waiting for transfers between devices, event(): self.have[name] = lax.ppermute(self.have[source], 'seq', pairs)  9.7 us
    ppermute x4, starting transfers between devices, butterfly_send(): lax.ppermute(x, axis, [(i, i ^ bit) for i in range(lax.axis_size(axis))])  5.84 us
    pallas_call x1, Pallas kernels, pick(): pl.pallas_call(functools.partial(pick_kernel, tok), grid_spec=pltpu.Prefe...  4.35 us
  transfers between devices with their start and end apart: 23, of which 12 were waited for; matrix products, arithmetic and copies ran while one was open for 7% of the time, Pallas kernels for 24%

profile of v12, /device:TPU:0, one launch (start us, length us, event | category | flops | bytes accessed | tf_op | source)
XLA Modules:
  0.0 100.6 jit_solution(12639296298570236315)
XLA Ops:
  0.7 1.3 %constant_dynamic-slice_fusion.1 = (bf16[128,2048]{1,0:T(8,128)(2,1)S(1)}, bf16[128,2048]{1,0:T(8,128)(2,1)S(1)}) fusion(bf16[128,4096]{1,0:T(8,128)(2,1)} %param.8, s32[]{:T(128)S(6)} %select_n.133, s32[]{:T(128)S(6)} %select_n.132), kind=kLoop, calls=%fused_computation.46 | loop fusion | bytes 2097160 | tf_op jit(solution)/shard_map/dynamic_slice | solution.py:88
  1.9 4.1 %collective-permute-start.3 = (bf16[128,2048]{1,0:T(8,128)(2,1)S(1)}, bf16[128,2048]{1,0:T(8,128)(2,1)S(1)}, u32[]{:S(2)}, u32[]{:S(2)}) collective-permute-start(bf16[128,2048]{1,0:T(8,128)(2,1)S(1)} %get-tuple-element.60.refs_3_), channel_id=1, source_target_pairs={{0,16},{2,10},{4,20},{6,14},{8,0},{10,26},{12,4},{14,30},{16,24},{... | collective-permute-start | bytes 1572872 | tf_op jit(solution)/shard_map/ppermute | solution.py:75
  6.0 1.5 %collective-permute-start.4 = (bf16[128,2048]{1,0:T(8,128)(2,1)S(1)}, bf16[128,2048]{1,0:T(8,128)(2,1)S(1)}, u32[]{:S(2)}, u32[]{:S(2)}) collective-permute-start(bf16[128,2048]{1,0:T(8,128)(2,1)S(1)} %get-tuple-element.60.refs_3_), channel_id=1, source_target_pairs={{0,4},{2,6},{4,0},{6,2},{8,12},{10,14},{12,8},{14,10},{16,20},{18,... | collective-permute-start | bytes 1572872 | tf_op jit(solution)/shard_map/ppermute | solution.py:75
  7.6 0.7 fusion.6.owners
  8.3 0.7 multiply_bitcast_fusion
  9.0 0.7 convert_multiply_fusion.3
  9.7 0.0 collective-permute-done.refs_4_
  9.7 1.7 %fusion = (f32[128]{0:T(128)S(1)}, f32[128]{0:T(128)S(1)}) fusion(bf16[128,4096]{1,0:T(8,128)(2,1)} %param.8, f32[4096]{0:T(1024)S(1)} %convert_multiply_fusion.3), kind=kLoop, calls=%fused_computation.2 | loop fusion | flops 2621184 | bytes 1065984 | tf_op jit(solution)/shard_map/reduce_sum | solution.py:408
  11.3 1.6 %collective-permute-start.5 = (f32[4,128]{1,0:T(4,128)S(1)}, f32[4,128]{1,0:T(4,128)S(1)}, u32[]{:S(2)}, u32[]{:S(2)}) collective-permute-start(f32[4,128]{1,0:T(4,128)S(1)} %pad_maximum_fusion.2), channel_id=1, source_target_pairs={{0,1},{1,0},{2,3},{3,2},{4,5},{5,4},{6,7},{7,6},{8,9},{9,8},{10,11... | collective-permute-start | bytes 6152 | tf_op jit(solution)/shard_map/ppermute | solution.py:18
  12.9 0.8 collective-permute-start.1
  13.7 0.5 collective-permute-start.2
  14.2 0.8 collective-permute-done.5
  15.0 4.3 %shard_map.111 = (bf16[896,2048]{1,0:T(8,128)(2,1)S(1)}, bf16[896,2048]{1,0:T(8,128)(2,1)}) custom-call(s32[32]{0:T(128)S(1)} %fusion.6.owners, bf16[896,2048]{1,0:T(8,128)(2,1)} %hidden), custom_call_target="tpu_custom_call" | custom-call | bytes 1 | tf_op jit(solution)/shard_map/pallas_call | solution.py:190
  19.4 0.8 collective-permute-done.3.refs_7_
  20.2 0.0 collective-permute-done.4.refs_5_
  20.2 1.1 %collective-permute-done.6 = f32[1,4,128]{2,1,0:T(4,128)S(1)} collective-permute-done((f32[1,4,128]{2,1,0:T(4,128)S(1)}, f32[1,4,128]{2,1,0:T(4,128)S(1)}, u32[]{:S(2)}, u32[]{:S(2)}) %collective-permute-start.6) | collective-permute-done | bytes 2080 | tf_op jit(solution)/shard_map/ppermute | solution.py:24
  21.4 0.1 broadcast_select_fusion.3
  21.4 2.2 %collective-permute-start.7 = (f32[2,4,128]{2,0,1:T(2,128)S(1)}, f32[2,4,128]{2,0,1:T(2,128)S(1)}, u32[]{:S(2)}, u32[]{:S(2)}) collective-permute-start(f32[2,4,128]{2,0,1:T(2,128)S(1)} %broadcast_select_fusion.3), channel_id=1, source_target_pairs={{0,8},{2,10},{4,12},{6,14},{8,0},{10,2},{12,4},{14,6},{16,24},{18,... | collective-permute-start | bytes 12296 | tf_op jit(solution)/shard_map/ppermute | solution.py:24
  23.6 3.9 %collective-permute-start.10 = (bf16[128,2048]{1,0:T(8,128)(2,1)S(1)}, bf16[128,2048]{1,0:T(8,128)(2,1)S(1)}, u32[]{:S(2)}, u32[]{:S(2)}) collective-permute-start(bf16[128,2048]{1,0:T(8,128)(2,1)S(1)} %collective-permute-done.3.refs_7_), channel_id=1, source_target_pairs={{0,16},{2,10},{4,20},{6,14},{8,0},{10,26},{12,4},{14,30},{16,24},{... | collective-permute-start | bytes 1572872 | tf_op jit(solution)/shard_map/ppermute | solution.py:75
  27.6 3.2 %collective-permute-start.11 = (bf16[128,2048]{1,0:T(8,128)(2,1)S(1)}, bf16[128,2048]{1,0:T(8,128)(2,1)S(1)}, u32[]{:S(2)}, u32[]{:S(2)}) collective-permute-start(bf16[128,2048]{1,0:T(8,128)(2,1)S(1)} %collective-permute-done.3.refs_7_), channel_id=1, source_target_pairs={{0,4},{2,6},{4,0},{6,2},{8,12},{10,14},{12,8},{14,10},{16,20},{18,... | collective-permute-start | bytes 1572872 | tf_op jit(solution)/shard_map/ppermute | solution.py:75
  30.7 0.0 collective-permute-done.7
  30.7 0.3 collective-permute-done.1.refs_8_
  31.1 0.0 collective-permute-done.2.refs_6_
  31.1 0.1 broadcast_select_fusion
  31.2 1.2 %collective-permute-start.12 = (f32[2,2,4,128]{3,1,0,2:T(2,128)S(1)}, f32[2,2,4,128]{3,1,0,2:T(2,128)S(1)}, u32[]{:S(2)}, u32[]{:S(2)}) collective-permute-start(f32[2,2,4,128]{3,1,0,2:T(2,128)S(1)} %broadcast_select_fusion), channel_id=1, source_target_pairs={{0,4},{2,6},{4,0},{6,2},{8,12},{10,14},{12,8},{14,10},{16,20},{18,... | collective-permute-start | bytes 24584 | tf_op jit(solution)/shard_map/ppermute | solution.py:24
  32.4 0.9 collective-permute-start.8
  33.3 2.0 %collective-permute-start.9 = (bf16[128,2048]{1,0:T(8,128)(2,1)S(1)}, bf16[128,2048]{1,0:T(8,128)(2,1)S(1)}, u32[]{:S(2)}, u32[]{:S(2)}) collective-permute-start(bf16[128,2048]{1,0:T(8,128)(2,1)S(1)} %collective-permute-done.1.refs_8_), channel_id=1, source_target_pairs={{0,4},{2,6},{4,0},{6,2},{8,12},{10,14},{12,8},{14,10},{16,20},{18,... | collective-permute-start | bytes 1572872 | tf_op jit(solution)/shard_map/ppermute | solution.py:75
  35.3 8.5 %collective-permute-done.12 = f32[2,2,4,128]{3,1,0,2:T(2,128)S(1)} collective-permute-done((f32[2,2,4,128]{3,1,0,2:T(2,128)S(1)}, f32[2,2,4,128]{3,1,0,2:T(2,128)S(1)}, u32[]{:S(2)}, u32[]{:S(2)}) %collective-permute-start.12) | collective-permute-done | bytes 8224 | tf_op jit(solution)/shard_map/ppermute | solution.py:24
  43.7 0.1 select_bitcast_fusion.1
  43.8 1.5 %collective-permute-done.10.refs_11_ = bf16[128,2048]{1,0:T(8,128)(2,1)S(1)} collective-permute-done((bf16[128,2048]{1,0:T(8,128)(2,1)S(1)}, bf16[128,2048]{1,0:T(8,128)(2,1)S(1)}, u32[]{:S(2)}, u32[]{:S(2)}) %collective-permute-start.10) | collective-permute-done | bytes 524320 | tf_op jit(solution)/shard_map/ppermute | solution.py:75
  45.3 0.0 collective-permute-done.11.refs_9_
  45.3 2.4 %collective-permute-start.13 = (f32[8,4,128]{2,0,1:T(8,128)S(1)}, f32[8,4,128]{2,0,1:T(8,128)S(1)}, u32[]{:S(2)}, u32[]{:S(2)}) collective-permute-start(f32[8,4,128]{2,0,1:T(8,128)S(1)} %bitcast.47), channel_id=1, source_target_pairs={{0,16},{2,18},{4,20},{6,22},{8,24},{10,26},{12,28},{14,30},{16,0},... | collective-permute-start | bytes 49160 | tf_op jit(solution)/shard_map/ppermute | solution.py:24
  47.8 0.5 collective-permute-start.16
  48.3 3.1 %collective-permute-start.17 = (bf16[128,2048]{1,0:T(8,128)(2,1)S(1)}, bf16[128,2048]{1,0:T(8,128)(2,1)S(1)}, u32[]{:S(2)}, u32[]{:S(2)}) collective-permute-start(bf16[128,2048]{1,0:T(8,128)(2,1)S(1)} %collective-permute-done.10.refs_11_), channel_id=1, source_target_pairs={{0,4},{2,6},{4,0},{6,2},{8,12},{10,14},{12,8},{14,10},{16,20},{18,... | collective-permute-start | bytes 1572872 | tf_op jit(solution)/shard_map/ppermute | solution.py:75
  51.3 4.9 %collective-permute-done.13 = f32[8,4,128]{2,0,1:T(8,128)S(1)} collective-permute-done((f32[8,4,128]{2,0,1:T(8,128)S(1)}, f32[8,4,128]{2,0,1:T(8,128)S(1)}, u32[]{:S(2)}, u32[]{:S(2)}) %collective-permute-start.13) | collective-permute-done | bytes 16416 | tf_op jit(solution)/shard_map/ppermute | solution.py:24
  56.3 0.1 collective-permute-start.19
  56.4 3.3 %collective-permute-start.14 = (bf16[128,2048]{1,0:T(8,128)(2,1)S(1)}, bf16[128,2048]{1,0:T(8,128)(2,1)S(1)}, u32[]{:S(2)}, u32[]{:S(2)}) collective-permute-start(bf16[128,2048]{1,0:T(8,128)(2,1)S(1)} %collective-permute-done.8.refs_12_), channel_id=1, source_target_pairs={{0,8},{2,18},{4,12},{6,22},{8,24},{10,2},{12,28},{14,6},{16,0},{18... | collective-permute-start | bytes 1572872 | tf_op jit(solution)/shard_map/ppermute | solution.py:75
  59.6 0.1 fusion.9
  59.8 0.3 select_reduce_fusion.1
  60.1 0.1 broadcast_compare_fusion
  60.2 0.1 select_reduce_fusion.5
  60.3 0.7 select_reduce_fusion
  61.0 0.1 slice_reduce_fusion
  61.1 0.1 select_reduce_fusion.2
  61.2 0.1 select_reduce_fusion.4
  61.3 0.1 broadcast_in_dim.207
  61.4 0.1 eq.119
  61.5 0.1 collective-permute-start.15
  61.6 7.6 %shard_map.112 = (f32[896,2048]{1,0:T(8,128)S(1)}, bf16[1280,2048]{1,0:T(8,128)(2,1)S(1)}, f32[16,1,2048]{2,1,0:T(1,128)S(1)}) custom-call(s32[32]{0:T(128)S(1)} %fusion.6.owners, s32[1]{0:T(128)} %constant.70.clone.1.where, bf16[896,2048]{1,0:T(8,128)(2,1)S(1)} %get-tuple-element.87.refs_0_, f32[8,2048]{1,0:T(8,128)S(1)} %select_maximum_fusion.refs_1_, ...), custom_call_target="tpu_custom_call" | custom-call | flops 46976204800 | bytes 86376448 | tf_op jit(solution)/shard_map/pallas_call | solution.py:309
  69.2 0.6 select_reduce_fusion.3
  69.9 1.5 %collective-permute-done.16.refs_5_ = bf16[128,2048]{1,0:T(8,128)(2,1)S(1)} collective-permute-done((bf16[128,2048]{1,0:T(8,128)(2,1)S(1)}, bf16[128,2048]{1,0:T(8,128)(2,1)S(1)}, u32[]{:S(2)}, u32[]{:S(2)}) %collective-permute-start.16) | collective-permute-done | bytes 524320 | tf_op jit(solution)/shard_map/ppermute | solution.py:75
  71.3 3.1 %collective-permute-start.18 = (bf16[128,2048]{1,0:T(8,128)(2,1)S(1)}, bf16[128,2048]{1,0:T(8,128)(2,1)S(1)}, u32[]{:S(2)}, u32[]{:S(2)}) collective-permute-start(bf16[128,2048]{1,0:T(8,128)(2,1)S(1)} %collective-permute-done.16.refs_5_), channel_id=1, source_target_pairs={{0,4},{2,6},{4,0},{6,2},{8,12},{10,14},{12,8},{14,10},{16,20},{18,... | collective-permute-start | bytes 1572872 | tf_op jit(solution)/shard_map/ppermute | solution.py:75
  74.4 0.9 collective-permute-done.19.refs_4_
  75.3 0.9 collective-permute-start.20
  76.3 8.1 %shard_map.113 = (f32[896,2048]{1,0:T(8,128)S(1)}, bf16[512,2048]{1,0:T(8,128)(2,1)S(1)}, f32[16,1,2048]{2,1,0:T(1,128)S(1)}) custom-call(s32[32]{0:T(128)S(1)} %fusion.6.owners, s32[1]{0:T(128)} %constant.70.clone.1.where, bf16[896,2048]{1,0:T(8,128)(2,1)S(1)} %collective-permute-done.15.refs_0_, f32[8,2048]{1,0:T(8,128)S(1)} %select_maximum_fusion.refs_1_, ...), custom_call_target="tpu_custom_call" | custom-call | flops 6576668672 | bytes 21561344 | tf_op jit(solution)/shard_map/pallas_call | solution.py:309
  84.4 1.6 %collective-permute-done.18.refs_3_ = bf16[128,2048]{1,0:T(8,128)(2,1)S(1)} collective-permute-done((bf16[128,2048]{1,0:T(8,128)(2,1)S(1)}, bf16[128,2048]{1,0:T(8,128)(2,1)S(1)}, u32[]{:S(2)}, u32[]{:S(2)}) %collective-permute-start.18) | collective-permute-done | bytes 524320 | tf_op jit(solution)/shard_map/ppermute | solution.py:75
  86.0 3.0 %collective-permute-done.20.refs_4_ = bf16[128,2048]{1,0:T(8,128)(2,1)S(1)} collective-permute-done((bf16[128,2048]{1,0:T(8,128)(2,1)S(1)}, bf16[128,2048]{1,0:T(8,128)(2,1)S(1)}, u32[]{:S(2)}, u32[]{:S(2)}) %collective-permute-start.20) | collective-permute-done | bytes 524320 | tf_op jit(solution)/shard_map/ppermute | solution.py:75
  89.0 2.4 %shard_map.114 = (bf16[896,2048]{1,0:T(8,128)(2,1)S(1)}, bf16[256,2048]{1,0:T(8,128)(2,1)S(1)}, f32[1,2048]{1,0:T(1,128)S(1)}) custom-call(s32[32]{0:T(128)S(1)} %fusion.6.owners, s32[1]{0:T(128)} %constant.70.clone.1.where, bf16[896,2048]{1,0:T(8,128)(2,1)S(1)} %collective-permute-done.15.refs_0_, f32[8,2048]{1,0:T(8,128)S(1)} %select_maximum_fusion.refs_1_, ...), custom_call_target="tpu_custom_call" | custom-call | flops 939524096 | bytes 12517376 | tf_op jit(solution)/shard_map/pallas_call | solution.py:309
  91.4 0.1 collective-permute-start.22
  91.5 0.5 collective-permute-start.21
  92.0 4.5 %shard_map.115.whole = bf16[896,4096]{1,0:T(8,128)(2,1)} custom-call(s32[32]{0:T(128)S(1)} %fusion.6.owners, s32[1]{0:T(128)} %bitcast.where, bf16[896,2048]{1,0:T(8,128)(2,1)S(1)} %get-tuple-element.87.refs_0_, bf16[256,2048]{1,0:T(8,128)(2,1)S(1)} %get-tuple-element.107.refs_1_, bf16[512,2048]{1,0:T(8,128)(2,1)S(1)} %get-tuple-element.108.refs_2_, ...), custom_call_target="tpu_custom_call" | custom-call | flops 2818572288 | bytes 15532032 | tf_op jit(solution)/shard_map/pallas_call | solution.py:309
  96.6 1.4 %collective-permute-done.21 = f32[2048]{0:T(1024)S(1)} collective-permute-done((f32[2048]{0:T(1024)S(1)}, f32[2048]{0:T(1024)S(1)}, u32[]{:S(2)}, u32[]{:S(2)}) %collective-permute-start.21) | collective-permute-done | bytes 8224 | tf_op jit(solution)/shard_map/ppermute | solution.py:395
  97.9 0.6 convert_multiply_fusion.2
  98.6 1.9 %shard_map.116 = bf16[896,4096]{1,0:T(8,128)(2,1)} custom-call(s32[1]{0:T(128)S(6)} %sub.26.where, bf16[896,2048]{1,0:T(8,128)(2,1)S(1)} %collective-permute-done.22.part, bf16[896,4096]{1,0:T(8,128)(2,1)} %shard_map.115.whole), custom_call_target="tpu_custom_call", output_to_operand_aliasing={{}: (2, {})} | custom-call | bytes 7340032 | tf_op jit(solution)/shard_map/pallas_call | solution.py:350
  (24 shorter events, 0.2 us)
Async XLA Ops:
  1.9 18.3 %collective-permute-start.3 = (bf16[128,2048]{1,0:T(8,128)(2,1)S(1)}, bf16[128,2048]{1,0:T(8,128)(2,1)S(1)}, u32[]{:S(2)}, u32[]{:S(2)}) collective-permute-start(bf16[128,2048]{1,0:T(8,128)(2,1)S(1)} %get-tuple-element.60.refs_3_), channel_id=1, source_target_pairs={{0,16},{2,10},{4,20},{6,14},{8,0},{10,26},{12,4},{14,30},{16,24},{... | collective-permute-start | bytes 1572872 | tf_op jit(solution)/shard_map/ppermute | solution.py:75
  6.0 14.2 %collective-permute-start.4 = (bf16[128,2048]{1,0:T(8,128)(2,1)S(1)}, bf16[128,2048]{1,0:T(8,128)(2,1)S(1)}, u32[]{:S(2)}, u32[]{:S(2)}) collective-permute-start(bf16[128,2048]{1,0:T(8,128)(2,1)S(1)} %get-tuple-element.60.refs_3_), channel_id=1, source_target_pairs={{0,4},{2,6},{4,0},{6,2},{8,12},{10,14},{12,8},{14,10},{16,20},{18,... | collective-permute-start | bytes 1572872 | tf_op jit(solution)/shard_map/ppermute | solution.py:75
  7.5 2.1 %collective-permute-start = (bf16[128,2048]{1,0:T(8,128)(2,1)S(1)}, bf16[128,2048]{1,0:T(8,128)(2,1)S(1)}, u32[]{:S(2)}, u32[]{:S(2)}) collective-permute-start(bf16[128,2048]{1,0:T(8,128)(2,1)S(1)} %get-tuple-element.57), channel_id=1, source_target_pairs={{0,2},{2,0},{4,6},{6,4},{8,10},{10,8},{12,14},{14,12},{16,18},{18,... | collective-permute-start | bytes 1572872 | tf_op jit(solution)/shard_map/ppermute | solution.py:75
  11.3 3.7 %collective-permute-start.5 = (f32[4,128]{1,0:T(4,128)S(1)}, f32[4,128]{1,0:T(4,128)S(1)}, u32[]{:S(2)}, u32[]{:S(2)}) collective-permute-start(f32[4,128]{1,0:T(4,128)S(1)} %pad_maximum_fusion.2), channel_id=1, source_target_pairs={{0,1},{1,0},{2,3},{3,2},{4,5},{5,4},{6,7},{7,6},{8,9},{9,8},{10,11... | collective-permute-start | bytes 6152 | tf_op jit(solution)/shard_map/ppermute | solution.py:18
  12.9 18.2 %collective-permute-start.1 = (bf16[128,2048]{1,0:T(8,128)(2,1)S(1)}, bf16[128,2048]{1,0:T(8,128)(2,1)S(1)}, u32[]{:S(2)}, u32[]{:S(2)}) collective-permute-start(bf16[128,2048]{1,0:T(8,128)(2,1)S(1)} %collective-permute-done.refs_4_), channel_id=1, source_target_pairs={{0,8},{2,18},{4,12},{6,22},{8,24},{10,2},{12,28},{14,6},{16,0},{18... | collective-permute-start | bytes 1572872 | tf_op jit(solution)/shard_map/ppermute | solution.py:75
  13.7 17.4 %collective-permute-start.2 = (bf16[128,2048]{1,0:T(8,128)(2,1)S(1)}, bf16[128,2048]{1,0:T(8,128)(2,1)S(1)}, u32[]{:S(2)}, u32[]{:S(2)}) collective-permute-start(bf16[128,2048]{1,0:T(8,128)(2,1)S(1)} %collective-permute-done.refs_4_), channel_id=1, source_target_pairs={{0,4},{2,6},{4,0},{6,2},{8,12},{10,14},{12,8},{14,10},{16,20},{18,... | collective-permute-start | bytes 1572872 | tf_op jit(solution)/shard_map/ppermute | solution.py:75
  20.2 1.2 %collective-permute-start.6 = (f32[1,4,128]{2,1,0:T(4,128)S(1)}, f32[1,4,128]{2,1,0:T(4,128)S(1)}, u32[]{:S(2)}, u32[]{:S(2)}) collective-permute-start(f32[1,4,128]{2,1,0:T(4,128)S(1)} %add_bitcast_fusion), channel_id=1, source_target_pairs={{0,2},{2,0},{4,6},{6,4},{8,10},{10,8},{12,14},{14,12},{16,18},{18,... | collective-permute-start | bytes 6152 | tf_op jit(solution)/shard_map/ppermute | solution.py:24
  21.4 9.3 %collective-permute-start.7 = (f32[2,4,128]{2,0,1:T(2,128)S(1)}, f32[2,4,128]{2,0,1:T(2,128)S(1)}, u32[]{:S(2)}, u32[]{:S(2)}) collective-permute-start(f32[2,4,128]{2,0,1:T(2,128)S(1)} %broadcast_select_fusion.3), channel_id=1, source_target_pairs={{0,8},{2,10},{4,12},{6,14},{8,0},{10,2},{12,4},{14,6},{16,24},{18,... | collective-permute-start | bytes 12296 | tf_op jit(solution)/shard_map/ppermute | solution.py:24
  23.6 21.7 %collective-permute-start.10 = (bf16[128,2048]{1,0:T(8,128)(2,1)S(1)}, bf16[128,2048]{1,0:T(8,128)(2,1)S(1)}, u32[]{:S(2)}, u32[]{:S(2)}) collective-permute-start(bf16[128,2048]{1,0:T(8,128)(2,1)S(1)} %collective-permute-done.3.refs_7_), channel_id=1, source_target_pairs={{0,16},{2,10},{4,20},{6,14},{8,0},{10,26},{12,4},{14,30},{16,24},{... | collective-permute-start | bytes 1572872 | tf_op jit(solution)/shard_map/ppermute | solution.py:75
  27.6 17.8 %collective-permute-start.11 = (bf16[128,2048]{1,0:T(8,128)(2,1)S(1)}, bf16[128,2048]{1,0:T(8,128)(2,1)S(1)}, u32[]{:S(2)}, u32[]{:S(2)}) collective-permute-start(bf16[128,2048]{1,0:T(8,128)(2,1)S(1)} %collective-permute-done.3.refs_7_), channel_id=1, source_target_pairs={{0,4},{2,6},{4,0},{6,2},{8,12},{10,14},{12,8},{14,10},{16,20},{18,... | collective-permute-start | bytes 1572872 | tf_op jit(solution)/shard_map/ppermute | solution.py:75
  31.2 12.6 %collective-permute-start.12 = (f32[2,2,4,128]{3,1,0,2:T(2,128)S(1)}, f32[2,2,4,128]{3,1,0,2:T(2,128)S(1)}, u32[]{:S(2)}, u32[]{:S(2)}) collective-permute-start(f32[2,2,4,128]{3,1,0,2:T(2,128)S(1)} %broadcast_select_fusion), channel_id=1, source_target_pairs={{0,4},{2,6},{4,0},{6,2},{8,12},{10,14},{12,8},{14,10},{16,20},{18,... | collective-permute-start | bytes 24584 | tf_op jit(solution)/shard_map/ppermute | solution.py:24
  32.4 23.9 %collective-permute-start.8 = (bf16[128,2048]{1,0:T(8,128)(2,1)S(1)}, bf16[128,2048]{1,0:T(8,128)(2,1)S(1)}, u32[]{:S(2)}, u32[]{:S(2)}) collective-permute-start(bf16[128,2048]{1,0:T(8,128)(2,1)S(1)} %collective-permute-done.1.refs_8_), channel_id=1, source_target_pairs={{0,8},{2,18},{4,12},{6,22},{8,24},{10,2},{12,28},{14,6},{16,0},{18... | collective-permute-start | bytes 1572872 | tf_op jit(solution)/shard_map/ppermute | solution.py:75
  33.3 23.0 %collective-permute-start.9 = (bf16[128,2048]{1,0:T(8,128)(2,1)S(1)}, bf16[128,2048]{1,0:T(8,128)(2,1)S(1)}, u32[]{:S(2)}, u32[]{:S(2)}) collective-permute-start(bf16[128,2048]{1,0:T(8,128)(2,1)S(1)} %collective-permute-done.1.refs_8_), channel_id=1, source_target_pairs={{0,4},{2,6},{4,0},{6,2},{8,12},{10,14},{12,8},{14,10},{16,20},{18,... | collective-permute-start | bytes 1572872 | tf_op jit(solution)/shard_map/ppermute | solution.py:75
  45.3 10.9 %collective-permute-start.13 = (f32[8,4,128]{2,0,1:T(8,128)S(1)}, f32[8,4,128]{2,0,1:T(8,128)S(1)}, u32[]{:S(2)}, u32[]{:S(2)}) collective-permute-start(f32[8,4,128]{2,0,1:T(8,128)S(1)} %bitcast.47), channel_id=1, source_target_pairs={{0,16},{2,18},{4,20},{6,22},{8,24},{10,26},{12,28},{14,30},{16,0},... | collective-permute-start | bytes 49160 | tf_op jit(solution)/shard_map/ppermute | solution.py:24
  47.8 23.6 %collective-permute-start.16 = (bf16[128,2048]{1,0:T(8,128)(2,1)S(1)}, bf16[128,2048]{1,0:T(8,128)(2,1)S(1)}, u32[]{:S(2)}, u32[]{:S(2)}) collective-permute-start(bf16[128,2048]{1,0:T(8,128)(2,1)S(1)} %collective-permute-done.10.refs_11_), channel_id=1, source_target_pairs={{0,16},{2,10},{4,20},{6,14},{8,0},{10,26},{12,4},{14,30},{16,24},{... | collective-permute-start | bytes 1572872 | tf_op jit(solution)/shard_map/ppermute | solution.py:75
  48.3 23.1 %collective-permute-start.17 = (bf16[128,2048]{1,0:T(8,128)(2,1)S(1)}, bf16[128,2048]{1,0:T(8,128)(2,1)S(1)}, u32[]{:S(2)}, u32[]{:S(2)}) collective-permute-start(bf16[128,2048]{1,0:T(8,128)(2,1)S(1)} %collective-permute-done.10.refs_11_), channel_id=1, source_target_pairs={{0,4},{2,6},{4,0},{6,2},{8,12},{10,14},{12,8},{14,10},{16,20},{18,... | collective-permute-start | bytes 1572872 | tf_op jit(solution)/shard_map/ppermute | solution.py:75
  56.3 19.0 %collective-permute-start.19 = (bf16[128,2048]{1,0:T(8,128)(2,1)S(1)}, bf16[128,2048]{1,0:T(8,128)(2,1)S(1)}, u32[]{:S(2)}, u32[]{:S(2)}) collective-permute-start(bf16[128,2048]{1,0:T(8,128)(2,1)S(1)} %collective-permute-done.8.refs_12_), channel_id=1, source_target_pairs={{0,4},{2,6},{4,0},{6,2},{8,12},{10,14},{12,8},{14,10},{16,20},{18,... | collective-permute-start | bytes 1572872 | tf_op jit(solution)/shard_map/ppermute | solution.py:75
  56.4 19.9 %collective-permute-start.14 = (bf16[128,2048]{1,0:T(8,128)(2,1)S(1)}, bf16[128,2048]{1,0:T(8,128)(2,1)S(1)}, u32[]{:S(2)}, u32[]{:S(2)}) collective-permute-start(bf16[128,2048]{1,0:T(8,128)(2,1)S(1)} %collective-permute-done.8.refs_12_), channel_id=1, source_target_pairs={{0,8},{2,18},{4,12},{6,22},{8,24},{10,2},{12,28},{14,6},{16,0},{18... | collective-permute-start | bytes 1572872 | tf_op jit(solution)/shard_map/ppermute | solution.py:75
  61.5 14.7 %collective-permute-start.15 = (bf16[896,2048]{1,0:T(8,128)(2,1)}, bf16[896,2048]{1,0:T(8,128)(2,1)S(1)}, u32[]{:S(2)}, u32[]{:S(2)}) collective-permute-start(bf16[896,2048]{1,0:T(8,128)(2,1)} %get-tuple-element.77), channel_id=1, source_target_pairs={{0,2},{2,0},{4,6},{6,4},{8,10},{10,8},{12,14},{14,12},{16,18},{18,... | collective-permute-start | bytes 11010056 | tf_op jit(solution)/shard_map/ppermute | solution.py:75
  71.3 14.6 %collective-permute-start.18 = (bf16[128,2048]{1,0:T(8,128)(2,1)S(1)}, bf16[128,2048]{1,0:T(8,128)(2,1)S(1)}, u32[]{:S(2)}, u32[]{:S(2)}) collective-permute-start(bf16[128,2048]{1,0:T(8,128)(2,1)S(1)} %collective-permute-done.16.refs_5_), channel_id=1, source_target_pairs={{0,4},{2,6},{4,0},{6,2},{8,12},{10,14},{12,8},{14,10},{16,20},{18,... | collective-permute-start | bytes 1572872 | tf_op jit(solution)/shard_map/ppermute | solution.py:75
  75.3 13.7 %collective-permute-start.20 = (bf16[128,2048]{1,0:T(8,128)(2,1)S(1)}, bf16[128,2048]{1,0:T(8,128)(2,1)S(1)}, u32[]{:S(2)}, u32[]{:S(2)}) collective-permute-start(bf16[128,2048]{1,0:T(8,128)(2,1)S(1)} %collective-permute-done.19.refs_4_), channel_id=1, source_target_pairs={{0,8},{2,18},{4,12},{6,22},{8,24},{10,2},{12,28},{14,6},{16,0},{18... | collective-permute-start | bytes 1572872 | tf_op jit(solution)/shard_map/ppermute | solution.py:75
  91.4 7.1 %collective-permute-start.22 = (bf16[896,2048]{1,0:T(8,128)(2,1)S(1)}, bf16[896,2048]{1,0:T(8,128)(2,1)S(1)}, u32[]{:S(2)}, u32[]{:S(2)}) collective-permute-start(bf16[896,2048]{1,0:T(8,128)(2,1)S(1)} %get-tuple-element.105), channel_id=1, source_target_pairs={{0,2},{2,0},{4,6},{6,4},{8,10},{10,8},{12,14},{14,12},{16,18},{18,... | collective-permute-start | bytes 11010056 | tf_op jit(solution)/shard_map/ppermute | solution.py:395
  91.5 6.4 %collective-permute-start.21 = (f32[2048]{0:T(1024)S(1)}, f32[2048]{0:T(1024)S(1)}, u32[]{:S(2)}, u32[]{:S(2)}) collective-permute-start(f32[2048]{0:T(1024)S(1)} %bitcast.39), channel_id=1, source_target_pairs={{0,2},{2,0},{4,6},{6,4},{8,10},{10,8},{12,14},{14,12},{16,18},{18,... | collective-permute-start | bytes 24584 | tf_op jit(solution)/shard_map/ppermute | solution.py:395
  92.0 5.9 %copy-start = (bf16[4096]{0:T(1024)(128)(2,1)S(1)}, bf16[4096]{0:T(1024)(128)(2,1)}, u32[]{:S(2)}) copy-start(bf16[4096]{0:T(1024)(128)(2,1)} %param.10) | copy-start | bytes 24580

commit v13 on v10

--- a/solution.py
+++ b/solution.py
@@ -124,20 +124,28 @@
     facts_merge()
     for k in range(2, m):
         for kind in range(2):
-            facts_step()
+            pending = bits and (k, kind) == (m - 2, 1)
+            if pending:
+                facts_send()
+            elif k < m - 1:
+                facts_step()
             if k < m - 1:
                 sends = [((k + 1, 0, kind), (k, 0, kind), ring[kind]), ((k, 1, kind), (k, 0, kind), across)]
             elif kind == 0:
                 sends = []
             else:
                 sends = [((k, 1, 0), (k - 1, 1, 0), ring[0]), ((k, 1, 1), (k, 0, 1), across)]
-            waits = [(k, 0, kind), (k - 1, 1, kind), "facts"]
-            if k == m - 2 and kind == 1:
+            waits = [(k, 0, kind), (k - 1, 1, kind)]
+            if (k, kind) != (m - 2, 1):
+                waits += ["facts"] + ["other facts"] * bool(bits)
+            if k == m - 1 and kind == 0:
                 sends.append(("other picks", "away picks", core))
             if k == m - 1 and kind == 1:
                 waits += ["other picks", "early own", "values", "returns"]
             f.event(waits, sends)
-            if k == m - 2 and kind == 1:
+            if k == m - 1 and kind == 0:
+                if bits:
+                    facts_merge()
                 while bits:
                     facts_step()
                 early_own(have)

time: 102 us -> 111 us (1.088)
  waiting for transfers between devices: 27.5 us -> 38.6 us
  starting transfers between devices: 34.7 us -> 32.4 us
    ppermute x16, waiting for transfers between devices: 10.9 us -> 20.5 us  [event(): self.have[name] = lax.ppermute(self.have[source], 'seq', pairs)]
    ppermute x4, starting transfers between devices: 5.84 us -> 2.44 us  [butterfly_send(): lax.ppermute(x, axis, [(i, i ^ bit) for i in range(lax.axis_size(axis))])]
    ppermute x1, waiting for transfers between devices: 0.75 us -> 2.09 us  [butterfly_sum(): x = x + lax.ppermute(x, axis, [(i, i ^ step) for i in range(count)])]
  transfers between devices with their start and end apart: 23 -> 23, of which waited for: 11 -> 11; matrix products, arithmetic and copies ran while one was open for 7% -> 7% of each run, Pallas kernels for 24% -> 23%
where the time goes in v13:
time: 111 us; the launch traced here: 109 us
  waiting for transfers between devices  38.6 us (35%)
  starting transfers between devices  32.4 us (29%)
  Pallas kernels  28.9 us (26%)
  other arithmetic  6.18 us (6%)
  local copies, waits for them, and re-layouts  2.23 us (2%)
    ppermute x16, starting transfers between devices, event(): self.have[name] = lax.ppermute(self.have[source], 'seq', pairs)  27.6 us
    pallas_call x4, Pallas kernels, product(): pl.pallas_call(functools.partial(product_kernel, tok, count, first, len(g...  22.7 us
    ppermute x16, waiting for transfers between devices, event(): self.have[name] = lax.ppermute(self.have[source], 'seq', pairs)  20.5 us
    ppermute x4, waiting for transfers between devices, butterfly_send(): lax.ppermute(x, axis, [(i, i ^ bit) for i in range(lax.axis_size(axis))])  14.6 us
    pallas_call x1, Pallas kernels, pick(): pl.pallas_call(functools.partial(pick_kernel, tok), grid_spec=pltpu.Prefe...  4.35 us
    ppermute x4, starting transfers between devices, butterfly_send(): lax.ppermute(x, axis, [(i, i ^ bit) for i in range(lax.axis_size(axis))])  2.44 us
  transfers between devices with their start and end apart: 23, of which 11 were waited for; matrix products, arithmetic and copies ran while one was open for 7% of the time, Pallas kernels for 23%

profile of v13, /device:TPU:0, one launch (start us, length us, event | category | flops | bytes accessed | tf_op | source)
XLA Modules:
  0.0 109.3 jit_solution(6105374446892677198)
XLA Ops:
  0.7 1.3 %constant_dynamic-slice_fusion.1 = (bf16[128,2048]{1,0:T(8,128)(2,1)S(1)}, bf16[128,2048]{1,0:T(8,128)(2,1)S(1)}) fusion(bf16[128,4096]{1,0:T(8,128)(2,1)} %param.8, s32[]{:T(128)S(6)} %select_n.133, s32[]{:T(128)S(6)} %select_n.132), kind=kLoop, calls=%fused_computation.58 | loop fusion | bytes 2097160 | tf_op jit(solution)/shard_map/dynamic_slice | solution.py:88
  1.9 4.1 %collective-permute-start.3 = (bf16[128,2048]{1,0:T(8,128)(2,1)S(1)}, bf16[128,2048]{1,0:T(8,128)(2,1)S(1)}, u32[]{:S(2)}, u32[]{:S(2)}) collective-permute-start(bf16[128,2048]{1,0:T(8,128)(2,1)S(1)} %get-tuple-element.62.refs_3_), channel_id=1, source_target_pairs={{0,16},{2,10},{4,20},{6,14},{8,0},{10,26},{12,4},{14,30},{16,24},{... | collective-permute-start | bytes 1572872 | tf_op jit(solution)/shard_map/ppermute | solution.py:75
  6.0 1.5 %collective-permute-start.4 = (bf16[128,2048]{1,0:T(8,128)(2,1)S(1)}, bf16[128,2048]{1,0:T(8,128)(2,1)S(1)}, u32[]{:S(2)}, u32[]{:S(2)}) collective-permute-start(bf16[128,2048]{1,0:T(8,128)(2,1)S(1)} %get-tuple-element.62.refs_3_), channel_id=1, source_target_pairs={{0,4},{2,6},{4,0},{6,2},{8,12},{10,14},{12,8},{14,10},{16,20},{18,... | collective-permute-start | bytes 1572872 | tf_op jit(solution)/shard_map/ppermute | solution.py:75
  7.5 0.0 collective-permute-start
  7.6 0.7 fusion.14.owners
  8.3 0.7 multiply_bitcast_fusion
  9.0 0.7 convert_multiply_fusion.3
  9.7 0.9 collective-permute-start.1
  10.5 0.5 collective-permute-start.2
  11.1 1.7 %fusion = (f32[128]{0:T(128)S(1)}, f32[128]{0:T(128)S(1)}) fusion(bf16[128,4096]{1,0:T(8,128)(2,1)} %param.8, f32[4096]{0:T(1024)S(1)} %convert_multiply_fusion.3), kind=kLoop, calls=%fused_computation.2 | loop fusion | flops 2621184 | bytes 1065984 | tf_op jit(solution)/shard_map/reduce_sum | solution.py:414
  12.7 1.6 %collective-permute-start.5 = (f32[4,128]{1,0:T(4,128)S(1)}, f32[4,128]{1,0:T(4,128)S(1)}, u32[]{:S(2)}, u32[]{:S(2)}) collective-permute-start(f32[4,128]{1,0:T(4,128)S(1)} %pad_maximum_fusion.2), channel_id=1, source_target_pairs={{0,1},{1,0},{2,3},{3,2},{4,5},{5,4},{6,7},{7,6},{8,9},{9,8},{10,11... | collective-permute-start | bytes 6152 | tf_op jit(solution)/shard_map/ppermute | solution.py:18
  14.3 2.1 %collective-permute-done.5 = f32[4,128]{1,0:T(4,128)S(1)} collective-permute-done((f32[4,128]{1,0:T(4,128)S(1)}, f32[4,128]{1,0:T(4,128)S(1)}, u32[]{:S(2)}, u32[]{:S(2)}) %collective-permute-start.5) | collective-permute-done | bytes 2080 | tf_op jit(solution)/shard_map/ppermute | solution.py:18
  16.4 4.3 %shard_map.111 = (bf16[896,2048]{1,0:T(8,128)(2,1)S(1)}, bf16[896,2048]{1,0:T(8,128)(2,1)}) custom-call(s32[32]{0:T(128)S(1)} %fusion.14.owners, bf16[896,2048]{1,0:T(8,128)(2,1)} %hidden), custom_call_target="tpu_custom_call" | custom-call | bytes 1 | tf_op jit(solution)/shard_map/pallas_call | solution.py:196
  20.7 3.8 %collective-permute-done.3.refs_7_ = bf16[128,2048]{1,0:T(8,128)(2,1)S(1)} collective-permute-done((bf16[128,2048]{1,0:T(8,128)(2,1)S(1)}, bf16[128,2048]{1,0:T(8,128)(2,1)S(1)}, u32[]{:S(2)}, u32[]{:S(2)}) %collective-permute-start.3) | collective-permute-done | bytes 524320 | tf_op jit(solution)/shard_map/ppermute | solution.py:75
  24.6 1.2 %collective-permute-done.6 = f32[1,4,128]{2,1,0:T(4,128)S(1)} collective-permute-done((f32[1,4,128]{2,1,0:T(4,128)S(1)}, f32[1,4,128]{2,1,0:T(4,128)S(1)}, u32[]{:S(2)}, u32[]{:S(2)}) %collective-permute-start.6) | collective-permute-done | bytes 2080 | tf_op jit(solution)/shard_map/ppermute | solution.py:24
  25.7 0.1 broadcast_select_fusion.3
  25.8 1.7 %collective-permute-start.7 = (f32[2,4,128]{2,0,1:T(2,128)S(1)}, f32[2,4,128]{2,0,1:T(2,128)S(1)}, u32[]{:S(2)}, u32[]{:S(2)}) collective-permute-start(f32[2,4,128]{2,0,1:T(2,128)S(1)} %broadcast_select_fusion.3), channel_id=1, source_target_pairs={{0,8},{2,10},{4,12},{6,14},{8,0},{10,2},{12,4},{14,6},{16,24},{18,... | collective-permute-start | bytes 12296 | tf_op jit(solution)/shard_map/ppermute | solution.py:24
  27.4 3.8 %collective-permute-start.12 = (bf16[128,2048]{1,0:T(8,128)(2,1)S(1)}, bf16[128,2048]{1,0:T(8,128)(2,1)S(1)}, u32[]{:S(2)}, u32[]{:S(2)}) collective-permute-start(bf16[128,2048]{1,0:T(8,128)(2,1)S(1)} %collective-permute-done.3.refs_7_), channel_id=1, source_target_pairs={{0,16},{2,10},{4,20},{6,14},{8,0},{10,26},{12,4},{14,30},{16,24},{... | collective-permute-start | bytes 1572872 | tf_op jit(solution)/shard_map/ppermute | solution.py:75
  31.2 2.0 %collective-permute-start.13 = (bf16[128,2048]{1,0:T(8,128)(2,1)S(1)}, bf16[128,2048]{1,0:T(8,128)(2,1)S(1)}, u32[]{:S(2)}, u32[]{:S(2)}) collective-permute-start(bf16[128,2048]{1,0:T(8,128)(2,1)S(1)} %collective-permute-done.3.refs_7_), channel_id=1, source_target_pairs={{0,4},{2,6},{4,0},{6,2},{8,12},{10,14},{12,8},{14,10},{16,20},{18,... | collective-permute-start | bytes 1572872 | tf_op jit(solution)/shard_map/ppermute | solution.py:75
  33.2 0.0 collective-permute-done.7
  33.2 0.0 collective-permute-done.1.refs_8_
  33.2 0.0 collective-permute-done.2.refs_6_
  33.3 0.1 broadcast_select_fusion
  33.3 0.0 collective-permute-start.14
  33.3 0.1 collective-permute-start.8
  33.4 1.9 %collective-permute-start.9 = (bf16[128,2048]{1,0:T(8,128)(2,1)S(1)}, bf16[128,2048]{1,0:T(8,128)(2,1)S(1)}, u32[]{:S(2)}, u32[]{:S(2)}) collective-permute-start(bf16[128,2048]{1,0:T(8,128)(2,1)S(1)} %collective-permute-done.1.refs_8_), channel_id=1, source_target_pairs={{0,4},{2,6},{4,0},{6,2},{8,12},{10,14},{12,8},{14,10},{16,20},{18,... | collective-permute-start | bytes 1572872 | tf_op jit(solution)/shard_map/ppermute | solution.py:75
  35.4 10.9 %collective-permute-done.14 = f32[2,2,4,128]{3,1,0,2:T(2,128)S(1)} collective-permute-done((f32[2,2,4,128]{3,1,0,2:T(2,128)S(1)}, f32[2,2,4,128]{3,1,0,2:T(2,128)S(1)}, u32[]{:S(2)}, u32[]{:S(2)}) %collective-permute-start.14) | collective-permute-done | bytes 8224 | tf_op jit(solution)/shard_map/ppermute | solution.py:24
  46.3 0.1 select_bitcast_fusion.1
  46.3 2.0 %collective-permute-done.12.refs_11_ = bf16[128,2048]{1,0:T(8,128)(2,1)S(1)} collective-permute-done((bf16[128,2048]{1,0:T(8,128)(2,1)S(1)}, bf16[128,2048]{1,0:T(8,128)(2,1)S(1)}, u32[]{:S(2)}, u32[]{:S(2)}) %collective-permute-start.12) | collective-permute-done | bytes 524320 | tf_op jit(solution)/shard_map/ppermute | solution.py:75
  48.3 0.0 collective-permute-start.15
  48.3 4.6 %collective-permute-start.16 = (bf16[128,2048]{1,0:T(8,128)(2,1)S(1)}, bf16[128,2048]{1,0:T(8,128)(2,1)S(1)}, u32[]{:S(2)}, u32[]{:S(2)}) collective-permute-start(bf16[128,2048]{1,0:T(8,128)(2,1)S(1)} %collective-permute-done.12.refs_11_), channel_id=1, source_target_pairs={{0,4},{2,6},{4,0},{6,2},{8,12},{10,14},{12,8},{14,10},{16,20},{18,... | collective-permute-start | bytes 1572872 | tf_op jit(solution)/shard_map/ppermute | solution.py:75
  53.0 0.8 collective-permute-start.17
  53.7 3.0 %collective-permute-done.8.refs_12_ = bf16[128,2048]{1,0:T(8,128)(2,1)S(1)} collective-permute-done((bf16[128,2048]{1,0:T(8,128)(2,1)S(1)}, bf16[128,2048]{1,0:T(8,128)(2,1)S(1)}, u32[]{:S(2)}, u32[]{:S(2)}) %collective-permute-start.8) | collective-permute-done | bytes 524320 | tf_op jit(solution)/shard_map/ppermute | solution.py:75
  56.8 2.3 %collective-permute-start.10 = (bf16[128,2048]{1,0:T(8,128)(2,1)S(1)}, bf16[128,2048]{1,0:T(8,128)(2,1)S(1)}, u32[]{:S(2)}, u32[]{:S(2)}) collective-permute-start(bf16[128,2048]{1,0:T(8,128)(2,1)S(1)} %collective-permute-done.8.refs_12_), channel_id=1, source_target_pairs={{0,8},{2,18},{4,12},{6,22},{8,24},{10,2},{12,28},{14,6},{16,0},{18... | collective-permute-start | bytes 1572872 | tf_op jit(solution)/shard_map/ppermute | solution.py:75
  59.1 0.0 collective-permute-start.11
  59.1 2.5 %collective-permute-done.17 = f32[8,4,128]{2,0,1:T(8,128)S(1)} collective-permute-done((f32[8,4,128]{2,0,1:T(8,128)S(1)}, f32[8,4,128]{2,0,1:T(8,128)S(1)}, u32[]{:S(2)}, u32[]{:S(2)}) %collective-permute-start.17) | collective-permute-done | bytes 16416 | tf_op jit(solution)/shard_map/ppermute | solution.py:24
  61.6 7.9 %collective-permute-done.15.refs_5_ = bf16[128,2048]{1,0:T(8,128)(2,1)S(1)} collective-permute-done((bf16[128,2048]{1,0:T(8,128)(2,1)S(1)}, bf16[128,2048]{1,0:T(8,128)(2,1)S(1)}, u32[]{:S(2)}, u32[]{:S(2)}) %collective-permute-start.15) | collective-permute-done | bytes 524320 | tf_op jit(solution)/shard_map/ppermute | solution.py:75
  69.5 0.0 collective-permute-done.16.refs_3_
  69.5 0.1 fusion.15
  69.6 0.3 select_reduce_fusion.1
  69.9 0.1 broadcast_compare_fusion
  70.0 0.1 select_reduce_fusion.5
  70.1 0.7 select_reduce_fusion
  70.8 0.1 slice_reduce_fusion
  70.9 0.1 select_reduce_fusion.2
  71.0 0.1 select_reduce_fusion.4
  71.2 0.6 select_reduce_fusion.3
  71.8 0.1 broadcast_in_dim.204
  71.8 0.1 eq.113
  72.0 2.6 %collective-permute-start.18 = (bf16[896,2048]{1,0:T(8,128)(2,1)}, bf16[896,2048]{1,0:T(8,128)(2,1)S(1)}, u32[]{:S(2)}, u32[]{:S(2)}) collective-permute-start(bf16[896,2048]{1,0:T(8,128)(2,1)} %get-tuple-element.82), channel_id=1, source_target_pairs={{0,2},{2,0},{4,6},{6,4},{8,10},{10,8},{12,14},{14,12},{16,18},{18,... | collective-permute-start | bytes 11010056 | tf_op jit(solution)/shard_map/ppermute | solution.py:75
  74.6 7.6 %shard_map.112 = (f32[896,2048]{1,0:T(8,128)S(1)}, bf16[1280,2048]{1,0:T(8,128)(2,1)S(1)}, f32[16,1,2048]{2,1,0:T(1,128)S(1)}) custom-call(s32[32]{0:T(128)S(1)} %fusion.14.owners, s32[1]{0:T(128)} %constant.68.clone.1.where, bf16[896,2048]{1,0:T(8,128)(2,1)S(1)} %get-tuple-element.84.refs_0_, f32[8,2048]{1,0:T(8,128)S(1)} %select_maximum_fusion.refs_1_, ...), custom_call_target="tpu_custom_call" | custom-call | flops 46976204800 | bytes 86376448 | tf_op jit(solution)/shard_map/pallas_call | solution.py:315
  82.2 0.0 collective-permute-done.18.refs_0_
  82.2 0.2 collective-permute-start.19
  82.5 3.0 %collective-permute-start.20 = (bf16[128,2048]{1,0:T(8,128)(2,1)S(1)}, bf16[128,2048]{1,0:T(8,128)(2,1)S(1)}, u32[]{:S(2)}, u32[]{:S(2)}) collective-permute-start(bf16[128,2048]{1,0:T(8,128)(2,1)S(1)} %collective-permute-done.10.refs_6_), channel_id=1, source_target_pairs={{0,4},{2,6},{4,0},{6,2},{8,12},{10,14},{12,8},{14,10},{16,20},{18,... | collective-permute-start | bytes 1572872 | tf_op jit(solution)/shard_map/ppermute | solution.py:75
  85.5 8.1 %shard_map.113 = (f32[896,2048]{1,0:T(8,128)S(1)}, bf16[512,2048]{1,0:T(8,128)(2,1)S(1)}, f32[16,1,2048]{2,1,0:T(1,128)S(1)}) custom-call(s32[32]{0:T(128)S(1)} %fusion.14.owners, s32[1]{0:T(128)} %constant.68.clone.1.where, bf16[896,2048]{1,0:T(8,128)(2,1)S(1)} %collective-permute-done.18.refs_0_, f32[8,2048]{1,0:T(8,128)S(1)} %select_maximum_fusion.refs_1_, ...), custom_call_target="tpu_custom_call" | custom-call | flops 6576668672 | bytes 21561344 | tf_op jit(solution)/shard_map/pallas_call | solution.py:315
  93.6 3.6 %collective-permute-done.19.refs_3_ = bf16[128,2048]{1,0:T(8,128)(2,1)S(1)} collective-permute-done((bf16[128,2048]{1,0:T(8,128)(2,1)S(1)}, bf16[128,2048]{1,0:T(8,128)(2,1)S(1)}, u32[]{:S(2)}, u32[]{:S(2)}) %collective-permute-start.19) | collective-permute-done | bytes 524320 | tf_op jit(solution)/shard_map/ppermute | solution.py:75
  97.2 0.2 collective-permute-done.20.refs_4_
  97.4 2.4 %shard_map.114 = (bf16[896,2048]{1,0:T(8,128)(2,1)S(1)}, bf16[256,2048]{1,0:T(8,128)(2,1)S(1)}, f32[1,2048]{1,0:T(1,128)S(1)}) custom-call(s32[32]{0:T(128)S(1)} %fusion.14.owners, s32[1]{0:T(128)} %constant.68.clone.1.where, bf16[896,2048]{1,0:T(8,128)(2,1)S(1)} %collective-permute-done.18.refs_0_, f32[8,2048]{1,0:T(8,128)S(1)} %select_maximum_fusion.refs_1_, ...), custom_call_target="tpu_custom_call" | custom-call | flops 939524096 | bytes 12517376 | tf_op jit(solution)/shard_map/pallas_call | solution.py:315
  99.9 0.7 collective-permute-start.22
  100.6 0.1 collective-permute-start.21
  100.7 4.5 %shard_map.115.whole = bf16[896,4096]{1,0:T(8,128)(2,1)} custom-call(s32[32]{0:T(128)S(1)} %fusion.14.owners, s32[1]{0:T(128)} %bitcast.where, bf16[896,2048]{1,0:T(8,128)(2,1)S(1)} %get-tuple-element.84.refs_0_, bf16[256,2048]{1,0:T(8,128)(2,1)S(1)} %get-tuple-element.111.refs_1_, bf16[512,2048]{1,0:T(8,128)(2,1)S(1)} %get-tuple-element.112.refs_2_, ...), custom_call_target="tpu_custom_call" | custom-call | flops 2818572288 | bytes 15532032 | tf_op jit(solution)/shard_map/pallas_call | solution.py:315
  105.2 1.4 %collective-permute-done.21 = f32[2048]{0:T(1024)S(1)} collective-permute-done((f32[2048]{0:T(1024)S(1)}, f32[2048]{0:T(1024)S(1)}, u32[]{:S(2)}, u32[]{:S(2)}) %collective-permute-start.21) | collective-permute-done | bytes 8224 | tf_op jit(solution)/shard_map/ppermute | solution.py:401
  106.7 0.6 convert_multiply_fusion.2
  107.3 1.9 %shard_map.116 = bf16[896,4096]{1,0:T(8,128)(2,1)} custom-call(s32[1]{0:T(128)S(6)} %sub.26.where, bf16[896,2048]{1,0:T(8,128)(2,1)S(1)} %collective-permute-done.22.part, bf16[896,4096]{1,0:T(8,128)(2,1)} %shard_map.115.whole), custom_call_target="tpu_custom_call", output_to_operand_aliasing={{}: (2, {})} | custom-call | bytes 7340032 | tf_op jit(solution)/shard_map/pallas_call | solution.py:356
  (23 shorter events, 0.2 us)
Async XLA Ops:
  1.9 22.6 %collective-permute-start.3 = (bf16[128,2048]{1,0:T(8,128)(2,1)S(1)}, bf16[128,2048]{1,0:T(8,128)(2,1)S(1)}, u32[]{:S(2)}, u32[]{:S(2)}) collective-permute-start(bf16[128,2048]{1,0:T(8,128)(2,1)S(1)} %get-tuple-element.62.refs_3_), channel_id=1, source_target_pairs={{0,16},{2,10},{4,20},{6,14},{8,0},{10,26},{12,4},{14,30},{16,24},{... | collective-permute-start | bytes 1572872 | tf_op jit(solution)/shard_map/ppermute | solution.py:75
  6.0 18.5 %collective-permute-start.4 = (bf16[128,2048]{1,0:T(8,128)(2,1)S(1)}, bf16[128,2048]{1,0:T(8,128)(2,1)S(1)}, u32[]{:S(2)}, u32[]{:S(2)}) collective-permute-start(bf16[128,2048]{1,0:T(8,128)(2,1)S(1)} %get-tuple-element.62.refs_3_), channel_id=1, source_target_pairs={{0,4},{2,6},{4,0},{6,2},{8,12},{10,14},{12,8},{14,10},{16,20},{18,... | collective-permute-start | bytes 1572872 | tf_op jit(solution)/shard_map/ppermute | solution.py:75
  7.5 2.1 %collective-permute-start = (bf16[128,2048]{1,0:T(8,128)(2,1)S(1)}, bf16[128,2048]{1,0:T(8,128)(2,1)S(1)}, u32[]{:S(2)}, u32[]{:S(2)}) collective-permute-start(bf16[128,2048]{1,0:T(8,128)(2,1)S(1)} %get-tuple-element.59), channel_id=1, source_target_pairs={{0,2},{2,0},{4,6},{6,4},{8,10},{10,8},{12,14},{14,12},{16,18},{18,... | collective-permute-start | bytes 1572872 | tf_op jit(solution)/shard_map/ppermute | solution.py:75
  9.7 23.6 %collective-permute-start.1 = (bf16[128,2048]{1,0:T(8,128)(2,1)S(1)}, bf16[128,2048]{1,0:T(8,128)(2,1)S(1)}, u32[]{:S(2)}, u32[]{:S(2)}) collective-permute-start(bf16[128,2048]{1,0:T(8,128)(2,1)S(1)} %collective-permute-done.refs_4_), channel_id=1, source_target_pairs={{0,8},{2,18},{4,12},{6,22},{8,24},{10,2},{12,28},{14,6},{16,0},{18... | collective-permute-start | bytes 1572872 | tf_op jit(solution)/shard_map/ppermute | solution.py:75
  10.5 22.7 %collective-permute-start.2 = (bf16[128,2048]{1,0:T(8,128)(2,1)S(1)}, bf16[128,2048]{1,0:T(8,128)(2,1)S(1)}, u32[]{:S(2)}, u32[]{:S(2)}) collective-permute-start(bf16[128,2048]{1,0:T(8,128)(2,1)S(1)} %collective-permute-done.refs_4_), channel_id=1, source_target_pairs={{0,4},{2,6},{4,0},{6,2},{8,12},{10,14},{12,8},{14,10},{16,20},{18,... | collective-permute-start | bytes 1572872 | tf_op jit(solution)/shard_map/ppermute | solution.py:75
  12.7 3.7 %collective-permute-start.5 = (f32[4,128]{1,0:T(4,128)S(1)}, f32[4,128]{1,0:T(4,128)S(1)}, u32[]{:S(2)}, u32[]{:S(2)}) collective-permute-start(f32[4,128]{1,0:T(4,128)S(1)} %pad_maximum_fusion.2), channel_id=1, source_target_pairs={{0,1},{1,0},{2,3},{3,2},{4,5},{5,4},{6,7},{7,6},{8,9},{9,8},{10,11... | collective-permute-start | bytes 6152 | tf_op jit(solution)/shard_map/ppermute | solution.py:18
  24.6 1.2 %collective-permute-start.6 = (f32[1,4,128]{2,1,0:T(4,128)S(1)}, f32[1,4,128]{2,1,0:T(4,128)S(1)}, u32[]{:S(2)}, u32[]{:S(2)}) collective-permute-start(f32[1,4,128]{2,1,0:T(4,128)S(1)} %add_bitcast_fusion), channel_id=1, source_target_pairs={{0,2},{2,0},{4,6},{6,4},{8,10},{10,8},{12,14},{14,12},{16,18},{18,... | collective-permute-start | bytes 6152 | tf_op jit(solution)/shard_map/ppermute | solution.py:24
  25.8 7.5 %collective-permute-start.7 = (f32[2,4,128]{2,0,1:T(2,128)S(1)}, f32[2,4,128]{2,0,1:T(2,128)S(1)}, u32[]{:S(2)}, u32[]{:S(2)}) collective-permute-start(f32[2,4,128]{2,0,1:T(2,128)S(1)} %broadcast_select_fusion.3), channel_id=1, source_target_pairs={{0,8},{2,10},{4,12},{6,14},{8,0},{10,2},{12,4},{14,6},{16,24},{18,... | collective-permute-start | bytes 12296 | tf_op jit(solution)/shard_map/ppermute | solution.py:24
  27.4 20.9 %collective-permute-start.12 = (bf16[128,2048]{1,0:T(8,128)(2,1)S(1)}, bf16[128,2048]{1,0:T(8,128)(2,1)S(1)}, u32[]{:S(2)}, u32[]{:S(2)}) collective-permute-start(bf16[128,2048]{1,0:T(8,128)(2,1)S(1)} %collective-permute-done.3.refs_7_), channel_id=1, source_target_pairs={{0,16},{2,10},{4,20},{6,14},{8,0},{10,26},{12,4},{14,30},{16,24},{... | collective-permute-start | bytes 1572872 | tf_op jit(solution)/shard_map/ppermute | solution.py:75
  31.2 17.1 %collective-permute-start.13 = (bf16[128,2048]{1,0:T(8,128)(2,1)S(1)}, bf16[128,2048]{1,0:T(8,128)(2,1)S(1)}, u32[]{:S(2)}, u32[]{:S(2)}) collective-permute-start(bf16[128,2048]{1,0:T(8,128)(2,1)S(1)} %collective-permute-done.3.refs_7_), channel_id=1, source_target_pairs={{0,4},{2,6},{4,0},{6,2},{8,12},{10,14},{12,8},{14,10},{16,20},{18,... | collective-permute-start | bytes 1572872 | tf_op jit(solution)/shard_map/ppermute | solution.py:75
  33.3 12.9 %collective-permute-start.14 = (f32[2,2,4,128]{3,1,0,2:T(2,128)S(1)}, f32[2,2,4,128]{3,1,0,2:T(2,128)S(1)}, u32[]{:S(2)}, u32[]{:S(2)}) collective-permute-start(f32[2,2,4,128]{3,1,0,2:T(2,128)S(1)} %broadcast_select_fusion), channel_id=1, source_target_pairs={{0,4},{2,6},{4,0},{6,2},{8,12},{10,14},{12,8},{14,10},{16,20},{18,... | collective-permute-start | bytes 24584 | tf_op jit(solution)/shard_map/ppermute | solution.py:24
  33.3 23.4 %collective-permute-start.8 = (bf16[128,2048]{1,0:T(8,128)(2,1)S(1)}, bf16[128,2048]{1,0:T(8,128)(2,1)S(1)}, u32[]{:S(2)}, u32[]{:S(2)}) collective-permute-start(bf16[128,2048]{1,0:T(8,128)(2,1)S(1)} %collective-permute-done.1.refs_8_), channel_id=1, source_target_pairs={{0,8},{2,18},{4,12},{6,22},{8,24},{10,2},{12,28},{14,6},{16,0},{18... | collective-permute-start | bytes 1572872 | tf_op jit(solution)/shard_map/ppermute | solution.py:75
  33.4 23.4 %collective-permute-start.9 = (bf16[128,2048]{1,0:T(8,128)(2,1)S(1)}, bf16[128,2048]{1,0:T(8,128)(2,1)S(1)}, u32[]{:S(2)}, u32[]{:S(2)}) collective-permute-start(bf16[128,2048]{1,0:T(8,128)(2,1)S(1)} %collective-permute-done.1.refs_8_), channel_id=1, source_target_pairs={{0,4},{2,6},{4,0},{6,2},{8,12},{10,14},{12,8},{14,10},{16,20},{18,... | collective-permute-start | bytes 1572872 | tf_op jit(solution)/shard_map/ppermute | solution.py:75
  48.3 21.2 %collective-permute-start.15 = (bf16[128,2048]{1,0:T(8,128)(2,1)S(1)}, bf16[128,2048]{1,0:T(8,128)(2,1)S(1)}, u32[]{:S(2)}, u32[]{:S(2)}) collective-permute-start(bf16[128,2048]{1,0:T(8,128)(2,1)S(1)} %collective-permute-done.12.refs_11_), channel_id=1, source_target_pairs={{0,16},{2,10},{4,20},{6,14},{8,0},{10,26},{12,4},{14,30},{16,24},{... | collective-permute-start | bytes 1572872 | tf_op jit(solution)/shard_map/ppermute | solution.py:75
  48.3 21.2 %collective-permute-start.16 = (bf16[128,2048]{1,0:T(8,128)(2,1)S(1)}, bf16[128,2048]{1,0:T(8,128)(2,1)S(1)}, u32[]{:S(2)}, u32[]{:S(2)}) collective-permute-start(bf16[128,2048]{1,0:T(8,128)(2,1)S(1)} %collective-permute-done.12.refs_11_), channel_id=1, source_target_pairs={{0,4},{2,6},{4,0},{6,2},{8,12},{10,14},{12,8},{14,10},{16,20},{18,... | collective-permute-start | bytes 1572872 | tf_op jit(solution)/shard_map/ppermute | solution.py:75
  53.0 8.6 %collective-permute-start.17 = (f32[8,4,128]{2,0,1:T(8,128)S(1)}, f32[8,4,128]{2,0,1:T(8,128)S(1)}, u32[]{:S(2)}, u32[]{:S(2)}) collective-permute-start(f32[8,4,128]{2,0,1:T(8,128)S(1)} %bitcast.47), channel_id=1, source_target_pairs={{0,16},{2,18},{4,20},{6,22},{8,24},{10,26},{12,28},{14,30},{16,0},... | collective-permute-start | bytes 49160 | tf_op jit(solution)/shard_map/ppermute | solution.py:24
  56.8 25.4 %collective-permute-start.10 = (bf16[128,2048]{1,0:T(8,128)(2,1)S(1)}, bf16[128,2048]{1,0:T(8,128)(2,1)S(1)}, u32[]{:S(2)}, u32[]{:S(2)}) collective-permute-start(bf16[128,2048]{1,0:T(8,128)(2,1)S(1)} %collective-permute-done.8.refs_12_), channel_id=1, source_target_pairs={{0,8},{2,18},{4,12},{6,22},{8,24},{10,2},{12,28},{14,6},{16,0},{18... | collective-permute-start | bytes 1572872 | tf_op jit(solution)/shard_map/ppermute | solution.py:75
  59.1 23.2 %collective-permute-start.11 = (bf16[128,2048]{1,0:T(8,128)(2,1)S(1)}, bf16[128,2048]{1,0:T(8,128)(2,1)S(1)}, u32[]{:S(2)}, u32[]{:S(2)}) collective-permute-start(bf16[128,2048]{1,0:T(8,128)(2,1)S(1)} %collective-permute-done.8.refs_12_), channel_id=1, source_target_pairs={{0,4},{2,6},{4,0},{6,2},{8,12},{10,14},{12,8},{14,10},{16,20},{18,... | collective-permute-start | bytes 1572872 | tf_op jit(solution)/shard_map/ppermute | solution.py:75
  72.0 10.3 %collective-permute-start.18 = (bf16[896,2048]{1,0:T(8,128)(2,1)}, bf16[896,2048]{1,0:T(8,128)(2,1)S(1)}, u32[]{:S(2)}, u32[]{:S(2)}) collective-permute-start(bf16[896,2048]{1,0:T(8,128)(2,1)} %get-tuple-element.82), channel_id=1, source_target_pairs={{0,2},{2,0},{4,6},{6,4},{8,10},{10,8},{12,14},{14,12},{16,18},{18,... | collective-permute-start | bytes 11010056 | tf_op jit(solution)/shard_map/ppermute | solution.py:75
  82.2 15.0 %collective-permute-start.19 = (bf16[128,2048]{1,0:T(8,128)(2,1)S(1)}, bf16[128,2048]{1,0:T(8,128)(2,1)S(1)}, u32[]{:S(2)}, u32[]{:S(2)}) collective-permute-start(bf16[128,2048]{1,0:T(8,128)(2,1)S(1)} %collective-permute-done.16.refs_3_), channel_id=1, source_target_pairs={{0,16},{2,10},{4,20},{6,14},{8,0},{10,26},{12,4},{14,30},{16,24},{... | collective-permute-start | bytes 1572872 | tf_op jit(solution)/shard_map/ppermute | solution.py:75
  82.5 14.9 %collective-permute-start.20 = (bf16[128,2048]{1,0:T(8,128)(2,1)S(1)}, bf16[128,2048]{1,0:T(8,128)(2,1)S(1)}, u32[]{:S(2)}, u32[]{:S(2)}) collective-permute-start(bf16[128,2048]{1,0:T(8,128)(2,1)S(1)} %collective-permute-done.10.refs_6_), channel_id=1, source_target_pairs={{0,4},{2,6},{4,0},{6,2},{8,12},{10,14},{12,8},{14,10},{16,20},{18,... | collective-permute-start | bytes 1572872 | tf_op jit(solution)/shard_map/ppermute | solution.py:75
  99.9 7.4 %collective-permute-start.22 = (bf16[896,2048]{1,0:T(8,128)(2,1)S(1)}, bf16[896,2048]{1,0:T(8,128)(2,1)S(1)}, u32[]{:S(2)}, u32[]{:S(2)}) collective-permute-start(bf16[896,2048]{1,0:T(8,128)(2,1)S(1)} %get-tuple-element.109), channel_id=1, source_target_pairs={{0,2},{2,0},{4,6},{6,4},{8,10},{10,8},{12,14},{14,12},{16,18},{18,... | collective-permute-start | bytes 11010056 | tf_op jit(solution)/shard_map/ppermute | solution.py:401
  100.6 6.0 %collective-permute-start.21 = (f32[2048]{0:T(1024)S(1)}, f32[2048]{0:T(1024)S(1)}, u32[]{:S(2)}, u32[]{:S(2)}) collective-permute-start(f32[2048]{0:T(1024)S(1)} %bitcast.39), channel_id=1, source_target_pairs={{0,2},{2,0},{4,6},{6,4},{8,10},{10,8},{12,14},{14,12},{16,18},{18,... | collective-permute-start | bytes 24584 | tf_op jit(solution)/shard_map/ppermute | solution.py:401
  100.7 6.0 %copy-start = (bf16[4096]{0:T(1024)(128)(2,1)S(1)}, bf16[4096]{0:T(1024)(128)(2,1)}, u32[]{:S(2)}) copy-start(bf16[4096]{0:T(1024)(128)(2,1)} %param.10) | copy-start | bytes 24580

commit v14 on v10

--- a/solution.py
+++ b/solution.py
@@ -328,7 +328,7 @@
     )
 
 
-def put_kernel(pieces, where, part, whole, out, sems):
+def put_kernel(pieces, where, part, head, other_head, gain, whole, out, grad, sems):
     units, width = part.shape
     start = pl.multiple_of(where[0] * width, width)
     rows = [pl.ds(n * (units // pieces), units // pieces) for n in range(pieces)]
@@ -337,28 +337,36 @@
     ]
     for copy in place:
         copy.start()
+    there = pl.ds(start, width)
+    here = pl.ds(pl.multiple_of((1 - where[0]) * width, width), width)
+    grad[:, there] = gain[:, there] * other_head[...]
+    grad[:, here] = gain[:, here] * head[...]
     for copy in place:
         copy.wait()
 
 
-def put(whole, part, where):
+def put(whole, part, where, head, other_head, gain):
     units, width = part.shape
     pieces = pieces_of(units)
     anywhere = pl.BlockSpec(memory_space=pl.ANY)
+    inside = pl.BlockSpec(memory_space=pltpu.VMEM)
     return pl.pallas_call(
         functools.partial(put_kernel, pieces),
         grid_spec=pltpu.PrefetchScalarGridSpec(
             num_scalar_prefetch=1,
             grid=(),
-            in_specs=[pl.BlockSpec(memory_space=pltpu.VMEM), anywhere],
-            out_specs=anywhere,
+            in_specs=[inside] * 4 + [anywhere],
+            out_specs=[anywhere, inside],
             scratch_shapes=[pltpu.SemaphoreType.DMA((pieces,))],
         ),
-        out_shape=jax.ShapeDtypeStruct(whole.shape, whole.dtype),
-        input_output_aliases={2: 0},
+        out_shape=[
+            jax.ShapeDtypeStruct(whole.shape, whole.dtype),
+            jax.ShapeDtypeStruct(gain.shape, jnp.float32),
+        ],
+        input_output_aliases={5: 0},
         compiler_params=params(0),
         cost_estimate=cost(0, 0, 0, 4 * units * width),
-    )(where, pltpu.with_memory_space_constraint(part, pltpu.VMEM), whole)
+    )(where, pltpu.with_memory_space_constraint(part, pltpu.VMEM), head, other_head, gain, whole)
 
 
 def all_returns(step_reward, resets):
@@ -452,16 +460,12 @@
             [have["early parts"], have["middle parts"]],
         )
         swapped = to_core(out)
-        grad_head = grad_head[0]
-        other_head = to_core(grad_head)
-        grad_head = gain * jnp.where(
-            have["first core"], jnp.concatenate([grad_head, other_head]), jnp.concatenate([other_head, grad_head])
-        )
+        other_head = to_core(grad_head[0])[None]
         (grad_down,) = product(
             have["owners"], 0, have["own picks"], None, [dstream, have["middle dstream"]], have["early own"], (), have["where"]
         )
-        grad_down = put(grad_down, swapped, have["elsewhere"])
-        return (have["values"], have["returns"], grad_head, grad_down)
+        grad_down, grad_head = put(grad_down, swapped, have["elsewhere"], grad_head, other_head, gain[None])
+        return (have["values"], have["returns"], grad_head[0], grad_down)
 
     return body
 

time: 102 us -> 102 us (level)
  transfers between devices with their start and end apart: 23 -> 23, of which waited for: 11 -> 11; matrix products, arithmetic and copies ran while one was open for 7% -> 6% of each run, Pallas kernels for 24% -> 24%
where the time goes in v14:
time: 102 us; the launch traced here: 101 us
  starting transfers between devices  34.7 us (34%)
  Pallas kernels  29.5 us (29%)
  waiting for transfers between devices  27.5 us (27%)
  other arithmetic  5.58 us (5%)
  local copies, waits for them, and re-layouts  2.23 us (2%)
    ppermute x16, starting transfers between devices, event(): self.have[name] = lax.ppermute(self.have[source], 'seq', pairs)  26.8 us
    pallas_call x4, Pallas kernels, product(): pl.pallas_call(functools.partial(product_kernel, tok, count, first, len(g...  22.7 us
    ppermute x4, waiting for transfers between devices, butterfly_send(): lax.ppermute(x, axis, [(i, i ^ bit) for i in range(lax.axis_size(axis))])  14.5 us
    ppermute x16, waiting for transfers between devices, event(): self.have[name] = lax.ppermute(self.have[source], 'seq', pairs)  10.9 us
    ppermute x4, starting transfers between devices, butterfly_send(): lax.ppermute(x, axis, [(i, i ^ bit) for i in range(lax.axis_size(axis))])  5.84 us
    pallas_call x1, Pallas kernels, pick(): pl.pallas_call(functools.partial(pick_kernel, tok), grid_spec=pltpu.Prefe...  4.35 us
    pallas_call x1, Pallas kernels, put(): pl.pallas_call(functools.partial(put_kernel, pieces), grid_spec=pltpu.Pre...  2.49 us
  transfers between devices with their start and end apart: 23, of which 11 were waited for; matrix products, arithmetic and copies ran while one was open for 6% of the time, Pallas kernels for 24%

profile of v14, /device:TPU:0, one launch (start us, length us, event | category | flops | bytes accessed | tf_op | source)
XLA Modules:
  0.0 100.6 jit_solution(15810259746652504250)
XLA Ops:
  0.7 1.3 %constant_dynamic-slice_fusion.1 = (bf16[128,2048]{1,0:T(8,128)(2,1)S(1)}, bf16[128,2048]{1,0:T(8,128)(2,1)S(1)}) fusion(bf16[128,4096]{1,0:T(8,128)(2,1)} %param.8, s32[]{:T(128)S(6)} %select_n.125, s32[]{:T(128)S(6)} %select_n.124), kind=kLoop, calls=%fused_computation.44 | loop fusion | bytes 2097160 | tf_op jit(solution)/shard_map/dynamic_slice | solution.py:88
  1.9 4.1 %collective-permute-start.3 = (bf16[128,2048]{1,0:T(8,128)(2,1)S(1)}, bf16[128,2048]{1,0:T(8,128)(2,1)S(1)}, u32[]{:S(2)}, u32[]{:S(2)}) collective-permute-start(bf16[128,2048]{1,0:T(8,128)(2,1)S(1)} %get-tuple-element.62.refs_3_), channel_id=1, source_target_pairs={{0,16},{2,10},{4,20},{6,14},{8,0},{10,26},{12,4},{14,30},{16,24},{... | collective-permute-start | bytes 1572872 | tf_op jit(solution)/shard_map/ppermute | solution.py:75
  6.0 1.5 %collective-permute-start.4 = (bf16[128,2048]{1,0:T(8,128)(2,1)S(1)}, bf16[128,2048]{1,0:T(8,128)(2,1)S(1)}, u32[]{:S(2)}, u32[]{:S(2)}) collective-permute-start(bf16[128,2048]{1,0:T(8,128)(2,1)S(1)} %get-tuple-element.62.refs_3_), channel_id=1, source_target_pairs={{0,4},{2,6},{4,0},{6,2},{8,12},{10,14},{12,8},{14,10},{16,20},{18,... | collective-permute-start | bytes 1572872 | tf_op jit(solution)/shard_map/ppermute | solution.py:75
  7.5 0.0 collective-permute-start
  7.6 0.7 fusion.6.owners
  8.3 0.7 multiply_bitcast_fusion
  9.0 0.7 convert_multiply_fusion.2
  9.7 0.0 collective-permute-done.refs_4_
  9.7 1.7 %fusion = (f32[128]{0:T(128)S(1)}, f32[128]{0:T(128)S(1)}) fusion(bf16[128,4096]{1,0:T(8,128)(2,1)} %param.8, f32[4096]{0:T(1024)S(1)} %convert_multiply_fusion.2), kind=kLoop, calls=%fused_computation.2 | loop fusion | flops 2621184 | bytes 1065984 | tf_op jit(solution)/shard_map/reduce_sum | solution.py:414
  11.3 1.6 %collective-permute-start.5 = (f32[4,128]{1,0:T(4,128)S(1)}, f32[4,128]{1,0:T(4,128)S(1)}, u32[]{:S(2)}, u32[]{:S(2)}) collective-permute-start(f32[4,128]{1,0:T(4,128)S(1)} %pad_maximum_fusion.2), channel_id=1, source_target_pairs={{0,1},{1,0},{2,3},{3,2},{4,5},{5,4},{6,7},{7,6},{8,9},{9,8},{10,11... | collective-permute-start | bytes 6152 | tf_op jit(solution)/shard_map/ppermute | solution.py:18
  12.9 0.8 collective-permute-start.1
  13.7 0.5 collective-permute-start.2
  14.2 0.8 collective-permute-done.5
  15.0 4.3 %shard_map.111 = (bf16[896,2048]{1,0:T(8,128)(2,1)S(1)}, bf16[896,2048]{1,0:T(8,128)(2,1)}) custom-call(s32[32]{0:T(128)S(1)} %fusion.6.owners, bf16[896,2048]{1,0:T(8,128)(2,1)} %hidden), custom_call_target="tpu_custom_call" | custom-call | bytes 1 | tf_op jit(solution)/shard_map/pallas_call | solution.py:188
  19.4 0.8 collective-permute-done.3.refs_7_
  20.2 0.0 collective-permute-done.4.refs_5_
  20.2 0.0 collective-permute-start.6
  20.2 1.1 %collective-permute-done.6 = f32[1,4,128]{2,1,0:T(4,128)S(1)} collective-permute-done((f32[1,4,128]{2,1,0:T(4,128)S(1)}, f32[1,4,128]{2,1,0:T(4,128)S(1)}, u32[]{:S(2)}, u32[]{:S(2)}) %collective-permute-start.6) | collective-permute-done | bytes 2080 | tf_op jit(solution)/shard_map/ppermute | solution.py:24
  21.4 0.1 broadcast_select_fusion.3
  21.4 2.2 %collective-permute-start.7 = (f32[2,4,128]{2,0,1:T(2,128)S(1)}, f32[2,4,128]{2,0,1:T(2,128)S(1)}, u32[]{:S(2)}, u32[]{:S(2)}) collective-permute-start(f32[2,4,128]{2,0,1:T(2,128)S(1)} %broadcast_select_fusion.3), channel_id=1, source_target_pairs={{0,8},{2,10},{4,12},{6,14},{8,0},{10,2},{12,4},{14,6},{16,24},{18,... | collective-permute-start | bytes 12296 | tf_op jit(solution)/shard_map/ppermute | solution.py:24
  23.6 3.9 %collective-permute-start.10 = (bf16[128,2048]{1,0:T(8,128)(2,1)S(1)}, bf16[128,2048]{1,0:T(8,128)(2,1)S(1)}, u32[]{:S(2)}, u32[]{:S(2)}) collective-permute-start(bf16[128,2048]{1,0:T(8,128)(2,1)S(1)} %collective-permute-done.3.refs_7_), channel_id=1, source_target_pairs={{0,16},{2,10},{4,20},{6,14},{8,0},{10,26},{12,4},{14,30},{16,24},{... | collective-permute-start | bytes 1572872 | tf_op jit(solution)/shard_map/ppermute | solution.py:75
  27.6 3.2 %collective-permute-start.11 = (bf16[128,2048]{1,0:T(8,128)(2,1)S(1)}, bf16[128,2048]{1,0:T(8,128)(2,1)S(1)}, u32[]{:S(2)}, u32[]{:S(2)}) collective-permute-start(bf16[128,2048]{1,0:T(8,128)(2,1)S(1)} %collective-permute-done.3.refs_7_), channel_id=1, source_target_pairs={{0,4},{2,6},{4,0},{6,2},{8,12},{10,14},{12,8},{14,10},{16,20},{18,... | collective-permute-start | bytes 1572872 | tf_op jit(solution)/shard_map/ppermute | solution.py:75
  30.7 0.3 collective-permute-done.1.refs_8_
  31.1 0.1 broadcast_select_fusion
  31.2 1.2 %collective-permute-start.12 = (f32[2,2,4,128]{3,1,0,2:T(2,128)S(1)}, f32[2,2,4,128]{3,1,0,2:T(2,128)S(1)}, u32[]{:S(2)}, u32[]{:S(2)}) collective-permute-start(f32[2,2,4,128]{3,1,0,2:T(2,128)S(1)} %broadcast_select_fusion), channel_id=1, source_target_pairs={{0,4},{2,6},{4,0},{6,2},{8,12},{10,14},{12,8},{14,10},{16,20},{18,... | collective-permute-start | bytes 24584 | tf_op jit(solution)/shard_map/ppermute | solution.py:24
  32.4 0.9 collective-permute-start.8
  33.3 2.0 %collective-permute-start.9 = (bf16[128,2048]{1,0:T(8,128)(2,1)S(1)}, bf16[128,2048]{1,0:T(8,128)(2,1)S(1)}, u32[]{:S(2)}, u32[]{:S(2)}) collective-permute-start(bf16[128,2048]{1,0:T(8,128)(2,1)S(1)} %collective-permute-done.1.refs_8_), channel_id=1, source_target_pairs={{0,4},{2,6},{4,0},{6,2},{8,12},{10,14},{12,8},{14,10},{16,20},{18,... | collective-permute-start | bytes 1572872 | tf_op jit(solution)/shard_map/ppermute | solution.py:75
  35.3 8.5 %collective-permute-done.12 = f32[2,2,4,128]{3,1,0,2:T(2,128)S(1)} collective-permute-done((f32[2,2,4,128]{3,1,0,2:T(2,128)S(1)}, f32[2,2,4,128]{3,1,0,2:T(2,128)S(1)}, u32[]{:S(2)}, u32[]{:S(2)}) %collective-permute-start.12) | collective-permute-done | bytes 8224 | tf_op jit(solution)/shard_map/ppermute | solution.py:24
  43.7 0.1 select_bitcast_fusion.1
  43.8 1.5 %collective-permute-done.10.refs_11_ = bf16[128,2048]{1,0:T(8,128)(2,1)S(1)} collective-permute-done((bf16[128,2048]{1,0:T(8,128)(2,1)S(1)}, bf16[128,2048]{1,0:T(8,128)(2,1)S(1)}, u32[]{:S(2)}, u32[]{:S(2)}) %collective-permute-start.10) | collective-permute-done | bytes 524320 | tf_op jit(solution)/shard_map/ppermute | solution.py:75
  45.3 2.4 %collective-permute-start.13 = (f32[8,4,128]{2,0,1:T(8,128)S(1)}, f32[8,4,128]{2,0,1:T(8,128)S(1)}, u32[]{:S(2)}, u32[]{:S(2)}) collective-permute-start(f32[8,4,128]{2,0,1:T(8,128)S(1)} %bitcast.51), channel_id=1, source_target_pairs={{0,16},{2,18},{4,20},{6,22},{8,24},{10,26},{12,28},{14,30},{16,0},... | collective-permute-start | bytes 49160 | tf_op jit(solution)/shard_map/ppermute | solution.py:24
  47.8 0.5 collective-permute-start.17
  48.3 3.1 %collective-permute-start.18 = (bf16[128,2048]{1,0:T(8,128)(2,1)S(1)}, bf16[128,2048]{1,0:T(8,128)(2,1)S(1)}, u32[]{:S(2)}, u32[]{:S(2)}) collective-permute-start(bf16[128,2048]{1,0:T(8,128)(2,1)S(1)} %collective-permute-done.10.refs_11_), channel_id=1, source_target_pairs={{0,4},{2,6},{4,0},{6,2},{8,12},{10,14},{12,8},{14,10},{16,20},{18,... | collective-permute-start | bytes 1572872 | tf_op jit(solution)/shard_map/ppermute | solution.py:75
  51.3 4.9 %collective-permute-done.13 = f32[8,4,128]{2,0,1:T(8,128)S(1)} collective-permute-done((f32[8,4,128]{2,0,1:T(8,128)S(1)}, f32[8,4,128]{2,0,1:T(8,128)S(1)}, u32[]{:S(2)}, u32[]{:S(2)}) %collective-permute-start.13) | collective-permute-done | bytes 16416 | tf_op jit(solution)/shard_map/ppermute | solution.py:24
  56.3 0.0 collective-permute-done.9.refs_10_
  56.3 2.0 %collective-permute-start.14 = (bf16[128,2048]{1,0:T(8,128)(2,1)S(1)}, bf16[128,2048]{1,0:T(8,128)(2,1)S(1)}, u32[]{:S(2)}, u32[]{:S(2)}) collective-permute-start(bf16[128,2048]{1,0:T(8,128)(2,1)S(1)} %collective-permute-done.8.refs_12_), channel_id=1, source_target_pairs={{0,8},{2,18},{4,12},{6,22},{8,24},{10,2},{12,28},{14,6},{16,0},{18... | collective-permute-start | bytes 1572872 | tf_op jit(solution)/shard_map/ppermute | solution.py:75
  58.2 1.4 %collective-permute-start.15 = (bf16[128,2048]{1,0:T(8,128)(2,1)S(1)}, bf16[128,2048]{1,0:T(8,128)(2,1)S(1)}, u32[]{:S(2)}, u32[]{:S(2)}) collective-permute-start(bf16[128,2048]{1,0:T(8,128)(2,1)S(1)} %collective-permute-done.8.refs_12_), channel_id=1, source_target_pairs={{0,4},{2,6},{4,0},{6,2},{8,12},{10,14},{12,8},{14,10},{16,20},{18,... | collective-permute-start | bytes 1572872 | tf_op jit(solution)/shard_map/ppermute | solution.py:75
  59.6 0.1 fusion.9
  59.7 0.3 select_reduce_fusion.1
  60.1 0.1 broadcast_compare_fusion
  60.2 0.1 select_reduce_fusion.5
  60.3 0.7 select_reduce_fusion
  60.9 0.1 slice_reduce_fusion
  61.1 0.1 select_reduce_fusion.2
  61.2 0.1 select_reduce_fusion.4
  61.3 0.1 broadcast_in_dim.210
  61.4 0.1 eq.110
  61.5 0.1 collective-permute-start.16
  61.6 7.6 %shard_map.112 = (f32[896,2048]{1,0:T(8,128)S(1)}, bf16[1280,2048]{1,0:T(8,128)(2,1)S(1)}, f32[16,1,2048]{2,1,0:T(1,128)S(1)}) custom-call(s32[32]{0:T(128)S(1)} %fusion.6.owners, s32[1]{0:T(128)} %constant.68.clone.1.where, bf16[896,2048]{1,0:T(8,128)(2,1)S(1)} %get-tuple-element.81.refs_0_, f32[8,2048]{1,0:T(8,128)S(1)} %select_maximum_fusion.refs_1_, ...), custom_call_target="tpu_custom_call" | custom-call | flops 46976204800 | bytes 86376448 | tf_op jit(solution)/shard_map/pallas_call | solution.py:307
  69.2 0.6 select_reduce_fusion.3
  69.8 3.0 %collective-permute-done.17.refs_5_ = bf16[128,2048]{1,0:T(8,128)(2,1)S(1)} collective-permute-done((bf16[128,2048]{1,0:T(8,128)(2,1)S(1)}, bf16[128,2048]{1,0:T(8,128)(2,1)S(1)}, u32[]{:S(2)}, u32[]{:S(2)}) %collective-permute-start.17) | collective-permute-done | bytes 524320 | tf_op jit(solution)/shard_map/ppermute | solution.py:75
  72.8 0.0 collective-permute-done.18.refs_3_
  72.9 2.9 %collective-permute-done.14.refs_6_ = bf16[128,2048]{1,0:T(8,128)(2,1)S(1)} collective-permute-done((bf16[128,2048]{1,0:T(8,128)(2,1)S(1)}, bf16[128,2048]{1,0:T(8,128)(2,1)S(1)}, u32[]{:S(2)}, u32[]{:S(2)}) %collective-permute-start.14) | collective-permute-done | bytes 524320 | tf_op jit(solution)/shard_map/ppermute | solution.py:75
  75.7 1.1 %collective-permute-start.19 = (bf16[128,2048]{1,0:T(8,128)(2,1)S(1)}, bf16[128,2048]{1,0:T(8,128)(2,1)S(1)}, u32[]{:S(2)}, u32[]{:S(2)}) collective-permute-start(bf16[128,2048]{1,0:T(8,128)(2,1)S(1)} %collective-permute-done.18.refs_3_), channel_id=1, source_target_pairs={{0,16},{2,10},{4,20},{6,14},{8,0},{10,26},{12,4},{14,30},{16,24},{... | collective-permute-start | bytes 1572872 | tf_op jit(solution)/shard_map/ppermute | solution.py:75
  76.8 1.7 %collective-permute-start.20 = (bf16[128,2048]{1,0:T(8,128)(2,1)S(1)}, bf16[128,2048]{1,0:T(8,128)(2,1)S(1)}, u32[]{:S(2)}, u32[]{:S(2)}) collective-permute-start(bf16[128,2048]{1,0:T(8,128)(2,1)S(1)} %collective-permute-done.14.refs_6_), channel_id=1, source_target_pairs={{0,4},{2,6},{4,0},{6,2},{8,12},{10,14},{12,8},{14,10},{16,20},{18,... | collective-permute-start | bytes 1572872 | tf_op jit(solution)/shard_map/ppermute | solution.py:75
  78.6 8.1 %shard_map.113 = (f32[896,2048]{1,0:T(8,128)S(1)}, bf16[512,2048]{1,0:T(8,128)(2,1)S(1)}, f32[16,1,2048]{2,1,0:T(1,128)S(1)}) custom-call(s32[32]{0:T(128)S(1)} %fusion.6.owners, s32[1]{0:T(128)} %constant.68.clone.1.where, bf16[896,2048]{1,0:T(8,128)(2,1)S(1)} %collective-permute-done.16.refs_0_, f32[8,2048]{1,0:T(8,128)S(1)} %select_maximum_fusion.refs_1_, ...), custom_call_target="tpu_custom_call" | custom-call | flops 6576668672 | bytes 21561344 | tf_op jit(solution)/shard_map/pallas_call | solution.py:307
  86.7 2.3 %collective-permute-done.19.refs_3_ = bf16[128,2048]{1,0:T(8,128)(2,1)S(1)} collective-permute-done((bf16[128,2048]{1,0:T(8,128)(2,1)S(1)}, bf16[128,2048]{1,0:T(8,128)(2,1)S(1)}, u32[]{:S(2)}, u32[]{:S(2)}) %collective-permute-start.19) | collective-permute-done | bytes 524320 | tf_op jit(solution)/shard_map/ppermute | solution.py:75
  89.0 2.4 %shard_map.114 = (bf16[896,2048]{1,0:T(8,128)(2,1)S(1)}, bf16[256,2048]{1,0:T(8,128)(2,1)S(1)}, f32[1,2048]{1,0:T(1,128)S(1)}) custom-call(s32[32]{0:T(128)S(1)} %fusion.6.owners, s32[1]{0:T(128)} %constant.68.clone.1.where, bf16[896,2048]{1,0:T(8,128)(2,1)S(1)} %collective-permute-done.16.refs_0_, f32[8,2048]{1,0:T(8,128)S(1)} %select_maximum_fusion.refs_1_, ...), custom_call_target="tpu_custom_call" | custom-call | flops 939524096 | bytes 12517376 | tf_op jit(solution)/shard_map/pallas_call | solution.py:307
  91.5 0.1 collective-permute-start.21
  91.6 0.5 collective-permute-start.22
  92.1 4.5 %shard_map.115.whole = bf16[896,4096]{1,0:T(8,128)(2,1)} custom-call(s32[32]{0:T(128)S(1)} %fusion.6.owners, s32[1]{0:T(128)} %bitcast.where, bf16[896,2048]{1,0:T(8,128)(2,1)S(1)} %get-tuple-element.81.refs_0_, bf16[256,2048]{1,0:T(8,128)(2,1)S(1)} %get-tuple-element.109.refs_1_, bf16[512,2048]{1,0:T(8,128)(2,1)S(1)} %get-tuple-element.110.refs_2_, ...), custom_call_target="tpu_custom_call" | custom-call | flops 2818572288 | bytes 15532032 | tf_op jit(solution)/shard_map/pallas_call | solution.py:307
  96.6 1.4 %collective-permute-done.22 = f32[2048]{0:T(1024)S(1)} collective-permute-done((f32[2048]{0:T(1024)S(1)}, f32[2048]{0:T(1024)S(1)}, u32[]{:S(2)}, u32[]{:S(2)}) %collective-permute-start.22) | collective-permute-done | bytes 8224 | tf_op jit(solution)/shard_map/ppermute | solution.py:401
  98.0 0.0 collective-permute-done.21.part
  98.0 2.5 %shard_map.116 = (bf16[896,4096]{1,0:T(8,128)(2,1)}, f32[1,4096]{1,0:T(1,128)}) custom-call(s32[1]{0:T(128)S(6)} %sub.26.where, bf16[896,2048]{1,0:T(8,128)(2,1)S(1)} %collective-permute-done.21.part, f32[1,2048]{1,0:T(1,128)S(1)} %get-tuple-element.107.head, f32[1,2048]{1,0:T(1,128)S(1)} %bitcast.44, ...), custom_call_target="tpu_custom_call", output_to_operand_aliasing={{0}: (5, {})} | custom-call | bytes 7340032 | tf_op jit(solution)/shard_map/pallas_call | solution.py:353
  (24 shorter events, 0.2 us)
Async XLA Ops:
  1.9 18.3 %collective-permute-start.3 = (bf16[128,2048]{1,0:T(8,128)(2,1)S(1)}, bf16[128,2048]{1,0:T(8,128)(2,1)S(1)}, u32[]{:S(2)}, u32[]{:S(2)}) collective-permute-start(bf16[128,2048]{1,0:T(8,128)(2,1)S(1)} %get-tuple-element.62.refs_3_), channel_id=1, source_target_pairs={{0,16},{2,10},{4,20},{6,14},{8,0},{10,26},{12,4},{14,30},{16,24},{... | collective-permute-start | bytes 1572872 | tf_op jit(solution)/shard_map/ppermute | solution.py:75
  6.0 14.2 %collective-permute-start.4 = (bf16[128,2048]{1,0:T(8,128)(2,1)S(1)}, bf16[128,2048]{1,0:T(8,128)(2,1)S(1)}, u32[]{:S(2)}, u32[]{:S(2)}) collective-permute-start(bf16[128,2048]{1,0:T(8,128)(2,1)S(1)} %get-tuple-element.62.refs_3_), channel_id=1, source_target_pairs={{0,4},{2,6},{4,0},{6,2},{8,12},{10,14},{12,8},{14,10},{16,20},{18,... | collective-permute-start | bytes 1572872 | tf_op jit(solution)/shard_map/ppermute | solution.py:75
  7.5 2.1 %collective-permute-start = (bf16[128,2048]{1,0:T(8,128)(2,1)S(1)}, bf16[128,2048]{1,0:T(8,128)(2,1)S(1)}, u32[]{:S(2)}, u32[]{:S(2)}) collective-permute-start(bf16[128,2048]{1,0:T(8,128)(2,1)S(1)} %get-tuple-element.59), channel_id=1, source_target_pairs={{0,2},{2,0},{4,6},{6,4},{8,10},{10,8},{12,14},{14,12},{16,18},{18,... | collective-permute-start | bytes 1572872 | tf_op jit(solution)/shard_map/ppermute | solution.py:75
  11.3 3.7 %collective-permute-start.5 = (f32[4,128]{1,0:T(4,128)S(1)}, f32[4,128]{1,0:T(4,128)S(1)}, u32[]{:S(2)}, u32[]{:S(2)}) collective-permute-start(f32[4,128]{1,0:T(4,128)S(1)} %pad_maximum_fusion.2), channel_id=1, source_target_pairs={{0,1},{1,0},{2,3},{3,2},{4,5},{5,4},{6,7},{7,6},{8,9},{9,8},{10,11... | collective-permute-start | bytes 6152 | tf_op jit(solution)/shard_map/ppermute | solution.py:18
  12.9 18.2 %collective-permute-start.1 = (bf16[128,2048]{1,0:T(8,128)(2,1)S(1)}, bf16[128,2048]{1,0:T(8,128)(2,1)S(1)}, u32[]{:S(2)}, u32[]{:S(2)}) collective-permute-start(bf16[128,2048]{1,0:T(8,128)(2,1)S(1)} %collective-permute-done.refs_4_), channel_id=1, source_target_pairs={{0,8},{2,18},{4,12},{6,22},{8,24},{10,2},{12,28},{14,6},{16,0},{18... | collective-permute-start | bytes 1572872 | tf_op jit(solution)/shard_map/ppermute | solution.py:75
  13.7 17.4 %collective-permute-start.2 = (bf16[128,2048]{1,0:T(8,128)(2,1)S(1)}, bf16[128,2048]{1,0:T(8,128)(2,1)S(1)}, u32[]{:S(2)}, u32[]{:S(2)}) collective-permute-start(bf16[128,2048]{1,0:T(8,128)(2,1)S(1)} %collective-permute-done.refs_4_), channel_id=1, source_target_pairs={{0,4},{2,6},{4,0},{6,2},{8,12},{10,14},{12,8},{14,10},{16,20},{18,... | collective-permute-start | bytes 1572872 | tf_op jit(solution)/shard_map/ppermute | solution.py:75
  20.2 1.2 %collective-permute-start.6 = (f32[1,4,128]{2,1,0:T(4,128)S(1)}, f32[1,4,128]{2,1,0:T(4,128)S(1)}, u32[]{:S(2)}, u32[]{:S(2)}) collective-permute-start(f32[1,4,128]{2,1,0:T(4,128)S(1)} %add_bitcast_fusion), channel_id=1, source_target_pairs={{0,2},{2,0},{4,6},{6,4},{8,10},{10,8},{12,14},{14,12},{16,18},{18,... | collective-permute-start | bytes 6152 | tf_op jit(solution)/shard_map/ppermute | solution.py:24
  21.4 9.3 %collective-permute-start.7 = (f32[2,4,128]{2,0,1:T(2,128)S(1)}, f32[2,4,128]{2,0,1:T(2,128)S(1)}, u32[]{:S(2)}, u32[]{:S(2)}) collective-permute-start(f32[2,4,128]{2,0,1:T(2,128)S(1)} %broadcast_select_fusion.3), channel_id=1, source_target_pairs={{0,8},{2,10},{4,12},{6,14},{8,0},{10,2},{12,4},{14,6},{16,24},{18,... | collective-permute-start | bytes 12296 | tf_op jit(solution)/shard_map/ppermute | solution.py:24
  23.6 21.7 %collective-permute-start.10 = (bf16[128,2048]{1,0:T(8,128)(2,1)S(1)}, bf16[128,2048]{1,0:T(8,128)(2,1)S(1)}, u32[]{:S(2)}, u32[]{:S(2)}) collective-permute-start(bf16[128,2048]{1,0:T(8,128)(2,1)S(1)} %collective-permute-done.3.refs_7_), channel_id=1, source_target_pairs={{0,16},{2,10},{4,20},{6,14},{8,0},{10,26},{12,4},{14,30},{16,24},{... | collective-permute-start | bytes 1572872 | tf_op jit(solution)/shard_map/ppermute | solution.py:75
  27.6 17.8 %collective-permute-start.11 = (bf16[128,2048]{1,0:T(8,128)(2,1)S(1)}, bf16[128,2048]{1,0:T(8,128)(2,1)S(1)}, u32[]{:S(2)}, u32[]{:S(2)}) collective-permute-start(bf16[128,2048]{1,0:T(8,128)(2,1)S(1)} %collective-permute-done.3.refs_7_), channel_id=1, source_target_pairs={{0,4},{2,6},{4,0},{6,2},{8,12},{10,14},{12,8},{14,10},{16,20},{18,... | collective-permute-start | bytes 1572872 | tf_op jit(solution)/shard_map/ppermute | solution.py:75
  31.2 12.6 %collective-permute-start.12 = (f32[2,2,4,128]{3,1,0,2:T(2,128)S(1)}, f32[2,2,4,128]{3,1,0,2:T(2,128)S(1)}, u32[]{:S(2)}, u32[]{:S(2)}) collective-permute-start(f32[2,2,4,128]{3,1,0,2:T(2,128)S(1)} %broadcast_select_fusion), channel_id=1, source_target_pairs={{0,4},{2,6},{4,0},{6,2},{8,12},{10,14},{12,8},{14,10},{16,20},{18,... | collective-permute-start | bytes 24584 | tf_op jit(solution)/shard_map/ppermute | solution.py:24
  32.4 23.9 %collective-permute-start.8 = (bf16[128,2048]{1,0:T(8,128)(2,1)S(1)}, bf16[128,2048]{1,0:T(8,128)(2,1)S(1)}, u32[]{:S(2)}, u32[]{:S(2)}) collective-permute-start(bf16[128,2048]{1,0:T(8,128)(2,1)S(1)} %collective-permute-done.1.refs_8_), channel_id=1, source_target_pairs={{0,8},{2,18},{4,12},{6,22},{8,24},{10,2},{12,28},{14,6},{16,0},{18... | collective-permute-start | bytes 1572872 | tf_op jit(solution)/shard_map/ppermute | solution.py:75
  33.3 23.0 %collective-permute-start.9 = (bf16[128,2048]{1,0:T(8,128)(2,1)S(1)}, bf16[128,2048]{1,0:T(8,128)(2,1)S(1)}, u32[]{:S(2)}, u32[]{:S(2)}) collective-permute-start(bf16[128,2048]{1,0:T(8,128)(2,1)S(1)} %collective-permute-done.1.refs_8_), channel_id=1, source_target_pairs={{0,4},{2,6},{4,0},{6,2},{8,12},{10,14},{12,8},{14,10},{16,20},{18,... | collective-permute-start | bytes 1572872 | tf_op jit(solution)/shard_map/ppermute | solution.py:75
  45.3 10.9 %collective-permute-start.13 = (f32[8,4,128]{2,0,1:T(8,128)S(1)}, f32[8,4,128]{2,0,1:T(8,128)S(1)}, u32[]{:S(2)}, u32[]{:S(2)}) collective-permute-start(f32[8,4,128]{2,0,1:T(8,128)S(1)} %bitcast.51), channel_id=1, source_target_pairs={{0,16},{2,18},{4,20},{6,22},{8,24},{10,26},{12,28},{14,30},{16,0},... | collective-permute-start | bytes 49160 | tf_op jit(solution)/shard_map/ppermute | solution.py:24
  47.8 25.1 %collective-permute-start.17 = (bf16[128,2048]{1,0:T(8,128)(2,1)S(1)}, bf16[128,2048]{1,0:T(8,128)(2,1)S(1)}, u32[]{:S(2)}, u32[]{:S(2)}) collective-permute-start(bf16[128,2048]{1,0:T(8,128)(2,1)S(1)} %collective-permute-done.10.refs_11_), channel_id=1, source_target_pairs={{0,16},{2,10},{4,20},{6,14},{8,0},{10,26},{12,4},{14,30},{16,24},{... | collective-permute-start | bytes 1572872 | tf_op jit(solution)/shard_map/ppermute | solution.py:75
  48.3 24.6 %collective-permute-start.18 = (bf16[128,2048]{1,0:T(8,128)(2,1)S(1)}, bf16[128,2048]{1,0:T(8,128)(2,1)S(1)}, u32[]{:S(2)}, u32[]{:S(2)}) collective-permute-start(bf16[128,2048]{1,0:T(8,128)(2,1)S(1)} %collective-permute-done.10.refs_11_), channel_id=1, source_target_pairs={{0,4},{2,6},{4,0},{6,2},{8,12},{10,14},{12,8},{14,10},{16,20},{18,... | collective-permute-start | bytes 1572872 | tf_op jit(solution)/shard_map/ppermute | solution.py:75
  56.3 19.4 %collective-permute-start.14 = (bf16[128,2048]{1,0:T(8,128)(2,1)S(1)}, bf16[128,2048]{1,0:T(8,128)(2,1)S(1)}, u32[]{:S(2)}, u32[]{:S(2)}) collective-permute-start(bf16[128,2048]{1,0:T(8,128)(2,1)S(1)} %collective-permute-done.8.refs_12_), channel_id=1, source_target_pairs={{0,8},{2,18},{4,12},{6,22},{8,24},{10,2},{12,28},{14,6},{16,0},{18... | collective-permute-start | bytes 1572872 | tf_op jit(solution)/shard_map/ppermute | solution.py:75
  58.2 17.5 %collective-permute-start.15 = (bf16[128,2048]{1,0:T(8,128)(2,1)S(1)}, bf16[128,2048]{1,0:T(8,128)(2,1)S(1)}, u32[]{:S(2)}, u32[]{:S(2)}) collective-permute-start(bf16[128,2048]{1,0:T(8,128)(2,1)S(1)} %collective-permute-done.8.refs_12_), channel_id=1, source_target_pairs={{0,4},{2,6},{4,0},{6,2},{8,12},{10,14},{12,8},{14,10},{16,20},{18,... | collective-permute-start | bytes 1572872 | tf_op jit(solution)/shard_map/ppermute | solution.py:75
  61.5 14.2 %collective-permute-start.16 = (bf16[896,2048]{1,0:T(8,128)(2,1)}, bf16[896,2048]{1,0:T(8,128)(2,1)S(1)}, u32[]{:S(2)}, u32[]{:S(2)}) collective-permute-start(bf16[896,2048]{1,0:T(8,128)(2,1)} %get-tuple-element.79), channel_id=1, source_target_pairs={{0,2},{2,0},{4,6},{6,4},{8,10},{10,8},{12,14},{14,12},{16,18},{18,... | collective-permute-start | bytes 11010056 | tf_op jit(solution)/shard_map/ppermute | solution.py:75
  75.7 13.3 %collective-permute-start.19 = (bf16[128,2048]{1,0:T(8,128)(2,1)S(1)}, bf16[128,2048]{1,0:T(8,128)(2,1)S(1)}, u32[]{:S(2)}, u32[]{:S(2)}) collective-permute-start(bf16[128,2048]{1,0:T(8,128)(2,1)S(1)} %collective-permute-done.18.refs_3_), channel_id=1, source_target_pairs={{0,16},{2,10},{4,20},{6,14},{8,0},{10,26},{12,4},{14,30},{16,24},{... | collective-permute-start | bytes 1572872 | tf_op jit(solution)/shard_map/ppermute | solution.py:75
  76.8 12.2 %collective-permute-start.20 = (bf16[128,2048]{1,0:T(8,128)(2,1)S(1)}, bf16[128,2048]{1,0:T(8,128)(2,1)S(1)}, u32[]{:S(2)}, u32[]{:S(2)}) collective-permute-start(bf16[128,2048]{1,0:T(8,128)(2,1)S(1)} %collective-permute-done.14.refs_6_), channel_id=1, source_target_pairs={{0,4},{2,6},{4,0},{6,2},{8,12},{10,14},{12,8},{14,10},{16,20},{18,... | collective-permute-start | bytes 1572872 | tf_op jit(solution)/shard_map/ppermute | solution.py:75
  89.0 2.5 %copy-start = (bf16[4096]{0:T(1024)(128)(2,1)S(1)}, bf16[4096]{0:T(1024)(128)(2,1)}, u32[]{:S(2)}) copy-start(bf16[4096]{0:T(1024)(128)(2,1)} %param.10) | copy-start | bytes 24580
  91.5 6.5 %collective-permute-start.21 = (bf16[896,2048]{1,0:T(8,128)(2,1)S(1)}, bf16[896,2048]{1,0:T(8,128)(2,1)S(1)}, u32[]{:S(2)}, u32[]{:S(2)}) collective-permute-start(bf16[896,2048]{1,0:T(8,128)(2,1)S(1)} %get-tuple-element.106), channel_id=1, source_target_pairs={{0,2},{2,0},{4,6},{6,4},{8,10},{10,8},{12,14},{14,12},{16,18},{18,... | collective-permute-start | bytes 11010056 | tf_op jit(solution)/shard_map/ppermute | solution.py:401
  91.6 6.4 %collective-permute-start.22 = (f32[2048]{0:T(1024)S(1)}, f32[2048]{0:T(1024)S(1)}, u32[]{:S(2)}, u32[]{:S(2)}) collective-permute-start(f32[2048]{0:T(1024)S(1)} %bitcast.43), channel_id=1, source_target_pairs={{0,2},{2,0},{4,6},{6,4},{8,10},{10,8},{12,14},{14,12},{16,18},{18,... | collective-permute-start | bytes 24584 | tf_op jit(solution)/shard_map/ppermute | solution.py:401

commit v15 on v10

--- a/solution.py
+++ b/solution.py
@@ -279,7 +279,7 @@
     count = len(blocks)
     tok = tokens // owners.shape[0] * 2
     k = count * tok + sum(g.shape[0] for g in given)
-    chunk = next(t for t in (512 if tokens <= 4096 else 256, 128, half) if half % t == 0)
+    chunk = next(t for t in (1024 if tokens <= 4096 else 256, 512, 128, half) if half % t == 0)
     steps = half // chunk
     added, wide = total is not None, where is not None
     anywhere = pl.BlockSpec(memory_space=pl.ANY)

time: 102 us -> 102 us (level)
  transfers between devices with their start and end apart: 23 -> 23, of which waited for: 11 -> 11; matrix products, arithmetic and copies ran while one was open for 7% -> 7% of each run, Pallas kernels for 24% -> 25%
where the time goes in v15:
time: 102 us; the launch traced here: 101 us
  starting transfers between devices  34.7 us (34%)
  Pallas kernels  29.2 us (29%)
  waiting for transfers between devices  27.3 us (27%)
  other arithmetic  6.19 us (6%)
  local copies, waits for them, and re-layouts  2.23 us (2%)
    ppermute x16, starting transfers between devices, event(): self.have[name] = lax.ppermute(self.have[source], 'seq', pairs)  26.8 us
    pallas_call x4, Pallas kernels, product(): pl.pallas_call(functools.partial(product_kernel, tok, count, first, len(g...  22.9 us
    ppermute x4, waiting for transfers between devices, butterfly_send(): lax.ppermute(x, axis, [(i, i ^ bit) for i in range(lax.axis_size(axis))])  14.5 us
    ppermute x16, waiting for transfers between devices, event(): self.have[name] = lax.ppermute(self.have[source], 'seq', pairs)  11 us
    ppermute x4, starting transfers between devices, butterfly_send(): lax.ppermute(x, axis, [(i, i ^ bit) for i in range(lax.axis_size(axis))])  5.84 us
    pallas_call x1, Pallas kernels, pick(): pl.pallas_call(functools.partial(pick_kernel, tok), grid_spec=pltpu.Prefe...  4.35 us
  transfers between devices with their start and end apart: 23, of which 11 were waited for; matrix products, arithmetic and copies ran while one was open for 7% of the time, Pallas kernels for 25%

profile of v15, /device:TPU:0, one launch (start us, length us, event | category | flops | bytes accessed | tf_op | source)
XLA Modules:
  0.0 100.6 jit_solution(6285383422482769754)
XLA Ops:
  0.7 1.3 %constant_dynamic-slice_fusion.1 = (bf16[128,2048]{1,0:T(8,128)(2,1)S(1)}, bf16[128,2048]{1,0:T(8,128)(2,1)S(1)}) fusion(bf16[128,4096]{1,0:T(8,128)(2,1)} %param.8, s32[]{:T(128)S(6)} %select_n.133, s32[]{:T(128)S(6)} %select_n.132), kind=kLoop, calls=%fused_computation.46 | loop fusion | bytes 2097160 | tf_op jit(solution)/shard_map/dynamic_slice | solution.py:88
  1.9 4.1 %collective-permute-start.3 = (bf16[128,2048]{1,0:T(8,128)(2,1)S(1)}, bf16[128,2048]{1,0:T(8,128)(2,1)S(1)}, u32[]{:S(2)}, u32[]{:S(2)}) collective-permute-start(bf16[128,2048]{1,0:T(8,128)(2,1)S(1)} %get-tuple-element.61.refs_3_), channel_id=1, source_target_pairs={{0,16},{2,10},{4,20},{6,14},{8,0},{10,26},{12,4},{14,30},{16,24},{... | collective-permute-start | bytes 1572872 | tf_op jit(solution)/shard_map/ppermute | solution.py:75
  6.0 1.5 %collective-permute-start.4 = (bf16[128,2048]{1,0:T(8,128)(2,1)S(1)}, bf16[128,2048]{1,0:T(8,128)(2,1)S(1)}, u32[]{:S(2)}, u32[]{:S(2)}) collective-permute-start(bf16[128,2048]{1,0:T(8,128)(2,1)S(1)} %get-tuple-element.61.refs_3_), channel_id=1, source_target_pairs={{0,4},{2,6},{4,0},{6,2},{8,12},{10,14},{12,8},{14,10},{16,20},{18,... | collective-permute-start | bytes 1572872 | tf_op jit(solution)/shard_map/ppermute | solution.py:75
  7.6 0.7 fusion.6.owners
  8.3 0.7 multiply_bitcast_fusion
  9.0 0.7 convert_multiply_fusion.3
  9.7 0.0 collective-permute-done.refs_4_
  9.7 1.7 %fusion = (f32[128]{0:T(128)S(1)}, f32[128]{0:T(128)S(1)}) fusion(bf16[128,4096]{1,0:T(8,128)(2,1)} %param.8, f32[4096]{0:T(1024)S(1)} %convert_multiply_fusion.3), kind=kLoop, calls=%fused_computation.2 | loop fusion | flops 2621184 | bytes 1065984 | tf_op jit(solution)/shard_map/reduce_sum | solution.py:406
  11.3 1.6 %collective-permute-start.5 = (f32[4,128]{1,0:T(4,128)S(1)}, f32[4,128]{1,0:T(4,128)S(1)}, u32[]{:S(2)}, u32[]{:S(2)}) collective-permute-start(f32[4,128]{1,0:T(4,128)S(1)} %pad_maximum_fusion.2), channel_id=1, source_target_pairs={{0,1},{1,0},{2,3},{3,2},{4,5},{5,4},{6,7},{7,6},{8,9},{9,8},{10,11... | collective-permute-start | bytes 6152 | tf_op jit(solution)/shard_map/ppermute | solution.py:18
  12.9 0.8 collective-permute-start.1
  13.7 0.5 collective-permute-start.2
  14.2 0.8 collective-permute-done.5
  15.0 4.3 %shard_map.111 = (bf16[896,2048]{1,0:T(8,128)(2,1)S(1)}, bf16[896,2048]{1,0:T(8,128)(2,1)}) custom-call(s32[32]{0:T(128)S(1)} %fusion.6.owners, bf16[896,2048]{1,0:T(8,128)(2,1)} %hidden), custom_call_target="tpu_custom_call" | custom-call | bytes 1 | tf_op jit(solution)/shard_map/pallas_call | solution.py:188
  19.4 0.8 collective-permute-done.3.refs_7_
  20.2 1.1 %collective-permute-done.6 = f32[1,4,128]{2,1,0:T(4,128)S(1)} collective-permute-done((f32[1,4,128]{2,1,0:T(4,128)S(1)}, f32[1,4,128]{2,1,0:T(4,128)S(1)}, u32[]{:S(2)}, u32[]{:S(2)}) %collective-permute-start.6) | collective-permute-done | bytes 2080 | tf_op jit(solution)/shard_map/ppermute | solution.py:24
  21.4 0.1 broadcast_select_fusion.3
  21.4 2.2 %collective-permute-start.7 = (f32[2,4,128]{2,0,1:T(2,128)S(1)}, f32[2,4,128]{2,0,1:T(2,128)S(1)}, u32[]{:S(2)}, u32[]{:S(2)}) collective-permute-start(f32[2,4,128]{2,0,1:T(2,128)S(1)} %broadcast_select_fusion.3), channel_id=1, source_target_pairs={{0,8},{2,10},{4,12},{6,14},{8,0},{10,2},{12,4},{14,6},{16,24},{18,... | collective-permute-start | bytes 12296 | tf_op jit(solution)/shard_map/ppermute | solution.py:24
  23.6 3.9 %collective-permute-start.10 = (bf16[128,2048]{1,0:T(8,128)(2,1)S(1)}, bf16[128,2048]{1,0:T(8,128)(2,1)S(1)}, u32[]{:S(2)}, u32[]{:S(2)}) collective-permute-start(bf16[128,2048]{1,0:T(8,128)(2,1)S(1)} %collective-permute-done.3.refs_7_), channel_id=1, source_target_pairs={{0,16},{2,10},{4,20},{6,14},{8,0},{10,26},{12,4},{14,30},{16,24},{... | collective-permute-start | bytes 1572872 | tf_op jit(solution)/shard_map/ppermute | solution.py:75
  27.6 3.2 %collective-permute-start.11 = (bf16[128,2048]{1,0:T(8,128)(2,1)S(1)}, bf16[128,2048]{1,0:T(8,128)(2,1)S(1)}, u32[]{:S(2)}, u32[]{:S(2)}) collective-permute-start(bf16[128,2048]{1,0:T(8,128)(2,1)S(1)} %collective-permute-done.3.refs_7_), channel_id=1, source_target_pairs={{0,4},{2,6},{4,0},{6,2},{8,12},{10,14},{12,8},{14,10},{16,20},{18,... | collective-permute-start | bytes 1572872 | tf_op jit(solution)/shard_map/ppermute | solution.py:75
  30.7 0.0 collective-permute-done.7
  30.7 0.3 collective-permute-done.1.refs_8_
  31.1 0.0 collective-permute-done.2.refs_6_
  31.1 0.1 broadcast_select_fusion
  31.2 1.2 %collective-permute-start.12 = (f32[2,2,4,128]{3,1,0,2:T(2,128)S(1)}, f32[2,2,4,128]{3,1,0,2:T(2,128)S(1)}, u32[]{:S(2)}, u32[]{:S(2)}) collective-permute-start(f32[2,2,4,128]{3,1,0,2:T(2,128)S(1)} %broadcast_select_fusion), channel_id=1, source_target_pairs={{0,4},{2,6},{4,0},{6,2},{8,12},{10,14},{12,8},{14,10},{16,20},{18,... | collective-permute-start | bytes 24584 | tf_op jit(solution)/shard_map/ppermute | solution.py:24
  32.4 0.9 collective-permute-start.8
  33.3 2.0 %collective-permute-start.9 = (bf16[128,2048]{1,0:T(8,128)(2,1)S(1)}, bf16[128,2048]{1,0:T(8,128)(2,1)S(1)}, u32[]{:S(2)}, u32[]{:S(2)}) collective-permute-start(bf16[128,2048]{1,0:T(8,128)(2,1)S(1)} %collective-permute-done.1.refs_8_), channel_id=1, source_target_pairs={{0,4},{2,6},{4,0},{6,2},{8,12},{10,14},{12,8},{14,10},{16,20},{18,... | collective-permute-start | bytes 1572872 | tf_op jit(solution)/shard_map/ppermute | solution.py:75
  35.3 8.5 %collective-permute-done.12 = f32[2,2,4,128]{3,1,0,2:T(2,128)S(1)} collective-permute-done((f32[2,2,4,128]{3,1,0,2:T(2,128)S(1)}, f32[2,2,4,128]{3,1,0,2:T(2,128)S(1)}, u32[]{:S(2)}, u32[]{:S(2)}) %collective-permute-start.12) | collective-permute-done | bytes 8224 | tf_op jit(solution)/shard_map/ppermute | solution.py:24
  43.7 0.1 select_bitcast_fusion.1
  43.8 1.5 %collective-permute-done.10.refs_11_ = bf16[128,2048]{1,0:T(8,128)(2,1)S(1)} collective-permute-done((bf16[128,2048]{1,0:T(8,128)(2,1)S(1)}, bf16[128,2048]{1,0:T(8,128)(2,1)S(1)}, u32[]{:S(2)}, u32[]{:S(2)}) %collective-permute-start.10) | collective-permute-done | bytes 524320 | tf_op jit(solution)/shard_map/ppermute | solution.py:75
  45.3 0.0 collective-permute-done.11.refs_9_
  45.3 2.4 %collective-permute-start.13 = (f32[8,4,128]{2,0,1:T(8,128)S(1)}, f32[8,4,128]{2,0,1:T(8,128)S(1)}, u32[]{:S(2)}, u32[]{:S(2)}) collective-permute-start(f32[8,4,128]{2,0,1:T(8,128)S(1)} %bitcast.47), channel_id=1, source_target_pairs={{0,16},{2,18},{4,20},{6,22},{8,24},{10,26},{12,28},{14,30},{16,0},... | collective-permute-start | bytes 49160 | tf_op jit(solution)/shard_map/ppermute | solution.py:24
  47.8 0.5 collective-permute-start.17
  48.3 3.1 %collective-permute-start.18 = (bf16[128,2048]{1,0:T(8,128)(2,1)S(1)}, bf16[128,2048]{1,0:T(8,128)(2,1)S(1)}, u32[]{:S(2)}, u32[]{:S(2)}) collective-permute-start(bf16[128,2048]{1,0:T(8,128)(2,1)S(1)} %collective-permute-done.10.refs_11_), channel_id=1, source_target_pairs={{0,4},{2,6},{4,0},{6,2},{8,12},{10,14},{12,8},{14,10},{16,20},{18,... | collective-permute-start | bytes 1572872 | tf_op jit(solution)/shard_map/ppermute | solution.py:75
  51.3 4.9 %collective-permute-done.13 = f32[8,4,128]{2,0,1:T(8,128)S(1)} collective-permute-done((f32[8,4,128]{2,0,1:T(8,128)S(1)}, f32[8,4,128]{2,0,1:T(8,128)S(1)}, u32[]{:S(2)}, u32[]{:S(2)}) %collective-permute-start.13) | collective-permute-done | bytes 16416 | tf_op jit(solution)/shard_map/ppermute | solution.py:24
  56.3 0.0 collective-permute-done.8.refs_12_
  56.3 0.0 collective-permute-done.9.refs_10_
  56.3 2.0 %collective-permute-start.14 = (bf16[128,2048]{1,0:T(8,128)(2,1)S(1)}, bf16[128,2048]{1,0:T(8,128)(2,1)S(1)}, u32[]{:S(2)}, u32[]{:S(2)}) collective-permute-start(bf16[128,2048]{1,0:T(8,128)(2,1)S(1)} %collective-permute-done.8.refs_12_), channel_id=1, source_target_pairs={{0,8},{2,18},{4,12},{6,22},{8,24},{10,2},{12,28},{14,6},{16,0},{18... | collective-permute-start | bytes 1572872 | tf_op jit(solution)/shard_map/ppermute | solution.py:75
  58.2 1.4 %collective-permute-start.15 = (bf16[128,2048]{1,0:T(8,128)(2,1)S(1)}, bf16[128,2048]{1,0:T(8,128)(2,1)S(1)}, u32[]{:S(2)}, u32[]{:S(2)}) collective-permute-start(bf16[128,2048]{1,0:T(8,128)(2,1)S(1)} %collective-permute-done.8.refs_12_), channel_id=1, source_target_pairs={{0,4},{2,6},{4,0},{6,2},{8,12},{10,14},{12,8},{14,10},{16,20},{18,... | collective-permute-start | bytes 1572872 | tf_op jit(solution)/shard_map/ppermute | solution.py:75
  59.6 0.1 fusion.9
  59.7 0.3 select_reduce_fusion.1
  60.1 0.1 broadcast_compare_fusion
  60.2 0.1 select_reduce_fusion.5
  60.3 0.7 select_reduce_fusion
  60.9 0.1 slice_reduce_fusion
  61.1 0.1 select_reduce_fusion.2
  61.2 0.1 select_reduce_fusion.4
  61.3 0.1 broadcast_in_dim.204
  61.4 0.1 eq.113
  61.5 0.1 collective-permute-start.16
  61.6 7.6 %shard_map.112 = (f32[896,2048]{1,0:T(8,128)S(1)}, bf16[1280,2048]{1,0:T(8,128)(2,1)S(1)}, f32[16,1,2048]{2,1,0:T(1,128)S(1)}) custom-call(s32[32]{0:T(128)S(1)} %fusion.6.owners, s32[1]{0:T(128)} %constant.68.clone.1.where, bf16[896,2048]{1,0:T(8,128)(2,1)S(1)} %get-tuple-element.80.refs_0_, f32[8,2048]{1,0:T(8,128)S(1)} %select_maximum_fusion.refs_1_, ...), custom_call_target="tpu_custom_call" | custom-call | flops 46976204800 | bytes 86376448 | tf_op jit(solution)/shard_map/pallas_call | solution.py:307
  69.2 0.6 select_reduce_fusion.3
  69.8 3.1 %collective-permute-done.17.refs_5_ = bf16[128,2048]{1,0:T(8,128)(2,1)S(1)} collective-permute-done((bf16[128,2048]{1,0:T(8,128)(2,1)S(1)}, bf16[128,2048]{1,0:T(8,128)(2,1)S(1)}, u32[]{:S(2)}, u32[]{:S(2)}) %collective-permute-start.17) | collective-permute-done | bytes 524320 | tf_op jit(solution)/shard_map/ppermute | solution.py:75
  72.9 2.9 %collective-permute-done.14.refs_6_ = bf16[128,2048]{1,0:T(8,128)(2,1)S(1)} collective-permute-done((bf16[128,2048]{1,0:T(8,128)(2,1)S(1)}, bf16[128,2048]{1,0:T(8,128)(2,1)S(1)}, u32[]{:S(2)}, u32[]{:S(2)}) %collective-permute-start.14) | collective-permute-done | bytes 524320 | tf_op jit(solution)/shard_map/ppermute | solution.py:75
  75.7 1.1 %collective-permute-start.19 = (bf16[128,2048]{1,0:T(8,128)(2,1)S(1)}, bf16[128,2048]{1,0:T(8,128)(2,1)S(1)}, u32[]{:S(2)}, u32[]{:S(2)}) collective-permute-start(bf16[128,2048]{1,0:T(8,128)(2,1)S(1)} %collective-permute-done.18.refs_3_), channel_id=1, source_target_pairs={{0,16},{2,10},{4,20},{6,14},{8,0},{10,26},{12,4},{14,30},{16,24},{... | collective-permute-start | bytes 1572872 | tf_op jit(solution)/shard_map/ppermute | solution.py:75
  76.8 1.7 %collective-permute-start.20 = (bf16[128,2048]{1,0:T(8,128)(2,1)S(1)}, bf16[128,2048]{1,0:T(8,128)(2,1)S(1)}, u32[]{:S(2)}, u32[]{:S(2)}) collective-permute-start(bf16[128,2048]{1,0:T(8,128)(2,1)S(1)} %collective-permute-done.14.refs_6_), channel_id=1, source_target_pairs={{0,4},{2,6},{4,0},{6,2},{8,12},{10,14},{12,8},{14,10},{16,20},{18,... | collective-permute-start | bytes 1572872 | tf_op jit(solution)/shard_map/ppermute | solution.py:75
  78.6 8.1 %shard_map.113 = (f32[896,2048]{1,0:T(8,128)S(1)}, bf16[512,2048]{1,0:T(8,128)(2,1)S(1)}, f32[16,1,2048]{2,1,0:T(1,128)S(1)}) custom-call(s32[32]{0:T(128)S(1)} %fusion.6.owners, s32[1]{0:T(128)} %constant.68.clone.1.where, bf16[896,2048]{1,0:T(8,128)(2,1)S(1)} %collective-permute-done.16.refs_0_, f32[8,2048]{1,0:T(8,128)S(1)} %select_maximum_fusion.refs_1_, ...), custom_call_target="tpu_custom_call" | custom-call | flops 6576668672 | bytes 21561344 | tf_op jit(solution)/shard_map/pallas_call | solution.py:307
  86.7 2.3 %collective-permute-done.19.refs_3_ = bf16[128,2048]{1,0:T(8,128)(2,1)S(1)} collective-permute-done((bf16[128,2048]{1,0:T(8,128)(2,1)S(1)}, bf16[128,2048]{1,0:T(8,128)(2,1)S(1)}, u32[]{:S(2)}, u32[]{:S(2)}) %collective-permute-start.19) | collective-permute-done | bytes 524320 | tf_op jit(solution)/shard_map/ppermute | solution.py:75
  89.0 2.4 %shard_map.114 = (bf16[896,2048]{1,0:T(8,128)(2,1)S(1)}, bf16[256,2048]{1,0:T(8,128)(2,1)S(1)}, f32[1,2048]{1,0:T(1,128)S(1)}) custom-call(s32[32]{0:T(128)S(1)} %fusion.6.owners, s32[1]{0:T(128)} %constant.68.clone.1.where, bf16[896,2048]{1,0:T(8,128)(2,1)S(1)} %collective-permute-done.16.refs_0_, f32[8,2048]{1,0:T(8,128)S(1)} %select_maximum_fusion.refs_1_, ...), custom_call_target="tpu_custom_call" | custom-call | flops 939524096 | bytes 12517376 | tf_op jit(solution)/shard_map/pallas_call | solution.py:307
  91.5 0.1 collective-permute-start.22
  91.6 0.5 collective-permute-start.21
  92.1 4.8 %shard_map.115.whole = bf16[896,4096]{1,0:T(8,128)(2,1)} custom-call(s32[32]{0:T(128)S(1)} %fusion.6.owners, s32[1]{0:T(128)} %bitcast.where, bf16[896,2048]{1,0:T(8,128)(2,1)S(1)} %get-tuple-element.80.refs_0_, bf16[256,2048]{1,0:T(8,128)(2,1)S(1)} %get-tuple-element.109.refs_1_, bf16[512,2048]{1,0:T(8,128)(2,1)S(1)} %get-tuple-element.110.refs_2_, ...), custom_call_target="tpu_custom_call" | custom-call | flops 2818572288 | bytes 15532032 | tf_op jit(solution)/shard_map/pallas_call | solution.py:307
  96.9 1.1 %collective-permute-done.21 = f32[2048]{0:T(1024)S(1)} collective-permute-done((f32[2048]{0:T(1024)S(1)}, f32[2048]{0:T(1024)S(1)}, u32[]{:S(2)}, u32[]{:S(2)}) %collective-permute-start.21) | collective-permute-done | bytes 8224 | tf_op jit(solution)/shard_map/ppermute | solution.py:393
  98.0 0.6 convert_multiply_fusion.2
  98.6 1.9 %shard_map.116 = bf16[896,4096]{1,0:T(8,128)(2,1)} custom-call(s32[1]{0:T(128)S(6)} %sub.26.where, bf16[896,2048]{1,0:T(8,128)(2,1)S(1)} %collective-permute-done.22.part, bf16[896,4096]{1,0:T(8,128)(2,1)} %shard_map.115.whole), custom_call_target="tpu_custom_call", output_to_operand_aliasing={{}: (2, {})} | custom-call | bytes 7340032 | tf_op jit(solution)/shard_map/pallas_call | solution.py:348
  (24 shorter events, 0.2 us)
Async XLA Ops:
  1.9 18.3 %collective-permute-start.3 = (bf16[128,2048]{1,0:T(8,128)(2,1)S(1)}, bf16[128,2048]{1,0:T(8,128)(2,1)S(1)}, u32[]{:S(2)}, u32[]{:S(2)}) collective-permute-start(bf16[128,2048]{1,0:T(8,128)(2,1)S(1)} %get-tuple-element.61.refs_3_), channel_id=1, source_target_pairs={{0,16},{2,10},{4,20},{6,14},{8,0},{10,26},{12,4},{14,30},{16,24},{... | collective-permute-start | bytes 1572872 | tf_op jit(solution)/shard_map/ppermute | solution.py:75
  6.0 14.2 %collective-permute-start.4 = (bf16[128,2048]{1,0:T(8,128)(2,1)S(1)}, bf16[128,2048]{1,0:T(8,128)(2,1)S(1)}, u32[]{:S(2)}, u32[]{:S(2)}) collective-permute-start(bf16[128,2048]{1,0:T(8,128)(2,1)S(1)} %get-tuple-element.61.refs_3_), channel_id=1, source_target_pairs={{0,4},{2,6},{4,0},{6,2},{8,12},{10,14},{12,8},{14,10},{16,20},{18,... | collective-permute-start | bytes 1572872 | tf_op jit(solution)/shard_map/ppermute | solution.py:75
  7.5 2.1 %collective-permute-start = (bf16[128,2048]{1,0:T(8,128)(2,1)S(1)}, bf16[128,2048]{1,0:T(8,128)(2,1)S(1)}, u32[]{:S(2)}, u32[]{:S(2)}) collective-permute-start(bf16[128,2048]{1,0:T(8,128)(2,1)S(1)} %get-tuple-element.58), channel_id=1, source_target_pairs={{0,2},{2,0},{4,6},{6,4},{8,10},{10,8},{12,14},{14,12},{16,18},{18,... | collective-permute-start | bytes 1572872 | tf_op jit(solution)/shard_map/ppermute | solution.py:75
  11.3 3.7 %collective-permute-start.5 = (f32[4,128]{1,0:T(4,128)S(1)}, f32[4,128]{1,0:T(4,128)S(1)}, u32[]{:S(2)}, u32[]{:S(2)}) collective-permute-start(f32[4,128]{1,0:T(4,128)S(1)} %pad_maximum_fusion.2), channel_id=1, source_target_pairs={{0,1},{1,0},{2,3},{3,2},{4,5},{5,4},{6,7},{7,6},{8,9},{9,8},{10,11... | collective-permute-start | bytes 6152 | tf_op jit(solution)/shard_map/ppermute | solution.py:18
  12.9 18.2 %collective-permute-start.1 = (bf16[128,2048]{1,0:T(8,128)(2,1)S(1)}, bf16[128,2048]{1,0:T(8,128)(2,1)S(1)}, u32[]{:S(2)}, u32[]{:S(2)}) collective-permute-start(bf16[128,2048]{1,0:T(8,128)(2,1)S(1)} %collective-permute-done.refs_4_), channel_id=1, source_target_pairs={{0,8},{2,18},{4,12},{6,22},{8,24},{10,2},{12,28},{14,6},{16,0},{18... | collective-permute-start | bytes 1572872 | tf_op jit(solution)/shard_map/ppermute | solution.py:75
  13.7 17.4 %collective-permute-start.2 = (bf16[128,2048]{1,0:T(8,128)(2,1)S(1)}, bf16[128,2048]{1,0:T(8,128)(2,1)S(1)}, u32[]{:S(2)}, u32[]{:S(2)}) collective-permute-start(bf16[128,2048]{1,0:T(8,128)(2,1)S(1)} %collective-permute-done.refs_4_), channel_id=1, source_target_pairs={{0,4},{2,6},{4,0},{6,2},{8,12},{10,14},{12,8},{14,10},{16,20},{18,... | collective-permute-start | bytes 1572872 | tf_op jit(solution)/shard_map/ppermute | solution.py:75
  20.2 1.2 %collective-permute-start.6 = (f32[1,4,128]{2,1,0:T(4,128)S(1)}, f32[1,4,128]{2,1,0:T(4,128)S(1)}, u32[]{:S(2)}, u32[]{:S(2)}) collective-permute-start(f32[1,4,128]{2,1,0:T(4,128)S(1)} %add_bitcast_fusion), channel_id=1, source_target_pairs={{0,2},{2,0},{4,6},{6,4},{8,10},{10,8},{12,14},{14,12},{16,18},{18,... | collective-permute-start | bytes 6152 | tf_op jit(solution)/shard_map/ppermute | solution.py:24
  21.4 9.3 %collective-permute-start.7 = (f32[2,4,128]{2,0,1:T(2,128)S(1)}, f32[2,4,128]{2,0,1:T(2,128)S(1)}, u32[]{:S(2)}, u32[]{:S(2)}) collective-permute-start(f32[2,4,128]{2,0,1:T(2,128)S(1)} %broadcast_select_fusion.3), channel_id=1, source_target_pairs={{0,8},{2,10},{4,12},{6,14},{8,0},{10,2},{12,4},{14,6},{16,24},{18,... | collective-permute-start | bytes 12296 | tf_op jit(solution)/shard_map/ppermute | solution.py:24
  23.6 21.7 %collective-permute-start.10 = (bf16[128,2048]{1,0:T(8,128)(2,1)S(1)}, bf16[128,2048]{1,0:T(8,128)(2,1)S(1)}, u32[]{:S(2)}, u32[]{:S(2)}) collective-permute-start(bf16[128,2048]{1,0:T(8,128)(2,1)S(1)} %collective-permute-done.3.refs_7_), channel_id=1, source_target_pairs={{0,16},{2,10},{4,20},{6,14},{8,0},{10,26},{12,4},{14,30},{16,24},{... | collective-permute-start | bytes 1572872 | tf_op jit(solution)/shard_map/ppermute | solution.py:75
  27.6 17.8 %collective-permute-start.11 = (bf16[128,2048]{1,0:T(8,128)(2,1)S(1)}, bf16[128,2048]{1,0:T(8,128)(2,1)S(1)}, u32[]{:S(2)}, u32[]{:S(2)}) collective-permute-start(bf16[128,2048]{1,0:T(8,128)(2,1)S(1)} %collective-permute-done.3.refs_7_), channel_id=1, source_target_pairs={{0,4},{2,6},{4,0},{6,2},{8,12},{10,14},{12,8},{14,10},{16,20},{18,... | collective-permute-start | bytes 1572872 | tf_op jit(solution)/shard_map/ppermute | solution.py:75
  31.2 12.6 %collective-permute-start.12 = (f32[2,2,4,128]{3,1,0,2:T(2,128)S(1)}, f32[2,2,4,128]{3,1,0,2:T(2,128)S(1)}, u32[]{:S(2)}, u32[]{:S(2)}) collective-permute-start(f32[2,2,4,128]{3,1,0,2:T(2,128)S(1)} %broadcast_select_fusion), channel_id=1, source_target_pairs={{0,4},{2,6},{4,0},{6,2},{8,12},{10,14},{12,8},{14,10},{16,20},{18,... | collective-permute-start | bytes 24584 | tf_op jit(solution)/shard_map/ppermute | solution.py:24
  32.4 23.9 %collective-permute-start.8 = (bf16[128,2048]{1,0:T(8,128)(2,1)S(1)}, bf16[128,2048]{1,0:T(8,128)(2,1)S(1)}, u32[]{:S(2)}, u32[]{:S(2)}) collective-permute-start(bf16[128,2048]{1,0:T(8,128)(2,1)S(1)} %collective-permute-done.1.refs_8_), channel_id=1, source_target_pairs={{0,8},{2,18},{4,12},{6,22},{8,24},{10,2},{12,28},{14,6},{16,0},{18... | collective-permute-start | bytes 1572872 | tf_op jit(solution)/shard_map/ppermute | solution.py:75
  33.3 23.0 %collective-permute-start.9 = (bf16[128,2048]{1,0:T(8,128)(2,1)S(1)}, bf16[128,2048]{1,0:T(8,128)(2,1)S(1)}, u32[]{:S(2)}, u32[]{:S(2)}) collective-permute-start(bf16[128,2048]{1,0:T(8,128)(2,1)S(1)} %collective-permute-done.1.refs_8_), channel_id=1, source_target_pairs={{0,4},{2,6},{4,0},{6,2},{8,12},{10,14},{12,8},{14,10},{16,20},{18,... | collective-permute-start | bytes 1572872 | tf_op jit(solution)/shard_map/ppermute | solution.py:75
  45.3 10.9 %collective-permute-start.13 = (f32[8,4,128]{2,0,1:T(8,128)S(1)}, f32[8,4,128]{2,0,1:T(8,128)S(1)}, u32[]{:S(2)}, u32[]{:S(2)}) collective-permute-start(f32[8,4,128]{2,0,1:T(8,128)S(1)} %bitcast.47), channel_id=1, source_target_pairs={{0,16},{2,18},{4,20},{6,22},{8,24},{10,26},{12,28},{14,30},{16,0},... | collective-permute-start | bytes 49160 | tf_op jit(solution)/shard_map/ppermute | solution.py:24
  47.8 25.1 %collective-permute-start.17 = (bf16[128,2048]{1,0:T(8,128)(2,1)S(1)}, bf16[128,2048]{1,0:T(8,128)(2,1)S(1)}, u32[]{:S(2)}, u32[]{:S(2)}) collective-permute-start(bf16[128,2048]{1,0:T(8,128)(2,1)S(1)} %collective-permute-done.10.refs_11_), channel_id=1, source_target_pairs={{0,16},{2,10},{4,20},{6,14},{8,0},{10,26},{12,4},{14,30},{16,24},{... | collective-permute-start | bytes 1572872 | tf_op jit(solution)/shard_map/ppermute | solution.py:75
  48.3 24.6 %collective-permute-start.18 = (bf16[128,2048]{1,0:T(8,128)(2,1)S(1)}, bf16[128,2048]{1,0:T(8,128)(2,1)S(1)}, u32[]{:S(2)}, u32[]{:S(2)}) collective-permute-start(bf16[128,2048]{1,0:T(8,128)(2,1)S(1)} %collective-permute-done.10.refs_11_), channel_id=1, source_target_pairs={{0,4},{2,6},{4,0},{6,2},{8,12},{10,14},{12,8},{14,10},{16,20},{18,... | collective-permute-start | bytes 1572872 | tf_op jit(solution)/shard_map/ppermute | solution.py:75
  56.3 19.4 %collective-permute-start.14 = (bf16[128,2048]{1,0:T(8,128)(2,1)S(1)}, bf16[128,2048]{1,0:T(8,128)(2,1)S(1)}, u32[]{:S(2)}, u32[]{:S(2)}) collective-permute-start(bf16[128,2048]{1,0:T(8,128)(2,1)S(1)} %collective-permute-done.8.refs_12_), channel_id=1, source_target_pairs={{0,8},{2,18},{4,12},{6,22},{8,24},{10,2},{12,28},{14,6},{16,0},{18... | collective-permute-start | bytes 1572872 | tf_op jit(solution)/shard_map/ppermute | solution.py:75
  58.2 17.5 %collective-permute-start.15 = (bf16[128,2048]{1,0:T(8,128)(2,1)S(1)}, bf16[128,2048]{1,0:T(8,128)(2,1)S(1)}, u32[]{:S(2)}, u32[]{:S(2)}) collective-permute-start(bf16[128,2048]{1,0:T(8,128)(2,1)S(1)} %collective-permute-done.8.refs_12_), channel_id=1, source_target_pairs={{0,4},{2,6},{4,0},{6,2},{8,12},{10,14},{12,8},{14,10},{16,20},{18,... | collective-permute-start | bytes 1572872 | tf_op jit(solution)/shard_map/ppermute | solution.py:75
  61.5 14.2 %collective-permute-start.16 = (bf16[896,2048]{1,0:T(8,128)(2,1)}, bf16[896,2048]{1,0:T(8,128)(2,1)S(1)}, u32[]{:S(2)}, u32[]{:S(2)}) collective-permute-start(bf16[896,2048]{1,0:T(8,128)(2,1)} %get-tuple-element.78), channel_id=1, source_target_pairs={{0,2},{2,0},{4,6},{6,4},{8,10},{10,8},{12,14},{14,12},{16,18},{18,... | collective-permute-start | bytes 11010056 | tf_op jit(solution)/shard_map/ppermute | solution.py:75
  75.7 13.3 %collective-permute-start.19 = (bf16[128,2048]{1,0:T(8,128)(2,1)S(1)}, bf16[128,2048]{1,0:T(8,128)(2,1)S(1)}, u32[]{:S(2)}, u32[]{:S(2)}) collective-permute-start(bf16[128,2048]{1,0:T(8,128)(2,1)S(1)} %collective-permute-done.18.refs_3_), channel_id=1, source_target_pairs={{0,16},{2,10},{4,20},{6,14},{8,0},{10,26},{12,4},{14,30},{16,24},{... | collective-permute-start | bytes 1572872 | tf_op jit(solution)/shard_map/ppermute | solution.py:75
  76.8 12.2 %collective-permute-start.20 = (bf16[128,2048]{1,0:T(8,128)(2,1)S(1)}, bf16[128,2048]{1,0:T(8,128)(2,1)S(1)}, u32[]{:S(2)}, u32[]{:S(2)}) collective-permute-start(bf16[128,2048]{1,0:T(8,128)(2,1)S(1)} %collective-permute-done.14.refs_6_), channel_id=1, source_target_pairs={{0,4},{2,6},{4,0},{6,2},{8,12},{10,14},{12,8},{14,10},{16,20},{18,... | collective-permute-start | bytes 1572872 | tf_op jit(solution)/shard_map/ppermute | solution.py:75
  91.5 7.1 %collective-permute-start.22 = (bf16[896,2048]{1,0:T(8,128)(2,1)S(1)}, bf16[896,2048]{1,0:T(8,128)(2,1)S(1)}, u32[]{:S(2)}, u32[]{:S(2)}) collective-permute-start(bf16[896,2048]{1,0:T(8,128)(2,1)S(1)} %get-tuple-element.107), channel_id=1, source_target_pairs={{0,2},{2,0},{4,6},{6,4},{8,10},{10,8},{12,14},{14,12},{16,18},{18,... | collective-permute-start | bytes 11010056 | tf_op jit(solution)/shard_map/ppermute | solution.py:393
  91.6 6.4 %collective-permute-start.21 = (f32[2048]{0:T(1024)S(1)}, f32[2048]{0:T(1024)S(1)}, u32[]{:S(2)}, u32[]{:S(2)}) collective-permute-start(f32[2048]{0:T(1024)S(1)} %bitcast.39), channel_id=1, source_target_pairs={{0,2},{2,0},{4,6},{6,4},{8,10},{10,8},{12,14},{14,12},{16,18},{18,... | collective-permute-start | bytes 24584 | tf_op jit(solution)/shard_map/ppermute | solution.py:393
  92.1 5.9 %copy-start = (bf16[4096]{0:T(1024)(128)(2,1)S(1)}, bf16[4096]{0:T(1024)(128)(2,1)}, u32[]{:S(2)}) copy-start(bf16[4096]{0:T(1024)(128)(2,1)} %param.10) | copy-start | bytes 24580
